TPU v7x, 128 devices: a whole 4x4x4 slice. The times are simulated.
128 devices in a mesh: ctx: 16 (over z, x), exp: 8 (over y, core).
Axes of the slice: x: 4, y: 4, z: 4, core: 2. Of those that a mesh axis runs over, the one named last changes fastest.
Arguments:
- tokens: bfloat16 [8, 2048, 768], P('exp', 'ctx'), may hold values from -6 to 6
- gain_attn: bfloat16 [768], P(('ctx', 'exp')), may hold values from 0.5 to 1.5
- w_qkv: bfloat16 [768, 2304], P(('ctx', 'exp')), may hold values from -0.21875 to 0.21875
- w_attn_out: bfloat16 [768, 768], P(('ctx', 'exp')), may hold values from -1.75 to 1.75
- rel_table: bfloat16 [32, 12], replicated, may hold values from -4 to 4
- gain_moe: bfloat16 [768], P(('ctx', 'exp')), may hold values from 0.5 to 1.5
- w_in: bfloat16 [128, 768, 1536], P(('ctx', 'exp')), may hold values from -0.21875 to 0.21875
- w_out: bfloat16 [128, 1536, 768], P(('ctx', 'exp')), may hold values from -0.109375 to 0.109375
- expert_ids: int32 [8, 2048, 2], P('exp', 'ctx'), may hold values from 0 to 63, all different within a row; in each aligned block of 128 rows (0 to 127, 128 to 255, ..., all dimensions but the last counted through in order) at most 8 rows name the same one
- gate_values: float32 [8, 2048, 2], P('exp', 'ctx'), may hold values from 0.25 to 1
- doc_ids: int32 [8, 2048], P('exp', 'ctx'), may hold values from 0 to 3, never falling along the last dimension, each value on 1 to 1984 neighbouring positions
- cotangent: bfloat16 [8, 2048, 768], P('exp', 'ctx'), may hold values from -6 to 6
Outputs:
- block_out: bfloat16 [8, 2048, 768], P('exp', 'ctx')
- input_grad: bfloat16 [8, 2048, 768], P('exp', 'ctx')
- gate_grad: float32 [8, 2048, 2], P('exp', 'ctx')
- gain_attn_grad: float32 [768], P(('ctx', 'exp'))
- qkv_grad: float32 [768, 2304], P(('ctx', 'exp'))
- attn_out_grad: float32 [768, 768], P(('ctx', 'exp'))
- table_grad: float32 [32, 12], replicated
- gain_moe_grad: float32 [768], P(('ctx', 'exp'))
- expert_in_grad: float32 [128, 768, 1536], P(('ctx', 'exp'))
- expert_out_grad: float32 [128, 1536, 768], P(('ctx', 'exp'))
Inputs may be any that keep to these rules, and one draw needn't show every extreme that they name: `expert_ids`: among the tokens of one device (128 in a row of a sequence) no expert is named more than 8 times, a bound that some block reaches; a token's two experts differ. `doc_ids`: document numbers never fall along a sequence, every number appears, and one document of each sequence holds exactly 1984 tokens.
All inputs are finite; a program needn't handle non-finite values.
Results may differ from a plain program's by a relative error of at most 0.024.
Values may be sent and summed in bfloat16 or wider, within the bound.
A program may use at most 192 MiB of HBM per device.

v0:
```python
import math

import jax
import jax.numpy as jnp
import numpy as np
from jax import lax
from jax.sharding import Mesh
from jax.sharding import PartitionSpec as P

D = 768
H = 12
HD = 64
BUCKETS = 32
CTX = ("ctx_0", "ctx_1")
EXP = ("exp_0", "exp_1")
CTX_EXP = ("ctx_0", "ctx_1", "exp_0", "exp_1")


norm_eps = 1e-06
bucket_edges = np.concatenate(
    [np.arange(1, 17), np.ceil(16.0 * 8.0 ** (np.arange(1, 16) / 16.0))]
).astype(np.int32)
largest_scores = lax.Precision.HIGHEST


def in_one_piece(arrays, axis, dim, along):
    widths = [math.prod(a.shape[along:]) for a in arrays]
    both = jnp.concatenate(
        [a.reshape(*a.shape[:along], w) for a, w in zip(arrays, widths)], axis=along
    )
    result = lax.all_gather(both, axis, axis=dim, tiled=True)
    pieces = jnp.split(result, [sum(widths[:k]) for k in range(1, len(widths))], axis=along)
    return tuple(
        (b.reshape(*result.shape[:along], *a.shape[along:]) for a, b in zip(arrays, pieces))
    )


def in_blocks(x, dim, devices):
    lengths = x.shape
    pieces = x.reshape(*lengths[:dim], devices, lengths[dim] // devices, *lengths[dim + 1 :])
    return jnp.moveaxis(pieces, dim, 0)


def sent_and_summed(x, axis, dim):
    devices = lax.axis_size(axis)
    pieces = lax.all_to_all(in_blocks(x, dim, devices), axis, 0, 0, tiled=True)
    return jnp.sum(pieces, axis=0)


def sum_in_two_steps(x, axes, dim):
    far, near = axes
    pieces = in_blocks(x, dim, lax.axis_size(far))
    nearer = sent_and_summed(pieces, near, dim + 1)
    arrived = lax.all_to_all(nearer, far, split_axis=0, concat_axis=0, tiled=True)
    return arrived.sum(axis=0)


def side_by_side(arrays, axis, dim, along):
    columns = [a.reshape(*a.shape[:along], -1) for a in arrays]
    both = jnp.concatenate(columns, axis=along)
    result, at, done = (sum_in_two_steps(both, axis, dim), 0, [])
    for a, column in zip(arrays, columns):
        share = result[..., at : at + column.shape[along]]
        done.append(share.reshape(*share.shape[:along], *a.shape[along:]))
        at += column.shape[along]
    return tuple(done)


def sent_to_all(x, axis):
    copies = jnp.broadcast_to(x, (lax.axis_size(axis), *x.shape))
    return lax.all_to_all(copies, axis, split_axis=0, concat_axis=0, tiled=True)


def over_copies(x, axis):
    return sent_to_all(x, axis).sum(axis=0)


def over_axes(x, axes):
    far, near = axes
    nearer = over_copies(x, near)
    return over_copies(nearer, far)


def scale_rows(values, gain):
    return values * lax.rsqrt(jnp.mean(values * values, axis=-1, keepdims=True) + norm_eps) * gain


def per_device(
    tokens,
    gain_attn,
    w_qkv,
    w_attn_out,
    rel_table,
    gain_moe,
    w_in,
    w_out,
    expert_ids,
    gate_values,
    doc_ids,
    cotangent,
):
    tok_rows = tokens.shape[1]
    ctx_count = lax.axis_size(CTX)
    exp_count = lax.axis_size(EXP)
    experts_all = ctx_count * exp_count // 2
    capacity = 4 * tok_rows // experts_all
    slot_count = experts_all * capacity
    ctx_place = lax.axis_index(CTX)
    gain_first, qkv_weight, attention_weight, gain_second = in_one_piece(
        (gain_attn, w_qkv, w_attn_out, gain_moe), CTX_EXP, 0, 1
    )
    gain_one = gain_first.astype(jnp.float32)
    gain_two = gain_second.astype(jnp.float32)
    inputs = tokens.reshape(tok_rows, D).astype(jnp.float32)
    normed_f, norm_one_back = jax.vjp(scale_rows, inputs, gain_one)
    normed = normed_f.astype(jnp.bfloat16)
    qkv_all = jnp.dot(normed, qkv_weight, preferred_element_type=jnp.float32).astype(jnp.bfloat16)
    queries = qkv_all[:, :D].reshape(tok_rows, H, HD)
    key_rows = qkv_all[:, D : 2 * D]
    value_rows = qkv_all[:, 2 * D :]
    doc_marks = doc_ids.reshape(tok_rows).astype(jnp.bfloat16)
    query_pos = ctx_place * tok_rows + jnp.arange(tok_rows, dtype=jnp.int32)
    bias_table = rel_table.astype(jnp.float32)
    edge_list = jnp.asarray(bucket_edges)
    bucket_ids = jnp.arange(BUCKETS, dtype=jnp.int32)

    def piece_layout(piece_docs, key_count):
        key_pos = jnp.arange(key_count, dtype=jnp.int32)
        distance = query_pos[:, None] - key_pos[None, :]
        bucket = jnp.sum((distance[:, :, None] >= edge_list).astype(jnp.int32), axis=2)
        one_hot = (bucket[:, :, None] == bucket_ids).astype(jnp.float32)
        added_bias = jnp.einsum("qkb,bh->hqk", one_hot, bias_table, precision=largest_scores)
        allowed = (distance >= 0) & (doc_marks[:, None] == piece_docs[None, :])
        return (one_hot, added_bias, allowed)

    piece = in_one_piece((key_rows, value_rows, doc_marks), CTX, 0, 1)
    key_count = piece[0].shape[0]
    row_max = jnp.full((H, tok_rows), -1e30, jnp.float32)
    row_sum = jnp.zeros((H, tok_rows), jnp.float32)
    accum_out = jnp.zeros((tok_rows, H, HD), jnp.float32)
    one_hot, added_bias, allowed = piece_layout(piece[2], key_count)
    key_heads = piece[0].reshape(key_count, H, HD)
    value_heads = piece[1].reshape(key_count, H, HD)
    scores = (
        jnp.einsum("qhd,khd->hqk", queries, key_heads, preferred_element_type=jnp.float32) * 0.125
        + added_bias
    )
    scores = jnp.where(allowed[None], scores, -1e30)
    new_max = jnp.maximum(row_max, jnp.max(scores, axis=2))
    weights_exp = jnp.where(allowed[None], jnp.exp(scores - new_max[:, :, None]), 0.0)
    fading = jnp.exp(row_max - new_max)
    row_sum = row_sum * fading + jnp.sum(weights_exp, axis=2)
    accum_out = accum_out * fading.T[:, :, None] + jnp.einsum(
        "hqk,khd->qhd",
        weights_exp.astype(jnp.bfloat16),
        value_heads,
        preferred_element_type=jnp.float32,
    )
    row_max, row_sum, accum_out = (new_max, row_sum, accum_out)
    log_total = row_max + jnp.log(row_sum)
    attn_float = accum_out / row_sum.T[:, :, None]
    attention_values = attn_float.reshape(tok_rows, D).astype(jnp.bfloat16)
    middle = inputs + jnp.dot(
        attention_values, attention_weight, preferred_element_type=jnp.float32
    )
    moe_float, norm_two_back = jax.vjp(scale_rows, middle, gain_two)
    moe_in = moe_float.astype(jnp.bfloat16)
    route_flat = expert_ids.reshape(tok_rows * 2)
    route_marks = (route_flat[:, None] == jnp.arange(experts_all, dtype=jnp.int32)[None, :]).astype(
        jnp.int32
    )
    earlier = jnp.cumsum(route_marks, axis=0) - route_marks
    slot_place = route_flat * capacity + jnp.sum(earlier * route_marks, axis=1)
    picks = (slot_place[:, None] == jnp.arange(slot_count, dtype=jnp.int32)[None, :]).astype(
        jnp.float32
    )
    gate_flat = gate_values.reshape(tok_rows * 2)
    combine_map = jnp.sum((picks * gate_flat[:, None]).reshape(tok_rows, 2, slot_count), axis=1)
    dispatch_map = jnp.sum(picks.reshape(tok_rows, 2, slot_count), axis=1)
    send_rows = jnp.einsum(
        "ts,td->sd", dispatch_map.astype(jnp.bfloat16), moe_in, preferred_element_type=jnp.float32
    ).astype(jnp.bfloat16)
    send_both = jnp.broadcast_to(
        send_rows.reshape(experts_all, 1, capacity, D), (experts_all, 2, capacity, D)
    ).reshape(2 * experts_all, capacity, D)
    recv_rows = lax.all_to_all(send_both, CTX_EXP, split_axis=0, concat_axis=0, tiled=True)
    first_half = w_in[0]
    second_half = w_out[0]
    recv_flat = recv_rows.reshape(-1, D)
    pre_act = jnp.dot(recv_flat, first_half, preferred_element_type=jnp.float32)
    gelu_vals, gelu_back = jax.vjp(jax.nn.gelu, pre_act)
    hidden = gelu_vals.astype(jnp.bfloat16)
    half_sums = jnp.dot(hidden, second_half, preferred_element_type=jnp.float32).reshape(
        2 * experts_all, capacity, D
    )
    returned = lax.all_to_all(
        half_sums.astype(jnp.bfloat16), CTX_EXP, split_axis=0, concat_axis=0, tiled=True
    ).astype(half_sums.dtype)
    expert_full = jnp.sum(returned.reshape(experts_all, 2, capacity, D), axis=1).reshape(
        slot_count, D
    )
    expert_back = expert_full.astype(jnp.bfloat16).astype(jnp.float32)
    block_out = middle + jnp.dot(combine_map, expert_back, precision=largest_scores)
    grad_out = cotangent.reshape(tok_rows, D).astype(jnp.float32)
    picked = jnp.dot(picks, expert_back, precision=largest_scores)
    gate_grad = jnp.sum(picked.reshape(tok_rows, 2, D) * grad_out[:, None, :], axis=2)
    slot_grads = jnp.einsum("ts,td->sd", combine_map, grad_out, precision=largest_scores).astype(
        jnp.bfloat16
    )
    grads_both = jnp.broadcast_to(
        slot_grads.reshape(experts_all, 1, capacity, D), (experts_all, 2, capacity, D)
    ).reshape(2 * experts_all, capacity, D)
    grad_recv = lax.all_to_all(grads_both, CTX_EXP, split_axis=0, concat_axis=0, tiled=True)
    grad_flat = grad_recv.reshape(-1, D)
    hidden_grad = jnp.einsum(
        "nd,fd->nf", grad_flat, second_half, preferred_element_type=jnp.float32
    )
    expert_out_grad = jnp.einsum(
        "nf,nd->fd", hidden, grad_flat, preferred_element_type=jnp.float32
    )[None]
    act_grad = gelu_back(hidden_grad)[0].astype(jnp.bfloat16)
    expert_in_grad = jnp.einsum(
        "nd,nf->df", recv_flat, act_grad, preferred_element_type=jnp.float32
    )[None]
    row_halves = jnp.einsum(
        "nf,df->nd", act_grad, first_half, preferred_element_type=jnp.float32
    ).reshape(2 * experts_all, capacity, D)
    home_halves = lax.all_to_all(
        row_halves.astype(jnp.bfloat16), CTX_EXP, split_axis=0, concat_axis=0, tiled=True
    ).astype(row_halves.dtype)
    home_grads = jnp.sum(home_halves.reshape(experts_all, 2, capacity, D), axis=1).reshape(
        slot_count, D
    )
    moe_in_grad = jnp.einsum("ts,sd->td", dispatch_map, home_grads, precision=largest_scores)
    middle_part, gain_two_grad = norm_two_back(moe_in_grad)
    middle_grad = grad_out + middle_part
    residual_branch_gradient = middle_grad.astype(jnp.bfloat16)
    attn_weight_grad = jnp.einsum(
        "td,te->de", attention_values, residual_branch_gradient, preferred_element_type=jnp.float32
    )
    out_grads = (
        jnp.einsum(
            "te,de->td",
            residual_branch_gradient,
            attention_weight,
            preferred_element_type=jnp.float32,
        )
        .astype(jnp.bfloat16)
        .reshape(tok_rows, H, HD)
    )
    delta_rows = jnp.sum(out_grads.astype(jnp.float32) * attn_float, axis=2).T
    piece = in_one_piece((key_rows, value_rows, doc_marks), CTX, 0, 1)
    key_count = piece[0].shape[0]
    query_grad = jnp.zeros((tok_rows, H, HD), jnp.float32)
    table_sum = jnp.zeros((BUCKETS, H), jnp.float32)
    one_hot, added_bias, allowed = piece_layout(piece[2], key_count)
    key_heads = piece[0].reshape(key_count, H, HD)
    value_heads = piece[1].reshape(key_count, H, HD)
    scores = (
        jnp.einsum("qhd,khd->hqk", queries, key_heads, preferred_element_type=jnp.float32) * 0.125
        + added_bias
    )
    soft_vals = jnp.where(allowed[None], jnp.exp(scores - log_total[:, :, None]), 0.0)
    value_dots = jnp.einsum(
        "qhd,khd->hqk", out_grads, value_heads, preferred_element_type=jnp.float32
    )
    score_grad = (soft_vals * (value_dots - delta_rows[:, :, None])).astype(jnp.bfloat16)
    query_grad = (
        query_grad
        + jnp.einsum("hqk,khd->qhd", score_grad, key_heads, preferred_element_type=jnp.float32)
        * 0.125
    )
    key_grad = (
        jnp.einsum("hqk,qhd->khd", score_grad, queries, preferred_element_type=jnp.float32) * 0.125
    )
    value_grad = jnp.einsum(
        "hqk,qhd->khd",
        soft_vals.astype(jnp.bfloat16),
        out_grads,
        preferred_element_type=jnp.float32,
    )
    piece_grad = jnp.concatenate(
        [key_grad.reshape(key_count, D), value_grad.reshape(key_count, D)], axis=1
    )
    key_value_grad = piece_grad
    table_sum = table_sum + jnp.einsum(
        "hqk,qkb->bh", score_grad.astype(jnp.float32), one_hot, precision=largest_scores
    )
    query_grad, key_value_grad, table_sum = (query_grad, key_value_grad, table_sum)
    own_key_grads = lax.psum_scatter(
        key_value_grad.astype(jnp.bfloat16), CTX, scatter_dimension=0, tiled=True
    )
    qkv_grads = jnp.concatenate(
        [query_grad.reshape(tok_rows, D).astype(jnp.bfloat16), own_key_grads], axis=1
    )
    qkv_weight_grad = jnp.einsum("td,te->de", normed, qkv_grads, preferred_element_type=jnp.float32)
    normed_grad = jnp.einsum("te,de->td", qkv_grads, qkv_weight, preferred_element_type=jnp.float32)
    input_part, gain_one_grad = norm_one_back(normed_grad)
    input_grad = middle_grad + input_part
    gain_attn_grad, qkv_grad, attn_out_grad, gain_moe_grad = side_by_side(
        (gain_one_grad, qkv_weight_grad, attn_weight_grad, gain_two_grad),
        (("ctx_0", "ctx_1", "exp_0"), "exp_1"),
        0,
        1,
    )
    table_grad = over_axes(table_sum, (("ctx_0", "ctx_1", "exp_0"), "exp_1"))
    return (
        block_out.reshape(1, tok_rows, D).astype(jnp.bfloat16),
        input_grad.reshape(1, tok_rows, D).astype(jnp.bfloat16),
        gate_grad.reshape(1, tok_rows, 2),
        gain_attn_grad,
        qkv_grad,
        attn_out_grad,
        table_grad,
        gain_moe_grad,
        expert_in_grad,
        expert_out_grad,
    )


def solution(mesh):
    torus = Mesh(mesh.devices.reshape(4, 4, 4, 2), ("ctx_0", "ctx_1", "exp_0", "exp_1"))
    in_specs = (
        P(EXP, CTX, None),
        P(CTX_EXP),
        P(CTX_EXP, None),
        P(CTX_EXP, None),
        P(),
        P(CTX_EXP),
        P(CTX_EXP, None, None),
        P(CTX_EXP, None, None),
        P(EXP, CTX, None),
        P(EXP, CTX, None),
        P(EXP, CTX),
        P(EXP, CTX, None),
    )
    out_specs = (
        P(EXP, CTX, None),
        P(EXP, CTX, None),
        P(EXP, CTX, None),
        P(CTX_EXP),
        P(CTX_EXP, None),
        P(CTX_EXP, None),
        P(),
        P(CTX_EXP),
        P(CTX_EXP, None, None),
        P(CTX_EXP, None, None),
    )
    return jax.shard_map(
        per_device, mesh=torus, in_specs=in_specs, out_specs=out_specs, check_vma=False
    )
```

profile of v0, /device:TPU:34, one launch (start us, length us, event | category | flops | bytes accessed | tf_op | source)
XLA Modules:
  0.0 625.3 jit_solution(14149657867443006154)
XLA Ops:
  12.9 67.1 %all-gather.6.cloned.1.call-done = bf16[128,6,3074]{2,1,0:T(8,128)(2,1)} async-done(((bf16[1,6,3074]{2,1,0:T(8,128)(2,1)}), bf16[128,6,3074]{2,1,0:T(8,128)(2,1)}) %all-gather.6.cloned.1.call-update) | async-done | bytes 4721680 | tf_op jit(solution)/shard_map/all_gather | solution.py:31
  80.0 9.9 %reshape.401 = bf16[768,3074]{1,0:T(8,128)(2,1)} reshape(bf16[128,6,3074]{2,1,0:T(8,128)(2,1)} %all-gather.6.cloned.1.call-done) | data formatting | bytes 9443328
  91.2 3.4 convolution_convert_fusion
  96.9 4.2 convert_reduce_fusion
  102.6 8.4 %fusion.1 = f32[128,2048,12]{0,2,1:T(8,128)} fusion(s32[128,2048]{0,1:T(8,128)S(1)} %copy.169, bf16[32,12]{0,1:T(8,128)(2,1)S(1)} %copy-done.22), kind=kOutput, calls=%fused_computation.2 | convolution fusion | flops 209715200 | bytes 13632256 | tf_op jit(solution)/shard_map/qkb,bh->hqk/dot_general | solution.py:132
  111.0 16.8 %copy.170 = f32[128,2048,12]{1,0,2:T(8,128)} copy(f32[128,2048,12]{0,2,1:T(8,128)} %fusion.1) | data formatting | bytes 25165824 | tf_op jit(solution)/shard_map/qkb,bh->hqk/dot_general | solution.py:132
  131.2 27.2 %all-gather.4.cloned.1.call-done = bf16[2048,1537]{1,0:T(8,128)(2,1)} async-done(((bf16[128,1537]{1,0:T(8,128)(2,1)}), bf16[2048,1537]{1,0:T(8,128)(2,1)}) %all-gather.4.cloned.1.call-update) | async-done | bytes 6295568 | tf_op jit(solution)/shard_map/all_gather | solution.py:31
  158.4 6.0 fusion.117
  164.4 5.3 copy.168
  171.5 8.2 %select_reduce_fusion = (f32[12,128]{1,0:T(8,128)S(1)}, f32[12,128,2048]{2,1,0:T(8,128)S(1)}) fusion(pred[128,2048]{1,0:T(8,128)(4,1)S(1)} %compare_and_fusion, f32[128,2048,12]{1,0,2:T(8,128)} %copy.170, bf16[128,12,64]{0,2,1:T(8,128)(2,1)S(1)} %bitcast.198, bf16[2048,12,64]{0,2,1:T(8,128)(2,1)} %bitcast.186), kind=kOutput, calls=%fused_computation.10 | convolution fusion | flops 415234560 | bytes 28776448 | tf_op jit(solution)/shard_map/qhd,khd->hqk/dot_general | solution.py:145
  179.8 3.5 fusion.5
  184.3 4.6 copy.171
  189.0 9.7 %fusion.118 = (bf16[128,12,64]{0,2,1:T(8,128)(2,1)S(1)}, f32[128,12,64]{0,2,1:T(8,128)}) fusion(f32[128,12]{0,1:T(8,128)S(1)} %bitcast_add_fusion.2, bf16[2048,12,64]{0,2,1:T(8,128)(2,1)} %bitcast.188, f32[12,128,2048]{2,1,0:T(8,128)} %copy-done.2, f32[12,128]{1,0:T(8,128)S(1)} %broadcast_maximum_fusion, pred[128,2048]{1,0:T(8,128)(4,1)S(1)} %compare_and_fusion, ...), kind=kOutput, calls=%fused_computation.162 | convolution fusion | flops 415531008 | bytes 16599040 | tf_op jit(solution)/shard_map/hqk,khd->qhd/dot_general | solution.py:153
  203.0 9.6 %all-to-all-start = ((bf16[128,8,768]{2,1,0:T(8,128)(2,1)}), bf16[128,8,768]{2,1,0:T(8,128)(2,1)}, u32[]{:S(2)}, u32[]{:S(2)}) async-start(bf16[128,8,768]{2,1,0:T(8,128)(2,1)} %bitcast.193), calls=%async_computation | async-start | bytes 3145728 | tf_op jit(solution)/shard_map/all_to_all | solution.py:186
  215.3 20.7 %all-to-all-done = bf16[128,8,768]{2,1,0:T(8,128)(2,1)} async-done(((bf16[128,8,768]{2,1,0:T(8,128)(2,1)}), bf16[128,8,768]{2,1,0:T(8,128)(2,1)}, u32[]{:S(2)}, u32[]{:S(2)}) %all-to-all-start) | async-done | bytes 1572896 | tf_op jit(solution)/shard_map/all_to_all | solution.py:186
  238.4 6.7 %all-to-all-start.2 = ((bf16[128,8,768]{2,1,0:T(8,128)(2,1)}), bf16[128,8,768]{2,1,0:T(8,128)(2,1)}, u32[]{:S(2)}, u32[]{:S(2)}) async-start(bf16[128,8,768]{2,1,0:T(8,128)(2,1)} %bitcast.192), calls=%async_computation.2 | async-start | bytes 3145728 | tf_op jit(solution)/shard_map/all_to_all | solution.py:213
  245.2 6.2 fusion.38
  251.4 17.1 %all-to-all-done.2 = bf16[128,8,768]{2,1,0:T(8,128)(2,1)} async-done(((bf16[128,8,768]{2,1,0:T(8,128)(2,1)}), bf16[128,8,768]{2,1,0:T(8,128)(2,1)}, u32[]{:S(2)}, u32[]{:S(2)}) %all-to-all-start.2) | async-done | bytes 1572896 | tf_op jit(solution)/shard_map/all_to_all | solution.py:213
  268.5 8.4 %fusion.13 = bf16[1024,1536]{1,0:T(8,128)(2,1)S(1)} fusion(f32[1024,1536]{1,0:T(8,128)} %fusion.38, bf16[1,1536,768]{2,1,0:T(8,128)(2,1)} %param.20, bf16[128,8,768]{2,1,0:T(8,128)(2,1)} %all-to-all-done.2), kind=kOutput, calls=%fused_computation.22 | convolution fusion | flops 2447376384 | bytes 13369344 | tf_op jit(solution)/shard_map/nd,fd->nf/dot_general | solution.py:215
  276.8 3.8 fusion.45
  281.5 28.9 %all_to_all.40 = bf16[128,8,768]{2,1,0:T(8,128)(2,1)S(1)} all-to-all(bf16[128,8,768]{2,1,0:T(8,128)(2,1)S(1)} %copy.182), channel_id=1, replica_groups=mesh['ctx_0'=4,'ctx_1'=4,'exp_0'=4,'exp_1'=2] {'ctx_0','ctx_1','exp_0','..., dimensions={0} | all-to-all | bytes 3145728 | tf_op jit(solution)/shard_map/all_to_all | solution.py:228
  315.3 8.9 %fusion.22 = bf16[12,64,2048]{2,1,0:T(8,128)(2,1)} fusion(bf16[128,12,64]{0,2,1:T(8,128)(2,1)S(1)} %bitcast.195, f32[12,128,2048]{2,1,0:T(8,128)} %copy-done.2, f32[12,128]{1,0:T(8,128)S(1)} %get-tuple-element.24, pred[128,2048]{1,0:T(8,128)(4,1)S(1)} %compare_and_fusion), kind=kOutput, calls=%fused_computation.35 | convolution fusion | flops 413663232 | bytes 16193536 | tf_op jit(solution)/shard_map/hqk,qhd->khd/dot_general | solution.py:276
  324.2 7.4 %multiply_convert_fusion = bf16[12,128,2048]{2,1,0:T(8,128)(2,1)S(1)} fusion(f32[12,128,2048]{2,1,0:T(8,128)} %copy-done.2, f32[12,128]{1,0:T(8,128)S(1)} %bitcast.204, f32[12,128]{1,0:T(8,128)S(1)} %get-tuple-element.24, pred[128,2048]{1,0:T(8,128)(4,1)S(1)} %compare_and_fusion, bf16[128,12,64]{0,2,1:T(8,128)(2,1)S(1)} %bitcast.196, ...), kind=kOutput, calls=%fused_computation.7 | convolution fusion | flops 418381824 | bytes 22491136 | tf_op jit(solution)/shard_map/qhd,khd->hqk/dot_general | solution.py:264
  331.6 2.7 copy-done.3
  334.3 2.7 multiply_convert_fusion.1
  337.0 4.7 copy.186
  341.6 4.6 copy.187
  346.3 6.0 pad_maximum_fusion
  354.0 4.1 fusion.116
  358.1 5.5 fusion.40
  365.6 13.1 %copy.196 = bf16[12,128,2048]{1,0,2:T(8,128)(2,1)} copy(bf16[12,128,2048]{2,1,0:T(8,128)(2,1)} %copy-done.3) | data formatting | bytes 12582912 | tf_op jit(solution)/shard_map/convert_element_type | solution.py:267
  378.7 7.3 %fusion.68 = f32[32,12]{0,1:T(8,128)S(1)} fusion(bf16[12,128,2048]{1,0,2:T(8,128)(2,1)} %copy.196, s32[128,2048]{0,1:T(8,128)S(1)} %copy-done.6), kind=kOutput, calls=%fused_computation.74 | convolution fusion | flops 209715200 | bytes 7341568 | tf_op jit(solution)/shard_map/hqk,qkb->bh/dot_general | solution.py:286
  386.1 3.7 all_to_all.41
  389.8 7.3 %all-to-all-start.1 = ((bf16[128,8,768]{2,1,0:T(8,128)(2,1)}), bf16[128,8,768]{2,1,0:T(8,128)(2,1)}, u32[]{:S(2)}, u32[]{:S(2)}) async-start(bf16[128,8,768]{2,1,0:T(8,128)(2,1)} %copy.178), calls=%async_computation.1 | async-start | bytes 3145728 | tf_op jit(solution)/shard_map/all_to_all | solution.py:196
  398.4 6.1 fusion.66
  409.6 33.1 %reduce-scatter.2.cloned.1.call-done = bf16[128,1536]{1,0:T(8,128)(2,1)} async-done(((bf16[2048,1536]{1,0:T(8,128)(2,1)}), bf16[128,1536]{1,0:T(8,128)(2,1)}) %reduce-scatter.2.cloned.1.call-update) | async-done | bytes 393232 | tf_op jit(solution)/shard_map/reduce_scatter | solution.py:290
  442.7 4.1 fusion.83
  450.2 5.0 fusion.76
  455.1 11.1 %concatenate.29 = f32[64,2,6,3074]{3,0,2,1:T(8,128)} concatenate(f32[64,2,6,1]{3,0,2,1:T(8,128)S(1)} %copy.193, f32[64,2,6,2304]{3,0,2,1:T(8,128)} %fusion.76, f32[64,2,6,768]{3,0,2,1:T(8,128)S(1)} %fusion.91, f32[64,2,6,1]{3,0,2,1:T(8,128)} %copy.194), dimensions={3} | concatenate | bytes 18886656 | tf_op jit(solution)/shard_map/concatenate | solution.py:60
  466.2 20.8 %all_to_all.42 = f32[2,64,6,3074]{3,1,2,0:T(8,128)} all-to-all(f32[2,64,6,3074]{3,1,2,0:T(8,128)} %bitcast.185), channel_id=1, replica_groups=mesh['ctx_0'=4,'ctx_1'=4,'exp_0'=4,'exp_1'=2] {'exp_1'}, dimensions={0} | all-to-all | bytes 18886656 | tf_op jit(solution)/shard_map/all_to_all | solution.py:46
  487.0 10.2 %all-to-all-start.7 = ((f32[64,1,384]{2,1,0:T(1,128)}), f32[64,1,384]{2,1,0:T(1,128)S(1)}, u32[]{:S(2)}, u32[]{:S(2)}) async-start(f32[64,1,384]{2,1,0:T(1,128)} %reshape.417), calls=%async_computation.8 | async-start | bytes 196608 | tf_op jit(solution)/shard_map/all_to_all | solution.py:71
  497.2 7.3 %reduce_sum.212 = f32[64,6,3074]{2,0,1:T(8,128)} reduce(f32[2,64,6,3074]{3,1,2,0:T(8,128)} %all_to_all.42, f32[]{:T(128)} %constant.26.clone.1), dimensions={0}, to_apply=%region_19.20 | reduce | flops 1180416 | bytes 14164996 | tf_op jit(solution)/shard_map/reduce_sum | solution.py:47
  504.5 8.1 %copy.195 = f32[64,6,3074]{2,1,0:T(8,128)} copy(f32[64,6,3074]{2,0,1:T(8,128)} %reduce_sum.212) | data formatting | bytes 9443328 | tf_op jit(solution)/shard_map/reduce_sum | solution.py:47
  512.5 11.0 %all-to-all-start.5 = ((f32[64,6,3074]{2,1,0:T(8,128)}), f32[64,6,3074]{2,1,0:T(8,128)}, u32[]{:S(2)}, u32[]{:S(2)}) async-start(f32[64,6,3074]{2,1,0:T(8,128)} %copy.195), calls=%async_computation.6 | async-start | bytes 13107200 | tf_op jit(solution)/shard_map/all_to_all | solution.py:54
  523.6 7.2 %convolution_bitcast_fusion.1 = f32[1,768,1536]{2,1,0:T(8,128)} fusion(bf16[1024,1536]{1,0:T(8,128)(2,1)} %copy-done.7, bf16[128,8,768]{2,1,0:T(8,128)(2,1)} %all-to-all-done), kind=kOutput, calls=%fused_computation.33 | convolution fusion | flops 2415919104 | bytes 9437184 | tf_op jit(solution)/shard_map/nd,nf->df/dot_general | solution.py:222
  530.8 9.2 %convolution_bitcast_fusion = f32[1,1536,768]{2,1,0:T(8,128)} fusion(bf16[128,8,768]{2,1,0:T(8,128)(2,1)} %all-to-all-done.2, f32[1024,1536]{1,0:T(8,128)} %fusion.38), kind=kOutput, calls=%fused_computation.32 | convolution fusion | flops 2430074880 | bytes 12582912 | tf_op jit(solution)/shard_map/nf,nd->fd/dot_general | solution.py:218
  545.7 67.4 %all-to-all-done.5 = f32[64,6,3074]{2,1,0:T(8,128)} async-done(((f32[64,6,3074]{2,1,0:T(8,128)}), f32[64,6,3074]{2,1,0:T(8,128)}, u32[]{:S(2)}, u32[]{:S(2)}) %all-to-all-start.5) | async-done | bytes 4721696 | tf_op jit(solution)/shard_map/all_to_all | solution.py:54
  613.1 3.3 reduce_sum.213
  (152 shorter events, 53.3 us)
Async XLA Ops:
  7.2 238.0 %copy-start = (bf16[1,768,1536]{2,1,0:T(8,128)(2,1)S(1)}, bf16[1,768,1536]{2,1,0:T(8,128)(2,1)}, u32[]{:S(2)}) copy-start(bf16[1,768,1536]{2,1,0:T(8,128)(2,1)} %param.19) | copy-start | bytes 7077892
  7.2 84.0 %copy-start.12 = (bf16[1,128,768]{2,1,0:T(8,128)(2,1)S(1)}, bf16[1,128,768]{2,1,0:T(8,128)(2,1)}, u32[]{:S(2)}) copy-start(bf16[1,128,768]{2,1,0:T(8,128)(2,1)} %param.13) | copy-start | bytes 589828
  7.2 72.8 %all-gather.6.cloned.1.call-start = ((), (), s32[]{:S(2)}) async-start(), calls=%async_computation.11 | async-start | bytes 6604800 | tf_op jit(solution)/shard_map/all_gather | solution.py:31
  10.5 147.9 %all-gather.4.cloned.1.call-start = ((), (), s32[]{:S(2)}) async-start(), calls=%async_computation.9 | async-start | bytes 7241728 | tf_op jit(solution)/shard_map/all_gather | solution.py:31
  12.9 81.7 %copy-start.28 = (f32[128]{0:T(128)}, f32[128]{0:T(128)S(1)}, u32[]{:S(2)}) copy-start(f32[128]{0:T(128)S(1)} %fusion.87) | copy-start | bytes 1540
  12.9 81.7 %copy-start.26 = (f32[128]{0:T(128)}, f32[128]{0:T(128)S(1)}, u32[]{:S(2)}) copy-start(f32[128]{0:T(128)S(1)} %fusion.109) | copy-start | bytes 1540
  89.9 6.4 %copy-start.25 = (s32[1,128,2]{1,2,0:T(2,128)S(1)}, s32[1,128,2]{1,2,0:T(2,128)}, u32[]{:S(2)}) copy-start(s32[1,128,2]{1,2,0:T(2,128)} %param.21) | copy-start | bytes 3076
  89.9 7.0 %copy-start.31 = (s32[31]{0:T(128)S(1)}, s32[31]{0:T(128)}, u32[]{:S(2)}) copy-start(s32[31]{0:T(128)} %constant.60.clone) | copy-start | bytes 376
  91.2 11.4 %copy-start.22 = (bf16[32,12]{0,1:T(8,128)(2,1)S(1)}, bf16[32,12]{0,1:T(8,128)(2,1)}, u32[]{:S(2)}) copy-start(bf16[32,12]{0,1:T(8,128)(2,1)} %param.17) | copy-start | bytes 2308
  94.6 0.8 copy-start.19
  102.6 8.4 %copy-start.5 = (s32[128,2048]{0,1:T(8,128)}, s32[128,2048]{0,1:T(8,128)S(1)}, u32[]{:S(2)}) copy-start(s32[128,2048]{0,1:T(8,128)S(1)} %copy.169) | copy-start | bytes 3145732
  129.0 35.3 %copy-start.23 = (s32[128,2]{0,1:T(2,128)}, s32[128,2]{0,1:T(2,128)S(1)}, u32[]{:S(2)}) copy-start(s32[128,2]{0,1:T(2,128)S(1)} %copy.176) | copy-start | bytes 3076
  129.9 82.7 %copy-start.8 = (f32[128,512]{1,0:T(8,128)}, f32[128,512]{1,0:T(8,128)S(1)}, u32[]{:S(2)}) copy-start(f32[128,512]{1,0:T(8,128)S(1)} %get-tuple-element.19) | copy-start | bytes 786436
  131.2 40.3 %copy-start.10 = (bf16[128,768]{0,1:T(8,128)(2,1)}, bf16[128,768]{0,1:T(8,128)(2,1)S(1)}, u32[]{:S(2)}) copy-start(bf16[128,768]{0,1:T(8,128)(2,1)S(1)} %copy.167) | copy-start | bytes 589828
  164.4 6.6 %copy-start.30 = (bf16[128]{0:T(256)(128)(2,1)S(1)}, bf16[128]{0:T(256)(128)(2,1)}, u32[]{:S(2)}) copy-start(bf16[128]{0:T(256)(128)(2,1)} %get-tuple-element.26) | copy-start | bytes 772
  179.7 4.6 copy-start.2
  189.0 9.7 %copy-start.13 = (bf16[1,128,768]{2,1,0:T(8,128)(2,1)S(1)}, bf16[1,128,768]{2,1,0:T(8,128)(2,1)}, u32[]{:S(2)}) copy-start(bf16[1,128,768]{2,1,0:T(8,128)(2,1)} %param.13) | copy-start | bytes 589828
  198.7 4.3 copy-start.17
  200.8 2.2 copy-start.32
  200.9 0.5 copy-start.20
  203.0 32.9 %all-to-all-start = ((bf16[128,8,768]{2,1,0:T(8,128)(2,1)}), bf16[128,8,768]{2,1,0:T(8,128)(2,1)}, u32[]{:S(2)}, u32[]{:S(2)}) async-start(bf16[128,8,768]{2,1,0:T(8,128)(2,1)} %bitcast.193), calls=%async_computation | async-start | bytes 3145728 | tf_op jit(solution)/shard_map/all_to_all | solution.py:186
  238.4 30.1 %all-to-all-start.2 = ((bf16[128,8,768]{2,1,0:T(8,128)(2,1)}), bf16[128,8,768]{2,1,0:T(8,128)(2,1)}, u32[]{:S(2)}, u32[]{:S(2)}) async-start(bf16[128,8,768]{2,1,0:T(8,128)(2,1)} %bitcast.192), calls=%async_computation.2 | async-start | bytes 3145728 | tf_op jit(solution)/shard_map/all_to_all | solution.py:213
  245.1 197.6 %reduce-scatter.2.cloned.1.call-start = ((), (), s32[]{:S(2)}) async-start(), calls=%async_computation.10 | async-start | bytes 6684672 | tf_op jit(solution)/shard_map/reduce_scatter | solution.py:290
  276.8 3.8 copy-start.7
  280.6 30.2 %copy-start.21 = (f32[128]{0:T(128)S(1)}, f32[128]{0:T(128)}, u32[]{:S(2)}) copy-start(f32[128]{0:T(128)} %copy-done.20) | copy-start | bytes 1540
  280.6 31.2 %copy-start.33 = (f32[128]{0:T(128)S(1)}, f32[128]{0:T(128)}, u32[]{:S(2)}) copy-start(f32[128]{0:T(128)} %copy-done.32) | copy-start | bytes 1540
  280.7 31.3 %copy-start.15 = (bf16[1,128,768]{2,1,0:T(8,128)(2,1)S(1)}, bf16[1,128,768]{2,1,0:T(8,128)(2,1)}, u32[]{:S(2)}) copy-start(bf16[1,128,768]{2,1,0:T(8,128)(2,1)} %param.24) | copy-start | bytes 589828
  315.3 8.9 %copy-start.4 = (bf16[2048,768]{0,1:T(8,128)(2,1)S(1)}, bf16[2048,768]{0,1:T(8,128)(2,1)}, u32[]{:S(2)}) copy-start(bf16[2048,768]{0,1:T(8,128)(2,1)} %copy.171) | copy-start | bytes 9437188
  324.2 10.1 %copy-start.11 = (bf16[128,768]{0,1:T(8,128)(2,1)S(1)}, bf16[128,768]{0,1:T(8,128)(2,1)}, u32[]{:S(2)}) copy-start(bf16[128,768]{0,1:T(8,128)(2,1)} %copy-done.10) | copy-start | bytes 589828
  331.6 2.7 copy-start.3
  352.3 0.9 copy-start.18
  365.6 13.1 %copy-start.6 = (s32[128,2048]{0,1:T(8,128)S(1)}, s32[128,2048]{0,1:T(8,128)}, u32[]{:S(2)}) copy-start(s32[128,2048]{0,1:T(8,128)} %copy-done.5) | copy-start | bytes 3145732
  389.8 76.4 %all-to-all-start.1 = ((bf16[128,8,768]{2,1,0:T(8,128)(2,1)}), bf16[128,8,768]{2,1,0:T(8,128)(2,1)}, u32[]{:S(2)}, u32[]{:S(2)}) async-start(bf16[128,8,768]{2,1,0:T(8,128)(2,1)} %copy.178), calls=%async_computation.1 | async-start | bytes 3145728 | tf_op jit(solution)/shard_map/all_to_all | solution.py:196
  398.4 44.3 %copy-start.14 = (bf16[1,128,768]{2,1,0:T(8,128)(2,1)S(1)}, bf16[1,128,768]{2,1,0:T(8,128)(2,1)}, u32[]{:S(2)}) copy-start(bf16[1,128,768]{2,1,0:T(8,128)(2,1)} %param.13) | copy-start | bytes 589828
  398.4 44.3 %copy-start.27 = (f32[128]{0:T(128)S(1)}, f32[128]{0:T(128)}, u32[]{:S(2)}) copy-start(f32[128]{0:T(128)} %copy-done.26) | copy-start | bytes 1540
  404.4 42.3 %copy-start.29 = (f32[128]{0:T(128)S(1)}, f32[128]{0:T(128)}, u32[]{:S(2)}) copy-start(f32[128]{0:T(128)} %copy-done.28) | copy-start | bytes 1540
  487.0 25.5 %all-to-all-start.7 = ((f32[64,1,384]{2,1,0:T(1,128)}), f32[64,1,384]{2,1,0:T(1,128)S(1)}, u32[]{:S(2)}, u32[]{:S(2)}) async-start(f32[64,1,384]{2,1,0:T(1,128)} %reshape.417), calls=%async_computation.8 | async-start | bytes 196608 | tf_op jit(solution)/shard_map/all_to_all | solution.py:71
  512.5 11.0 %copy-start.16 = (bf16[1,128,768]{2,1,0:T(8,128)(2,1)S(1)}, bf16[1,128,768]{2,1,0:T(8,128)(2,1)}, u32[]{:S(2)}) copy-start(bf16[1,128,768]{2,1,0:T(8,128)(2,1)} %param.24) | copy-start | bytes 589828
  512.5 100.6 %all-to-all-start.5 = ((f32[64,6,3074]{2,1,0:T(8,128)}), f32[64,6,3074]{2,1,0:T(8,128)}, u32[]{:S(2)}, u32[]{:S(2)}) async-start(f32[64,6,3074]{2,1,0:T(8,128)} %copy.195), calls=%async_computation.6 | async-start | bytes 13107200 | tf_op jit(solution)/shard_map/all_to_all | solution.py:54
  530.8 10.9 %copy-start.9 = (f32[128,512]{1,0:T(8,128)S(1)}, f32[128,512]{1,0:T(8,128)}, u32[]{:S(2)}) copy-start(f32[128,512]{1,0:T(8,128)} %copy-done.8) | copy-start | bytes 786436
  530.8 12.1 %copy-start.24 = (s32[128,2]{0,1:T(2,128)S(1)}, s32[128,2]{0,1:T(2,128)}, u32[]{:S(2)}) copy-start(s32[128,2]{0,1:T(2,128)} %copy-done.23) | copy-start | bytes 3076
  530.8 87.7 %copy-start.1 = (bf16[1,768,1536]{2,1,0:T(8,128)(2,1)S(1)}, bf16[1,768,1536]{2,1,0:T(8,128)(2,1)}, u32[]{:S(2)}) copy-start(bf16[1,768,1536]{2,1,0:T(8,128)(2,1)} %param.19) | copy-start | bytes 7077892
Sparse Core Ops, SparseCore 0:
  11.6 68.3 all-gather.5
  96.4 61.9 all-gather.3
  352.4 90.2 reduce-scatter.1
where the time goes:
time: 636 us; the launch traced here: 625 us
  waiting for transfers between devices  233 us (37%)
  matrix products  123 us (19%)
  local copies, waits for them, and re-layouts  115 us (18%)
  blocking collectives  53.4 us (8%)
  starting transfers between devices  44.9 us (7%)
  other arithmetic  41.6 us (7%)
  between operations  14.7 us (2%)
    all_gather x2, waiting for transfers between devices, in_one_piece(): result = lax.all_gather(both, axis, axis=dim, tiled=True)  94.3 us
    all_to_all x1, waiting for transfers between devices, sum_in_two_steps(): lax.all_to_all(nearer, far, split_axis=0, concat_axis=0, tiled=True)  67.4 us
    reduce_scatter x1, waiting for transfers between devices, per_device(): lax.psum_scatter(key_value_grad.astype(jnp.bfloat16), CTX, scatter_dimens...  33.1 us
    all_to_all x1, blocking collectives, per_device(): lax.all_to_all(row_halves.astype(jnp.bfloat16), CTX_EXP, split_axis=0, co...  28.9 us
    all_to_all x1, blocking collectives, sent_and_summed(): pieces = lax.all_to_all(in_blocks(x, dim, devices), axis, 0, 0, tiled=True)  20.8 us
    all_to_all x1, waiting for transfers between devices, per_device(): lax.all_to_all(send_both, CTX_EXP, split_axis=0, concat_axis=0, tiled=True)  20.7 us
    unnamed x76, local copies, waits for them, and re-layouts  17.3 us
    split x4, local copies, waits for them, and re-layouts, in_one_piece(): jnp.split(result, [sum(widths[:k]) for k in range(1, len(widths))], axis=...  17.2 us
  transfers between devices with their start and end apart: 8, of which 6 were waited for; matrix products, arithmetic and copies ran while one was open for 24% of the time, Pallas kernels for 0%

commit v1 on v0

v1 whole, which is shorter than its diff:
```python
import functools

import jax
import jax.numpy as jnp
import numpy as np
from jax import lax
from jax.experimental import pallas as pl
from jax.experimental.pallas import tpu as pltpu
from jax.sharding import Mesh
from jax.sharding import PartitionSpec as P

D = 768
H = 12
HD = 64
BUCKETS = 32
GROUPS = 4
GH = H // GROUPS
GW = GH * HD
TOK = 128
CTX = ("ctx_0", "ctx_1")
EXP = ("exp_0", "exp_1")
AXES = ("ctx_0", "ctx_1", "exp_0", "exp_1")
MESH = pl.DeviceIdType.MESH
ANY = pl.BlockSpec(memory_space=pl.ANY)
BF = jnp.bfloat16
F32 = jnp.float32

norm_eps = 1e-06
bucket_edges = [int(e) for e in np.concatenate(
    [np.arange(1, 17), np.ceil(16.0 * 8.0 ** (np.arange(1, 16) / 16.0))]
).astype(np.int32)]
masked = -1e30


def scale_rows(values, gain):
    return values * lax.rsqrt(jnp.mean(values * values, axis=-1, keepdims=True) + norm_eps) * gain


def place():
    return tuple(lax.axis_index(a) for a in AXES)


def chip_of(z, x, y):
    return (z * 4 + x) * 4 + y


def chip_peer(i, z, x, y):
    return (z + i // 16) % 4, (x + (i // 4) % 4) % 4, (y + i % 4) % 4


def loop(first, last, body):
    lax.fori_loop(first, last, lambda i, carry: (body(i), carry)[1], 0)


def signal(device):
    pl.semaphore_signal(
        pltpu.get_barrier_semaphore(), inc=1, device_id=device, device_id_type=MESH
    )


def arrive(count):
    pl.semaphore_wait(pltpu.get_barrier_semaphore(), count)


def push(src, dst, send, recv, device):
    pltpu.make_async_remote_copy(
        src_ref=src, dst_ref=dst, send_sem=send, recv_sem=recv, device_id=device, device_id_type=MESH
    ).start()


def keep(src, dst, sem):
    pltpu.make_async_copy(src, dst, sem).start()


def wait_bytes(ref, sem):
    pltpu.make_async_copy(ref, ref, sem).wait()


def comm_call(kernel, outs, scratch, collective_id, name):
    return pl.pallas_call(
        kernel,
        out_shape=outs,
        in_specs=None,
        out_specs=jax.tree.map(lambda _: ANY, outs),
        scratch_shapes=scratch,
        compiler_params=pltpu.CompilerParams(
            collective_id=collective_id, has_side_effects=True, vmem_limit_bytes=32 * 2**20
        ),
        name=name,
    )


def run_comm(kernel, args, outs, scratch, collective_id, name):
    return pl.pallas_call(
        kernel,
        out_shape=outs,
        in_specs=[ANY] * len(args),
        out_specs=jax.tree.map(lambda _: ANY, outs),
        scratch_shapes=scratch,
        compiler_params=pltpu.CompilerParams(
            collective_id=collective_id, has_side_effects=True, vmem_limit_bytes=32 * 2**20
        ),
        name=name,
    )(*args)


DMA = pltpu.SemaphoreType.DMA


def start_kernel(tok, wmsg, rows, tok_all, w_all, rows_all, send, recv, core_recv):
    z, x, y, c = place()
    me = chip_of(z, x, y)
    sib = (z, x, y, 1 - c)

    def greet(i):
        signal((*chip_peer(i, z, x, y), c))

    loop(1, 64, greet)
    signal(sib)
    arrive(64)
    for k in range(1, 4):
        push(tok, tok_all.at[z], send.at[0], recv.at[0], ((z + k) % 4, x, y, c))
    keep(tok, tok_all.at[z], recv.at[0])

    def weights(i):
        there = chip_peer(i, z, x, y)
        push(wmsg.at[there[0]], w_all.at[me, c], send.at[1], recv.at[1], (*there, c))

    loop(1, 64, weights)
    keep(wmsg.at[z], w_all.at[me, c], recv.at[1])

    def routes(i):
        there = chip_peer(i, z, x, y)
        push(rows.at[chip_of(*there)], rows_all.at[c, me], send.at[2], recv.at[2], (*there, c))

    loop(1, 64, routes)
    keep(rows.at[me], rows_all.at[c, me], recv.at[2])
    wait_bytes(w_all.at[:, c], recv.at[1])
    push(w_all.at[:, c], w_all.at[:, c], send.at[3], core_recv.at[0], sib)
    wait_bytes(rows_all.at[c], recv.at[2])
    push(rows_all.at[c], rows_all.at[c], send.at[4], core_recv.at[1], sib)
    wait_bytes(tok_all, recv.at[0])
    wait_bytes(w_all.at[:, 1 - c], core_recv.at[0])
    wait_bytes(rows_all.at[1 - c], core_recv.at[1])
    wait_bytes(tok_all.at[pl.ds(0, 3)], send.at[0])
    wait_bytes(w_all.at[pl.ds(0, 63), c], send.at[1])
    wait_bytes(rows_all.at[c, pl.ds(0, 63)], send.at[2])
    wait_bytes(w_all.at[:, c], send.at[3])
    wait_bytes(rows_all.at[c], send.at[4])


def start_exchange(tok, wmsg, rows):
    return run_comm(
        start_kernel,
        (tok, wmsg, rows),
        (
            jax.ShapeDtypeStruct((4, TOK, D), BF),
            jax.ShapeDtypeStruct((64, 2, 8, 3 * GW), BF),
            jax.ShapeDtypeStruct((2, 64, 8, D), BF),
        ),
        [DMA((5,)), DMA((3,)), DMA((2,))],
        0,
        "start_exchange",
    )


def dispatch_kernel(rows, rows_all, send, recv, core_recv):
    z, x, y, c = place()
    me = chip_of(z, x, y)
    sib = (z, x, y, 1 - c)

    def greet(i):
        signal((*chip_peer(i, z, x, y), c))

    loop(1, 64, greet)
    signal(sib)
    arrive(64)

    def routes(i):
        there = chip_peer(i, z, x, y)
        push(rows.at[chip_of(*there)], rows_all.at[c, me], send.at[0], recv.at[0], (*there, c))

    loop(1, 64, routes)
    keep(rows.at[me], rows_all.at[c, me], recv.at[0])
    wait_bytes(rows_all.at[c], recv.at[0])
    push(rows_all.at[c], rows_all.at[c], send.at[1], core_recv, sib)
    wait_bytes(rows_all.at[1 - c], core_recv)
    wait_bytes(rows_all.at[c, pl.ds(0, 63)], send.at[0])
    wait_bytes(rows_all.at[c], send.at[1])


def dispatch(rows):
    return run_comm(
        dispatch_kernel,
        (rows,),
        jax.ShapeDtypeStruct((2, 64, 8, D), BF),
        [DMA((2,)), DMA((1,)), DMA],
        1,
        "dispatch",
    )


def home_kernel(halves, home, own, other, total, send, recv, core_recv, own_sem):
    z, x, y, c = place()
    me = chip_of(z, x, y)
    sib = (z, x, y, 1 - c)

    def greet(i):
        signal((*chip_peer(i, z, x, y), c))

    loop(1, 64, greet)
    signal(sib)
    arrive(64)
    push(halves.at[1 - c], other, send.at[0], core_recv, sib)
    keep(halves.at[c], own, own_sem)
    wait_bytes(own, own_sem)
    wait_bytes(other, core_recv)

    def both(i):
        there = chip_peer(i, z, x, y)
        at = chip_of(*there)
        total[at] = (own[at].astype(F32) + other[at].astype(F32)).astype(BF)
        push(total.at[at], home.at[me], send.at[1], recv.at[0], (*there, c))

    loop(1, 64, both)
    total[me] = (own[me].astype(F32) + other[me].astype(F32)).astype(BF)
    keep(total.at[me], home.at[me], recv.at[0])
    wait_bytes(home, recv.at[0])
    wait_bytes(total.at[pl.ds(0, 63)], send.at[1])
    wait_bytes(other, send.at[0])


def go_home(halves, collective_id, name):
    rows = pltpu.VMEM((64, 8, D), BF)
    return run_comm(
        home_kernel,
        (halves,),
        jax.ShapeDtypeStruct((64, 8, D), BF),
        [rows, rows, rows, DMA((2,)), DMA((1,)), DMA, DMA],
        collective_id,
        name,
    )


def z_kernel(blocks, out, send, recv):
    z, x, y, c = place()
    for k in range(1, 4):
        signal(((z + k) % 4, x, y, c))
    arrive(3)
    for k in range(1, 4):
        there = (z + k) % 4
        push(blocks.at[there], out.at[z], send, recv, (there, x, y, c))
    keep(blocks.at[z], out.at[z], recv)
    wait_bytes(out, recv)
    wait_bytes(out.at[pl.ds(0, 3)], send)


def z_exchange(blocks, collective_id, name):
    return run_comm(
        z_kernel,
        (blocks,),
        jax.ShapeDtypeStruct(blocks.shape, blocks.dtype),
        [DMA, DMA],
        collective_id,
        name,
    )


def kv_kernel(kv, kv_all, send, recv):
    z, x, y, c = place()
    for k in range(1, 4):
        signal((z, (x + k) % 4, y, c))
    arrive(3)
    for k in range(1, 4):
        for b in range(4):
            push(kv.at[b], kv_all.at[b, x], send, recv, (z, (x + k) % 4, y, c))
    for b in range(4):
        keep(kv.at[b], kv_all.at[b, x], recv)
    wait_bytes(kv_all, recv)
    wait_bytes(kv_all.at[pl.ds(0, 3)], send)


def kv_gather(kv):
    return run_comm(
        kv_kernel,
        (kv,),
        jax.ShapeDtypeStruct((4, 4, TOK, 2 * GW), BF),
        [DMA, DMA],
        2,
        "kv_gather",
    )


def kv_back_kernel(dkv, branch, parts, branch_all, send, recv):
    z, x, y, c = place()
    for k in range(1, 4):
        signal((z, (x + k) % 4, y, c))
        signal(((z + k) % 4, x, y, c))
    arrive(6)
    for k in range(1, 4):
        there = (x + k) % 4
        for b in range(4):
            push(dkv.at[b, there], parts.at[x, b], send.at[0], recv.at[0], (z, there, y, c))
    for k in range(1, 4):
        push(branch, branch_all.at[z], send.at[1], recv.at[1], ((z + k) % 4, x, y, c))
    for b in range(4):
        keep(dkv.at[b, x], parts.at[x, b], recv.at[0])
    keep(branch, branch_all.at[z], recv.at[1])
    wait_bytes(parts, recv.at[0])
    wait_bytes(branch_all, recv.at[1])
    wait_bytes(parts.at[pl.ds(0, 3)], send.at[0])
    wait_bytes(branch_all.at[pl.ds(0, 3)], send.at[1])


def kv_back(dkv, branch):
    return run_comm(
        kv_back_kernel,
        (dkv, branch),
        (
            jax.ShapeDtypeStruct((4, 4, TOK, 2 * GW), BF),
            jax.ShapeDtypeStruct((4, TOK, D), BF),
        ),
        [DMA((2,)), DMA((2,))],
        3,
        "kv_back",
    )


def device_of(d):
    return d // 32, (d // 8) % 4, (d // 2) % 4, d % 2


def sums_kernel(
    qkv, att, small, qkv_out, att_out, small_out,
    qkv_in, att_in, small_in, qkv_sum, att_sum, small_sum, send, recv, out_sem,
):
    z, x, y, c = place()
    p = x * 8 + y * 2 + c
    me = z * 32 + p

    def peer(i):
        return (z, (x + i // 8) % 4, (y + (i // 2) % 4) % 4, (c + i % 2) % 2)

    loop(1, 32, lambda i: signal(peer(i)))
    source = me // 4

    def greet(k):
        from_me = (k == z) & (source == p)

        @pl.when(jnp.logical_not(from_me))
        def _():
            signal((k, source // 8, (source // 2) % 4, source % 2))

    loop(0, 4, greet)
    arrive(31 + 4 - jnp.where(source == p, 1, 0))

    def out(i):
        there = peer(i)
        q = there[1] * 8 + there[2] * 2 + there[3]
        push(qkv.at[q], qkv_in.at[p], send.at[0], recv.at[0], there)
        push(att.at[q], att_in.at[p], send.at[1], recv.at[1], there)
        push(small.at[q], small_in.at[p], send.at[2], recv.at[2], there)

    loop(1, 32, out)
    keep(qkv.at[p], qkv_in.at[p], recv.at[0])
    keep(att.at[p], att_in.at[p], recv.at[1])
    keep(small.at[p], small_in.at[p], recv.at[2])
    wait_bytes(qkv_in, recv.at[0])
    total = qkv_in[0].astype(F32)
    for q in range(1, 32):
        total = total + qkv_in[q].astype(F32)
    for k in range(4):
        qkv_sum[k, 0:6, :] = total[6 * k : 6 * k + 6]
        qkv_sum[k, 6:8, :] = jnp.zeros((2, 3 * GW), F32)
    wait_bytes(small_in, recv.at[2])
    small_total = small_in[0]
    for q in range(1, 32):
        small_total = small_total + small_in[q]
    small_sum[...] = small_total

    def final(k):
        d = 4 * p + k
        there = device_of(d)

        @pl.when(d != me)
        def _():
            push(qkv_sum.at[k], qkv_out.at[z], send.at[3], recv.at[3], there)
            push(small_sum, small_out.at[z], send.at[4], recv.at[4], there)

        @pl.when(d == me)
        def _():
            keep(qkv_sum.at[k], qkv_out.at[z], recv.at[3])
            keep(small_sum, small_out.at[z], recv.at[4])

    loop(0, 4, final)
    wait_bytes(att_in, recv.at[1])
    att_total = att_in[0].astype(F32)
    for q in range(1, 32):
        att_total = att_total + att_in[q].astype(F32)
    att_sum[...] = att_total
    keep(att_sum, att_out, out_sem)
    wait_bytes(att_sum, out_sem)
    wait_bytes(qkv_out, recv.at[3])
    wait_bytes(small_out, recv.at[4])
    wait_bytes(qkv_in.at[pl.ds(0, 31)], send.at[0])
    wait_bytes(att_in.at[pl.ds(0, 31)], send.at[1])
    wait_bytes(small_in.at[pl.ds(0, 31)], send.at[2])

    def sent(k):
        @pl.when(4 * p + k != me)
        def _():
            wait_bytes(qkv_sum.at[0], send.at[3])
            wait_bytes(small_sum, send.at[4])

    loop(0, 4, sent)


def weight_sums(qkv, att, small):
    return run_comm(
        sums_kernel,
        (qkv, att, small),
        (
            jax.ShapeDtypeStruct((4, 8, 3 * GW), F32),
            jax.ShapeDtypeStruct((8, D), F32),
            jax.ShapeDtypeStruct((4, 8, 128), F32),
        ),
        [
            pltpu.VMEM((32, 24, 3 * GW), BF),
            pltpu.VMEM((32, 8, D), BF),
            pltpu.VMEM((32, 8, 128), F32),
            pltpu.VMEM((4, 8, 3 * GW), F32),
            pltpu.VMEM((8, D), F32),
            pltpu.VMEM((8, 128), F32),
            DMA((5,)),
            DMA((5,)),
            DMA,
        ],
        4,
        "weight_sums",
    )


NT = (((1,), (1,)), ((), ()))
NN = (((1,), (0,)), ((), ()))
TN = (((0,), (0,)), ((), ()))


def dot(a, b, dims):
    return lax.dot_general(a, b, dims, preferred_element_type=F32)


def near_distance(dist):
    a = lax.broadcasted_iota(jnp.int32, (TOK, TOK), 0)
    b = lax.broadcasted_iota(jnp.int32, (TOK, TOK), 1)
    return dist * TOK + a - b


def table_kind(zq, zk, x, kx):
    return jnp.clip((zq - zk) * 4 + x - kx + 1, 0, 3)


def attn_forward_kernel(pos, tab, q, kv, qd, kd, out, p_out, bias, v_s, s_s):
    h = pl.program_id(0)
    x = pos[0]

    @pl.when(h == 0)
    def _():
        v_s[...] = kv[:, GW:]

    for dist in range(2):
        n = near_distance(dist)
        acc = jnp.full((TOK, TOK), tab[0, h], F32)
        for k, edge in enumerate(bucket_edges):
            acc = jnp.where(n >= edge, tab[k + 1, h], acc)
        bias[1 + dist] = jnp.where(n >= 0, acc, masked)
    bias[0] = jnp.full((TOK, TOK), masked, F32)
    far = tab[BUCKETS - 1, h]
    bias[3] = jnp.full((TOK, TOK), far, F32)
    head_cols = lax.broadcasted_iota(jnp.int32, (1, GW), 1) // HD == h
    for zk in range(4):
        qm = jnp.where(head_cols, q[zk * TOK :, :] * 0.125, 0.0).astype(BF)
        s_s[zk * TOK :, zk * 512 : (zk + 1) * 512] = dot(qm, kv[zk * 512 : (zk + 1) * 512, :GW], NT)
    for zq in range(4):
        rows = pl.ds(zq * TOK, TOK)
        docs = qd[rows, :]
        top = None
        for zk in range(zq + 1):
            for kx in range(4):
                cols = pl.ds((zk * 4 + kx) * TOK, TOK)
                s = s_s[rows, cols]
                if zk < zq - 1:
                    s = s + far
                else:
                    s = s + bias[table_kind(zq, zk, x, kx)]
                s = jnp.where(docs == kd[:, cols], s, masked)
                s_s[rows, cols] = s
                top = s if top is None else jnp.maximum(top, s)
        top = jnp.max(top, axis=1, keepdims=True)
        total = jnp.zeros((TOK, TOK), F32)
        for kb in range(4 * (zq + 1)):
            cols = pl.ds(kb * TOK, TOK)
            e = jnp.exp(s_s[rows, cols] - top)
            s_s[rows, cols] = e
            total = total + e
        inv = 1.0 / jnp.sum(total, axis=1, keepdims=True)
        for kb in range(4 * (zq + 1)):
            cols = pl.ds(kb * TOK, TOK)
            p_out[0, rows, cols] = (s_s[rows, cols] * inv).astype(BF)
        width = (zq + 1) * 512
        o = dot(p_out[0, rows, :width], v_s[:width, :], NN).astype(BF)

        @pl.when(h == 0)
        def _():
            out[rows, :] = o

        @pl.when(h > 0)
        def _():
            out[rows, :] = jnp.where(head_cols, o, out[rows, :])


def whole(shape):
    return pl.BlockSpec(shape, lambda h: (0,) * len(shape))


def attn_forward(pos, tab, q, kv, qd, kd):
    smem = pl.BlockSpec(memory_space=pltpu.SMEM)
    return pl.pallas_call(
        attn_forward_kernel,
        grid=(GH,),
        out_shape=(
            jax.ShapeDtypeStruct((512, GW), BF),
            jax.ShapeDtypeStruct((GH, 512, 2048), BF),
        ),
        in_specs=[
            smem, smem, whole((512, GW)), whole((2048, 2 * GW)), whole((512, 1)), whole((1, 2048)),
        ],
        out_specs=(whole((512, GW)), pl.BlockSpec((1, 512, 2048), lambda h: (h, 0, 0))),
        scratch_shapes=[
            pltpu.VMEM((4, TOK, TOK), F32),
            pltpu.VMEM((2048, GW), BF),
            pltpu.VMEM((512, 2048), F32),
        ],
        compiler_params=pltpu.CompilerParams(
            dimension_semantics=("arbitrary",), vmem_limit_bytes=40 * 2**20
        ),
        name="attn_forward",
    )(pos, tab, q, kv, qd, kd)


def attn_backward_kernel(pos, p, q, kv, do, dq, dkv, tab, v_s, dk_s, dv_s, dp_s, ds_s, near):
    h = pl.program_id(0)
    x = pos[0]

    @pl.when(h == 0)
    def _():
        v_s[...] = kv[:, GW:]

    head_cols = lax.broadcasted_iota(jnp.int32, (1, GW), 1) // HD == h
    for zk in range(4):
        dm = jnp.where(head_cols, do[zk * TOK :, :], 0.0).astype(BF)
        cols = pl.ds(zk * 512, 512)
        dp_s[zk * TOK :, cols] = dot(dm, v_s[cols, :], NT)
        dv = dot(p[0, zk * TOK :, cols], dm, TN)

        @pl.when(h == 0)
        def _():
            dv_s[cols, :] = dv

        @pl.when(h > 0)
        def _():
            dv_s[cols, :] += dv

    near[...] = jnp.zeros_like(near)
    for zq in range(4):
        rows = pl.ds(zq * TOK, TOK)
        acc = jnp.zeros((TOK, TOK), F32)
        for kb in range(4 * (zq + 1)):
            cols = pl.ds(kb * TOK, TOK)
            acc = acc + p[0, rows, cols].astype(F32) * dp_s[rows, cols]
        delta = jnp.sum(acc, axis=1, keepdims=True)
        far = jnp.zeros((TOK, TOK), F32)
        for zk in range(zq + 1):
            for kx in range(4):
                cols = pl.ds((zk * 4 + kx) * TOK, TOK)
                ds = (p[0, rows, cols].astype(F32) * (dp_s[rows, cols] - delta)).astype(BF)
                ds_s[rows, cols] = ds
                if zk < zq - 1:
                    far = far + ds.astype(F32)
                else:
                    near[table_kind(zq, zk, x, kx)] += ds.astype(F32)
        near[3] += far
        width = (zq + 1) * 512
        o = (dot(ds_s[rows, :width], kv[:width, :GW], NN) * 0.125).astype(BF)

        @pl.when(h == 0)
        def _():
            dq[rows, :] = o

        @pl.when(h > 0)
        def _():
            dq[rows, :] = jnp.where(head_cols, o, dq[rows, :])

    for zk in range(4):
        qm = jnp.where(head_cols, q[zk * TOK :, :] * 0.125, 0.0).astype(BF)
        cols = pl.ds(zk * 512, 512)
        dk = dot(ds_s[zk * TOK :, cols], qm, TN)

        @pl.when(h == 0)
        def _():
            dk_s[cols, :] = dk

        @pl.when(h > 0)
        def _():
            dk_s[cols, :] += dk

    for dist in range(2):
        n = near_distance(dist)
        held = near[1 + dist]
        bounds = [-(10**6)] + bucket_edges + [10**6]
        for b in range(BUCKETS):
            low, high = bounds[b], bounds[b + 1]
            if high <= dist * TOK - TOK + 1 or low > dist * TOK + TOK - 1:
                if dist == 0:
                    tab[0, b : b + 1, :] = jnp.zeros((1, TOK), F32)
                continue
            part = jnp.sum(jnp.where((n >= low) & (n < high), held, 0.0), axis=0, keepdims=True)
            if dist == 0:
                tab[0, b : b + 1, :] = part
            else:
                tab[0, b : b + 1, :] += part
    tab[0, BUCKETS - 1 :, :] += jnp.sum(near[3], axis=0, keepdims=True)

    @pl.when(h == GH - 1)
    def _():
        dkv[:, :GW] = dk_s[...].astype(BF)
        dkv[:, GW:] = dv_s[...].astype(BF)


def attn_backward(pos, p, q, kv, do):
    smem = pl.BlockSpec(memory_space=pltpu.SMEM)
    return pl.pallas_call(
        attn_backward_kernel,
        grid=(GH,),
        out_shape=(
            jax.ShapeDtypeStruct((512, GW), BF),
            jax.ShapeDtypeStruct((2048, 2 * GW), BF),
            jax.ShapeDtypeStruct((GH, BUCKETS, TOK), F32),
        ),
        in_specs=[
            smem,
            pl.BlockSpec((1, 512, 2048), lambda h: (h, 0, 0)),
            whole((512, GW)), whole((2048, 2 * GW)), whole((512, GW)),
        ],
        out_specs=(
            whole((512, GW)),
            whole((2048, 2 * GW)),
            pl.BlockSpec((1, BUCKETS, TOK), lambda h: (h, 0, 0)),
        ),
        scratch_shapes=[
            pltpu.VMEM((2048, GW), BF),
            pltpu.VMEM((2048, GW), F32),
            pltpu.VMEM((2048, GW), F32),
            pltpu.VMEM((512, 2048), F32),
            pltpu.VMEM((512, 2048), BF),
            pltpu.VMEM((4, TOK, TOK), F32),
        ],
        compiler_params=pltpu.CompilerParams(
            dimension_semantics=("arbitrary",), vmem_limit_bytes=48 * 2**20
        ),
        name="attn_backward",
    )(pos, p, q, kv, do)


def per_device(
    tokens,
    gain_attn,
    w_qkv,
    w_attn_out,
    rel_table,
    gain_moe,
    w_in,
    w_out,
    expert_ids,
    gate_values,
    doc_ids,
    cotangent,
):
    z, x, y, c = place()
    experts = 64
    capacity = 8
    slots = experts * capacity
    own_tokens = tokens.reshape(TOK, D)
    grad_bf = cotangent.reshape(TOK, D)
    grad_out = grad_bf.astype(F32)

    route = expert_ids.reshape(TOK * 2)
    marks = (route[:, None] == jnp.arange(experts, dtype=jnp.int32)[None, :]).astype(jnp.int32)
    earlier = jnp.cumsum(marks, axis=0) - marks
    slot = route * capacity + jnp.sum(earlier * marks, axis=1)
    slot_pair = slot.reshape(TOK, 2)
    gates = gate_values.reshape(TOK, 2)
    slot_ids = jnp.arange(slots, dtype=jnp.int32)
    pick_0 = slot_pair[:, 0][:, None] == slot_ids[None, :]
    pick_1 = slot_pair[:, 1][:, None] == slot_ids[None, :]
    pick = (pick_0 | pick_1).astype(BF)
    gate_of = jnp.where(pick_0, gates[:, :1], 0.0) + jnp.where(pick_1, gates[:, 1:], 0.0)
    gate_slot = jnp.sum(gate_of, axis=0)
    d_eo = (dot(pick, grad_bf, TN) * gate_slot[:, None]).astype(BF).reshape(experts, capacity, D)

    slab = w_qkv.reshape(6, 3, GROUPS, GW).transpose(2, 0, 1, 3).reshape(GROUPS, 6, 3 * GW)
    notes = jnp.concatenate(
        [
            gain_attn, gain_moe, jnp.zeros((116,), BF),
            doc_ids.reshape(TOK).astype(BF), jnp.zeros((3 * GW - 256,), BF),
        ]
    )
    notes = jnp.concatenate([notes[None], jnp.zeros((1, 3 * GW), BF)], axis=0)
    message = jnp.concatenate([slab, jnp.broadcast_to(notes, (GROUPS, 2, 3 * GW))], axis=1)
    attention_weight = lax.all_gather(w_attn_out, AXES, axis=0, tiled=True)
    tok_all, w_all, d_eo_all = start_exchange(own_tokens, message, d_eo)

    weight = w_all[:, :, :6, :].reshape(D, 3 * GW)
    gain_one = w_all[:, :, 6, 0:6].reshape(D).astype(F32)
    gain_two = w_all[:, :, 6, 6:12].reshape(D).astype(F32)
    doc_rows = w_all[:, :, 6, 128:256].reshape(16, 4, 2, TOK)
    doc_rows = lax.dynamic_slice(doc_rows, (0, y, c, 0), (16, 1, 1, TOK)).reshape(16, TOK).astype(F32)
    key_docs = doc_rows.reshape(1, 2048)
    query_docs = lax.dynamic_slice(doc_rows.reshape(4, 4, TOK), (0, x, 0), (4, 1, TOK)).reshape(512, 1)

    inputs_all = tok_all.reshape(512, D).astype(F32)
    normed = scale_rows(inputs_all, gain_one).astype(BF)
    qkv = dot(normed, weight, NN).astype(BF)
    queries = qkv[:, :GW]
    kv_all = kv_gather(qkv[:, GW:].reshape(4, TOK, 2 * GW)).reshape(2048, 2 * GW)
    table = lax.dynamic_slice(rel_table, (0, z * GH), (BUCKETS, GH)).astype(F32)
    pos = jnp.full((1,), x, jnp.int32)
    attn_part, probs = attn_forward(pos, table, queries, kv_all, query_docs, key_docs)
    attn = z_exchange(attn_part.reshape(4, TOK, GW), 5, "attn_exchange")
    attn = attn.transpose(1, 0, 2).reshape(TOK, D)

    inputs = own_tokens.astype(F32)
    middle = inputs + dot(attn, attention_weight, NN)
    moe_float, norm_two_back = jax.vjp(scale_rows, middle, gain_two)
    moe_in = moe_float.astype(BF)
    send_rows = dot(pick, moe_in, TN).astype(BF).reshape(experts, capacity, D)
    rows = dispatch(send_rows).reshape(-1, D)
    first_half = w_in[0]
    second_half = w_out[0]
    d_rows = d_eo_all.reshape(-1, D)
    hidden_grad = dot(d_rows, second_half, NT)
    pre_act = dot(rows, first_half, NN)
    gelu_vals, gelu_back = jax.vjp(jax.nn.gelu, pre_act)
    hidden = gelu_vals.astype(BF)
    act_grad = gelu_back(hidden_grad)[0].astype(BF)
    in_halves = dot(act_grad, first_half, NT).astype(BF).reshape(2, experts, capacity, D)
    home = go_home(in_halves, 6, "home_grads").reshape(slots, D)
    moe_in_grad = dot(pick, home, NN)
    middle_part, gain_two_grad = norm_two_back(moe_in_grad)
    middle_grad = grad_out + middle_part
    branch = middle_grad.astype(BF)
    d_attn = dot(branch, attention_weight, NT).astype(BF)
    d_attn = d_attn.reshape(TOK, GROUPS, GW).transpose(1, 0, 2)
    d_attn = z_exchange(d_attn, 7, "d_attn_exchange").reshape(512, GW)

    d_q, d_kv, table_part = attn_backward(pos, probs, queries, kv_all, d_attn)
    kv_parts, branch_all = kv_back(d_kv.reshape(4, 4, TOK, 2 * GW), branch)
    d_kv = jnp.sum(kv_parts.astype(F32), axis=0).astype(BF).reshape(512, 2 * GW)
    d_qkv = jnp.concatenate([d_q, d_kv], axis=1)
    normed_part = dot(d_qkv, weight, NT).astype(BF).reshape(4, TOK, D)
    normed_part = z_exchange(normed_part, 8, "normed_grads")
    normed_grad = jnp.sum(normed_part.astype(F32), axis=0)
    _, norm_one_back = jax.vjp(scale_rows, inputs, gain_one)
    input_part, gain_one_grad = norm_one_back(normed_grad)
    input_grad = middle_grad + input_part

    out_halves = dot(hidden, second_half, NN).astype(BF).reshape(2, experts, capacity, D)
    expert_out = go_home(out_halves, 9, "home_outputs").reshape(slots, D)
    both = jnp.concatenate([pick_0, pick_1], axis=0).astype(BF)
    picked = dot(both, expert_out, NN).reshape(2, TOK, D)
    block_out = middle + gates[:, :1] * picked[0] + gates[:, 1:] * picked[1]
    gate_grad = jnp.sum(picked * grad_out[None], axis=2).T
    expert_out_grad = dot(hidden, d_rows, TN)[None]
    expert_in_grad = dot(rows, act_grad, TN)[None]

    qkv_part = dot(normed, d_qkv, TN).astype(BF).reshape(32, 24, 3 * GW)
    att_part = dot(attn_part, branch_all.reshape(512, D), TN).astype(BF).reshape(32, 6, D)
    att_part = jnp.pad(att_part, ((0, 0), (0, 2), (0, 0)))
    table_sum = jnp.sum(table_part, axis=2).reshape(1, GH * BUCKETS)
    small = jnp.stack(
        [
            jnp.pad(gain_one_grad.reshape(32, 24), ((0, 0), (0, 104))),
            jnp.pad(gain_two_grad.reshape(32, 24), ((0, 0), (0, 104))),
            jnp.broadcast_to(jnp.pad(table_sum, ((0, 0), (0, 128 - GH * BUCKETS))), (32, 128)),
        ],
        axis=1,
    )
    small = jnp.pad(small, ((0, 0), (0, 5), (0, 0)))
    qkv_sum, att_sum, small_sum = weight_sums(qkv_part, att_part, small)
    qkv_grad = qkv_sum[:, :6, :].reshape(GROUPS, 6, 3, GW).transpose(1, 2, 0, 3).reshape(6, 3 * D)
    attn_out_grad = att_sum[:6]
    place_in = (y * 2 + c) % 4
    gains = lax.dynamic_slice(jnp.sum(small_sum[:, :2, :], axis=0), (0, place_in * 6), (2, 6))
    table_grad = (
        small_sum[:, 2, : GH * BUCKETS].reshape(GROUPS * GH, BUCKETS).T
    )
    return (
        block_out.reshape(1, TOK, D).astype(BF),
        input_grad.reshape(1, TOK, D).astype(BF),
        gate_grad.reshape(1, TOK, 2),
        gains[0],
        qkv_grad,
        attn_out_grad,
        table_grad,
        gains[1],
        expert_in_grad,
        expert_out_grad,
    )


def solution(mesh):
    torus = Mesh(mesh.devices.reshape(4, 4, 4, 2), AXES)
    in_specs = (
        P(EXP, CTX, None),
        P(AXES),
        P(AXES, None),
        P(AXES, None),
        P(),
        P(AXES),
        P(AXES, None, None),
        P(AXES, None, None),
        P(EXP, CTX, None),
        P(EXP, CTX, None),
        P(EXP, CTX),
        P(EXP, CTX, None),
    )
    out_specs = (
        P(EXP, CTX, None),
        P(EXP, CTX, None),
        P(EXP, CTX, None),
        P(AXES),
        P(AXES, None),
        P(AXES, None),
        P(),
        P(AXES),
        P(AXES, None, None),
        P(AXES, None, None),
    )
    return jax.shard_map(
        per_device, mesh=torus, in_specs=in_specs, out_specs=out_specs, check_vma=False
    )
```

time: 636 us -> 368 us (0.58)
  the two profiles are of different devices: /device:TPU:34 before, /device:TPU:1 now
where the time goes in v1:
time: 368 us; the launch traced here: 366 us
  Pallas kernels  237 us (64%)
  matrix products  49.1 us (13%)
  local copies, waits for them, and re-layouts  47.8 us (13%)
  other arithmetic  17.1 us (5%)
  between operations  14.8 us (4%)
    pallas_call x10, Pallas kernels, run_comm(): pl.pallas_call(kernel, out_shape=outs, in_specs=[ANY] * len(args), out_sp...  206 us
    dot_general x16, matrix products, dot(): return lax.dot_general(a, b, dims, preferred_element_type=F32)  49.1 us
    unnamed x104, local copies, waits for them, and re-layouts  22.4 us
    pallas_call x1, Pallas kernels, attn_backward(): pl.pallas_call(attn_backward_kernel, grid=(GH,), out_shape=(jax.ShapeDtyp...  21.1 us
    pallas_call x1, Pallas kernels, attn_forward(): pl.pallas_call(attn_forward_kernel, grid=(GH,), out_shape=(jax.ShapeDtype...  9.47 us
  transfers between devices with their start and end apart: 1, of which 0 were waited for; matrix products, arithmetic and copies ran while one was open for 9% of the time, Pallas kernels for 21%

profile of v1, /device:TPU:1, one launch (start us, length us, event | category | flops | bytes accessed | tf_op | source)
XLA Modules:
  0.0 366.2 jit_solution(17606047953132969145)
XLA Ops:
  9.7 1.4 concatenate.15
  14.4 1.4 fusion.25.rows
  16.8 40.4 %start_exchange.1 = (bf16[4,128,768]{2,1,0:T(8,128)(2,1)S(1)}, bf16[64,2,8,576]{3,2,1,0:T(8,128)(2,1)S(1)}, bf16[2,64,8,768]{3,2,1,0:T(8,128)(2,1)S(1)}) custom-call(bf16[128,768]{1,0:T(8,128)(2,1)S(1)} %bitcast.167, bf16[4,8,576]{2,1,0:T(8,128)(2,1)S(1)} %pad_maximum_fusion.3.wmsg, bf16[64,8,768]{2,1,0:T(8,128)(2,1)S(1)} %fusion.25.rows), custom_call_target="tpu_custom_call" | custom-call | tf_op jit(solution)/shard_map/start_exchange/pallas_call | solution.py:94
  57.3 1.2 copy-done.20
  58.5 1.1 copy-done.11
  59.5 1.0 convert_reduce_fusion.1
  60.5 3.0 reshape.269
  64.8 2.0 convolution_convert_fusion.3
  68.4 1.7 slice.74
  73.2 21.9 %kv_gather.1 = bf16[4,4,128,384]{3,2,1,0:T(8,128)(2,1)S(1)} custom-call(bf16[4,128,384]{2,1,0:T(8,128)(2,1)S(1)} %bitcast.173), custom_call_target="tpu_custom_call" | custom-call | tf_op jit(solution)/shard_map/kv_gather/pallas_call | solution.py:94
  95.1 1.1 copy-done.1
  96.3 1.5 copy.87
  99.1 1.5 copy.89.qd
  101.3 1.4 copy-done.2
  104.6 9.5 %attn_forward.1 = (bf16[512,192]{1,0:T(8,128)(2,1)S(1)}, bf16[3,512,2048]{2,1,0:T(8,128)(2,1)S(1)}) custom-call(s32[1]{0:T(128)} %bitcast.1.pos, f32[32,3]{1,0:T(8,128)S(1)} %convert_element_type.148.tab, bf16[512,192]{1,0:T(8,128)(2,1)S(1)} %copy-done.9, bf16[2048,384]{1,0:T(8,128)(2,1)S(1)} %bitcast.163, f32[512,1]{1,0:T(8,128)S(1)} %copy-done.15, ...), custom_call_target="tpu_custom_call" | custom-call | tf_op jit(solution)/shard_map/attn_forward/pallas_call | solution.py:527
  114.1 2.6 copy-done.5
  116.8 6.4 %attn_exchange.1 = bf16[4,128,192]{2,1,0:T(8,128)(2,1)S(1)} custom-call(bf16[4,128,192]{2,1,0:T(8,128)(2,1)S(1)} %bitcast.177), custom_call_target="tpu_custom_call" | custom-call | tf_op jit(solution)/shard_map/attn_exchange/pallas_call | solution.py:94
  123.9 1.8 copy.90
  127.3 1.5 iota_compare_fusion
  129.6 1.9 fusion.24
  131.5 3.2 reshape.302
  134.7 2.0 multiply_reduce_fusion.3
  137.2 21.1 %dispatch.1 = bf16[2,64,8,768]{3,2,1,0:T(8,128)(2,1)S(1)} custom-call(bf16[64,8,768]{2,1,0:T(8,128)(2,1)S(1)} %fusion.26.rows), custom_call_target="tpu_custom_call" | custom-call | tf_op jit(solution)/shard_map/dispatch/pallas_call | solution.py:94
  158.3 2.6 fusion.15
  160.9 4.8 %fusion.20 = bf16[1024,768]{1,0:T(8,128)(2,1)} fusion(bf16[1,1536,768]{2,1,0:T(8,128)(2,1)S(1)} %copy-done, f32[1024,1536]{1,0:T(8,128)S(1)} %fusion.15), kind=kOutput, calls=%fused_computation.21 | convolution fusion | flops 2430861312 | bytes 10223616 | tf_op jit(solution)/shard_map/dot_general | solution.py:449
  165.8 6.3 %fusion.6 = bf16[1024,1536]{1,0:T(8,128)(2,1)S(1)} fusion(f32[1024,1536]{1,0:T(8,128)S(1)} %fusion.15, bf16[1024,768]{1,0:T(8,128)(2,1)S(1)} %bitcast.182, bf16[1,1536,768]{2,1,0:T(8,128)(2,1)S(1)} %copy-done), kind=kOutput, calls=%fused_computation.8 | convolution fusion | flops 2447376384 | bytes 13369344 | tf_op jit(solution)/shard_map/dot_general | solution.py:449
  172.1 2.6 fusion.17
  174.8 21.3 %home_grads.1 = bf16[64,8,768]{2,1,0:T(8,128)(2,1)S(1)} custom-call(bf16[2,64,8,768]{3,2,1,0:T(8,128)(2,1)S(1)} %bitcast.172), custom_call_target="tpu_custom_call" | custom-call | tf_op jit(solution)/shard_map/home_grads/pallas_call | solution.py:94
  199.1 6.1 %d_attn_exchange.1 = bf16[4,128,192]{2,1,0:T(8,128)(2,1)S(1)} custom-call(bf16[4,128,192]{2,1,0:T(8,128)(2,1)S(1)} %bitcast.175), custom_call_target="tpu_custom_call" | custom-call | tf_op jit(solution)/shard_map/d_attn_exchange/pallas_call | solution.py:94
  205.2 1.4 copy-done.3
  206.6 21.1 %attn_backward.1 = (bf16[512,192]{1,0:T(8,128)(2,1)S(1)}, bf16[2048,384]{1,0:T(8,128)(2,1)S(1)}, f32[3,32,128]{2,1,0:T(8,128)S(1)}) custom-call(s32[1]{0:T(128)} %bitcast.1.pos, bf16[3,512,2048]{2,1,0:T(8,128)(2,1)} %copy-done.5, bf16[512,192]{1,0:T(8,128)(2,1)S(1)} %copy-done.10, bf16[2048,384]{1,0:T(8,128)(2,1)S(1)} %bitcast.164, ...), custom_call_target="tpu_custom_call" | custom-call | tf_op jit(solution)/shard_map/attn_backward/pallas_call | solution.py:641
  227.7 19.0 %kv_back.1 = (bf16[4,4,128,384]{3,2,1,0:T(8,128)(2,1)S(1)}, bf16[4,128,768]{2,1,0:T(8,128)(2,1)S(1)}) custom-call(bf16[4,4,128,384]{3,2,1,0:T(8,128)(2,1)S(1)} %bitcast.171, bf16[128,768]{1,0:T(8,128)(2,1)S(1)} %fusion.70.branch), custom_call_target="tpu_custom_call" | custom-call | tf_op jit(solution)/shard_map/kv_back/pallas_call | solution.py:94
  246.8 1.1 copy-done.13
  248.8 1.7 reduce_sum.155
  250.5 2.2 convolution_convert_fusion.1
  252.7 9.5 %normed_grads.1 = bf16[4,128,768]{2,1,0:T(8,128)(2,1)S(1)} custom-call(bf16[4,128,768]{2,1,0:T(8,128)(2,1)S(1)} %bitcast.178), custom_call_target="tpu_custom_call" | custom-call | tf_op jit(solution)/shard_map/normed_grads/pallas_call | solution.py:94
  263.1 2.9 convolution_convert_fusion
  266.0 2.3 copy.93
  268.2 2.2 convolution_convert_fusion.4
  270.5 1.8 reshape.290
  272.3 1.1 pad.22.att
  274.0 1.2 copy-done.8
  275.2 34.1 %weight_sums.1 = (f32[4,8,576]{2,1,0:T(8,128)S(1)}, f32[8,768]{1,0:T(8,128)S(1)}, f32[4,8,128]{2,1,0:T(8,128)S(1)}) custom-call(bf16[32,24,576]{2,1,0:T(8,128)(2,1)S(1)} %bitcast.168, bf16[32,8,768]{2,1,0:T(8,128)(2,1)S(1)} %pad.22.att, f32[32,8,128]{2,1,0:T(8,128)S(1)} %select_maximum_fusion.small), custom_call_target="tpu_custom_call" | custom-call | tf_op jit(solution)/shard_map/weight_sums/pallas_call | solution.py:94
  309.3 7.3 %convolution_bitcast_fusion.1 = f32[1,768,1536]{2,1,0:T(8,128)} fusion(bf16[1024,768]{1,0:T(8,128)(2,1)} %bitcast.166, bf16[1024,1536]{1,0:T(8,128)(2,1)} %copy-done.27), kind=kOutput, calls=%fused_computation.11 | convolution fusion | flops 2415919104 | bytes 9437184 | tf_op jit(solution)/shard_map/dot_general | solution.py:449
  316.6 8.8 %convolution_bitcast_fusion = f32[1,1536,768]{2,1,0:T(8,128)} fusion(bf16[1024,768]{1,0:T(8,128)(2,1)S(1)} %bitcast.183, f32[1024,1536]{1,0:T(8,128)} %copy-done.49), kind=kOutput, calls=%fused_computation.10 | convolution fusion | flops 2430074880 | bytes 12582912 | tf_op jit(solution)/shard_map/dot_general | solution.py:449
  325.9 26.2 %home_outputs.1 = bf16[64,8,768]{2,1,0:T(8,128)(2,1)S(1)} custom-call(bf16[2,64,8,768]{3,2,1,0:T(8,128)(2,1)S(1)} %bitcast.170), custom_call_target="tpu_custom_call" | custom-call | tf_op jit(solution)/shard_map/home_outputs/pallas_call | solution.py:94
  354.3 2.1 fusion.27
  356.4 2.3 fusion.46
  (165 shorter events, 28.9 us)
Async XLA Ops:
  7.2 153.7 %copy-start = (bf16[1,1536,768]{2,1,0:T(8,128)(2,1)S(1)}, bf16[1,1536,768]{2,1,0:T(8,128)(2,1)}, u32[]{:S(2)}) copy-start(bf16[1,1536,768]{2,1,0:T(8,128)(2,1)} %param.19) | copy-start | bytes 7077892
  7.2 124.3 %all-gather.3.cloned.1.call-start = ((), (), s32[]{:S(2)}) async-start(), calls=%async_computation | async-start | bytes 1585152 | tf_op jit(solution)/shard_map/all_gather | solution.py:719
  12.9 3.0 copy-start.44
  12.9 3.0 copy-start.45
  14.2 1.7 copy-start.35
  14.2 1.7 copy-start.37
  15.9 0.9 copy-start.6
  57.3 1.2 copy-start.20
  58.5 1.1 copy-start.11
  63.7 3.1 copy-start.31
  67.5 59.2 %copy-start.7 = (bf16[1,128,768]{2,1,0:T(8,128)(2,1)S(1)}, bf16[1,128,768]{2,1,0:T(8,128)(2,1)}, u32[]{:S(2)}) copy-start(bf16[1,128,768]{2,1,0:T(8,128)(2,1)} %param.12) | copy-start | bytes 589828
  68.4 60.4 %copy-start.28 = (bf16[1,128,768]{2,1,0:T(8,128)(2,1)S(1)}, bf16[1,128,768]{2,1,0:T(8,128)(2,1)}, u32[]{:S(2)}) copy-start(bf16[1,128,768]{2,1,0:T(8,128)(2,1)} %param.23) | copy-start | bytes 589828
  72.2 1.0 copy-start.14
  95.1 1.1 copy-start.1
  101.3 1.4 copy-start.2
  102.7 0.9 copy-start.9
  103.7 0.9 copy-start.15
  114.1 2.6 copy-start.5
  116.8 6.5 %copy-start.17 = (bf16[512,192]{1,0:T(8,128)(2,1)}, bf16[512,192]{1,0:T(8,128)(2,1)S(1)}, u32[]{:S(2)}) copy-start(bf16[512,192]{1,0:T(8,128)(2,1)S(1)} %get-tuple-element.25) | copy-start | bytes 589828
  126.7 71.0 %copy-start.33 = (f32[768]{0:T(1024)}, f32[768]{0:T(1024)S(1)}, u32[]{:S(2)}) copy-start(f32[768]{0:T(1024)S(1)} %reshape.299) | copy-start | bytes 9220
  129.6 7.1 %copy-start.36 = (s32[128]{0:T(128)S(1)}, s32[128]{0:T(128)}, u32[]{:S(2)}) copy-start(s32[128]{0:T(128)} %copy-done.35) | copy-start | bytes 1540
  129.6 7.1 %copy-start.38 = (s32[128]{0:T(128)S(1)}, s32[128]{0:T(128)}, u32[]{:S(2)}) copy-start(s32[128]{0:T(128)} %copy-done.37) | copy-start | bytes 1540
  134.7 23.6 %copy-start.48 = (bf16[1,768,1536]{2,1,0:T(8,128)(2,1)S(1)}, bf16[1,768,1536]{2,1,0:T(8,128)(2,1)}, u32[]{:S(2)}) copy-start(bf16[1,768,1536]{2,1,0:T(8,128)(2,1)} %param.18) | copy-start | bytes 7077892
  136.6 61.1 %copy-start.24 = (f32[128,768]{1,0:T(8,128)}, f32[128,768]{1,0:T(8,128)S(1)}, u32[]{:S(2)}) copy-start(f32[128,768]{1,0:T(8,128)S(1)} %get-tuple-element.53) | copy-start | bytes 1179652
  136.7 61.1 %copy-start.40 = (f32[128]{0:T(128)}, f32[128]{0:T(128)S(1)}, u32[]{:S(2)}) copy-start(f32[128]{0:T(128)S(1)} %fusion.64) | copy-start | bytes 1540
  158.3 2.6 copy-start.4
  160.9 4.9 %copy-start.49 = (f32[1024,1536]{1,0:T(8,128)}, f32[1024,1536]{1,0:T(8,128)S(1)}, u32[]{:S(2)}) copy-start(f32[1024,1536]{1,0:T(8,128)S(1)} %fusion.15) | copy-start | bytes 18874372
  160.9 4.9 %copy-start.21 = (bf16[2,64,8,768]{3,2,1,0:T(8,128)(2,1)S(1)}, bf16[2,64,8,768]{3,2,1,0:T(8,128)(2,1)}, u32[]{:S(2)}) copy-start(bf16[2,64,8,768]{3,2,1,0:T(8,128)(2,1)} %copy-done.20) | copy-start | bytes 4718596
  172.1 2.6 copy-start.27
  174.8 22.3 %copy-start.46 = (f32[128]{0:T(128)S(1)}, f32[128]{0:T(128)}, u32[]{:S(2)}) copy-start(f32[128]{0:T(128)} %fusion.38) | copy-start | bytes 1540
  174.8 23.5 %copy-start.23 = (bf16[768,768]{1,0:T(8,128)(2,1)S(1)}, bf16[768,768]{1,0:T(8,128)(2,1)}, u32[]{:S(2)}) copy-start(bf16[768,768]{1,0:T(8,128)(2,1)} %reshape.302) | copy-start | bytes 3538948
  196.1 9.0 %copy-start.10 = (bf16[512,192]{1,0:T(8,128)(2,1)S(1)}, bf16[512,192]{1,0:T(8,128)(2,1)}, u32[]{:S(2)}) copy-start(bf16[512,192]{1,0:T(8,128)(2,1)} %slice.87.q) | copy-start | bytes 589828
  205.2 1.4 copy-start.3
  246.8 1.1 copy-start.13
  247.9 0.9 copy-start.19
  250.5 2.2 copy-start.30
  250.5 12.6 %copy-start.29 = (bf16[512,768]{1,0:T(8,128)(2,1)S(1)}, bf16[512,768]{1,0:T(8,128)(2,1)}, u32[]{:S(2)}) copy-start(bf16[512,768]{1,0:T(8,128)(2,1)} %fusion.24) | copy-start | bytes 2359300
  262.2 6.0 %copy-start.18 = (bf16[512,192]{1,0:T(8,128)(2,1)S(1)}, bf16[512,192]{1,0:T(8,128)(2,1)}, u32[]{:S(2)}) copy-start(bf16[512,192]{1,0:T(8,128)(2,1)} %copy-done.17) | copy-start | bytes 589828
  263.1 10.4 %copy-start.39 = (f32[768]{0:T(1024)S(1)}, f32[768]{0:T(1024)}, u32[]{:S(2)}) copy-start(f32[768]{0:T(1024)} %get-tuple-element.38) | copy-start | bytes 9220
  266.0 7.7 %copy-start.25 = (f32[128,768]{1,0:T(8,128)S(1)}, f32[128,768]{1,0:T(8,128)}, u32[]{:S(2)}) copy-start(f32[128,768]{1,0:T(8,128)} %convert_reduce_fusion) | copy-start | bytes 1179652
  266.0 7.7 %copy-start.32 = (f32[768]{0:T(1024)S(1)}, f32[768]{0:T(1024)}, u32[]{:S(2)}) copy-start(f32[768]{0:T(1024)} %copy-done.31) | copy-start | bytes 9220
  266.0 7.7 %copy-start.43 = (f32[128]{0:T(128)S(1)}, f32[128]{0:T(128)}, u32[]{:S(2)}) copy-start(f32[128]{0:T(128)} %get-tuple-element.60) | copy-start | bytes 1540
  274.0 1.2 copy-start.8
  309.3 7.3 %copy-start.22 = (bf16[2,64,8,768]{3,2,1,0:T(8,128)(2,1)S(1)}, bf16[2,64,8,768]{3,2,1,0:T(8,128)(2,1)}, u32[]{:S(2)}) copy-start(bf16[2,64,8,768]{3,2,1,0:T(8,128)(2,1)} %copy-done.20) | copy-start | bytes 4718596
  316.6 8.8 %copy-start.47 = (f32[128]{0:T(128)S(1)}, f32[128]{0:T(128)}, u32[]{:S(2)}) copy-start(f32[128]{0:T(128)} %fusion.38) | copy-start | bytes 1540
  316.6 9.3 %copy-start.12 = (bf16[1024,768]{1,0:T(8,128)(2,1)S(1)}, bf16[1024,768]{1,0:T(8,128)(2,1)}, u32[]{:S(2)}) copy-start(bf16[1024,768]{1,0:T(8,128)(2,1)} %fusion.20) | copy-start | bytes 4718596
  325.4 31.0 %copy-start.34 = (f32[768]{0:T(1024)S(1)}, f32[768]{0:T(1024)}, u32[]{:S(2)}) copy-start(f32[768]{0:T(1024)} %copy-done.33) | copy-start | bytes 9220
  325.4 31.0 %copy-start.41 = (f32[128]{0:T(128)S(1)}, f32[128]{0:T(128)}, u32[]{:S(2)}) copy-start(f32[128]{0:T(128)} %copy-done.40) | copy-start | bytes 1540
  (3 other events, 2.0 us)
Sparse Core Ops, SparseCore 0:
  10.8 81.7 all-gather.2

commit v2 on v1

--- a/solution.py
+++ b/solution.py
@@ -107,46 +107,104 @@
 DMA = pltpu.SemaphoreType.DMA
 
 
-def start_kernel(tok, wmsg, rows, tok_all, w_all, rows_all, send, recv, core_recv):
+def half_peer(i, z, x, y, c):
+    return (z + i // 8) % 4, (x + (i // 2) % 4) % 4, c + 2 * ((y // 2 + i % 2) % 2), y % 2
+
+
+def block_of(z, x, y):
+    return pl.multiple_of((y % 2) * 512 + ((z * 4 + x) * 2 + y // 2) * 16, 16)
+
+
+def greet_chips(z, x, y, c):
+    loop(1, 32, lambda i: signal(half_peer(i, z, x, y, c)))
+
+    @pl.when(y % 2 != c)
+    def _():
+        signal(half_peer(0, z, x, y, c))
+
+    signal((z, x, y, 1 - c))
+    return 32 + jnp.where(y % 2 == c, 0, 1)
+
+
+def to_chips(z, x, y, c, source, target, send, recv):
+    def one(i):
+        there = half_peer(i, z, x, y, c)
+        push(source(there), target, send, recv, there)
+
+    loop(1, 32, one)
+    first = half_peer(0, z, x, y, c)
+
+    @pl.when(y % 2 == c)
+    def _():
+        keep(source(first), target, recv)
+
+    @pl.when(y % 2 != c)
+    def _():
+        push(source(first), target, send, recv, first)
+
+
+def sent_to_chips(rows, y, c, send):
+    wait_bytes(rows.at[pl.ds(0, 496)], send)
+
+    @pl.when(y % 2 != c)
+    def _():
+        wait_bytes(rows.at[pl.ds(0, 16)], send)
+
+
+def start_kernel(
+    tok, wmsg, rows, tok_all, w_all, rows_all,
+    wm, wo, xs, xo, send, recv, core_recv, own,
+):
     z, x, y, c = place()
-    me = chip_of(z, x, y)
     sib = (z, x, y, 1 - c)
-
-    def greet(i):
-        signal((*chip_peer(i, z, x, y), c))
-
-    loop(1, 64, greet)
-    signal(sib)
-    arrive(64)
+    mine = pl.ds(pl.multiple_of(c * 512, 512), 512)
+    theirs = pl.ds(pl.multiple_of((1 - c) * 512, 512), 512)
+    keep(wmsg, wm, own.at[0])
+    keep(rows.at[mine], xs, own.at[1])
+    expected = greet_chips(z, x, y, c)
     for k in range(1, 4):
-        push(tok, tok_all.at[z], send.at[0], recv.at[0], ((z + k) % 4, x, y, c))
+        signal(((z + k) % 4, x, y, c))
+    arrive(expected + 3)
+    push(wmsg, wo, send.at[0], core_recv.at[0], sib)
+    push(rows.at[theirs], xo, send.at[1], core_recv.at[1], sib)
+    for k in range(1, 4):
+        push(tok, tok_all.at[z], send.at[2], recv.at[0], ((z + k) % 4, x, y, c))
     keep(tok, tok_all.at[z], recv.at[0])
-
-    def weights(i):
-        there = chip_peer(i, z, x, y)
-        push(wmsg.at[there[0]], w_all.at[me, c], send.at[1], recv.at[1], (*there, c))
-
-    loop(1, 64, weights)
-    keep(wmsg.at[z], w_all.at[me, c], recv.at[1])
-
-    def routes(i):
-        there = chip_peer(i, z, x, y)
-        push(rows.at[chip_of(*there)], rows_all.at[c, me], send.at[2], recv.at[2], (*there, c))
-
-    loop(1, 64, routes)
-    keep(rows.at[me], rows_all.at[c, me], recv.at[2])
+    wait_bytes(wm, own.at[0])
+    wait_bytes(wo, core_recv.at[0])
+    wm[...] = wm[...] + wo[...]
+    half = z * 8 + x * 2 + y // 2
+    to_chips(
+        z, x, y, c, lambda there: wm.at[there[0]], w_all.at[half, y % 2], send.at[3], recv.at[1]
+    )
+    wait_bytes(xs, own.at[1])
+    wait_bytes(xo, core_recv.at[1])
+    xs[...] = xs[...] + xo[...]
+    me = block_of(z, x, y)
+    to_chips(
+        z, x, y, c,
+        lambda there: xs.at[pl.ds(pl.multiple_of(block_of(*there[:3]) - c * 512, 16), 16)],
+        rows_all.at[pl.ds(me, 16)], send.at[4], recv.at[2],
+    )
     wait_bytes(w_all.at[:, c], recv.at[1])
-    push(w_all.at[:, c], w_all.at[:, c], send.at[3], core_recv.at[0], sib)
-    wait_bytes(rows_all.at[c], recv.at[2])
-    push(rows_all.at[c], rows_all.at[c], send.at[4], core_recv.at[1], sib)
+    push(w_all.at[:, c], w_all.at[:, c], send.at[5], core_recv.at[2], sib)
+    wait_bytes(rows_all.at[mine], recv.at[2])
+    push(rows_all.at[mine], rows_all.at[mine], send.at[6], core_recv.at[3], sib)
     wait_bytes(tok_all, recv.at[0])
-    wait_bytes(w_all.at[:, 1 - c], core_recv.at[0])
-    wait_bytes(rows_all.at[1 - c], core_recv.at[1])
-    wait_bytes(tok_all.at[pl.ds(0, 3)], send.at[0])
-    wait_bytes(w_all.at[pl.ds(0, 63), c], send.at[1])
-    wait_bytes(rows_all.at[c, pl.ds(0, 63)], send.at[2])
-    wait_bytes(w_all.at[:, c], send.at[3])
-    wait_bytes(rows_all.at[c], send.at[4])
+    wait_bytes(w_all.at[:, 1 - c], core_recv.at[2])
+    wait_bytes(rows_all.at[theirs], core_recv.at[3])
+    wait_bytes(wo, send.at[0])
+    wait_bytes(xo, send.at[1])
+    wait_bytes(tok_all.at[pl.ds(0, 3)], send.at[2])
+    wait_bytes(w_all.at[pl.ds(0, 31), c], send.at[3])
+
+    @pl.when(y % 2 != c)
+    def _():
+        wait_bytes(w_all.at[0, c], send.at[3])
+
+    sent_to_chips(rows_all, y, c, send.at[4])
+    wait_bytes(w_all.at[:, c], send.at[5])
+    wait_bytes(rows_all.at[mine], send.at[6])
 
 
 def start_exchange(tok, wmsg, rows):
@@ -155,91 +213,196 @@
         (tok, wmsg, rows),
         (
             jax.ShapeDtypeStruct((4, TOK, D), BF),
-            jax.ShapeDtypeStruct((64, 2, 8, 3 * GW), BF),
-            jax.ShapeDtypeStruct((2, 64, 8, D), BF),
-        ),
-        [DMA((5,)), DMA((3,)), DMA((2,))],
+            jax.ShapeDtypeStruct((32, 2, 16, 3 * GW), BF),
+            jax.ShapeDtypeStruct((1024, D), BF),
+        ),
+        [
+            pltpu.VMEM((4, 16, 3 * GW), BF),
+            pltpu.VMEM((4, 16, 3 * GW), BF),
+            pltpu.VMEM((512, D), BF),
+            pltpu.VMEM((512, D), BF),
+            DMA((7,)),
+            DMA((3,)),
+            DMA((4,)),
+            DMA((2,)),
+        ],
         0,
         "start_exchange",
     )
 
 
-def dispatch_kernel(rows, rows_all, send, recv, core_recv):
+FH = 1536
+WIDE = 256
+
+
+def experts_kernel(
+    x16, d_rows, w_in, w_out, home_in, home_out, g_in, g_out,
+    xs, xo, rows, dv, w1, w2, dh, hidden, dact, in_h, out_h, in_o, out_o, stage_out, stage_in,
+    send, recv, core_recv, own, staged,
+):
     z, x, y, c = place()
-    me = chip_of(z, x, y)
     sib = (z, x, y, 1 - c)
-
-    def greet(i):
-        signal((*chip_peer(i, z, x, y), c))
-
-    loop(1, 64, greet)
-    signal(sib)
-    arrive(64)
-
-    def routes(i):
-        there = chip_peer(i, z, x, y)
-        push(rows.at[chip_of(*there)], rows_all.at[c, me], send.at[0], recv.at[0], (*there, c))
-
-    loop(1, 64, routes)
-    keep(rows.at[me], rows_all.at[c, me], recv.at[0])
-    wait_bytes(rows_all.at[c], recv.at[0])
-    push(rows_all.at[c], rows_all.at[c], send.at[1], core_recv, sib)
-    wait_bytes(rows_all.at[1 - c], core_recv)
-    wait_bytes(rows_all.at[c, pl.ds(0, 63)], send.at[0])
-    wait_bytes(rows_all.at[c], send.at[1])
-
-
-def dispatch(rows):
-    return run_comm(
-        dispatch_kernel,
-        (rows,),
-        jax.ShapeDtypeStruct((2, 64, 8, D), BF),
-        [DMA((2,)), DMA((1,)), DMA],
-        1,
-        "dispatch",
-    )
-
-
-def home_kernel(halves, home, own, other, total, send, recv, core_recv, own_sem):
-    z, x, y, c = place()
-    me = chip_of(z, x, y)
-    sib = (z, x, y, 1 - c)
-
-    def greet(i):
-        signal((*chip_peer(i, z, x, y), c))
-
-    loop(1, 64, greet)
-    signal(sib)
-    arrive(64)
-    push(halves.at[1 - c], other, send.at[0], core_recv, sib)
-    keep(halves.at[c], own, own_sem)
-    wait_bytes(own, own_sem)
-    wait_bytes(other, core_recv)
-
-    def both(i):
-        there = chip_peer(i, z, x, y)
-        at = chip_of(*there)
-        total[at] = (own[at].astype(F32) + other[at].astype(F32)).astype(BF)
-        push(total.at[at], home.at[me], send.at[1], recv.at[0], (*there, c))
-
-    loop(1, 64, both)
-    total[me] = (own[me].astype(F32) + other[me].astype(F32)).astype(BF)
-    keep(total.at[me], home.at[me], recv.at[0])
-    wait_bytes(home, recv.at[0])
-    wait_bytes(total.at[pl.ds(0, 63)], send.at[1])
-    wait_bytes(other, send.at[0])
-
-
-def go_home(halves, collective_id, name):
-    rows = pltpu.VMEM((64, 8, D), BF)
-    return run_comm(
-        home_kernel,
-        (halves,),
-        jax.ShapeDtypeStruct((64, 8, D), BF),
-        [rows, rows, rows, DMA((2,)), DMA((1,)), DMA, DMA],
-        collective_id,
-        name,
-    )
+    at_mine = pl.multiple_of(c * 512, 512)
+    at_theirs = pl.multiple_of((1 - c) * 512, 512)
+    mine, theirs = pl.ds(at_mine, 512), pl.ds(at_theirs, 512)
+    me = block_of(z, x, y)
+    keep(x16.at[mine], xs, own.at[0])
+    keep(d_rows, dv, own.at[1])
+    keep(w_out, w2, own.at[2])
+    keep(w_in, w1, own.at[3])
+    expected = greet_chips(z, x, y, c)
+    arrive(expected)
+    push(x16.at[theirs], xo, send.at[0], core_recv.at[0], sib)
+    wait_bytes(xs, own.at[0])
+    wait_bytes(xo, core_recv.at[0])
+    xs[...] = xs[...] + xo[...]
+    to_chips(
+        z, x, y, c,
+        lambda there: xs.at[pl.ds(pl.multiple_of(block_of(*there[:3]) - c * 512, 16), 16)],
+        rows.at[pl.ds(me, 16)], send.at[1], recv.at[0],
+    )
+    wait_bytes(dv, own.at[1])
+    wait_bytes(w2, own.at[2])
+
+    def hidden_grads(n):
+        cols = pl.ds(pl.multiple_of(n * WIDE, WIDE), WIDE)
+        dh[:, cols] = dot(dv[...], w2[cols, :], NT)
+
+    loop(0, FH // WIDE, hidden_grads)
+    wait_bytes(w1, own.at[3])
+    wait_bytes(rows.at[mine], recv.at[0])
+    push(rows.at[mine], rows.at[mine], send.at[2], core_recv.at[1], sib)
+
+    def activate(at):
+        part = pl.ds(at, 512)
+
+        def one(n):
+            cols = pl.ds(pl.multiple_of(n * WIDE, WIDE), WIDE)
+            a = dot(rows[part, :], w1[:, cols], NN)
+            square = a * a
+            t = jnp.tanh(0.7978845608028654 * (a + 0.044715 * (square * a)))
+            cdf = 0.5 * (1.0 + t)
+            hidden[part, cols] = (a * cdf).astype(BF)
+            slope = cdf + 0.5 * a * (1.0 - t * t) * (
+                0.7978845608028654 * (1.0 + 0.134145 * square)
+            )
+            dact[part, cols] = (slope * dh[part, cols]).astype(BF)
+
+        loop(0, FH // WIDE, one)
+
+    def in_half(at):
+        part = pl.ds(at, 512)
+
+        def one(n):
+            cols = pl.ds(pl.multiple_of(n * WIDE, WIDE), WIDE)
+            in_h[part, cols] = dot(dact[part, :], w1[cols, :], NT).astype(BF)
+
+        loop(0, D // WIDE, one)
+
+    def out_half(at):
+        part = pl.ds(at, 512)
+
+        def one(n):
+            cols = pl.ds(pl.multiple_of(n * WIDE, WIDE), WIDE)
+            out_h[part, cols] = dot(hidden[part, :], w2[:, cols], NN).astype(BF)
+
+        loop(0, D // WIDE, one)
+
+    activate(at_mine)
+    wait_bytes(rows.at[theirs], core_recv.at[1])
+    activate(at_theirs)
+    in_half(at_theirs)
+    push(in_h.at[theirs], in_o, send.at[3], core_recv.at[2], sib)
+    in_half(at_mine)
+    wait_bytes(in_o, core_recv.at[2])
+    in_o[...] = (in_o[...].astype(F32) + in_h[mine, :].astype(F32)).astype(BF)
+    to_chips(
+        z, x, y, c,
+        lambda there: in_o.at[pl.ds(pl.multiple_of(block_of(*there[:3]) - c * 512, 16), 16)],
+        home_in.at[pl.ds(me, 16)], send.at[4], recv.at[1],
+    )
+    out_half(at_theirs)
+    push(out_h.at[theirs], out_o, send.at[5], core_recv.at[3], sib)
+    out_half(at_mine)
+    wait_bytes(out_o, core_recv.at[3])
+    out_o[...] = (out_o[...].astype(F32) + out_h[mine, :].astype(F32)).astype(BF)
+    to_chips(
+        z, x, y, c,
+        lambda there: out_o.at[pl.ds(pl.multiple_of(block_of(*there[:3]) - c * 512, 16), 16)],
+        home_out.at[pl.ds(me, 16)], send.at[6], recv.at[2],
+    )
+
+    def out_grads(n):
+        cols = pl.ds(pl.multiple_of(n * WIDE, WIDE), WIDE)
+        slot = n % 2
+
+        @pl.when(n >= 2)
+        def _():
+            wait_bytes(stage_out.at[slot], staged.at[slot])
+
+        stage_out[slot] = dot(hidden[:, cols], dv[...], TN)
+        keep(stage_out.at[slot], g_out.at[cols], staged.at[slot])
+
+    loop(0, FH // WIDE, out_grads)
+    wait_bytes(home_in.at[mine], recv.at[1])
+    push(home_in.at[mine], home_in.at[mine], send.at[7], core_recv.at[4], sib)
+
+    def in_grads(n):
+        cols = pl.ds(pl.multiple_of(n * WIDE, WIDE), WIDE)
+        slot = n % 2
+
+        @pl.when(n >= 2)
+        def _():
+            wait_bytes(stage_in.at[slot], staged.at[2 + slot])
+
+        stage_in[slot] = dot(rows[:, cols], dact[...], TN)
+        keep(stage_in.at[slot], g_in.at[cols], staged.at[2 + slot])
+
+    loop(0, D // WIDE, in_grads)
+    wait_bytes(home_out.at[mine], recv.at[2])
+    push(home_out.at[mine], home_out.at[mine], send.at[8], core_recv.at[5], sib)
+    for slot in range(2):
+        wait_bytes(stage_out.at[slot], staged.at[slot])
+        wait_bytes(stage_in.at[slot], staged.at[2 + slot])
+    wait_bytes(xo, send.at[0])
+    sent_to_chips(rows, y, c, send.at[1])
+    wait_bytes(rows.at[mine], send.at[2])
+    wait_bytes(in_o, send.at[3])
+    sent_to_chips(home_in, y, c, send.at[4])
+    wait_bytes(out_o, send.at[5])
+    sent_to_chips(home_out, y, c, send.at[6])
+    wait_bytes(home_in.at[theirs], core_recv.at[4])
+    wait_bytes(home_out.at[theirs], core_recv.at[5])
+    wait_bytes(home_in.at[mine], send.at[7])
+    wait_bytes(home_out.at[mine], send.at[8])
+
+
+def run_experts(x16, d_rows, w_in, w_out):
+    whole_rows = pltpu.VMEM((1024, D), BF)
+    half_rows = pltpu.VMEM((512, D), BF)
+    hid = pltpu.VMEM((1024, FH), BF)
+    return pl.pallas_call(
+        experts_kernel,
+        out_shape=(
+            jax.ShapeDtypeStruct((1024, D), BF),
+            jax.ShapeDtypeStruct((1024, D), BF),
+            jax.ShapeDtypeStruct((D, FH), F32),
+            jax.ShapeDtypeStruct((FH, D), F32),
+        ),
+        in_specs=[ANY] * 4,
+        out_specs=(ANY,) * 4,
+        scratch_shapes=[
+            half_rows, half_rows, whole_rows, whole_rows,
+            pltpu.VMEM((D, FH), BF), pltpu.VMEM((FH, D), BF), pltpu.VMEM((1024, FH), F32),
+            hid, hid, whole_rows, whole_rows, half_rows, half_rows,
+            pltpu.VMEM((2, WIDE, D), F32), pltpu.VMEM((2, WIDE, FH), F32),
+            DMA((9,)), DMA((3,)), DMA((6,)), DMA((4,)), DMA((4,)),
+        ],
+        compiler_params=pltpu.CompilerParams(
+            collective_id=1, has_side_effects=True, vmem_limit_bytes=48 * 2**20
+        ),
+        name="experts",
+    )(x16, d_rows, w_in, w_out)
 
 
 def z_kernel(blocks, out, send, recv):
@@ -688,7 +851,7 @@
     z, x, y, c = place()
     experts = 64
     capacity = 8
-    slots = experts * capacity
+    slots = 2 * experts * capacity
     own_tokens = tokens.reshape(TOK, D)
     grad_bf = cotangent.reshape(TOK, D)
     grad_out = grad_bf.astype(F32)
@@ -696,7 +859,8 @@
     route = expert_ids.reshape(TOK * 2)
     marks = (route[:, None] == jnp.arange(experts, dtype=jnp.int32)[None, :]).astype(jnp.int32)
     earlier = jnp.cumsum(marks, axis=0) - marks
-    slot = route * capacity + jnp.sum(earlier * marks, axis=1)
+    block = (route % 2) * 32 + (route // 4) * 2 + (route % 4) // 2
+    slot = block * 16 + c * capacity + jnp.sum(earlier * marks, axis=1)
     slot_pair = slot.reshape(TOK, 2)
     gates = gate_values.reshape(TOK, 2)
     slot_ids = jnp.arange(slots, dtype=jnp.int32)
@@ -705,7 +869,7 @@
     pick = (pick_0 | pick_1).astype(BF)
     gate_of = jnp.where(pick_0, gates[:, :1], 0.0) + jnp.where(pick_1, gates[:, 1:], 0.0)
     gate_slot = jnp.sum(gate_of, axis=0)
-    d_eo = (dot(pick, grad_bf, TN) * gate_slot[:, None]).astype(BF).reshape(experts, capacity, D)
+    d_eo = (dot(pick, grad_bf, TN) * gate_slot[:, None]).astype(BF)
 
     slab = w_qkv.reshape(6, 3, GROUPS, GW).transpose(2, 0, 1, 3).reshape(GROUPS, 6, 3 * GW)
     notes = jnp.concatenate(
@@ -714,15 +878,20 @@
             doc_ids.reshape(TOK).astype(BF), jnp.zeros((3 * GW - 256,), BF),
         ]
     )
-    notes = jnp.concatenate([notes[None], jnp.zeros((1, 3 * GW), BF)], axis=0)
-    message = jnp.concatenate([slab, jnp.broadcast_to(notes, (GROUPS, 2, 3 * GW))], axis=1)
+    notes = jnp.broadcast_to(notes, (GROUPS, 1, 3 * GW))
+    nothing = jnp.zeros((GROUPS, 6, 3 * GW), BF)
+    message = jnp.where(
+        c == 0,
+        jnp.concatenate([slab, nothing, notes, nothing[:, :3]], axis=1),
+        jnp.concatenate([nothing, slab, nothing[:, :1], notes, nothing[:, :2]], axis=1),
+    )
     attention_weight = lax.all_gather(w_attn_out, AXES, axis=0, tiled=True)
     tok_all, w_all, d_eo_all = start_exchange(own_tokens, message, d_eo)
 
-    weight = w_all[:, :, :6, :].reshape(D, 3 * GW)
-    gain_one = w_all[:, :, 6, 0:6].reshape(D).astype(F32)
-    gain_two = w_all[:, :, 6, 6:12].reshape(D).astype(F32)
-    doc_rows = w_all[:, :, 6, 128:256].reshape(16, 4, 2, TOK)
+    weight = w_all[:, :, :12, :].reshape(D, 3 * GW)
+    gain_one = w_all[:, :, 12:14, 0:6].reshape(D).astype(F32)
+    gain_two = w_all[:, :, 12:14, 6:12].reshape(D).astype(F32)
+    doc_rows = w_all[:, :, 12:14, 128:256].reshape(16, 4, 2, TOK)
     doc_rows = lax.dynamic_slice(doc_rows, (0, y, c, 0), (16, 1, 1, TOK)).reshape(16, TOK).astype(F32)
     key_docs = doc_rows.reshape(1, 2048)
     query_docs = lax.dynamic_slice(doc_rows.reshape(4, 4, TOK), (0, x, 0), (4, 1, TOK)).reshape(512, 1)
@@ -742,18 +911,10 @@
     middle = inputs + dot(attn, attention_weight, NN)
     moe_float, norm_two_back = jax.vjp(scale_rows, middle, gain_two)
     moe_in = moe_float.astype(BF)
-    send_rows = dot(pick, moe_in, TN).astype(BF).reshape(experts, capacity, D)
-    rows = dispatch(send_rows).reshape(-1, D)
-    first_half = w_in[0]
-    second_half = w_out[0]
-    d_rows = d_eo_all.reshape(-1, D)
-    hidden_grad = dot(d_rows, second_half, NT)
-    pre_act = dot(rows, first_half, NN)
-    gelu_vals, gelu_back = jax.vjp(jax.nn.gelu, pre_act)
-    hidden = gelu_vals.astype(BF)
-    act_grad = gelu_back(hidden_grad)[0].astype(BF)
-    in_halves = dot(act_grad, first_half, NT).astype(BF).reshape(2, experts, capacity, D)
-    home = go_home(in_halves, 6, "home_grads").reshape(slots, D)
+    send_rows = dot(pick, moe_in, TN).astype(BF)
+    home, expert_out, expert_in_grad, expert_out_grad = run_experts(
+        send_rows, d_eo_all, w_in[0], w_out[0]
+    )
     moe_in_grad = dot(pick, home, NN)
     middle_part, gain_two_grad = norm_two_back(moe_in_grad)
     middle_grad = grad_out + middle_part
@@ -773,14 +934,10 @@
     input_part, gain_one_grad = norm_one_back(normed_grad)
     input_grad = middle_grad + input_part
 
-    out_halves = dot(hidden, second_half, NN).astype(BF).reshape(2, experts, capacity, D)
-    expert_out = go_home(out_halves, 9, "home_outputs").reshape(slots, D)
     both = jnp.concatenate([pick_0, pick_1], axis=0).astype(BF)
     picked = dot(both, expert_out, NN).reshape(2, TOK, D)
     block_out = middle + gates[:, :1] * picked[0] + gates[:, 1:] * picked[1]
     gate_grad = jnp.sum(picked * grad_out[None], axis=2).T
-    expert_out_grad = dot(hidden, d_rows, TN)[None]
-    expert_in_grad = dot(rows, act_grad, TN)[None]
 
     qkv_part = dot(normed, d_qkv, TN).astype(BF).reshape(32, 24, 3 * GW)
     att_part = dot(attn_part, branch_all.reshape(512, D), TN).astype(BF).reshape(32, 6, D)
@@ -812,8 +969,8 @@
         attn_out_grad,
         table_grad,
         gains[1],
-        expert_in_grad,
-        expert_out_grad,
+        expert_in_grad[None],
+        expert_out_grad[None],
     )
 
 

time: 368 us -> 299 us (0.81)
  matrix products: 49.1 us -> 13.2 us
  local copies, waits for them, and re-layouts: 47.8 us -> 28.7 us
  Pallas kernels: 237 us -> 225 us
  other arithmetic: 17.1 us -> 13 us
    pallas_call x10 -> x7, Pallas kernels: 206 us -> 137 us  [run_comm(): pl.pallas_call(kernel, out_shape=outs, in_specs=[ANY] * len(args), out_sp...]
    pallas_call x0 -> x1, Pallas kernels: none -> 56.9 us  [run_experts(): pl.pallas_call(experts_kernel, out_shape=(jax.ShapeDtypeStruct((1024, D),...]
    dot_general x16 -> x10, matrix products: 49.1 us -> 13.2 us  [dot(): return lax.dot_general(a, b, dims, preferred_element_type=F32)]
    unnamed x104 -> x88, local copies, waits for them, and re-layouts: 22.4 us -> 14.8 us
  transfers between devices with their start and end apart: 1 -> 1, of which waited for: 0 -> 0; matrix products, arithmetic and copies ran while one was open for 9% -> 7% of each run, Pallas kernels for 21% -> 26%
where the time goes in v2:
time: 299 us; the launch traced here: 296 us
  Pallas kernels  225 us (75%)
  local copies, waits for them, and re-layouts  28.7 us (10%)
  between operations  14.9 us (5%)
  matrix products  13.2 us (4%)
  other arithmetic  13 us (4%)
    pallas_call x7, Pallas kernels, run_comm(): pl.pallas_call(kernel, out_shape=outs, in_specs=[ANY] * len(args), out_sp...  137 us
    pallas_call x1, Pallas kernels, run_experts(): pl.pallas_call(experts_kernel, out_shape=(jax.ShapeDtypeStruct((1024, D),...  56.9 us
    pallas_call x1, Pallas kernels, attn_backward(): pl.pallas_call(attn_backward_kernel, grid=(GH,), out_shape=(jax.ShapeDtyp...  21.5 us
    unnamed x88, local copies, waits for them, and re-layouts  14.8 us
    dot_general x10, matrix products, dot(): return lax.dot_general(a, b, dims, preferred_element_type=F32)  13.2 us
    pallas_call x1, Pallas kernels, attn_forward(): pl.pallas_call(attn_forward_kernel, grid=(GH,), out_shape=(jax.ShapeDtype...  9.71 us
  transfers between devices with their start and end apart: 1, of which 0 were waited for; matrix products, arithmetic and copies ran while one was open for 7% of the time, Pallas kernels for 26%

profile of v2, /device:TPU:1, one launch (start us, length us, event | category | flops | bytes accessed | tf_op | source)
XLA Modules:
  0.0 295.6 jit_solution(3996147711678796118)
XLA Ops:
  7.3 0.7 all-gather.3.cloned.1.call-update
  8.0 0.8 copy.83
  9.0 0.9 reshape.244
  10.1 0.7 convert_bitcast_fusion
  10.8 0.8 slice_bitcast_fusion.3
  11.5 0.6 reduce-window.6
  13.2 1.7 multiply_convert_fusion.rows
  15.5 40.6 %start_exchange.1 = (bf16[4,128,768]{2,1,0:T(8,128)(2,1)S(1)}, bf16[32,2,16,576]{3,2,1,0:T(8,128)(2,1)S(1)}, bf16[1024,768]{1,0:T(8,128)(2,1)S(1)}) custom-call(bf16[128,768]{1,0:T(8,128)(2,1)S(1)} %bitcast.146, bf16[4,16,576]{2,1,0:T(8,128)(2,1)S(1)} %maximum_select_fusion.wmsg, bf16[1024,768]{1,0:T(8,128)(2,1)S(1)} %multiply_convert_fusion.rows), custom_call_target="tpu_custom_call" | custom-call | tf_op jit(solution)/shard_map/start_exchange/pallas_call | solution.py:94
  56.1 1.1 copy-done.5
  57.2 1.1 copy-done.6
  58.3 0.7 slice_convert_fusion
  59.0 2.3 reshape.250
  62.5 0.8 convolution_convert_fusion.3
  63.5 0.9 slice.86
  64.7 20.6 %kv_gather.1 = bf16[4,4,128,384]{3,2,1,0:T(8,128)(2,1)S(1)} custom-call(bf16[4,128,384]{2,1,0:T(8,128)(2,1)S(1)} %bitcast.149), custom_call_target="tpu_custom_call" | custom-call | tf_op jit(solution)/shard_map/kv_gather/pallas_call | solution.py:94
  85.5 9.7 %attn_forward.1 = (bf16[512,192]{1,0:T(8,128)(2,1)S(1)}, bf16[3,512,2048]{2,1,0:T(8,128)(2,1)S(1)}) custom-call(s32[1]{0:T(128)} %bitcast.1.pos, f32[32,3]{1,0:T(8,128)S(1)} %convert_element_type.136.tab, bf16[512,192]{1,0:T(8,128)(2,1)S(1)} %slice.99.q, bf16[2048,384]{1,0:T(8,128)(2,1)S(1)} %bitcast.144, f32[512,1]{1,0:T(8,128)S(1)} %copy.89.qd, ...), custom_call_target="tpu_custom_call" | custom-call | tf_op jit(solution)/shard_map/attn_forward/pallas_call | solution.py:690
  95.2 2.6 copy-done.1
  97.9 5.3 %attn_exchange.1 = bf16[4,128,192]{2,1,0:T(8,128)(2,1)S(1)} custom-call(bf16[4,128,192]{2,1,0:T(8,128)(2,1)S(1)} %bitcast.154), custom_call_target="tpu_custom_call" | custom-call | tf_op jit(solution)/shard_map/attn_exchange/pallas_call | solution.py:94
  103.2 0.8 copy.90
  104.0 1.0 reshape.274
  105.1 1.6 iota_compare_fusion
  106.7 0.8 bitcast_convert_fusion
  107.5 1.8 fusion.1
  109.3 3.2 %reshape.277 = bf16[768,768]{1,0:T(8,128)(2,1)} reshape(bf16[128,6,768]{2,1,0:T(8,128)(2,1)} %all-gather.3.cloned.1.call-done) | data formatting | bytes 2359296
  112.6 1.7 multiply_reduce_fusion.3
  114.3 0.7 convolution_convert_fusion.x16
  115.1 56.9 %experts.1 = (bf16[1024,768]{1,0:T(8,128)(2,1)S(1)}, bf16[1024,768]{1,0:T(8,128)(2,1)S(1)}, f32[768,1536]{1,0:T(8,128)}, f32[1536,768]{1,0:T(8,128)}) custom-call(bf16[1024,768]{1,0:T(8,128)(2,1)S(1)} %convolution_convert_fusion.x16, bf16[1024,768]{1,0:T(8,128)(2,1)} %copy-done.5, bf16[768,1536]{1,0:T(8,128)(2,1)} %bitcast.165, bf16[1536,768]{1,0:T(8,128)(2,1)} %bitcast.166), custom_call_target="tpu_custom_call" | custom-call | tf_op jit(solution)/shard_map/experts/pallas_call | solution.py:384
  172.0 1.1 multiply_reduce_fusion.1
  174.7 7.5 %d_attn_exchange.1 = bf16[4,128,192]{2,1,0:T(8,128)(2,1)S(1)} custom-call(bf16[4,128,192]{2,1,0:T(8,128)(2,1)S(1)} %bitcast.152), custom_call_target="tpu_custom_call" | custom-call | tf_op jit(solution)/shard_map/d_attn_exchange/pallas_call | solution.py:94
  182.2 21.5 %attn_backward.1 = (bf16[512,192]{1,0:T(8,128)(2,1)S(1)}, bf16[2048,384]{1,0:T(8,128)(2,1)S(1)}, f32[3,32,128]{2,1,0:T(8,128)S(1)}) custom-call(s32[1]{0:T(128)} %bitcast.1.pos, bf16[3,512,2048]{2,1,0:T(8,128)(2,1)} %copy-done.1, bf16[512,192]{1,0:T(8,128)(2,1)S(1)} %slice.99.q, bf16[2048,384]{1,0:T(8,128)(2,1)S(1)} %bitcast.145, bf16[512,192]{1,0:T(8,128)(2,1)S(1)} %bitcast.151), custom_call_target="tpu_custom_call" | custom-call | tf_op jit(solution)/shard_map/attn_backward/pallas_call | solution.py:804
  203.8 0.7 copy-done.9
  204.5 19.8 %kv_back.1 = (bf16[4,4,128,384]{3,2,1,0:T(8,128)(2,1)S(1)}, bf16[4,128,768]{2,1,0:T(8,128)(2,1)S(1)}) custom-call(bf16[4,4,128,384]{3,2,1,0:T(8,128)(2,1)S(1)} %bitcast.148, bf16[128,768]{1,0:T(8,128)(2,1)S(1)} %fusion.58.branch), custom_call_target="tpu_custom_call" | custom-call | tf_op jit(solution)/shard_map/kv_back/pallas_call | solution.py:94
  224.3 1.1 reduce_sum.155
  225.4 2.1 convolution_convert_fusion.2
  227.6 10.3 %normed_grads.1 = bf16[4,128,768]{2,1,0:T(8,128)(2,1)S(1)} custom-call(bf16[4,128,768]{2,1,0:T(8,128)(2,1)S(1)} %bitcast.155), custom_call_target="tpu_custom_call" | custom-call | tf_op jit(solution)/shard_map/normed_grads/pallas_call | solution.py:94
  237.9 0.9 convert_reduce_fusion
  238.7 1.8 convolution_convert_fusion.1
  240.6 1.6 copy.93
  243.0 0.9 reshape.267
  243.9 1.2 fusion.13
  245.2 32.7 %weight_sums.1 = (f32[4,8,576]{2,1,0:T(8,128)S(1)}, f32[8,768]{1,0:T(8,128)S(1)}, f32[4,8,128]{2,1,0:T(8,128)S(1)}) custom-call(bf16[32,24,576]{2,1,0:T(8,128)(2,1)S(1)} %bitcast.147, bf16[32,8,768]{2,1,0:T(8,128)(2,1)S(1)} %pad.21.att, f32[32,8,128]{2,1,0:T(8,128)S(1)} %select_maximum_fusion.small), custom_call_target="tpu_custom_call" | custom-call | tf_op jit(solution)/shard_map/weight_sums/pallas_call | solution.py:94
  278.8 0.7 reshape.270
  279.6 0.7 reshape_squeeze.3
  280.2 2.4 fusion.6
  282.7 1.0 fusion.29
  283.7 0.6 copy.111
  284.3 2.2 copy.112
  286.5 2.2 copy.113
  (145 shorter events, 7.3 us)
Async XLA Ops:
  7.2 57.3 %copy-start = (bf16[32,12]{0,1:T(8,128)(2,1)S(1)}, bf16[32,12]{0,1:T(8,128)(2,1)}, u32[]{:S(2)}) copy-start(bf16[32,12]{0,1:T(8,128)(2,1)} %param.16) | copy-start | bytes 2308
  7.2 7.7 %copy-start.37 = (bf16[6]{0:T(256)(128)(2,1)S(1)}, bf16[6]{0:T(256)(128)(2,1)}, u32[]{:S(2)}) copy-start(bf16[6]{0:T(256)(128)(2,1)} %param.13) | copy-start | bytes 40
  7.2 7.7 %copy-start.38 = (bf16[6]{0:T(256)(128)(2,1)S(1)}, bf16[6]{0:T(256)(128)(2,1)}, u32[]{:S(2)}) copy-start(bf16[6]{0:T(256)(128)(2,1)} %param.17) | copy-start | bytes 40
  7.2 102.1 %all-gather.3.cloned.1.call-start = ((), (), s32[]{:S(2)}) async-start(), calls=%async_computation | async-start | bytes 1585152 | tf_op jit(solution)/shard_map/all_gather | solution.py:888
  10.0 5.4 %copy-start.2 = (bf16[1,128,768]{2,1,0:T(8,128)(2,1)S(1)}, bf16[1,128,768]{2,1,0:T(8,128)(2,1)}, u32[]{:S(2)}) copy-start(bf16[1,128,768]{2,1,0:T(8,128)(2,1)} %param.12) | copy-start | bytes 589828
  11.5 44.5 %copy-start.29 = (f32[128]{0:T(128)}, f32[128]{0:T(128)S(1)}, u32[]{:S(2)}) copy-start(f32[128]{0:T(128)S(1)} %get-tuple-element.58) | copy-start | bytes 1540
  11.5 44.5 %copy-start.31 = (f32[128]{0:T(128)}, f32[128]{0:T(128)S(1)}, u32[]{:S(2)}) copy-start(f32[128]{0:T(128)S(1)} %get-tuple-element.59) | copy-start | bytes 1540
  12.9 43.1 %copy-start.26 = (s32[128]{0:T(128)}, s32[128]{0:T(128)S(1)}, u32[]{:S(2)}) copy-start(s32[128]{0:T(128)S(1)} %get-tuple-element.49) | copy-start | bytes 1540
  56.1 1.1 copy-start.5
  57.2 1.1 copy-start.6
  61.3 2.0 copy-start.20
  95.2 2.7 copy-start.1
  97.8 8.9 %copy-start.16 = (bf16[1,128,768]{2,1,0:T(8,128)(2,1)S(1)}, bf16[1,128,768]{2,1,0:T(8,128)(2,1)}, u32[]{:S(2)}) copy-start(bf16[1,128,768]{2,1,0:T(8,128)(2,1)} %param.23) | copy-start | bytes 589828
  105.1 67.9 %copy-start.35 = (f32[128]{0:T(128)}, f32[128]{0:T(128)S(1)}, u32[]{:S(2)}) copy-start(f32[128]{0:T(128)S(1)} %fusion.10) | copy-start | bytes 1540
  109.3 3.3 %copy-start.21 = (bf16[128,4,192]{0,2,1:T(8,128)(2,1)S(1)}, bf16[128,4,192]{0,2,1:T(8,128)(2,1)}, u32[]{:S(2)}) copy-start(bf16[128,4,192]{0,2,1:T(8,128)(2,1)} %copy.90) | copy-start | bytes 589828
  112.6 1.8 copy-start.27
  114.3 59.3 %copy-start.12 = (f32[128,768]{1,0:T(8,128)}, f32[128,768]{1,0:T(8,128)S(1)}, u32[]{:S(2)}) copy-start(f32[128,768]{1,0:T(8,128)S(1)} %get-tuple-element.61) | copy-start | bytes 1179652
  114.3 59.3 %copy-start.33 = (f32[128]{0:T(128)}, f32[128]{0:T(128)S(1)}, u32[]{:S(2)}) copy-start(f32[128]{0:T(128)S(1)} %fusion.52) | copy-start | bytes 1540
  171.9 1.8 copy-start.3
  172.0 1.8 copy-start.11
  173.0 0.8 copy-start.18
  203.8 0.7 copy-start.9
  204.5 20.9 %copy-start.10 = (bf16[512,192]{1,0:T(8,128)(2,1)S(1)}, bf16[512,192]{1,0:T(8,128)(2,1)}, u32[]{:S(2)}) copy-start(bf16[512,192]{1,0:T(8,128)(2,1)} %copy-done.9) | copy-start | bytes 589828
  224.3 3.3 %copy-start.7 = (bf16[4,128,768]{2,1,0:T(8,128)(2,1)}, bf16[4,128,768]{2,1,0:T(8,128)(2,1)S(1)}, u32[]{:S(2)}) copy-start(bf16[4,128,768]{2,1,0:T(8,128)(2,1)S(1)} %get-tuple-element.37) | copy-start | bytes 2359300
  227.6 11.2 %copy-start.22 = (bf16[512,768]{1,0:T(8,128)(2,1)S(1)}, bf16[512,768]{1,0:T(8,128)(2,1)}, u32[]{:S(2)}) copy-start(bf16[512,768]{1,0:T(8,128)(2,1)} %fusion.1) | copy-start | bytes 2359300
  227.6 11.2 %copy-start.25 = (bf16[4,128,384]{2,1,0:T(8,128)(2,1)S(1)}, bf16[4,128,384]{2,1,0:T(8,128)(2,1)}, u32[]{:S(2)}) copy-start(bf16[4,128,384]{2,1,0:T(8,128)(2,1)} %reduce_sum.155) | copy-start | bytes 1179652
  240.6 1.6 copy-start.8
  242.6 35.3 %copy-start.36 = (f32[128]{0:T(128)S(1)}, f32[128]{0:T(128)}, u32[]{:S(2)}) copy-start(f32[128]{0:T(128)} %copy-done.35) | copy-start | bytes 1540
  242.7 37.5 %copy-start.4 = (bf16[1024,768]{1,0:T(8,128)(2,1)S(1)}, bf16[1024,768]{1,0:T(8,128)(2,1)}, u32[]{:S(2)}) copy-start(bf16[1024,768]{1,0:T(8,128)(2,1)} %copy-done.3) | copy-start | bytes 4718596
  242.7 37.5 %copy-start.23 = (pred[128,1024]{1,0:T(32,128)(4,1)S(1)}, pred[128,1024]{1,0:T(32,128)(4,1)}, u32[]{:S(2)}) copy-start(pred[128,1024]{1,0:T(32,128)(4,1)} %get-tuple-element.65) | copy-start | bytes 393220
  242.8 37.5 %copy-start.24 = (pred[128,1024]{1,0:T(32,128)(4,1)S(1)}, pred[128,1024]{1,0:T(32,128)(4,1)}, u32[]{:S(2)}) copy-start(pred[128,1024]{1,0:T(32,128)(4,1)} %get-tuple-element.66) | copy-start | bytes 393220
  278.7 3.9 %copy-start.19 = (f32[128,768]{1,0:T(8,128)S(1)}, f32[128,768]{1,0:T(8,128)}, u32[]{:S(2)}) copy-start(f32[128,768]{1,0:T(8,128)} %copy-done.18) | copy-start | bytes 1179652
  278.7 3.9 %copy-start.13 = (f32[128,768]{1,0:T(8,128)S(1)}, f32[128,768]{1,0:T(8,128)}, u32[]{:S(2)}) copy-start(f32[128,768]{1,0:T(8,128)} %copy-done.12) | copy-start | bytes 1179652
  278.8 3.9 %copy-start.15 = (f32[128,768]{1,0:T(8,128)S(1)}, f32[128,768]{1,0:T(8,128)}, u32[]{:S(2)}) copy-start(f32[128,768]{1,0:T(8,128)} %convert_reduce_fusion) | copy-start | bytes 1179652
  278.8 3.9 %copy-start.17 = (bf16[1,128,768]{2,1,0:T(8,128)(2,1)S(1)}, bf16[1,128,768]{2,1,0:T(8,128)(2,1)}, u32[]{:S(2)}) copy-start(bf16[1,128,768]{2,1,0:T(8,128)(2,1)} %param.23) | copy-start | bytes 589828
  278.8 3.9 %copy-start.28 = (f32[128]{0:T(128)S(1)}, f32[128]{0:T(128)}, u32[]{:S(2)}) copy-start(f32[128]{0:T(128)} %get-tuple-element.68) | copy-start | bytes 1540
  278.8 3.9 %copy-start.30 = (f32[128]{0:T(128)S(1)}, f32[128]{0:T(128)}, u32[]{:S(2)}) copy-start(f32[128]{0:T(128)} %copy-done.29) | copy-start | bytes 1540
  278.8 3.9 %copy-start.32 = (f32[128]{0:T(128)S(1)}, f32[128]{0:T(128)}, u32[]{:S(2)}) copy-start(f32[128]{0:T(128)} %copy-done.31) | copy-start | bytes 1540
  278.8 3.9 %copy-start.34 = (f32[128]{0:T(128)S(1)}, f32[128]{0:T(128)}, u32[]{:S(2)}) copy-start(f32[128]{0:T(128)} %copy-done.33) | copy-start | bytes 1540
  280.2 4.1 %copy-start.14 = (f32[768,1536]{1,0:T(8,128)S(1)}, f32[768,1536]{1,0:T(8,128)}, u32[]{:S(2)}) copy-start(f32[768,1536]{1,0:T(8,128)} %get-tuple-element.42) | copy-start | bytes 14155780
  282.7 3.8 %slice-start = ((s8[4718592]{0:T(1024)(128)(4,1)}), s8[4194304]{0:T(1024)(128)(4,1)S(1)}, s32[]{:S(2)}) async-start(s8[4718592]{0:T(1024)(128)(4,1)} %bitcast.161), calls=%async_computation.1 | async-start | bytes 8388608
  284.3 2.2 slice-start.1
Sparse Core Ops, SparseCore 0:
  10.8 86.9 all-gather.2

commit v3 on v2

--- a/solution.py
+++ b/solution.py
@@ -151,80 +151,55 @@
         wait_bytes(rows.at[pl.ds(0, 16)], send)
 
 
-def start_kernel(
-    tok, wmsg, rows, tok_all, w_all, rows_all,
-    wm, wo, xs, xo, send, recv, core_recv, own,
-):
+def start_kernel(tok, wmsg, tok_all, w_all, wm, wo, send, recv, core_recv, own):
     z, x, y, c = place()
     sib = (z, x, y, 1 - c)
-    mine = pl.ds(pl.multiple_of(c * 512, 512), 512)
-    theirs = pl.ds(pl.multiple_of((1 - c) * 512, 512), 512)
-    keep(wmsg, wm, own.at[0])
-    keep(rows.at[mine], xs, own.at[1])
+    keep(wmsg, wm, own)
     expected = greet_chips(z, x, y, c)
     for k in range(1, 4):
         signal(((z + k) % 4, x, y, c))
     arrive(expected + 3)
     push(wmsg, wo, send.at[0], core_recv.at[0], sib)
-    push(rows.at[theirs], xo, send.at[1], core_recv.at[1], sib)
     for k in range(1, 4):
-        push(tok, tok_all.at[z], send.at[2], recv.at[0], ((z + k) % 4, x, y, c))
+        push(tok, tok_all.at[z], send.at[1], recv.at[0], ((z + k) % 4, x, y, c))
     keep(tok, tok_all.at[z], recv.at[0])
-    wait_bytes(wm, own.at[0])
+    wait_bytes(wm, own)
     wait_bytes(wo, core_recv.at[0])
     wm[...] = wm[...] + wo[...]
     half = z * 8 + x * 2 + y // 2
     to_chips(
-        z, x, y, c, lambda there: wm.at[there[0]], w_all.at[half, y % 2], send.at[3], recv.at[1]
-    )
-    wait_bytes(xs, own.at[1])
-    wait_bytes(xo, core_recv.at[1])
-    xs[...] = xs[...] + xo[...]
-    me = block_of(z, x, y)
-    to_chips(
-        z, x, y, c,
-        lambda there: xs.at[pl.ds(pl.multiple_of(block_of(*there[:3]) - c * 512, 16), 16)],
-        rows_all.at[pl.ds(me, 16)], send.at[4], recv.at[2],
+        z, x, y, c, lambda there: wm.at[there[0]], w_all.at[half, y % 2], send.at[2], recv.at[1]
     )
     wait_bytes(w_all.at[:, c], recv.at[1])
-    push(w_all.at[:, c], w_all.at[:, c], send.at[5], core_recv.at[2], sib)
-    wait_bytes(rows_all.at[mine], recv.at[2])
-    push(rows_all.at[mine], rows_all.at[mine], send.at[6], core_recv.at[3], sib)
+    push(w_all.at[:, c], w_all.at[:, c], send.at[3], core_recv.at[1], sib)
     wait_bytes(tok_all, recv.at[0])
-    wait_bytes(w_all.at[:, 1 - c], core_recv.at[2])
-    wait_bytes(rows_all.at[theirs], core_recv.at[3])
+    wait_bytes(w_all.at[:, 1 - c], core_recv.at[1])
     wait_bytes(wo, send.at[0])
-    wait_bytes(xo, send.at[1])
-    wait_bytes(tok_all.at[pl.ds(0, 3)], send.at[2])
-    wait_bytes(w_all.at[pl.ds(0, 31), c], send.at[3])
+    wait_bytes(tok_all.at[pl.ds(0, 3)], send.at[1])
+    wait_bytes(w_all.at[pl.ds(0, 31), c], send.at[2])
 
     @pl.when(y % 2 != c)
     def _():
-        wait_bytes(w_all.at[0, c], send.at[3])
-
-    sent_to_chips(rows_all, y, c, send.at[4])
-    wait_bytes(w_all.at[:, c], send.at[5])
-    wait_bytes(rows_all.at[mine], send.at[6])
-
-
-def start_exchange(tok, wmsg, rows):
+        wait_bytes(w_all.at[0, c], send.at[2])
+
+    wait_bytes(w_all.at[:, c], send.at[3])
+
+
+def start_exchange(tok, wmsg):
     return run_comm(
         start_kernel,
-        (tok, wmsg, rows),
+        (tok, wmsg),
         (
             jax.ShapeDtypeStruct((4, TOK, D), BF),
             jax.ShapeDtypeStruct((32, 2, 16, 3 * GW), BF),
-            jax.ShapeDtypeStruct((1024, D), BF),
         ),
         [
             pltpu.VMEM((4, 16, 3 * GW), BF),
             pltpu.VMEM((4, 16, 3 * GW), BF),
-            pltpu.VMEM((512, D), BF),
-            pltpu.VMEM((512, D), BF),
-            DMA((7,)),
-            DMA((3,)),
             DMA((4,)),
             DMA((2,)),
+            DMA((2,)),
+            DMA,
         ],
         0,
         "start_exchange",
@@ -429,66 +404,6 @@
     )
 
 
-def kv_kernel(kv, kv_all, send, recv):
-    z, x, y, c = place()
-    for k in range(1, 4):
-        signal((z, (x + k) % 4, y, c))
-    arrive(3)
-    for k in range(1, 4):
-        for b in range(4):
-            push(kv.at[b], kv_all.at[b, x], send, recv, (z, (x + k) % 4, y, c))
-    for b in range(4):
-        keep(kv.at[b], kv_all.at[b, x], recv)
-    wait_bytes(kv_all, recv)
-    wait_bytes(kv_all.at[pl.ds(0, 3)], send)
-
-
-def kv_gather(kv):
-    return run_comm(
-        kv_kernel,
-        (kv,),
-        jax.ShapeDtypeStruct((4, 4, TOK, 2 * GW), BF),
-        [DMA, DMA],
-        2,
-        "kv_gather",
-    )
-
-
-def kv_back_kernel(dkv, branch, parts, branch_all, send, recv):
-    z, x, y, c = place()
-    for k in range(1, 4):
-        signal((z, (x + k) % 4, y, c))
-        signal(((z + k) % 4, x, y, c))
-    arrive(6)
-    for k in range(1, 4):
-        there = (x + k) % 4
-        for b in range(4):
-            push(dkv.at[b, there], parts.at[x, b], send.at[0], recv.at[0], (z, there, y, c))
-    for k in range(1, 4):
-        push(branch, branch_all.at[z], send.at[1], recv.at[1], ((z + k) % 4, x, y, c))
-    for b in range(4):
-        keep(dkv.at[b, x], parts.at[x, b], recv.at[0])
-    keep(branch, branch_all.at[z], recv.at[1])
-    wait_bytes(parts, recv.at[0])
-    wait_bytes(branch_all, recv.at[1])
-    wait_bytes(parts.at[pl.ds(0, 3)], send.at[0])
-    wait_bytes(branch_all.at[pl.ds(0, 3)], send.at[1])
-
-
-def kv_back(dkv, branch):
-    return run_comm(
-        kv_back_kernel,
-        (dkv, branch),
-        (
-            jax.ShapeDtypeStruct((4, 4, TOK, 2 * GW), BF),
-            jax.ShapeDtypeStruct((4, TOK, D), BF),
-        ),
-        [DMA((2,)), DMA((2,))],
-        3,
-        "kv_back",
-    )
-
-
 def device_of(d):
     return d // 32, (d // 8) % 4, (d // 2) % 4, d % 2
 
@@ -622,216 +537,338 @@
     return jnp.clip((zq - zk) * 4 + x - kx + 1, 0, 3)
 
 
-def attn_forward_kernel(pos, tab, q, kv, qd, kd, out, p_out, bias, v_s, s_s):
-    h = pl.program_id(0)
-    x = pos[0]
-
-    @pl.when(h == 0)
+def block_cols(zk, kx):
+    return pl.ds(pl.multiple_of((zk * 4 + kx) * TOK, TOK), TOK)
+
+
+VMEM = pl.BlockSpec(memory_space=pltpu.VMEM)
+SMEM = pl.BlockSpec(memory_space=pltpu.SMEM)
+
+
+def attn_forward_kernel(
+    tab, q, kv, qd, kd, d_eo, wa,
+    attn_all, part, p_out, kv_out, d_rows, wa_all,
+    kv_s, v_s, qm, bias, s_s, p_s, xs, xo, wm, wo,
+    send, recv, kv_recv, core_recv, own,
+):
+    z, x, y, c = place()
+    sib = (z, x, y, 1 - c)
+    mine = pl.ds(pl.multiple_of(c * 512, 512), 512)
+    theirs = pl.ds(pl.multiple_of((1 - c) * 512, 512), 512)
+    keep(d_eo.at[mine], xs, own.at[0])
+    expected = greet_chips(z, x, y, c)
+    for k in range(1, 4):
+        signal(((z + k) % 4, x, y, c))
+        signal((z, (x + k) % 4, y, c))
+    arrive(expected + 6)
+    for k in range(1, 4):
+        for b in range(4):
+            push(
+                kv.at[b], kv_s.at[block_cols(b, x)], send.at[0], kv_recv.at[4 - k],
+                (z, (x + k) % 4, y, c),
+            )
+    for b in range(4):
+        keep(kv.at[b], kv_s.at[block_cols(b, x)], kv_recv.at[0])
+    push(wa, wo, send.at[1], core_recv.at[0], sib)
+    push(d_eo.at[theirs], xo, send.at[2], core_recv.at[1], sib)
+    for h in range(GH):
+        head_cols = lax.broadcasted_iota(jnp.int32, (1, GW), 1) // HD == h
+        qm[h] = jnp.where(head_cols, q[...] * 0.125, 0.0).astype(BF)
+    wait_bytes(wo, core_recv.at[0])
+    wm[...] = wa[...] + wo[...]
+    half = z * 8 + x * 2 + y // 2
+    to_chips(z, x, y, c, lambda there: wm, wa_all.at[half, y % 2], send.at[3], recv.at[0])
+    wait_bytes(xs, own.at[0])
+    wait_bytes(xo, core_recv.at[1])
+    xs[...] = xs[...] + xo[...]
+    me = block_of(z, x, y)
+    to_chips(
+        z, x, y, c,
+        lambda there: xs.at[pl.ds(pl.multiple_of(block_of(*there[:3]) - c * 512, 16), 16)],
+        d_rows.at[pl.ds(me, 16)], send.at[4], recv.at[1],
+    )
+
+    def tables(h):
+        for dist in range(2):
+            n = near_distance(dist)
+            acc = jnp.full((TOK, TOK), tab[0, h], F32)
+            for k, edge in enumerate(bucket_edges):
+                acc = jnp.where(n >= edge, tab[k + 1, h], acc)
+            bias[h, 1 + dist] = jnp.where(n >= 0, acc, masked)
+        bias[h, 0] = jnp.full((TOK, TOK), masked, F32)
+        bias[h, 3] = jnp.full((TOK, TOK), tab[BUCKETS - 1, h], F32)
+
+    loop(0, GH, tables)
+    for k in range(4):
+        kx = (x + k) % 4
+        if k == 0:
+            for b in range(4):
+                wait_bytes(kv_s.at[block_cols(b, kx)], kv_recv.at[0])
+        else:
+            wait_bytes(kv_s.at[pl.ds(0, 512)], kv_recv.at[k])
+        for b in range(4):
+            cols = block_cols(b, kx)
+            v_s[cols, :] = kv_s[cols, GW:]
+            for h in range(GH):
+                s_s[h, b * TOK :, cols] = dot(qm[h, b * TOK :, :], kv_s[cols, :GW], NT)
+    keep(kv_s, kv_out, own.at[1])
+    wait_bytes(wa_all.at[:, c], recv.at[0])
+    push(wa_all.at[:, c], wa_all.at[:, c], send.at[5], core_recv.at[2], sib)
+
+    def head(h):
+        head_cols = lax.broadcasted_iota(jnp.int32, (1, GW), 1) // HD == h
+        far = tab[BUCKETS - 1, h]
+        for zq in range(4):
+            rows = pl.ds(zq * TOK, TOK)
+            docs = qd[rows, :]
+            top = None
+            for zk in range(zq + 1):
+                for kx in range(4):
+                    cols = pl.ds((zk * 4 + kx) * TOK, TOK)
+                    s = s_s[h, rows, cols]
+                    if zk < zq - 1:
+                        s = s + far
+                    else:
+                        s = s + bias[h, table_kind(zq, zk, x, kx)]
+                    s = jnp.where(docs == kd[:, cols], s, masked)
+                    s_s[h, rows, cols] = s
+                    top = s if top is None else jnp.maximum(top, s)
+            top = jnp.max(top, axis=1, keepdims=True)
+            total = jnp.zeros((TOK, TOK), F32)
+            for kb in range(4 * (zq + 1)):
+                cols = pl.ds(kb * TOK, TOK)
+                e = jnp.exp(s_s[h, rows, cols] - top)
+                s_s[h, rows, cols] = e
+                total = total + e
+            inv = 1.0 / jnp.sum(total, axis=1, keepdims=True)
+            for kb in range(4 * (zq + 1)):
+                cols = pl.ds(kb * TOK, TOK)
+                p_s[h, rows, cols] = (s_s[h, rows, cols] * inv).astype(BF)
+            width = (zq + 1) * 512
+            o = dot(p_s[h, rows, :width], v_s[:width, :], NN).astype(BF)
+
+            @pl.when(h == 0)
+            def _():
+                part[rows, :] = o
+
+            @pl.when(h > 0)
+            def _():
+                part[rows, :] = jnp.where(head_cols, o, part[rows, :])
+
+    loop(0, GH, head)
+    for k in range(1, 4):
+        there = (z + k) % 4
+        push(
+            part.at[pl.ds(pl.multiple_of(there * TOK, TOK), TOK)], attn_all.at[z],
+            send.at[6], recv.at[2], (there, x, y, c),
+        )
+    keep(part.at[pl.ds(pl.multiple_of(z * TOK, TOK), TOK)], attn_all.at[z], recv.at[2])
+    keep(p_s, p_out, own.at[2])
+    wait_bytes(d_rows.at[mine], recv.at[1])
+    push(d_rows.at[mine], d_rows.at[mine], send.at[7], core_recv.at[3], sib)
+    wait_bytes(attn_all, recv.at[2])
+    wait_bytes(wa_all.at[:, 1 - c], core_recv.at[2])
+    wait_bytes(d_rows.at[theirs], core_recv.at[3])
+    wait_bytes(kv_s, own.at[1])
+    wait_bytes(p_s, own.at[2])
+    wait_bytes(kv_s.at[pl.ds(0, 1536)], send.at[0])
+    wait_bytes(wo, send.at[1])
+    wait_bytes(xo, send.at[2])
+    wait_bytes(wa_all.at[pl.ds(0, 31), c], send.at[3])
+
+    @pl.when(y % 2 != c)
     def _():
-        v_s[...] = kv[:, GW:]
-
-    for dist in range(2):
-        n = near_distance(dist)
-        acc = jnp.full((TOK, TOK), tab[0, h], F32)
-        for k, edge in enumerate(bucket_edges):
-            acc = jnp.where(n >= edge, tab[k + 1, h], acc)
-        bias[1 + dist] = jnp.where(n >= 0, acc, masked)
-    bias[0] = jnp.full((TOK, TOK), masked, F32)
-    far = tab[BUCKETS - 1, h]
-    bias[3] = jnp.full((TOK, TOK), far, F32)
-    head_cols = lax.broadcasted_iota(jnp.int32, (1, GW), 1) // HD == h
-    for zk in range(4):
-        qm = jnp.where(head_cols, q[zk * TOK :, :] * 0.125, 0.0).astype(BF)
-        s_s[zk * TOK :, zk * 512 : (zk + 1) * 512] = dot(qm, kv[zk * 512 : (zk + 1) * 512, :GW], NT)
-    for zq in range(4):
-        rows = pl.ds(zq * TOK, TOK)
-        docs = qd[rows, :]
-        top = None
-        for zk in range(zq + 1):
-            for kx in range(4):
-                cols = pl.ds((zk * 4 + kx) * TOK, TOK)
-                s = s_s[rows, cols]
-                if zk < zq - 1:
-                    s = s + far
-                else:
-                    s = s + bias[table_kind(zq, zk, x, kx)]
-                s = jnp.where(docs == kd[:, cols], s, masked)
-                s_s[rows, cols] = s
-                top = s if top is None else jnp.maximum(top, s)
-        top = jnp.max(top, axis=1, keepdims=True)
-        total = jnp.zeros((TOK, TOK), F32)
-        for kb in range(4 * (zq + 1)):
-            cols = pl.ds(kb * TOK, TOK)
-            e = jnp.exp(s_s[rows, cols] - top)
-            s_s[rows, cols] = e
-            total = total + e
-        inv = 1.0 / jnp.sum(total, axis=1, keepdims=True)
-        for kb in range(4 * (zq + 1)):
-            cols = pl.ds(kb * TOK, TOK)
-            p_out[0, rows, cols] = (s_s[rows, cols] * inv).astype(BF)
-        width = (zq + 1) * 512
-        o = dot(p_out[0, rows, :width], v_s[:width, :], NN).astype(BF)
-
-        @pl.when(h == 0)
-        def _():
-            out[rows, :] = o
-
-        @pl.when(h > 0)
-        def _():
-            out[rows, :] = jnp.where(head_cols, o, out[rows, :])
-
-
-def whole(shape):
-    return pl.BlockSpec(shape, lambda h: (0,) * len(shape))
-
-
-def attn_forward(pos, tab, q, kv, qd, kd):
-    smem = pl.BlockSpec(memory_space=pltpu.SMEM)
+        wait_bytes(wa_all.at[0, c], send.at[3])
+
+    sent_to_chips(d_rows, y, c, send.at[4])
+    wait_bytes(wa_all.at[:, c], send.at[5])
+    wait_bytes(attn_all.at[pl.ds(0, 3)], send.at[6])
+    wait_bytes(d_rows.at[mine], send.at[7])
+
+
+def attn_forward(tab, q, kv, qd, kd, d_eo, wa):
+    probs = (GH, 512, 2048)
     return pl.pallas_call(
         attn_forward_kernel,
-        grid=(GH,),
+        out_shape=(
+            jax.ShapeDtypeStruct((4, TOK, GW), BF),
+            jax.ShapeDtypeStruct((512, GW), BF),
+            jax.ShapeDtypeStruct(probs, BF),
+            jax.ShapeDtypeStruct((2048, 2 * GW), BF),
+            jax.ShapeDtypeStruct((1024, D), BF),
+            jax.ShapeDtypeStruct((32, 2, 16, D), BF),
+        ),
+        in_specs=[SMEM, VMEM, VMEM, VMEM, VMEM, ANY, VMEM],
+        out_specs=(ANY, VMEM, ANY, ANY, ANY, ANY),
+        scratch_shapes=[
+            pltpu.VMEM((2048, 2 * GW), BF),
+            pltpu.VMEM((2048, GW), BF),
+            pltpu.VMEM((GH, 512, GW), BF),
+            pltpu.VMEM((GH, 4, TOK, TOK), F32),
+            pltpu.VMEM(probs, F32),
+            pltpu.VMEM(probs, BF),
+            pltpu.VMEM((512, D), BF),
+            pltpu.VMEM((512, D), BF),
+            pltpu.VMEM((16, D), BF),
+            pltpu.VMEM((16, D), BF),
+            DMA((8,)),
+            DMA((3,)),
+            DMA((4,)),
+            DMA((4,)),
+            DMA((3,)),
+        ],
+        compiler_params=pltpu.CompilerParams(
+            collective_id=2, has_side_effects=True, vmem_limit_bytes=44 * 2**20
+        ),
+        name="attn_forward",
+    )(tab, q, kv, qd, kd, d_eo, wa)
+
+
+def attn_backward_kernel(
+    p, q, kv, d_attn, branch, dq, tab, parts, branch_all,
+    p_s, v_s, do_s, dm, qm, dp_s, ds_s, near, messages,
+    send, recv, own,
+):
+    z, x, y, c = place()
+    keep(p, p_s, own)
+    for k in range(1, 4):
+        signal(((z + k) % 4, x, y, c))
+        signal((z, (x + k) % 4, y, c))
+    arrive(6)
+    for k in range(1, 4):
+        there = (z + k) % 4
+        push(d_attn.at[there], do_s.at[z], send.at[0], recv.at[0], (there, x, y, c))
+    keep(d_attn.at[z], do_s.at[z], recv.at[0])
+    for k in range(1, 4):
+        push(branch, branch_all.at[z], send.at[1], recv.at[1], ((z + k) % 4, x, y, c))
+    keep(branch, branch_all.at[z], recv.at[1])
+    v_s[...] = kv[:, GW:]
+    for h in range(GH):
+        head_cols = lax.broadcasted_iota(jnp.int32, (1, GW), 1) // HD == h
+        qm[h] = jnp.where(head_cols, q[...] * 0.125, 0.0).astype(BF)
+    wait_bytes(do_s, recv.at[0])
+    for h in range(GH):
+        head_cols = lax.broadcasted_iota(jnp.int32, (1, GW), 1) // HD == h
+        for b in range(4):
+            dm[h, b * TOK : (b + 1) * TOK, :] = jnp.where(head_cols, do_s[b], 0.0).astype(BF)
+    wait_bytes(p_s, own)
+
+    def key_sums(left, right, first):
+        for k in (1, 2, 3, 0):
+            kx = (x + k) % 4
+            for b in range(4):
+                cols = block_cols(b, kx)
+                total = None
+                for h in range(GH):
+                    one = dot(left[h, b * TOK :, cols], right[h, b * TOK :, :], TN)
+                    total = one if total is None else total + one
+                side = GW * (b % 2)
+                messages[k, first + b // 2, :, side : side + GW] = total.astype(BF)
+            for m in range(first, first + 2):
+                if k:
+                    push(
+                        messages.at[k, m], parts.at[x, m], send.at[2], recv.at[2],
+                        (z, kx, y, c),
+                    )
+                else:
+                    keep(messages.at[k, m], parts.at[x, m], recv.at[2])
+
+    key_sums(p_s, dm, 0)
+
+    def head(h):
+        head_cols = lax.broadcasted_iota(jnp.int32, (1, GW), 1) // HD == h
+        for zk in range(4):
+            cols = pl.ds(zk * 512, 512)
+            dp_s[zk * TOK :, cols] = dot(dm[h, zk * TOK :, :], v_s[cols, :], NT)
+        near[...] = jnp.zeros_like(near)
+        for zq in range(4):
+            rows = pl.ds(zq * TOK, TOK)
+            acc = jnp.zeros((TOK, TOK), F32)
+            for kb in range(4 * (zq + 1)):
+                cols = pl.ds(kb * TOK, TOK)
+                acc = acc + p_s[h, rows, cols].astype(F32) * dp_s[rows, cols]
+            delta = jnp.sum(acc, axis=1, keepdims=True)
+            far = jnp.zeros((TOK, TOK), F32)
+            for zk in range(zq + 1):
+                for kx in range(4):
+                    cols = pl.ds((zk * 4 + kx) * TOK, TOK)
+                    ds = (p_s[h, rows, cols].astype(F32) * (dp_s[rows, cols] - delta)).astype(BF)
+                    ds_s[h, rows, cols] = ds
+                    if zk < zq - 1:
+                        far = far + ds.astype(F32)
+                    else:
+                        near[table_kind(zq, zk, x, kx)] += ds.astype(F32)
+            near[3] += far
+            width = (zq + 1) * 512
+            o = (dot(ds_s[h, rows, :width], kv[:width, :GW], NN) * 0.125).astype(BF)
+
+            @pl.when(h == 0)
+            def _():
+                dq[rows, :] = o
+
+            @pl.when(h > 0)
+            def _():
+                dq[rows, :] = jnp.where(head_cols, o, dq[rows, :])
+
+        for dist in range(2):
+            n = near_distance(dist)
+            held = near[1 + dist]
+            bounds = [-(10**6)] + bucket_edges + [10**6]
+            for b in range(BUCKETS):
+                low, high = bounds[b], bounds[b + 1]
+                if high <= dist * TOK - TOK + 1 or low > dist * TOK + TOK - 1:
+                    if dist == 0:
+                        tab[h, b : b + 1, :] = jnp.zeros((1, TOK), F32)
+                    continue
+                inside = jnp.sum(
+                    jnp.where((n >= low) & (n < high), held, 0.0), axis=0, keepdims=True
+                )
+                if dist == 0:
+                    tab[h, b : b + 1, :] = inside
+                else:
+                    tab[h, b : b + 1, :] += inside
+        tab[h, BUCKETS - 1 :, :] += jnp.sum(near[3], axis=0, keepdims=True)
+
+    loop(0, GH, head)
+    key_sums(ds_s, qm, 2)
+    wait_bytes(parts, recv.at[2])
+    wait_bytes(branch_all, recv.at[1])
+    wait_bytes(do_s.at[pl.ds(0, 3)], send.at[0])
+    wait_bytes(branch_all.at[pl.ds(0, 3)], send.at[1])
+    wait_bytes(parts.at[pl.ds(0, 3)], send.at[2])
+
+
+def attn_backward(p, q, kv, d_attn, branch):
+    probs = (GH, 512, 2048)
+    return pl.pallas_call(
+        attn_backward_kernel,
         out_shape=(
             jax.ShapeDtypeStruct((512, GW), BF),
-            jax.ShapeDtypeStruct((GH, 512, 2048), BF),
+            jax.ShapeDtypeStruct((GH, BUCKETS, TOK), F32),
+            jax.ShapeDtypeStruct((4, 4, TOK, 2 * GW), BF),
+            jax.ShapeDtypeStruct((4, TOK, D), BF),
         ),
-        in_specs=[
-            smem, smem, whole((512, GW)), whole((2048, 2 * GW)), whole((512, 1)), whole((1, 2048)),
-        ],
-        out_specs=(whole((512, GW)), pl.BlockSpec((1, 512, 2048), lambda h: (h, 0, 0))),
+        in_specs=[ANY, VMEM, VMEM, VMEM, VMEM],
+        out_specs=(VMEM, VMEM, ANY, ANY),
         scratch_shapes=[
+            pltpu.VMEM(probs, BF),
+            pltpu.VMEM((2048, GW), BF),
+            pltpu.VMEM((4, TOK, GW), BF),
+            pltpu.VMEM((GH, 512, GW), BF),
+            pltpu.VMEM((GH, 512, GW), BF),
+            pltpu.VMEM((512, 2048), F32),
+            pltpu.VMEM(probs, BF),
             pltpu.VMEM((4, TOK, TOK), F32),
-            pltpu.VMEM((2048, GW), BF),
-            pltpu.VMEM((512, 2048), F32),
+            pltpu.VMEM((4, 4, TOK, 2 * GW), BF),
+            DMA((3,)),
+            DMA((3,)),
+            DMA,
         ],
         compiler_params=pltpu.CompilerParams(
-            dimension_semantics=("arbitrary",), vmem_limit_bytes=40 * 2**20
-        ),
-        name="attn_forward",
-    )(pos, tab, q, kv, qd, kd)
-
-
-def attn_backward_kernel(pos, p, q, kv, do, dq, dkv, tab, v_s, dk_s, dv_s, dp_s, ds_s, near):
-    h = pl.program_id(0)
-    x = pos[0]
-
-    @pl.when(h == 0)
-    def _():
-        v_s[...] = kv[:, GW:]
-
-    head_cols = lax.broadcasted_iota(jnp.int32, (1, GW), 1) // HD == h
-    for zk in range(4):
-        dm = jnp.where(head_cols, do[zk * TOK :, :], 0.0).astype(BF)
-        cols = pl.ds(zk * 512, 512)
-        dp_s[zk * TOK :, cols] = dot(dm, v_s[cols, :], NT)
-        dv = dot(p[0, zk * TOK :, cols], dm, TN)
-
-        @pl.when(h == 0)
-        def _():
-            dv_s[cols, :] = dv
-
-        @pl.when(h > 0)
-        def _():
-            dv_s[cols, :] += dv
-
-    near[...] = jnp.zeros_like(near)
-    for zq in range(4):
-        rows = pl.ds(zq * TOK, TOK)
-        acc = jnp.zeros((TOK, TOK), F32)
-        for kb in range(4 * (zq + 1)):
-            cols = pl.ds(kb * TOK, TOK)
-            acc = acc + p[0, rows, cols].astype(F32) * dp_s[rows, cols]
-        delta = jnp.sum(acc, axis=1, keepdims=True)
-        far = jnp.zeros((TOK, TOK), F32)
-        for zk in range(zq + 1):
-            for kx in range(4):
-                cols = pl.ds((zk * 4 + kx) * TOK, TOK)
-                ds = (p[0, rows, cols].astype(F32) * (dp_s[rows, cols] - delta)).astype(BF)
-                ds_s[rows, cols] = ds
-                if zk < zq - 1:
-                    far = far + ds.astype(F32)
-                else:
-                    near[table_kind(zq, zk, x, kx)] += ds.astype(F32)
-        near[3] += far
-        width = (zq + 1) * 512
-        o = (dot(ds_s[rows, :width], kv[:width, :GW], NN) * 0.125).astype(BF)
-
-        @pl.when(h == 0)
-        def _():
-            dq[rows, :] = o
-
-        @pl.when(h > 0)
-        def _():
-            dq[rows, :] = jnp.where(head_cols, o, dq[rows, :])
-
-    for zk in range(4):
-        qm = jnp.where(head_cols, q[zk * TOK :, :] * 0.125, 0.0).astype(BF)
-        cols = pl.ds(zk * 512, 512)
-        dk = dot(ds_s[zk * TOK :, cols], qm, TN)
-
-        @pl.when(h == 0)
-        def _():
-            dk_s[cols, :] = dk
-
-        @pl.when(h > 0)
-        def _():
-            dk_s[cols, :] += dk
-
-    for dist in range(2):
-        n = near_distance(dist)
-        held = near[1 + dist]
-        bounds = [-(10**6)] + bucket_edges + [10**6]
-        for b in range(BUCKETS):
-            low, high = bounds[b], bounds[b + 1]
-            if high <= dist * TOK - TOK + 1 or low > dist * TOK + TOK - 1:
-                if dist == 0:
-                    tab[0, b : b + 1, :] = jnp.zeros((1, TOK), F32)
-                continue
-            part = jnp.sum(jnp.where((n >= low) & (n < high), held, 0.0), axis=0, keepdims=True)
-            if dist == 0:
-                tab[0, b : b + 1, :] = part
-            else:
-                tab[0, b : b + 1, :] += part
-    tab[0, BUCKETS - 1 :, :] += jnp.sum(near[3], axis=0, keepdims=True)
-
-    @pl.when(h == GH - 1)
-    def _():
-        dkv[:, :GW] = dk_s[...].astype(BF)
-        dkv[:, GW:] = dv_s[...].astype(BF)
-
-
-def attn_backward(pos, p, q, kv, do):
-    smem = pl.BlockSpec(memory_space=pltpu.SMEM)
-    return pl.pallas_call(
-        attn_backward_kernel,
-        grid=(GH,),
-        out_shape=(
-            jax.ShapeDtypeStruct((512, GW), BF),
-            jax.ShapeDtypeStruct((2048, 2 * GW), BF),
-            jax.ShapeDtypeStruct((GH, BUCKETS, TOK), F32),
-        ),
-        in_specs=[
-            smem,
-            pl.BlockSpec((1, 512, 2048), lambda h: (h, 0, 0)),
-            whole((512, GW)), whole((2048, 2 * GW)), whole((512, GW)),
-        ],
-        out_specs=(
-            whole((512, GW)),
-            whole((2048, 2 * GW)),
-            pl.BlockSpec((1, BUCKETS, TOK), lambda h: (h, 0, 0)),
-        ),
-        scratch_shapes=[
-            pltpu.VMEM((2048, GW), BF),
-            pltpu.VMEM((2048, GW), F32),
-            pltpu.VMEM((2048, GW), F32),
-            pltpu.VMEM((512, 2048), F32),
-            pltpu.VMEM((512, 2048), BF),
-            pltpu.VMEM((4, TOK, TOK), F32),
-        ],
-        compiler_params=pltpu.CompilerParams(
-            dimension_semantics=("arbitrary",), vmem_limit_bytes=48 * 2**20
+            collective_id=3, has_side_effects=True, vmem_limit_bytes=44 * 2**20
         ),
         name="attn_backward",
-    )(pos, p, q, kv, do)
+    )(p, q, kv, d_attn, branch)
 
 
 def per_device(
@@ -885,8 +922,13 @@
         jnp.concatenate([slab, nothing, notes, nothing[:, :3]], axis=1),
         jnp.concatenate([nothing, slab, nothing[:, :1], notes, nothing[:, :2]], axis=1),
     )
-    attention_weight = lax.all_gather(w_attn_out, AXES, axis=0, tiled=True)
-    tok_all, w_all, d_eo_all = start_exchange(own_tokens, message, d_eo)
+    zero_rows = jnp.zeros((6, D), BF)
+    out_slab = jnp.where(
+        c == 0,
+        jnp.concatenate([w_attn_out, zero_rows, zero_rows[:4]], axis=0),
+        jnp.concatenate([zero_rows, w_attn_out, zero_rows[:4]], axis=0),
+    )
+    tok_all, w_all = start_exchange(own_tokens, message)
 
     weight = w_all[:, :, :12, :].reshape(D, 3 * GW)
     gain_one = w_all[:, :, 12:14, 0:6].reshape(D).astype(F32)
@@ -900,12 +942,12 @@
     normed = scale_rows(inputs_all, gain_one).astype(BF)
     qkv = dot(normed, weight, NN).astype(BF)
     queries = qkv[:, :GW]
-    kv_all = kv_gather(qkv[:, GW:].reshape(4, TOK, 2 * GW)).reshape(2048, 2 * GW)
     table = lax.dynamic_slice(rel_table, (0, z * GH), (BUCKETS, GH)).astype(F32)
-    pos = jnp.full((1,), x, jnp.int32)
-    attn_part, probs = attn_forward(pos, table, queries, kv_all, query_docs, key_docs)
-    attn = z_exchange(attn_part.reshape(4, TOK, GW), 5, "attn_exchange")
+    attn, attn_part, probs, kv_all, d_eo_all, out_weights = attn_forward(
+        table, queries, qkv[:, GW:].reshape(4, TOK, 2 * GW), query_docs, key_docs, d_eo, out_slab
+    )
     attn = attn.transpose(1, 0, 2).reshape(TOK, D)
+    attention_weight = out_weights[:, :, :12, :].reshape(D, D)
 
     inputs = own_tokens.astype(F32)
     middle = inputs + dot(attn, attention_weight, NN)
@@ -921,11 +963,11 @@
     branch = middle_grad.astype(BF)
     d_attn = dot(branch, attention_weight, NT).astype(BF)
     d_attn = d_attn.reshape(TOK, GROUPS, GW).transpose(1, 0, 2)
-    d_attn = z_exchange(d_attn, 7, "d_attn_exchange").reshape(512, GW)
-
-    d_q, d_kv, table_part = attn_backward(pos, probs, queries, kv_all, d_attn)
-    kv_parts, branch_all = kv_back(d_kv.reshape(4, 4, TOK, 2 * GW), branch)
-    d_kv = jnp.sum(kv_parts.astype(F32), axis=0).astype(BF).reshape(512, 2 * GW)
+
+    d_q, table_part, kv_parts, branch_all = attn_backward(probs, queries, kv_all, d_attn, branch)
+    d_kv = jnp.sum(kv_parts.astype(F32), axis=0).astype(BF)
+    d_kv = d_kv.reshape(2, 2, TOK, 2, GW).transpose(0, 1, 3, 2, 4).reshape(2, 512, GW)
+    d_kv = jnp.concatenate([d_kv[1], d_kv[0]], axis=1)
     d_qkv = jnp.concatenate([d_q, d_kv], axis=1)
     normed_part = dot(d_qkv, weight, NT).astype(BF).reshape(4, TOK, D)
     normed_part = z_exchange(normed_part, 8, "normed_grads")

time: 299 us -> 268 us (0.90)
  Pallas kernels: 225 us -> 208 us
  between operations: 14.9 us -> 1.6 us
  local copies, waits for them, and re-layouts: 28.7 us -> 36.7 us
  other arithmetic: 13 us -> 8.81 us
  matrix products: 13.2 us -> 9.96 us
    pallas_call x7 -> x3, Pallas kernels: 137 us -> 76.3 us  [run_comm(): pl.pallas_call(kernel, out_shape=outs, in_specs=[ANY] * len(args), out_sp...]
    pallas_call x2, Pallas kernels: 31.3 us -> 74.6 us  [the longest x1 48.4 us: attn_forward(): pl.pallas_call(attn_forward_kernel, out_shape=(jax.ShapeDtypeStruct((4, T...]
    unnamed x88 -> x95, local copies, waits for them, and re-layouts: 14.8 us -> 23.1 us
    dot_general x10, matrix products: 13.2 us -> 9.96 us  [dot(): return lax.dot_general(a, b, dims, preferred_element_type=F32)]
  transfers between devices with their start and end apart: 1 -> 0, of which waited for: 0 -> 0; matrix products, arithmetic and copies ran while one was open for 7% -> 0% of each run, Pallas kernels for 26% -> 0%
where the time goes in v3:
time: 268 us; the launch traced here: 265 us
  Pallas kernels  208 us (78%)
  local copies, waits for them, and re-layouts  36.7 us (14%)
  matrix products  9.96 us (4%)
  other arithmetic  8.81 us (3%)
    pallas_call x3, Pallas kernels, run_comm(): pl.pallas_call(kernel, out_shape=outs, in_specs=[ANY] * len(args), out_sp...  76.3 us
    pallas_call x1, Pallas kernels, run_experts(): pl.pallas_call(experts_kernel, out_shape=(jax.ShapeDtypeStruct((1024, D),...  56.6 us
    pallas_call x1, Pallas kernels, attn_forward(): pl.pallas_call(attn_forward_kernel, out_shape=(jax.ShapeDtypeStruct((4, T...  48.4 us
    pallas_call x1, Pallas kernels, attn_backward(): pl.pallas_call(attn_backward_kernel, out_shape=(jax.ShapeDtypeStruct((512...  26.2 us
    unnamed x95, local copies, waits for them, and re-layouts  23.1 us
    dot_general x10, matrix products, dot(): return lax.dot_general(a, b, dims, preferred_element_type=F32)  9.96 us

profile of v3, /device:TPU:1, one launch (start us, length us, event | category | flops | bytes accessed | tf_op | source)
XLA Modules:
  0.0 264.7 jit_solution(13703636088801069840)
XLA Ops:
  0.7 0.8 copy.92
  1.7 0.6 reduce-window.6
  3.2 0.8 slice_bitcast_fusion.3
  4.2 1.7 multiply_convert_fusion.d_eo
  6.8 31.3 %start_exchange.1 = (bf16[4,128,768]{2,1,0:T(8,128)(2,1)S(1)}, bf16[32,2,16,576]{3,2,1,0:T(8,128)(2,1)S(1)}) custom-call(bf16[128,768]{1,0:T(8,128)(2,1)S(1)} %bitcast.143, bf16[4,16,576]{2,1,0:T(8,128)(2,1)S(1)} %maximum_select_fusion.wmsg), custom_call_target="tpu_custom_call" | custom-call | tf_op jit(solution)/shard_map/start_exchange/pallas_call | solution.py:94
  38.2 1.0 copy-done.9
  39.2 0.7 slice_convert_fusion
  40.3 0.6 fusion.57
  40.9 1.1 multiply_convert_fusion.1
  42.0 2.3 reshape.242
  44.3 0.9 copy-done.28
  45.2 1.9 convolution_convert_fusion.3
  47.4 0.9 slice.91
  48.9 48.4 %attn_forward.1 = (bf16[4,128,192]{2,1,0:T(8,128)(2,1)S(1)}, bf16[512,192]{1,0:T(8,128)(2,1)S(1)}, bf16[3,512,2048]{2,1,0:T(8,128)(2,1)}, bf16[2048,384]{1,0:T(8...) custom-call(f32[32,3]{1,0:T(8,128)S(1)} %convert_element_type.136.tab, ...), custom_call_target="tpu_custom_call" | custom-call | tf_op jit(solution)/shard_map/attn_forward/pallas_call | solution.py:691
  97.3 1.1 copy-done.2
  98.4 1.1 copy-done.7
  99.6 1.1 copy-done.8
  100.7 0.7 copy-done.12
  101.4 0.7 copy-done.14
  102.1 2.3 reshape.251
  104.6 0.5 multiply_reduce_fusion.3
  105.5 0.7 convolution_convert_fusion.x16
  106.2 56.6 %experts.1 = (bf16[1024,768]{1,0:T(8,128)(2,1)S(1)}, bf16[1024,768]{1,0:T(8,128)(2,1)S(1)}, f32[768,1536]{1,0:T(8,128)}, f32[1536,768]{1,0:T(8,128)}) custom-call(bf16[1024,768]{1,0:T(8,128)(2,1)S(1)} %convolution_convert_fusion.x16, bf16[1024,768]{1,0:T(8,128)(2,1)} %copy-done.8, bf16[768,1536]{1,0:T(8,128)(2,1)} %bitcast.160, bf16[1536,768]{1,0:T(8,128)(2,1)} %bitcast.161), custom_call_target="tpu_custom_call" | custom-call | tf_op jit(solution)/shard_map/experts/pallas_call | solution.py:359
  162.9 0.5 multiply_reduce_fusion.1
  164.2 0.8 copy-done.19
  165.0 0.5 convolution_convert_fusion.5
  165.9 1.4 copy-done.3
  167.3 26.2 %attn_backward.1 = (bf16[512,192]{1,0:T(8,128)(2,1)S(1)}, f32[3,32,128]{2,1,0:T(8,128)S(1)}, bf16[4,4,128,384]{3,2,1,0:T(8,128)(2,1)S(1)}, bf16[4,128,768]{2,1,0:T(8,128)(2,1)S(1)}) custom-call(bf16[3,512,2048]{2,1,0:T(8,128)(2,1)} %get-tuple-element.36.p, bf16[512,192]{1,0:T(8,128)(2,1)S(1)} %slice.110.q, bf16[2048,384]{1,0:T(8,128)(2,1)S(1)} %copy-done.3, ...), custom_call_target="tpu_custom_call" | custom-call | tf_op jit(solution)/shard_map/attn_backward/pallas_call | solution.py:843
  193.5 1.1 copy-done.4
  194.6 0.9 copy-done.10
  195.5 0.7 copy-done.16
  196.2 1.7 reduce_sum.155
  199.2 0.8 convolution_convert_fusion.2
  200.1 8.3 %normed_grads.1 = bf16[4,128,768]{2,1,0:T(8,128)(2,1)S(1)} custom-call(bf16[4,128,768]{2,1,0:T(8,128)(2,1)S(1)} %bitcast.149), custom_call_target="tpu_custom_call" | custom-call | tf_op jit(solution)/shard_map/normed_grads/pallas_call | solution.py:94
  208.5 0.7 copy-done.22
  210.7 0.5 copy-done.31
  211.2 1.7 convolution_convert_fusion.1
  212.9 1.5 copy.103
  214.4 36.7 %weight_sums.1 = (f32[4,8,576]{2,1,0:T(8,128)S(1)}, f32[8,768]{1,0:T(8,128)S(1)}, f32[4,8,128]{2,1,0:T(8,128)S(1)}) custom-call(bf16[32,24,576]{2,1,0:T(8,128)(2,1)S(1)} %bitcast.144, bf16[32,8,768]{2,1,0:T(8,128)(2,1)S(1)} %pad.21.att, f32[32,8,128]{2,1,0:T(8,128)S(1)} %select_maximum_fusion.small), custom_call_target="tpu_custom_call" | custom-call | tf_op jit(solution)/shard_map/weight_sums/pallas_call | solution.py:94
  251.4 0.7 reshape.263
  252.2 0.5 slice_bitcast_fusion
  252.7 0.7 reshape_squeeze.3
  253.6 1.0 bitcast_convert_fusion
  254.7 1.2 fusion.6
  256.0 1.0 fusion.29
  257.0 0.6 copy.121
  257.6 4.9 %copy.122 = f32[1,768,1536]{2,1,0:T(8,128)} copy(f32[1,768,1536]{2,1,0:T(8,128)} %bitcast.159) | data formatting | bytes 9437184
  262.5 2.2 copy.123
  (154 shorter events, 8.0 us)
Async XLA Ops:
  0.6 48.0 %copy-start = (bf16[32,12]{0,1:T(8,128)(2,1)S(1)}, bf16[32,12]{0,1:T(8,128)(2,1)}, u32[]{:S(2)}) copy-start(bf16[32,12]{0,1:T(8,128)(2,1)} %param.16) | copy-start | bytes 2308
  0.7 5.2 %copy-start.33 = (bf16[6,2304]{1,0:T(8,128)(2,1)S(1)}, bf16[6,2304]{1,0:T(8,128)(2,1)}, u32[]{:S(2)}) copy-start(bf16[6,2304]{1,0:T(8,128)(2,1)} %param.14) | copy-start | bytes 82948
  0.7 5.5 %copy-start.42 = (s32[1,128]{1,0:T(1,128)S(1)}, s32[1,128]{1,0:T(1,128)}, u32[]{:S(2)}) copy-start(s32[1,128]{1,0:T(1,128)} %param.22) | copy-start | bytes 1540
  0.7 5.5 %copy-start.40 = (bf16[6]{0:T(256)(128)(2,1)S(1)}, bf16[6]{0:T(256)(128)(2,1)}, u32[]{:S(2)}) copy-start(bf16[6]{0:T(256)(128)(2,1)} %param.13) | copy-start | bytes 40
  0.7 5.5 %copy-start.41 = (bf16[6]{0:T(256)(128)(2,1)S(1)}, bf16[6]{0:T(256)(128)(2,1)}, u32[]{:S(2)}) copy-start(bf16[6]{0:T(256)(128)(2,1)} %param.17) | copy-start | bytes 40
  2.7 4.1 %copy-start.1 = (bf16[1,128,768]{2,1,0:T(8,128)(2,1)S(1)}, bf16[1,128,768]{2,1,0:T(8,128)(2,1)}, u32[]{:S(2)}) copy-start(bf16[1,128,768]{2,1,0:T(8,128)(2,1)} %param.12) | copy-start | bytes 589828
  4.0 2.2 copy-start.36
  4.0 2.3 copy-start.38
  38.1 1.1 copy-start.9
  44.3 0.9 copy-start.28
  47.2 1.6 copy-start.34
  97.3 1.1 copy-start.2
  98.4 1.1 copy-start.7
  99.6 1.1 copy-start.8
  100.7 0.7 copy-start.12
  101.4 0.7 copy-start.14
  102.1 2.3 copy-start.13
  104.4 1.8 copy-start.18
  104.4 0.9 copy-start.32
  105.1 58.5 %copy-start.20 = (f32[128,768]{1,0:T(8,128)}, f32[128,768]{1,0:T(8,128)S(1)}, u32[]{:S(2)}) copy-start(f32[128,768]{1,0:T(8,128)S(1)} %get-tuple-element.67) | copy-start | bytes 1179652
  162.9 1.3 copy-start.5
  162.9 1.1 copy-start.24
  162.9 2.1 copy-start.19
  163.5 2.2 copy-start.26
  165.8 1.4 copy-start.3
  193.5 1.1 copy-start.4
  194.6 0.9 copy-start.10
  195.5 0.7 copy-start.16
  197.9 1.0 copy-start.17
  197.9 1.3 copy-start.29
  198.5 1.5 copy-start.30
  200.1 9.8 %copy-start.11 = (bf16[4,128,768]{2,1,0:T(8,128)(2,1)S(1)}, bf16[4,128,768]{2,1,0:T(8,128)(2,1)}, u32[]{:S(2)}) copy-start(bf16[4,128,768]{2,1,0:T(8,128)(2,1)} %copy-done.10) | copy-start | bytes 2359300
  200.1 9.8 %copy-start.15 = (bf16[512,192]{1,0:T(8,128)(2,1)S(1)}, bf16[512,192]{1,0:T(8,128)(2,1)}, u32[]{:S(2)}) copy-start(bf16[512,192]{1,0:T(8,128)(2,1)} %copy-done.14) | copy-start | bytes 589828
  208.5 0.7 copy-start.22
  209.5 1.0 copy-start.35
  210.2 1.0 copy-start.31
  214.4 40.2 %copy-start.6 = (bf16[1024,768]{1,0:T(8,128)(2,1)S(1)}, bf16[1024,768]{1,0:T(8,128)(2,1)}, u32[]{:S(2)}) copy-start(bf16[1024,768]{1,0:T(8,128)(2,1)} %copy-done.5) | copy-start | bytes 4718596
  254.6 1.3 copy-start.21
  254.6 1.3 copy-start.23
  254.6 1.3 copy-start.25
  254.6 1.3 copy-start.27
  254.7 1.3 copy-start.37
  254.7 1.3 copy-start.39
  256.0 6.6 %slice-start = ((s8[4718592]{0:T(1024)(128)(4,1)}), s8[4194304]{0:T(1024)(128)(4,1)S(1)}, s32[]{:S(2)}) async-start(s8[4718592]{0:T(1024)(128)(4,1)} %bitcast.156), calls=%async_computation | async-start | bytes 8388608
  257.6 4.9 %slice-start.1 = ((s8[4718592]{0:T(1024)(128)(4,1)}), s8[524288]{0:T(1024)(128)(4,1)S(1)}, s32[]{:S(2)}) async-start(s8[4718592]{0:T(1024)(128)(4,1)} %bitcast.156), calls=%async_computation.1 | async-start | bytes 1048576

commit v4 on v3

--- a/solution.py
+++ b/solution.py
@@ -211,8 +211,8 @@
 
 
 def experts_kernel(
-    x16, d_rows, w_in, w_out, home_in, home_out, g_in, g_out,
-    xs, xo, rows, dv, w1, w2, dh, hidden, dact, in_h, out_h, in_o, out_o, stage_out, stage_in,
+    x16, d_eo, w_in, w_out, home_in, home_out, g_in, g_out,
+    xs, xo, es, eo, rows, dv, w1, w2, slope, hidden, dact, in_h, out_h, in_o, out_o, stage_out, stage_in,
     send, recv, core_recv, own, staged,
 ):
     z, x, y, c = place()
@@ -222,12 +222,13 @@
     mine, theirs = pl.ds(at_mine, 512), pl.ds(at_theirs, 512)
     me = block_of(z, x, y)
     keep(x16.at[mine], xs, own.at[0])
-    keep(d_rows, dv, own.at[1])
+    keep(d_eo.at[mine], es, own.at[1])
     keep(w_out, w2, own.at[2])
     keep(w_in, w1, own.at[3])
     expected = greet_chips(z, x, y, c)
     arrive(expected)
     push(x16.at[theirs], xo, send.at[0], core_recv.at[0], sib)
+    push(d_eo.at[theirs], eo, send.at[9], core_recv.at[6], sib)
     wait_bytes(xs, own.at[0])
     wait_bytes(xo, core_recv.at[0])
     xs[...] = xs[...] + xo[...]
@@ -236,15 +237,16 @@
         lambda there: xs.at[pl.ds(pl.multiple_of(block_of(*there[:3]) - c * 512, 16), 16)],
         rows.at[pl.ds(me, 16)], send.at[1], recv.at[0],
     )
-    wait_bytes(dv, own.at[1])
+    wait_bytes(es, own.at[1])
+    wait_bytes(eo, core_recv.at[6])
+    es[...] = es[...] + eo[...]
+    to_chips(
+        z, x, y, c,
+        lambda there: es.at[pl.ds(pl.multiple_of(block_of(*there[:3]) - c * 512, 16), 16)],
+        dv.at[pl.ds(me, 16)], send.at[10], recv.at[3],
+    )
+    wait_bytes(w1, own.at[3])
     wait_bytes(w2, own.at[2])
-
-    def hidden_grads(n):
-        cols = pl.ds(pl.multiple_of(n * WIDE, WIDE), WIDE)
-        dh[:, cols] = dot(dv[...], w2[cols, :], NT)
-
-    loop(0, FH // WIDE, hidden_grads)
-    wait_bytes(w1, own.at[3])
     wait_bytes(rows.at[mine], recv.at[0])
     push(rows.at[mine], rows.at[mine], send.at[2], core_recv.at[1], sib)
 
@@ -258,10 +260,19 @@
             t = jnp.tanh(0.7978845608028654 * (a + 0.044715 * (square * a)))
             cdf = 0.5 * (1.0 + t)
             hidden[part, cols] = (a * cdf).astype(BF)
-            slope = cdf + 0.5 * a * (1.0 - t * t) * (
+            slope[part, cols] = cdf + 0.5 * a * (1.0 - t * t) * (
                 0.7978845608028654 * (1.0 + 0.134145 * square)
             )
-            dact[part, cols] = (slope * dh[part, cols]).astype(BF)
+
+        loop(0, FH // WIDE, one)
+
+    def act_grads(at):
+        part = pl.ds(at, 512)
+
+        def one(n):
+            cols = pl.ds(pl.multiple_of(n * WIDE, WIDE), WIDE)
+            d_hidden = dot(dv[part, :], w2[cols, :], NT)
+            dact[part, cols] = (slope[part, cols] * d_hidden).astype(BF)
 
         loop(0, FH // WIDE, one)
 
@@ -284,10 +295,15 @@
         loop(0, D // WIDE, one)
 
     activate(at_mine)
+    wait_bytes(dv.at[mine], recv.at[3])
+    push(dv.at[mine], dv.at[mine], send.at[11], core_recv.at[7], sib)
     wait_bytes(rows.at[theirs], core_recv.at[1])
     activate(at_theirs)
+    wait_bytes(dv.at[theirs], core_recv.at[7])
+    act_grads(at_theirs)
     in_half(at_theirs)
     push(in_h.at[theirs], in_o, send.at[3], core_recv.at[2], sib)
+    act_grads(at_mine)
     in_half(at_mine)
     wait_bytes(in_o, core_recv.at[2])
     in_o[...] = (in_o[...].astype(F32) + in_h[mine, :].astype(F32)).astype(BF)
@@ -350,9 +366,12 @@
     wait_bytes(home_out.at[theirs], core_recv.at[5])
     wait_bytes(home_in.at[mine], send.at[7])
     wait_bytes(home_out.at[mine], send.at[8])
-
-
-def run_experts(x16, d_rows, w_in, w_out):
+    wait_bytes(eo, send.at[9])
+    sent_to_chips(dv, y, c, send.at[10])
+    wait_bytes(dv.at[mine], send.at[11])
+
+
+def run_experts(x16, d_eo, w_in, w_out):
     whole_rows = pltpu.VMEM((1024, D), BF)
     half_rows = pltpu.VMEM((512, D), BF)
     hid = pltpu.VMEM((1024, FH), BF)
@@ -367,17 +386,17 @@
         in_specs=[ANY] * 4,
         out_specs=(ANY,) * 4,
         scratch_shapes=[
-            half_rows, half_rows, whole_rows, whole_rows,
+            half_rows, half_rows, half_rows, half_rows, whole_rows, whole_rows,
             pltpu.VMEM((D, FH), BF), pltpu.VMEM((FH, D), BF), pltpu.VMEM((1024, FH), F32),
             hid, hid, whole_rows, whole_rows, half_rows, half_rows,
             pltpu.VMEM((2, WIDE, D), F32), pltpu.VMEM((2, WIDE, FH), F32),
-            DMA((9,)), DMA((3,)), DMA((6,)), DMA((4,)), DMA((4,)),
+            DMA((12,)), DMA((4,)), DMA((8,)), DMA((4,)), DMA((4,)),
         ],
         compiler_params=pltpu.CompilerParams(
             collective_id=1, has_side_effects=True, vmem_limit_bytes=48 * 2**20
         ),
         name="experts",
-    )(x16, d_rows, w_in, w_out)
+    )(x16, d_eo, w_in, w_out)
 
 
 def z_kernel(blocks, out, send, recv):
@@ -408,114 +427,175 @@
     return d // 32, (d // 8) % 4, (d // 2) % 4, d % 2
 
 
-def sums_kernel(
-    qkv, att, small, qkv_out, att_out, small_out,
-    qkv_in, att_in, small_in, qkv_sum, att_sum, small_sum, send, recv, out_sem,
+def finish_kernel(
+    normed, qkv, att, small, tok, gain, d_middle,
+    input_grad, qkv_out, att_out, small_out,
+    normed_in, q_own, q_sib, q_in, a_own, a_sib, a_in, s_own, s_sib, s_tot, s_in,
+    qkv_sum, att_sum, s_sum, send, recv, core_recv, own,
 ):
     z, x, y, c = place()
-    p = x * 8 + y * 2 + c
+    sib = (z, x, y, 1 - c)
+    p16 = x * 4 + y
+    p = p16 * 2 + c
     me = z * 32 + p
+    source = me // 4
 
     def peer(i):
-        return (z, (x + i // 8) % 4, (y + (i // 2) % 4) % 4, (c + i % 2) % 2)
-
-    loop(1, 32, lambda i: signal(peer(i)))
-    source = me // 4
+        return z, (x + i // 4) % 4, (y + i % 4) % 4, c
+
+    keep(qkv.at[:, c], q_own, own.at[0])
+    keep(att.at[:, c], a_own, own.at[1])
+    loop(1, 16, lambda i: signal(peer(i)))
+    for k in range(1, 4):
+        signal(((z + k) % 4, x, y, c))
+    signal(sib)
 
     def greet(k):
-        from_me = (k == z) & (source == p)
-
-        @pl.when(jnp.logical_not(from_me))
+        @pl.when(jnp.logical_not((k == z) & (source == p)))
         def _():
             signal((k, source // 8, (source // 2) % 4, source % 2))
 
     loop(0, 4, greet)
-    arrive(31 + 4 - jnp.where(source == p, 1, 0))
-
-    def out(i):
+    arrive(15 + 3 + 1 + 4 - jnp.where(source == p, 1, 0))
+    for k in range(1, 4):
+        there = (z + k) % 4
+        push(normed.at[there], normed_in.at[z], send.at[0], recv.at[0], (there, x, y, c))
+    keep(normed.at[z], normed_in.at[z], recv.at[0])
+    push(qkv.at[:, 1 - c], q_sib, send.at[1], core_recv.at[0], sib)
+    push(att.at[:, 1 - c], a_sib, send.at[2], core_recv.at[1], sib)
+    wait_bytes(q_own, own.at[0])
+    wait_bytes(q_sib, core_recv.at[0])
+
+    def qkv_blocks(i):
         there = peer(i)
-        q = there[1] * 8 + there[2] * 2 + there[3]
-        push(qkv.at[q], qkv_in.at[p], send.at[0], recv.at[0], there)
-        push(att.at[q], att_in.at[p], send.at[1], recv.at[1], there)
-        push(small.at[q], small_in.at[p], send.at[2], recv.at[2], there)
-
-    loop(1, 32, out)
-    keep(qkv.at[p], qkv_in.at[p], recv.at[0])
-    keep(att.at[p], att_in.at[p], recv.at[1])
-    keep(small.at[p], small_in.at[p], recv.at[2])
-    wait_bytes(qkv_in, recv.at[0])
-    total = qkv_in[0].astype(F32)
-    for q in range(1, 32):
-        total = total + qkv_in[q].astype(F32)
+        j = there[1] * 4 + there[2]
+        q_own[j] = (q_own[j].astype(F32) + q_sib[j].astype(F32)).astype(BF)
+        push(q_own.at[j], q_in.at[p16], send.at[3], recv.at[1], there)
+
+    loop(1, 16, qkv_blocks)
+    q_own[p16] = (q_own[p16].astype(F32) + q_sib[p16].astype(F32)).astype(BF)
+    keep(q_own.at[p16], q_in.at[p16], recv.at[1])
+    wait_bytes(a_own, own.at[1])
+    wait_bytes(a_sib, core_recv.at[1])
+
+    def att_blocks(i):
+        there = peer(i)
+        j = there[1] * 4 + there[2]
+        a_own[j] = (a_own[j].astype(F32) + a_sib[j].astype(F32)).astype(BF)
+        push(a_own.at[j], a_in.at[p16], send.at[4], recv.at[2], there)
+
+    loop(1, 16, att_blocks)
+    a_own[p16] = (a_own[p16].astype(F32) + a_sib[p16].astype(F32)).astype(BF)
+    keep(a_own.at[p16], a_in.at[p16], recv.at[2])
+
+    wait_bytes(normed_in, recv.at[0])
+    d_normed = normed_in[0].astype(F32)
+    for k in range(1, 4):
+        d_normed = d_normed + normed_in[k].astype(F32)
+    v = tok[...].astype(F32)
+    r = lax.rsqrt(jnp.mean(v * v, axis=1, keepdims=True) + norm_eps)
+    unit = v * r
+    s_own[...] = small[...]
+    s_own[0:1, :] = jnp.sum(d_normed * unit, axis=0, keepdims=True)
+    push(s_own, s_sib, send.at[5], core_recv.at[2], sib)
+    d_unit = d_normed * gain[...]
+    d_in = r * (d_unit - unit * jnp.mean(d_unit * unit, axis=1, keepdims=True))
+    input_grad[...] = (d_middle[...] + d_in).astype(BF)
+    wait_bytes(s_sib, core_recv.at[2])
+    s_tot[...] = s_own[...] + s_sib[...]
+    loop(1, 16, lambda i: push(s_tot, s_in.at[p16], send.at[6], recv.at[3], peer(i)))
+    keep(s_tot, s_in.at[p16], recv.at[3])
+
+    wait_bytes(q_in, recv.at[1])
+    total = q_in[0].astype(F32)
+    for q in range(1, 16):
+        total = total + q_in[q].astype(F32)
     for k in range(4):
         qkv_sum[k, 0:6, :] = total[6 * k : 6 * k + 6]
         qkv_sum[k, 6:8, :] = jnp.zeros((2, 3 * GW), F32)
-    wait_bytes(small_in, recv.at[2])
-    small_total = small_in[0]
-    for q in range(1, 32):
-        small_total = small_total + small_in[q]
-    small_sum[...] = small_total
 
     def final(k):
         d = 4 * p + k
-        there = device_of(d)
 
         @pl.when(d != me)
         def _():
-            push(qkv_sum.at[k], qkv_out.at[z], send.at[3], recv.at[3], there)
-            push(small_sum, small_out.at[z], send.at[4], recv.at[4], there)
+            push(qkv_sum.at[k], qkv_out.at[z], send.at[7], recv.at[4], device_of(d))
 
         @pl.when(d == me)
         def _():
-            keep(qkv_sum.at[k], qkv_out.at[z], recv.at[3])
-            keep(small_sum, small_out.at[z], recv.at[4])
+            keep(qkv_sum.at[k], qkv_out.at[z], recv.at[4])
 
     loop(0, 4, final)
-    wait_bytes(att_in, recv.at[1])
-    att_total = att_in[0].astype(F32)
-    for q in range(1, 32):
-        att_total = att_total + att_in[q].astype(F32)
+    wait_bytes(a_in, recv.at[2])
+    att_total = a_in[0].astype(F32)
+    for q in range(1, 16):
+        att_total = att_total + a_in[q].astype(F32)
     att_sum[...] = att_total
-    keep(att_sum, att_out, out_sem)
-    wait_bytes(att_sum, out_sem)
-    wait_bytes(qkv_out, recv.at[3])
-    wait_bytes(small_out, recv.at[4])
-    wait_bytes(qkv_in.at[pl.ds(0, 31)], send.at[0])
-    wait_bytes(att_in.at[pl.ds(0, 31)], send.at[1])
-    wait_bytes(small_in.at[pl.ds(0, 31)], send.at[2])
+    keep(att_sum, att_out, own.at[2])
+    wait_bytes(s_in, recv.at[3])
+    s_total = s_in[0]
+    for q in range(1, 16):
+        s_total = s_total + s_in[q]
+    s_sum[...] = s_total
+    for k in range(1, 4):
+        push(s_sum, small_out.at[z], send.at[8], recv.at[5], ((z + k) % 4, x, y, c))
+    keep(s_sum, small_out.at[z], recv.at[5])
+    wait_bytes(att_sum, own.at[2])
+    wait_bytes(qkv_out, recv.at[4])
+    wait_bytes(small_out, recv.at[5])
+    wait_bytes(normed_in.at[pl.ds(0, 3)], send.at[0])
+    wait_bytes(q_sib, send.at[1])
+    wait_bytes(a_sib, send.at[2])
+    wait_bytes(q_in.at[pl.ds(0, 15)], send.at[3])
+    wait_bytes(a_in.at[pl.ds(0, 15)], send.at[4])
+    wait_bytes(s_own, send.at[5])
+    wait_bytes(s_in.at[pl.ds(0, 15)], send.at[6])
 
     def sent(k):
         @pl.when(4 * p + k != me)
         def _():
-            wait_bytes(qkv_sum.at[0], send.at[3])
-            wait_bytes(small_sum, send.at[4])
+            wait_bytes(qkv_sum.at[0], send.at[7])
 
     loop(0, 4, sent)
-
-
-def weight_sums(qkv, att, small):
-    return run_comm(
-        sums_kernel,
-        (qkv, att, small),
-        (
+    wait_bytes(small_out.at[pl.ds(0, 3)], send.at[8])
+
+
+def finish(normed, qkv, att, small, tok, gain, d_middle):
+    return pl.pallas_call(
+        finish_kernel,
+        out_shape=(
+            jax.ShapeDtypeStruct((TOK, D), BF),
             jax.ShapeDtypeStruct((4, 8, 3 * GW), F32),
             jax.ShapeDtypeStruct((8, D), F32),
-            jax.ShapeDtypeStruct((4, 8, 128), F32),
+            jax.ShapeDtypeStruct((4, 8, D), F32),
         ),
-        [
-            pltpu.VMEM((32, 24, 3 * GW), BF),
-            pltpu.VMEM((32, 8, D), BF),
-            pltpu.VMEM((32, 8, 128), F32),
+        in_specs=[ANY, ANY, ANY] + [pl.BlockSpec(memory_space=pltpu.VMEM)] * 4,
+        out_specs=(pl.BlockSpec(memory_space=pltpu.VMEM), ANY, ANY, ANY),
+        scratch_shapes=[
+            pltpu.VMEM((4, TOK, D), BF),
+            pltpu.VMEM((16, 24, 3 * GW), BF),
+            pltpu.VMEM((16, 24, 3 * GW), BF),
+            pltpu.VMEM((16, 24, 3 * GW), BF),
+            pltpu.VMEM((16, 8, D), BF),
+            pltpu.VMEM((16, 8, D), BF),
+            pltpu.VMEM((16, 8, D), BF),
+            pltpu.VMEM((8, D), F32),
+            pltpu.VMEM((8, D), F32),
+            pltpu.VMEM((8, D), F32),
+            pltpu.VMEM((16, 8, D), F32),
             pltpu.VMEM((4, 8, 3 * GW), F32),
             pltpu.VMEM((8, D), F32),
-            pltpu.VMEM((8, 128), F32),
-            DMA((5,)),
-            DMA((5,)),
-            DMA,
+            pltpu.VMEM((8, D), F32),
+            DMA((9,)),
+            DMA((6,)),
+            DMA((3,)),
+            DMA((3,)),
         ],
-        4,
-        "weight_sums",
-    )
+        compiler_params=pltpu.CompilerParams(
+            collective_id=4, has_side_effects=True, vmem_limit_bytes=32 * 2**20
+        ),
+        name="finish",
+    )(normed, qkv, att, small, tok, gain, d_middle)
 
 
 NT = (((1,), (1,)), ((), ()))
@@ -546,16 +626,13 @@
 
 
 def attn_forward_kernel(
-    tab, q, kv, qd, kd, d_eo, wa,
-    attn_all, part, p_out, kv_out, d_rows, wa_all,
-    kv_s, v_s, qm, bias, s_s, p_s, xs, xo, wm, wo,
+    tab, q, kv, qd, kd, wa,
+    attn_all, part, p_out, kv_out, wa_all,
+    kv_s, v_s, qm, bias, s_s, p_s, wm, wo,
     send, recv, kv_recv, core_recv, own,
 ):
     z, x, y, c = place()
     sib = (z, x, y, 1 - c)
-    mine = pl.ds(pl.multiple_of(c * 512, 512), 512)
-    theirs = pl.ds(pl.multiple_of((1 - c) * 512, 512), 512)
-    keep(d_eo.at[mine], xs, own.at[0])
     expected = greet_chips(z, x, y, c)
     for k in range(1, 4):
         signal(((z + k) % 4, x, y, c))
@@ -570,23 +647,11 @@
     for b in range(4):
         keep(kv.at[b], kv_s.at[block_cols(b, x)], kv_recv.at[0])
     push(wa, wo, send.at[1], core_recv.at[0], sib)
-    push(d_eo.at[theirs], xo, send.at[2], core_recv.at[1], sib)
     for h in range(GH):
         head_cols = lax.broadcasted_iota(jnp.int32, (1, GW), 1) // HD == h
         qm[h] = jnp.where(head_cols, q[...] * 0.125, 0.0).astype(BF)
     wait_bytes(wo, core_recv.at[0])
     wm[...] = wa[...] + wo[...]
-    half = z * 8 + x * 2 + y // 2
-    to_chips(z, x, y, c, lambda there: wm, wa_all.at[half, y % 2], send.at[3], recv.at[0])
-    wait_bytes(xs, own.at[0])
-    wait_bytes(xo, core_recv.at[1])
-    xs[...] = xs[...] + xo[...]
-    me = block_of(z, x, y)
-    to_chips(
-        z, x, y, c,
-        lambda there: xs.at[pl.ds(pl.multiple_of(block_of(*there[:3]) - c * 512, 16), 16)],
-        d_rows.at[pl.ds(me, 16)], send.at[4], recv.at[1],
-    )
 
     def tables(h):
         for dist in range(2):
@@ -612,8 +677,8 @@
             for h in range(GH):
                 s_s[h, b * TOK :, cols] = dot(qm[h, b * TOK :, :], kv_s[cols, :GW], NT)
     keep(kv_s, kv_out, own.at[1])
-    wait_bytes(wa_all.at[:, c], recv.at[0])
-    push(wa_all.at[:, c], wa_all.at[:, c], send.at[5], core_recv.at[2], sib)
+    half = z * 8 + x * 2 + y // 2
+    to_chips(z, x, y, c, lambda there: wm, wa_all.at[half, y % 2], send.at[3], recv.at[0])
 
     def head(h):
         head_cols = lax.broadcasted_iota(jnp.int32, (1, GW), 1) // HD == h
@@ -664,29 +729,25 @@
         )
     keep(part.at[pl.ds(pl.multiple_of(z * TOK, TOK), TOK)], attn_all.at[z], recv.at[2])
     keep(p_s, p_out, own.at[2])
-    wait_bytes(d_rows.at[mine], recv.at[1])
-    push(d_rows.at[mine], d_rows.at[mine], send.at[7], core_recv.at[3], sib)
+    wait_bytes(wa_all.at[:, c], recv.at[0])
+    push(wa_all.at[:, c], wa_all.at[:, c], send.at[5], core_recv.at[2], sib)
     wait_bytes(attn_all, recv.at[2])
     wait_bytes(wa_all.at[:, 1 - c], core_recv.at[2])
-    wait_bytes(d_rows.at[theirs], core_recv.at[3])
     wait_bytes(kv_s, own.at[1])
     wait_bytes(p_s, own.at[2])
     wait_bytes(kv_s.at[pl.ds(0, 1536)], send.at[0])
     wait_bytes(wo, send.at[1])
-    wait_bytes(xo, send.at[2])
     wait_bytes(wa_all.at[pl.ds(0, 31), c], send.at[3])
 
     @pl.when(y % 2 != c)
     def _():
         wait_bytes(wa_all.at[0, c], send.at[3])
 
-    sent_to_chips(d_rows, y, c, send.at[4])
     wait_bytes(wa_all.at[:, c], send.at[5])
     wait_bytes(attn_all.at[pl.ds(0, 3)], send.at[6])
-    wait_bytes(d_rows.at[mine], send.at[7])
-
-
-def attn_forward(tab, q, kv, qd, kd, d_eo, wa):
+
+
+def attn_forward(tab, q, kv, qd, kd, wa):
     probs = (GH, 512, 2048)
     return pl.pallas_call(
         attn_forward_kernel,
@@ -695,11 +756,10 @@
             jax.ShapeDtypeStruct((512, GW), BF),
             jax.ShapeDtypeStruct(probs, BF),
             jax.ShapeDtypeStruct((2048, 2 * GW), BF),
-            jax.ShapeDtypeStruct((1024, D), BF),
             jax.ShapeDtypeStruct((32, 2, 16, D), BF),
         ),
-        in_specs=[SMEM, VMEM, VMEM, VMEM, VMEM, ANY, VMEM],
-        out_specs=(ANY, VMEM, ANY, ANY, ANY, ANY),
+        in_specs=[SMEM, VMEM, VMEM, VMEM, VMEM, VMEM],
+        out_specs=(ANY, VMEM, ANY, ANY, ANY),
         scratch_shapes=[
             pltpu.VMEM((2048, 2 * GW), BF),
             pltpu.VMEM((2048, GW), BF),
@@ -707,8 +767,6 @@
             pltpu.VMEM((GH, 4, TOK, TOK), F32),
             pltpu.VMEM(probs, F32),
             pltpu.VMEM(probs, BF),
-            pltpu.VMEM((512, D), BF),
-            pltpu.VMEM((512, D), BF),
             pltpu.VMEM((16, D), BF),
             pltpu.VMEM((16, D), BF),
             DMA((8,)),
@@ -721,7 +779,7 @@
             collective_id=2, has_side_effects=True, vmem_limit_bytes=44 * 2**20
         ),
         name="attn_forward",
-    )(tab, q, kv, qd, kd, d_eo, wa)
+    )(tab, q, kv, qd, kd, wa)
 
 
 def attn_backward_kernel(
@@ -943,8 +1001,8 @@
     qkv = dot(normed, weight, NN).astype(BF)
     queries = qkv[:, :GW]
     table = lax.dynamic_slice(rel_table, (0, z * GH), (BUCKETS, GH)).astype(F32)
-    attn, attn_part, probs, kv_all, d_eo_all, out_weights = attn_forward(
-        table, queries, qkv[:, GW:].reshape(4, TOK, 2 * GW), query_docs, key_docs, d_eo, out_slab
+    attn, attn_part, probs, kv_all, out_weights = attn_forward(
+        table, queries, qkv[:, GW:].reshape(4, TOK, 2 * GW), query_docs, key_docs, out_slab
     )
     attn = attn.transpose(1, 0, 2).reshape(TOK, D)
     attention_weight = out_weights[:, :, :12, :].reshape(D, D)
@@ -955,7 +1013,7 @@
     moe_in = moe_float.astype(BF)
     send_rows = dot(pick, moe_in, TN).astype(BF)
     home, expert_out, expert_in_grad, expert_out_grad = run_experts(
-        send_rows, d_eo_all, w_in[0], w_out[0]
+        send_rows, d_eo, w_in[0], w_out[0]
     )
     moe_in_grad = dot(pick, home, NN)
     middle_part, gain_two_grad = norm_two_back(moe_in_grad)
@@ -970,41 +1028,34 @@
     d_kv = jnp.concatenate([d_kv[1], d_kv[0]], axis=1)
     d_qkv = jnp.concatenate([d_q, d_kv], axis=1)
     normed_part = dot(d_qkv, weight, NT).astype(BF).reshape(4, TOK, D)
-    normed_part = z_exchange(normed_part, 8, "normed_grads")
-    normed_grad = jnp.sum(normed_part.astype(F32), axis=0)
-    _, norm_one_back = jax.vjp(scale_rows, inputs, gain_one)
-    input_part, gain_one_grad = norm_one_back(normed_grad)
-    input_grad = middle_grad + input_part
-
     both = jnp.concatenate([pick_0, pick_1], axis=0).astype(BF)
     picked = dot(both, expert_out, NN).reshape(2, TOK, D)
     block_out = middle + gates[:, :1] * picked[0] + gates[:, 1:] * picked[1]
     gate_grad = jnp.sum(picked * grad_out[None], axis=2).T
 
-    qkv_part = dot(normed, d_qkv, TN).astype(BF).reshape(32, 24, 3 * GW)
-    att_part = dot(attn_part, branch_all.reshape(512, D), TN).astype(BF).reshape(32, 6, D)
-    att_part = jnp.pad(att_part, ((0, 0), (0, 2), (0, 0)))
+    qkv_part = dot(normed, d_qkv, TN).astype(BF).reshape(16, 2, 24, 3 * GW)
+    att_part = dot(attn_part, branch_all.reshape(512, D), TN).astype(BF).reshape(16, 2, 6, D)
+    att_part = jnp.pad(att_part, ((0, 0), (0, 0), (0, 2), (0, 0)))
     table_sum = jnp.sum(table_part, axis=2).reshape(1, GH * BUCKETS)
-    small = jnp.stack(
+    small = jnp.concatenate(
         [
-            jnp.pad(gain_one_grad.reshape(32, 24), ((0, 0), (0, 104))),
-            jnp.pad(gain_two_grad.reshape(32, 24), ((0, 0), (0, 104))),
-            jnp.broadcast_to(jnp.pad(table_sum, ((0, 0), (0, 128 - GH * BUCKETS))), (32, 128)),
-        ],
-        axis=1,
-    )
-    small = jnp.pad(small, ((0, 0), (0, 5), (0, 0)))
-    qkv_sum, att_sum, small_sum = weight_sums(qkv_part, att_part, small)
+            jnp.zeros((1, D), F32),
+            gain_two_grad.reshape(1, D),
+            jnp.pad(table_sum, ((0, 0), (0, D - GH * BUCKETS))),
+            jnp.zeros((5, D), F32),
+        ]
+    )
+    input_grad, qkv_sum, att_sum, small_sum = finish(
+        normed_part, qkv_part, att_part, small, own_tokens, gain_one.reshape(1, D), middle_grad
+    )
     qkv_grad = qkv_sum[:, :6, :].reshape(GROUPS, 6, 3, GW).transpose(1, 2, 0, 3).reshape(6, 3 * D)
     attn_out_grad = att_sum[:6]
-    place_in = (y * 2 + c) % 4
+    place_in = chip_of(z, x, y) * 2 + c
     gains = lax.dynamic_slice(jnp.sum(small_sum[:, :2, :], axis=0), (0, place_in * 6), (2, 6))
-    table_grad = (
-        small_sum[:, 2, : GH * BUCKETS].reshape(GROUPS * GH, BUCKETS).T
-    )
+    table_grad = small_sum[:, 2, : GH * BUCKETS].reshape(GROUPS * GH, BUCKETS).T
     return (
         block_out.reshape(1, TOK, D).astype(BF),
-        input_grad.reshape(1, TOK, D).astype(BF),
+        input_grad.reshape(1, TOK, D),
         gate_grad.reshape(1, TOK, 2),
         gains[0],
         qkv_grad,

time: 268 us -> 263 us (0.981)
  Pallas kernels: 208 us -> 198 us
  matrix products: 9.96 us -> 14.2 us
    pallas_call x3 -> x1, Pallas kernels: 76.3 us -> 31.2 us  [run_comm(): pl.pallas_call(kernel, out_shape=outs, in_specs=[ANY] * len(args), out_sp...]
    pallas_call x0 -> x1, Pallas kernels: none -> 28.5 us  [finish(): pl.pallas_call(finish_kernel, out_shape=(jax.ShapeDtypeStruct((TOK, D), B...]
    pallas_call x1, Pallas kernels: 56.6 us -> 67.7 us  [run_experts(): pl.pallas_call(experts_kernel, out_shape=(jax.ShapeDtypeStruct((1024, D),...]
    unnamed x95 -> x68, local copies, waits for them, and re-layouts: 23.1 us -> 16.7 us
    pallas_call x1, Pallas kernels: 48.4 us -> 42.3 us  [attn_forward(): pl.pallas_call(attn_forward_kernel, out_shape=(jax.ShapeDtypeStruct((4, T...]
    dot_general x10, matrix products: 9.96 us -> 14.2 us  [dot(): return lax.dot_general(a, b, dims, preferred_element_type=F32)]
where the time goes in v4:
time: 263 us; the launch traced here: 260 us
  Pallas kernels  198 us (75%)
  local copies, waits for them, and re-layouts  35.7 us (14%)
  matrix products  14.2 us (5%)
  other arithmetic  10.9 us (4%)
    pallas_call x1, Pallas kernels, run_experts(): pl.pallas_call(experts_kernel, out_shape=(jax.ShapeDtypeStruct((1024, D),...  67.7 us
    pallas_call x1, Pallas kernels, attn_forward(): pl.pallas_call(attn_forward_kernel, out_shape=(jax.ShapeDtypeStruct((4, T...  42.3 us
    pallas_call x1, Pallas kernels, run_comm(): pl.pallas_call(kernel, out_shape=outs, in_specs=[ANY] * len(args), out_sp...  31.2 us
    pallas_call x1, Pallas kernels, finish(): pl.pallas_call(finish_kernel, out_shape=(jax.ShapeDtypeStruct((TOK, D), B...  28.5 us
    pallas_call x1, Pallas kernels, attn_backward(): pl.pallas_call(attn_backward_kernel, out_shape=(jax.ShapeDtypeStruct((512...  28.4 us
    unnamed x68, local copies, waits for them, and re-layouts  16.7 us
    dot_general x10, matrix products, dot(): return lax.dot_general(a, b, dims, preferred_element_type=F32)  14.2 us

profile of v4, /device:TPU:1, one launch (start us, length us, event | category | flops | bytes accessed | tf_op | source)
XLA Modules:
  0.0 260.2 jit_solution(4682451678538182550)
XLA Ops:
  0.7 0.9 reshape.223
  1.7 0.7 convert_bitcast_fusion
  2.4 1.4 concatenate.24
  4.3 0.9 copy-done.1
  5.2 31.2 %start_exchange.1 = (bf16[4,128,768]{2,1,0:T(8,128)(2,1)S(1)}, bf16[32,2,16,576]{3,2,1,0:T(8,128)(2,1)S(1)}) custom-call(bf16[128,768]{1,0:T(8,128)(2,1)S(1)} %bitcast.133, bf16[4,16,576]{2,1,0:T(8,128)(2,1)S(1)} %maximum_select_fusion.wmsg), custom_call_target="tpu_custom_call" | custom-call | tf_op jit(solution)/shard_map/start_exchange/pallas_call | solution.py:94
  36.4 0.7 slice_convert_fusion
  37.6 1.1 multiply_convert_fusion.1
  39.2 2.3 convolution_convert_fusion.3
  42.3 42.3 %attn_forward.1 = (bf16[4,128,192]{2,1,0:T(8,128)(2,1)S(1)}, bf16[512,192]{1,0:T(8,128)(2,1)S(1)}, bf16[3,512,2048]{2,1,0:T(8,128)(2,1)}, bf16[2048,384]{1,0:T(8,128)(2,1)S(1)}, bf16[32,2,16,768]{3,2,1,0:T(8,128)(2,1)S(1)}) custom-call(f32[32,3]{1,0:T(8,128)S(1)} %convert_element_type.131.tab, bf16[512,192]{1,0:T(8,128)(2,1)S(1)} %slice.110.q, ...), custom_call_target="tpu_custom_call" | custom-call | tf_op jit(solution)/shard_map/attn_forward/pallas_call | solution.py:752
  84.6 1.1 copy-done.5
  85.8 0.7 copy-done.8
  86.5 0.7 copy-done.10
  87.2 3.2 %reshape.230 = bf16[768,768]{1,0:T(8,128)(2,1)} reshape(bf16[32,2,12,768]{3,2,1,0:T(8,128)(2,1)} %bitcast.136) | data formatting | bytes 2359296 | tf_op jit(solution)/shard_map/reshape | solution.py:1008
  90.4 0.8 copy.93
  91.2 1.8 multiply_reduce_fusion.3
  93.8 0.6 fusion.42
  94.5 1.3 reduce-window.6
  95.8 0.8 slice_reduce_fusion.2
  96.6 0.7 reduce-window.9
  97.8 0.7 eq.63
  98.5 0.8 fusion.36
  99.8 1.0 reshape.250
  100.8 1.4 convolution_convert_fusion.x16
  102.2 0.8 slice_bitcast_fusion.3
  103.1 1.9 multiply_convert_fusion.d_eo
  105.0 67.7 %experts.1 = (bf16[1024,768]{1,0:T(8,128)(2,1)S(1)}, bf16[1024,768]{1,0:T(8,128)(2,1)S(1)}, f32[768,1536]{1,0:T(8,128)}, f32[1536,768]{1,0:T(8,128)}) custom-call(bf16[1024,768]{1,0:T(8,128)(2,1)S(1)} %convolution_convert_fusion.x16, bf16[1024,768]{1,0:T(8,128)(2,1)} %multiply_convert_fusion.d_eo, bf16[768,1536]{1,0:T(8,128)(2,1)} %bitcast.151, ...), custom_call_target="tpu_custom_call" | custom-call | tf_op jit(solution)/shard_map/experts/pallas_call | solution.py:378
  172.9 1.2 fusion.6
  175.1 1.0 fusion.52
  177.0 28.4 %attn_backward.1 = (bf16[512,192]{1,0:T(8,128)(2,1)S(1)}, f32[3,32,128]{2,1,0:T(8,128)S(1)}, bf16[4,4,128,384]{3,2,1,0:T(8,128)(2,1)S(1)}, bf16[4,128,768]{2,1,0:T(8,128)(2,1)S(1)}) custom-call(bf16[3,512,2048]{2,1,0:T(8,128)(2,1)} %get-tuple-element.34.p, bf16[512,192]{1,0:T(8,128)(2,1)S(1)} %slice.110.q, bf16[2048,384]{1,0:T(8,128)(2,1)S(1)} %get-tuple-element.35.kv, ...), custom_call_target="tpu_custom_call" | custom-call | tf_op jit(solution)/shard_map/attn_backward/pallas_call | solution.py:901
  205.4 1.1 copy-done.3
  206.5 0.9 copy-done.7
  207.4 0.6 copy-done.12
  208.0 0.7 copy-done.13
  208.7 1.0 reduce_sum.113
  210.0 1.5 convolution_convert_fusion.4
  211.5 0.8 reshape.240
  212.3 1.1 pad.8.att
  213.4 1.1 reduce_sum.111
  214.5 1.2 copy.100
  216.8 0.8 convolution_convert_fusion.1
  217.6 0.6 copy.103
  218.5 2.2 convolution_convert_fusion.2
  220.9 28.5 %finish.1 = (bf16[128,768]{1,0:T(8,128)(2,1)S(1)}, f32[4,8,576]{2,1,0:T(8,128)S(1)}, f32[8,768]{1,0:T(8,128)S(1)}, f32[4,8,768]{2,1,0:T(8,128)S(1)}) custom-call(bf16[4,128,768]{2,1,0:T(8,128)(2,1)S(1)} %bitcast.140, bf16[16,2,24,576]{3,2,1,0:T(8,128)(2,1)S(1)} %bitcast.132, bf16[16,2,8,768]{3,2,1,0:T(8,128)(2,1)S(1)} %pad.8.att, ...), custom_call_target="tpu_custom_call" | custom-call | tf_op jit(solution)/shard_map/finish/pallas_call | solution.py:564
  249.7 0.7 reshape.246
  251.0 0.7 reshape_squeeze.3
  251.7 0.7 copy.122
  253.0 5.0 %copy.124 = f32[1,768,1536]{2,1,0:T(8,128)} copy(f32[1,768,1536]{2,1,0:T(8,128)} %bitcast.150) | data formatting | bytes 9437184
  258.0 2.2 copy.125
  (120 shorter events, 9.4 us)
Async XLA Ops:
  0.6 41.4 %copy-start = (bf16[32,12]{0,1:T(8,128)(2,1)S(1)}, bf16[32,12]{0,1:T(8,128)(2,1)}, u32[]{:S(2)}) copy-start(bf16[32,12]{0,1:T(8,128)(2,1)} %param.16) | copy-start | bytes 2308
  4.3 0.9 copy-start.1
  37.2 2.0 copy-start.20
  39.2 2.3 copy-start.19
  41.5 0.7 copy-start.24
  84.6 1.1 copy-start.5
  85.8 0.7 copy-start.8
  86.5 0.7 copy-start.10
  87.2 3.2 %copy-start.9 = (bf16[4,128,192]{2,1,0:T(8,128)(2,1)S(1)}, bf16[4,128,192]{2,1,0:T(8,128)(2,1)}, u32[]{:S(2)}) copy-start(bf16[4,128,192]{2,1,0:T(8,128)(2,1)} %copy-done.8) | copy-start | bytes 589828
  87.2 4.0 %copy-start.2 = (bf16[1,128,768]{2,1,0:T(8,128)(2,1)S(1)}, bf16[1,128,768]{2,1,0:T(8,128)(2,1)}, u32[]{:S(2)}) copy-start(bf16[1,128,768]{2,1,0:T(8,128)(2,1)} %param.12) | copy-start | bytes 589828
  90.4 3.2 %copy-start.26 = (s32[1,128,2]{1,2,0:T(2,128)S(1)}, s32[1,128,2]{1,2,0:T(2,128)}, u32[]{:S(2)}) copy-start(s32[1,128,2]{1,2,0:T(2,128)} %param.20) | copy-start | bytes 3076
  93.0 0.8 copy-start.27
  93.0 10.1 %copy-start.17 = (bf16[1,128,768]{2,1,0:T(8,128)(2,1)S(1)}, bf16[1,128,768]{2,1,0:T(8,128)(2,1)}, u32[]{:S(2)}) copy-start(bf16[1,128,768]{2,1,0:T(8,128)(2,1)} %param.23) | copy-start | bytes 589828
  172.9 1.3 copy-start.25
  174.2 0.7 copy-start.28
  174.2 0.9 copy-start.18
  174.7 1.4 copy-start.16
  177.0 33.0 %copy-start.11 = (bf16[512,192]{1,0:T(8,128)(2,1)S(1)}, bf16[512,192]{1,0:T(8,128)(2,1)}, u32[]{:S(2)}) copy-start(bf16[512,192]{1,0:T(8,128)(2,1)} %copy-done.10) | copy-start | bytes 589828
  205.4 1.1 copy-start.3
  206.5 0.9 copy-start.7
  207.4 0.6 copy-start.12
  208.0 0.7 copy-start.13
  208.7 4.7 %copy-start.4 = (bf16[4,4,128,384]{3,2,1,0:T(8,128)(2,1)S(1)}, bf16[4,4,128,384]{3,2,1,0:T(8,128)(2,1)}, u32[]{:S(2)}) copy-start(bf16[4,4,128,384]{3,2,1,0:T(8,128)(2,1)} %copy-done.3) | copy-start | bytes 4718596
  215.7 1.1 copy-start.14
  215.9 0.7 copy-start.22
  216.1 0.7 copy-start.23
  217.6 1.0 copy-start.15
  218.5 2.3 copy-start.21
  218.5 2.4 copy-start.6
  250.4 7.6 %slice-start = ((s8[4718592]{0:T(1024)(128)(4,1)}), s8[524288]{0:T(1024)(128)(4,1)S(1)}, s32[]{:S(2)}) async-start(s8[4718592]{0:T(1024)(128)(4,1)} %bitcast.147), calls=%async_computation | async-start | bytes 1048576
  253.0 5.0 %slice-start.1 = ((s8[4718592]{0:T(1024)(128)(4,1)}), s8[4194304]{0:T(1024)(128)(4,1)S(1)}, s32[]{:S(2)}) async-start(s8[4718592]{0:T(1024)(128)(4,1)} %bitcast.147), calls=%async_computation.1 | async-start | bytes 8388608

commit v5 on v3

--- a/solution.py
+++ b/solution.py
@@ -380,142 +380,8 @@
     )(x16, d_rows, w_in, w_out)
 
 
-def z_kernel(blocks, out, send, recv):
-    z, x, y, c = place()
-    for k in range(1, 4):
-        signal(((z + k) % 4, x, y, c))
-    arrive(3)
-    for k in range(1, 4):
-        there = (z + k) % 4
-        push(blocks.at[there], out.at[z], send, recv, (there, x, y, c))
-    keep(blocks.at[z], out.at[z], recv)
-    wait_bytes(out, recv)
-    wait_bytes(out.at[pl.ds(0, 3)], send)
-
-
-def z_exchange(blocks, collective_id, name):
-    return run_comm(
-        z_kernel,
-        (blocks,),
-        jax.ShapeDtypeStruct(blocks.shape, blocks.dtype),
-        [DMA, DMA],
-        collective_id,
-        name,
-    )
-
-
 def device_of(d):
     return d // 32, (d // 8) % 4, (d // 2) % 4, d % 2
-
-
-def sums_kernel(
-    qkv, att, small, qkv_out, att_out, small_out,
-    qkv_in, att_in, small_in, qkv_sum, att_sum, small_sum, send, recv, out_sem,
-):
-    z, x, y, c = place()
-    p = x * 8 + y * 2 + c
-    me = z * 32 + p
-
-    def peer(i):
-        return (z, (x + i // 8) % 4, (y + (i // 2) % 4) % 4, (c + i % 2) % 2)
-
-    loop(1, 32, lambda i: signal(peer(i)))
-    source = me // 4
-
-    def greet(k):
-        from_me = (k == z) & (source == p)
-
-        @pl.when(jnp.logical_not(from_me))
-        def _():
-            signal((k, source // 8, (source // 2) % 4, source % 2))
-
-    loop(0, 4, greet)
-    arrive(31 + 4 - jnp.where(source == p, 1, 0))
-
-    def out(i):
-        there = peer(i)
-        q = there[1] * 8 + there[2] * 2 + there[3]
-        push(qkv.at[q], qkv_in.at[p], send.at[0], recv.at[0], there)
-        push(att.at[q], att_in.at[p], send.at[1], recv.at[1], there)
-        push(small.at[q], small_in.at[p], send.at[2], recv.at[2], there)
-
-    loop(1, 32, out)
-    keep(qkv.at[p], qkv_in.at[p], recv.at[0])
-    keep(att.at[p], att_in.at[p], recv.at[1])
-    keep(small.at[p], small_in.at[p], recv.at[2])
-    wait_bytes(qkv_in, recv.at[0])
-    total = qkv_in[0].astype(F32)
-    for q in range(1, 32):
-        total = total + qkv_in[q].astype(F32)
-    for k in range(4):
-        qkv_sum[k, 0:6, :] = total[6 * k : 6 * k + 6]
-        qkv_sum[k, 6:8, :] = jnp.zeros((2, 3 * GW), F32)
-    wait_bytes(small_in, recv.at[2])
-    small_total = small_in[0]
-    for q in range(1, 32):
-        small_total = small_total + small_in[q]
-    small_sum[...] = small_total
-
-    def final(k):
-        d = 4 * p + k
-        there = device_of(d)
-
-        @pl.when(d != me)
-        def _():
-            push(qkv_sum.at[k], qkv_out.at[z], send.at[3], recv.at[3], there)
-            push(small_sum, small_out.at[z], send.at[4], recv.at[4], there)
-
-        @pl.when(d == me)
-        def _():
-            keep(qkv_sum.at[k], qkv_out.at[z], recv.at[3])
-            keep(small_sum, small_out.at[z], recv.at[4])
-
-    loop(0, 4, final)
-    wait_bytes(att_in, recv.at[1])
-    att_total = att_in[0].astype(F32)
-    for q in range(1, 32):
-        att_total = att_total + att_in[q].astype(F32)
-    att_sum[...] = att_total
-    keep(att_sum, att_out, out_sem)
-    wait_bytes(att_sum, out_sem)
-    wait_bytes(qkv_out, recv.at[3])
-    wait_bytes(small_out, recv.at[4])
-    wait_bytes(qkv_in.at[pl.ds(0, 31)], send.at[0])
-    wait_bytes(att_in.at[pl.ds(0, 31)], send.at[1])
-    wait_bytes(small_in.at[pl.ds(0, 31)], send.at[2])
-
-    def sent(k):
-        @pl.when(4 * p + k != me)
-        def _():
-            wait_bytes(qkv_sum.at[0], send.at[3])
-            wait_bytes(small_sum, send.at[4])
-
-    loop(0, 4, sent)
-
-
-def weight_sums(qkv, att, small):
-    return run_comm(
-        sums_kernel,
-        (qkv, att, small),
-        (
-            jax.ShapeDtypeStruct((4, 8, 3 * GW), F32),
-            jax.ShapeDtypeStruct((8, D), F32),
-            jax.ShapeDtypeStruct((4, 8, 128), F32),
-        ),
-        [
-            pltpu.VMEM((32, 24, 3 * GW), BF),
-            pltpu.VMEM((32, 8, D), BF),
-            pltpu.VMEM((32, 8, 128), F32),
-            pltpu.VMEM((4, 8, 3 * GW), F32),
-            pltpu.VMEM((8, D), F32),
-            pltpu.VMEM((8, 128), F32),
-            DMA((5,)),
-            DMA((5,)),
-            DMA,
-        ],
-        4,
-        "weight_sums",
-    )
 
 
 NT = (((1,), (1,)), ((), ()))
@@ -546,16 +412,15 @@
 
 
 def attn_forward_kernel(
-    tab, q, kv, qd, kd, d_eo, wa,
-    attn_all, part, p_out, kv_out, d_rows, wa_all,
-    kv_s, v_s, qm, bias, s_s, p_s, xs, xo, wm, wo,
+    tab, q, kv, qd, kd, wa, d_eo,
+    attn_all, part, p_out, kv_out, wa_all, d_rows,
+    kv_s, v_s, qm, bias, s_s, p_s, wm, wo, xo,
     send, recv, kv_recv, core_recv, own,
 ):
     z, x, y, c = place()
     sib = (z, x, y, 1 - c)
     mine = pl.ds(pl.multiple_of(c * 512, 512), 512)
     theirs = pl.ds(pl.multiple_of((1 - c) * 512, 512), 512)
-    keep(d_eo.at[mine], xs, own.at[0])
     expected = greet_chips(z, x, y, c)
     for k in range(1, 4):
         signal(((z + k) % 4, x, y, c))
@@ -576,17 +441,8 @@
         qm[h] = jnp.where(head_cols, q[...] * 0.125, 0.0).astype(BF)
     wait_bytes(wo, core_recv.at[0])
     wm[...] = wa[...] + wo[...]
-    half = z * 8 + x * 2 + y // 2
-    to_chips(z, x, y, c, lambda there: wm, wa_all.at[half, y % 2], send.at[3], recv.at[0])
-    wait_bytes(xs, own.at[0])
     wait_bytes(xo, core_recv.at[1])
-    xs[...] = xs[...] + xo[...]
-    me = block_of(z, x, y)
-    to_chips(
-        z, x, y, c,
-        lambda there: xs.at[pl.ds(pl.multiple_of(block_of(*there[:3]) - c * 512, 16), 16)],
-        d_rows.at[pl.ds(me, 16)], send.at[4], recv.at[1],
-    )
+    xo[...] = xo[...] + d_eo[mine, :]
 
     def tables(h):
         for dist in range(2):
@@ -612,8 +468,14 @@
             for h in range(GH):
                 s_s[h, b * TOK :, cols] = dot(qm[h, b * TOK :, :], kv_s[cols, :GW], NT)
     keep(kv_s, kv_out, own.at[1])
-    wait_bytes(wa_all.at[:, c], recv.at[0])
-    push(wa_all.at[:, c], wa_all.at[:, c], send.at[5], core_recv.at[2], sib)
+    half = z * 8 + x * 2 + y // 2
+    to_chips(z, x, y, c, lambda there: wm, wa_all.at[half, y % 2], send.at[3], recv.at[0])
+    me = block_of(z, x, y)
+    to_chips(
+        z, x, y, c,
+        lambda there: xo.at[pl.ds(pl.multiple_of(block_of(*there[:3]) - c * 512, 16), 16)],
+        d_rows.at[pl.ds(me, 16)], send.at[4], recv.at[1],
+    )
 
     def head(h):
         head_cols = lax.broadcasted_iota(jnp.int32, (1, GW), 1) // HD == h
@@ -664,6 +526,8 @@
         )
     keep(part.at[pl.ds(pl.multiple_of(z * TOK, TOK), TOK)], attn_all.at[z], recv.at[2])
     keep(p_s, p_out, own.at[2])
+    wait_bytes(wa_all.at[:, c], recv.at[0])
+    push(wa_all.at[:, c], wa_all.at[:, c], send.at[5], core_recv.at[2], sib)
     wait_bytes(d_rows.at[mine], recv.at[1])
     push(d_rows.at[mine], d_rows.at[mine], send.at[7], core_recv.at[3], sib)
     wait_bytes(attn_all, recv.at[2])
@@ -673,20 +537,20 @@
     wait_bytes(p_s, own.at[2])
     wait_bytes(kv_s.at[pl.ds(0, 1536)], send.at[0])
     wait_bytes(wo, send.at[1])
-    wait_bytes(xo, send.at[2])
     wait_bytes(wa_all.at[pl.ds(0, 31), c], send.at[3])
 
     @pl.when(y % 2 != c)
     def _():
         wait_bytes(wa_all.at[0, c], send.at[3])
 
-    sent_to_chips(d_rows, y, c, send.at[4])
     wait_bytes(wa_all.at[:, c], send.at[5])
     wait_bytes(attn_all.at[pl.ds(0, 3)], send.at[6])
+    wait_bytes(xo, send.at[2])
+    sent_to_chips(d_rows, y, c, send.at[4])
     wait_bytes(d_rows.at[mine], send.at[7])
 
 
-def attn_forward(tab, q, kv, qd, kd, d_eo, wa):
+def attn_forward(tab, q, kv, qd, kd, wa, d_eo):
     probs = (GH, 512, 2048)
     return pl.pallas_call(
         attn_forward_kernel,
@@ -695,10 +559,10 @@
             jax.ShapeDtypeStruct((512, GW), BF),
             jax.ShapeDtypeStruct(probs, BF),
             jax.ShapeDtypeStruct((2048, 2 * GW), BF),
+            jax.ShapeDtypeStruct((32, 2, 16, D), BF),
             jax.ShapeDtypeStruct((1024, D), BF),
-            jax.ShapeDtypeStruct((32, 2, 16, D), BF),
         ),
-        in_specs=[SMEM, VMEM, VMEM, VMEM, VMEM, ANY, VMEM],
+        in_specs=[SMEM] + [VMEM] * 6,
         out_specs=(ANY, VMEM, ANY, ANY, ANY, ANY),
         scratch_shapes=[
             pltpu.VMEM((2048, 2 * GW), BF),
@@ -707,10 +571,9 @@
             pltpu.VMEM((GH, 4, TOK, TOK), F32),
             pltpu.VMEM(probs, F32),
             pltpu.VMEM(probs, BF),
-            pltpu.VMEM((512, D), BF),
-            pltpu.VMEM((512, D), BF),
             pltpu.VMEM((16, D), BF),
             pltpu.VMEM((16, D), BF),
+            pltpu.VMEM((512, D), BF),
             DMA((8,)),
             DMA((3,)),
             DMA((4,)),
@@ -721,27 +584,47 @@
             collective_id=2, has_side_effects=True, vmem_limit_bytes=44 * 2**20
         ),
         name="attn_forward",
-    )(tab, q, kv, qd, kd, d_eo, wa)
+    )(tab, q, kv, qd, kd, wa, d_eo)
 
 
 def attn_backward_kernel(
-    p, q, kv, d_attn, branch, dq, tab, parts, branch_all,
-    p_s, v_s, do_s, dm, qm, dp_s, ds_s, near, messages,
-    send, recv, own,
+    p, q, kv, d_attn, branch, weight, normed, attn_part, small, tok, gain, d_middle,
+    input_grad, qkv_out, att_out, small_out,
+    p_s, v_s, do_s, dm, qm, dp_s, ds_s, near, messages, parts, branch_all, dq, tab,
+    d_qkv, n_part, normed_in, att_f, q_blk, q_sib, q_tot, q_in, a_blk, a_sib, a_tot, a_in,
+    s_own, s_sib, s_tot, s_in, qkv_sum, att_sum, s_sum, send, recv, core_recv, own,
 ):
     z, x, y, c = place()
-    keep(p, p_s, own)
+    sib = (z, x, y, 1 - c)
+    p16 = x * 4 + y
+    p32 = p16 * 2 + c
+    me = z * 32 + p32
+    source = me // 4
+
+    def peer(i):
+        return z, (x + i // 4) % 4, (y + i % 4) % 4, c
+
+    keep(p, p_s, own.at[0])
+    loop(1, 16, lambda i: signal(peer(i)))
     for k in range(1, 4):
         signal(((z + k) % 4, x, y, c))
-        signal((z, (x + k) % 4, y, c))
-    arrive(6)
+    signal(sib)
+
+    def greet(k):
+        @pl.when(jnp.logical_not((k == z) & (source == p32)))
+        def _():
+            signal((k, source // 8, (source // 2) % 4, source % 2))
+
+    loop(0, 4, greet)
+    arrive(15 + 3 + 1 + 4 - jnp.where(source == p32, 1, 0))
     for k in range(1, 4):
         there = (z + k) % 4
         push(d_attn.at[there], do_s.at[z], send.at[0], recv.at[0], (there, x, y, c))
     keep(d_attn.at[z], do_s.at[z], recv.at[0])
+    z_rows = pl.ds(pl.multiple_of(z * TOK, TOK), TOK)
     for k in range(1, 4):
-        push(branch, branch_all.at[z], send.at[1], recv.at[1], ((z + k) % 4, x, y, c))
-    keep(branch, branch_all.at[z], recv.at[1])
+        push(branch, branch_all.at[z_rows], send.at[1], recv.at[1], ((z + k) % 4, x, y, c))
+    keep(branch, branch_all.at[z_rows], recv.at[1])
     v_s[...] = kv[:, GW:]
     for h in range(GH):
         head_cols = lax.broadcasted_iota(jnp.int32, (1, GW), 1) // HD == h
@@ -751,7 +634,7 @@
         head_cols = lax.broadcasted_iota(jnp.int32, (1, GW), 1) // HD == h
         for b in range(4):
             dm[h, b * TOK : (b + 1) * TOK, :] = jnp.where(head_cols, do_s[b], 0.0).astype(BF)
-    wait_bytes(p_s, own)
+    wait_bytes(p_s, own.at[0])
 
     def key_sums(left, right, first):
         for k in (1, 2, 3, 0):
@@ -831,44 +714,167 @@
 
     loop(0, GH, head)
     key_sums(ds_s, qm, 2)
+
+    wait_bytes(branch_all, recv.at[1])
+    att_f[0:GW, :] = dot(attn_part[...], branch_all[...], TN)
+    att_f[GW:, :] = jnp.zeros((8, D), F32)
+    for j in range(32):
+        a_blk[j // 2, j % 2] = att_f[6 * j : 6 * j + 8, :].astype(BF)
+    push(a_blk.at[:, 1 - c], a_sib, send.at[4], core_recv.at[1], sib)
+    s_own[...] = small[...]
+    for h in range(GH):
+        s_own[2:3, BUCKETS * h : BUCKETS * (h + 1)] = jnp.sum(tab[h].T, axis=0, keepdims=True)
+
     wait_bytes(parts, recv.at[2])
-    wait_bytes(branch_all, recv.at[1])
+    d_qkv[:, :GW] = dq[...]
+    for b in range(4):
+        rows = slice(b * TOK, (b + 1) * TOK)
+        side = GW * (b % 2)
+        for m, at in ((2 + b // 2, GW), (b // 2, 2 * GW)):
+            total = parts[0, m, :, side : side + GW].astype(F32)
+            for k in range(1, 4):
+                total = total + parts[k, m, :, side : side + GW].astype(F32)
+            d_qkv[rows, at : at + GW] = total.astype(BF)
+    n_part[...] = dot(d_qkv[...], weight[...], NT).astype(BF)
+    for k in range(1, 4):
+        there = (z + k) % 4
+        push(
+            n_part.at[pl.ds(pl.multiple_of(there * TOK, TOK), TOK)], normed_in.at[z],
+            send.at[3], recv.at[3], (there, x, y, c),
+        )
+    keep(n_part.at[z_rows], normed_in.at[z], recv.at[3])
+    total = dot(normed[...], d_qkv[...], TN)
+    for j in range(32):
+        q_blk[j // 2, j % 2] = total[24 * j : 24 * j + 24].astype(BF)
+    push(q_blk.at[:, 1 - c], q_sib, send.at[5], core_recv.at[0], sib)
+    wait_bytes(a_sib, core_recv.at[1])
+
+    def att_blocks(i):
+        there = peer(i)
+        j = there[1] * 4 + there[2]
+        a_tot[j] = (a_blk[j, c].astype(F32) + a_sib[j].astype(F32)).astype(BF)
+        push(a_tot.at[j], a_in.at[p16], send.at[6], recv.at[4], there)
+
+    loop(1, 16, att_blocks)
+    a_tot[p16] = (a_blk[p16, c].astype(F32) + a_sib[p16].astype(F32)).astype(BF)
+    keep(a_tot.at[p16], a_in.at[p16], recv.at[4])
+    wait_bytes(q_sib, core_recv.at[0])
+
+    def qkv_blocks(i):
+        there = peer(i)
+        j = there[1] * 4 + there[2]
+        q_tot[j] = (q_blk[j, c].astype(F32) + q_sib[j].astype(F32)).astype(BF)
+        push(q_tot.at[j], q_in.at[p16], send.at[7], recv.at[5], there)
+
+    loop(1, 16, qkv_blocks)
+    q_tot[p16] = (q_blk[p16, c].astype(F32) + q_sib[p16].astype(F32)).astype(BF)
+    keep(q_tot.at[p16], q_in.at[p16], recv.at[5])
+
+    wait_bytes(normed_in, recv.at[3])
+    d_normed = normed_in[0].astype(F32)
+    for k in range(1, 4):
+        d_normed = d_normed + normed_in[k].astype(F32)
+    v = tok[...].astype(F32)
+    r = lax.rsqrt(jnp.mean(v * v, axis=1, keepdims=True) + norm_eps)
+    unit = v * r
+    s_own[0:1, :] = jnp.sum(d_normed * unit, axis=0, keepdims=True)
+    push(s_own, s_sib, send.at[8], core_recv.at[2], sib)
+    d_unit = d_normed * gain[...]
+    d_in = r * (d_unit - unit * jnp.mean(d_unit * unit, axis=1, keepdims=True))
+    input_grad[...] = (d_middle[...] + d_in).astype(BF)
+    wait_bytes(s_sib, core_recv.at[2])
+    s_tot[...] = s_own[...] + s_sib[...]
+    loop(1, 16, lambda i: push(s_tot, s_in.at[p16], send.at[9], recv.at[6], peer(i)))
+    keep(s_tot, s_in.at[p16], recv.at[6])
+
+    wait_bytes(q_in, recv.at[5])
+    q_total = q_in[0].astype(F32)
+    for k in range(1, 16):
+        q_total = q_total + q_in[k].astype(F32)
+    for k in range(4):
+        qkv_sum[k, 0:6, :] = q_total[6 * k : 6 * k + 6]
+        qkv_sum[k, 6:8, :] = jnp.zeros((2, 3 * GW), F32)
+
+    def final(k):
+        d = 4 * p32 + k
+
+        @pl.when(d != me)
+        def _():
+            push(qkv_sum.at[k], qkv_out.at[z], send.at[10], recv.at[7], device_of(d))
+
+        @pl.when(d == me)
+        def _():
+            keep(qkv_sum.at[k], qkv_out.at[z], recv.at[7])
+
+    loop(0, 4, final)
+    wait_bytes(a_in, recv.at[4])
+    a_total = a_in[0].astype(F32)
+    for k in range(1, 16):
+        a_total = a_total + a_in[k].astype(F32)
+    att_sum[...] = a_total
+    keep(att_sum, att_out, own.at[1])
+    wait_bytes(s_in, recv.at[6])
+    s_total = s_in[0]
+    for k in range(1, 16):
+        s_total = s_total + s_in[k]
+    s_sum[...] = s_total
+    for k in range(1, 4):
+        push(s_sum, small_out.at[z], send.at[11], recv.at[8], ((z + k) % 4, x, y, c))
+    keep(s_sum, small_out.at[z], recv.at[8])
+    wait_bytes(att_sum, own.at[1])
+    wait_bytes(qkv_out, recv.at[7])
+    wait_bytes(small_out, recv.at[8])
     wait_bytes(do_s.at[pl.ds(0, 3)], send.at[0])
-    wait_bytes(branch_all.at[pl.ds(0, 3)], send.at[1])
+    wait_bytes(branch_all.at[pl.ds(0, 3 * TOK)], send.at[1])
     wait_bytes(parts.at[pl.ds(0, 3)], send.at[2])
-
-
-def attn_backward(p, q, kv, d_attn, branch):
+    wait_bytes(normed_in.at[pl.ds(0, 3)], send.at[3])
+    wait_bytes(a_sib, send.at[4])
+    wait_bytes(q_sib, send.at[5])
+    wait_bytes(a_in.at[pl.ds(0, 15)], send.at[6])
+    wait_bytes(q_in.at[pl.ds(0, 15)], send.at[7])
+    wait_bytes(s_own, send.at[8])
+    wait_bytes(s_in.at[pl.ds(0, 15)], send.at[9])
+
+    def sent(k):
+        @pl.when(4 * p32 + k != me)
+        def _():
+            wait_bytes(qkv_sum.at[0], send.at[10])
+
+    loop(0, 4, sent)
+    wait_bytes(small_out.at[pl.ds(0, 3)], send.at[11])
+
+
+def attn_backward(p, *rest):
     probs = (GH, 512, 2048)
+    vm = pltpu.VMEM
     return pl.pallas_call(
         attn_backward_kernel,
         out_shape=(
-            jax.ShapeDtypeStruct((512, GW), BF),
-            jax.ShapeDtypeStruct((GH, BUCKETS, TOK), F32),
-            jax.ShapeDtypeStruct((4, 4, TOK, 2 * GW), BF),
-            jax.ShapeDtypeStruct((4, TOK, D), BF),
+            jax.ShapeDtypeStruct((TOK, D), BF),
+            jax.ShapeDtypeStruct((4, 8, 3 * GW), F32),
+            jax.ShapeDtypeStruct((8, D), F32),
+            jax.ShapeDtypeStruct((4, 8, D), F32),
         ),
-        in_specs=[ANY, VMEM, VMEM, VMEM, VMEM],
-        out_specs=(VMEM, VMEM, ANY, ANY),
+        in_specs=[ANY] + [VMEM] * len(rest),
+        out_specs=(VMEM, ANY, ANY, ANY),
         scratch_shapes=[
-            pltpu.VMEM(probs, BF),
-            pltpu.VMEM((2048, GW), BF),
-            pltpu.VMEM((4, TOK, GW), BF),
-            pltpu.VMEM((GH, 512, GW), BF),
-            pltpu.VMEM((GH, 512, GW), BF),
-            pltpu.VMEM((512, 2048), F32),
-            pltpu.VMEM(probs, BF),
-            pltpu.VMEM((4, TOK, TOK), F32),
-            pltpu.VMEM((4, 4, TOK, 2 * GW), BF),
-            DMA((3,)),
-            DMA((3,)),
-            DMA,
+            vm(probs, BF), vm((2048, GW), BF), vm((4, TOK, GW), BF), vm((GH, 512, GW), BF),
+            vm((GH, 512, GW), BF), vm((512, 2048), F32), vm(probs, BF), vm((4, TOK, TOK), F32),
+            vm((4, 4, TOK, 2 * GW), BF), vm((4, 4, TOK, 2 * GW), BF), vm((512, D), BF),
+            vm((512, GW), BF), vm((GH, BUCKETS, TOK), F32),
+            vm((512, 3 * GW), BF), vm((512, D), BF), vm((4, TOK, D), BF), vm((GW + 8, D), F32),
+            vm((16, 2, 24, 3 * GW), BF), vm((16, 24, 3 * GW), BF),
+            vm((16, 24, 3 * GW), BF), vm((16, 24, 3 * GW), BF),
+            vm((16, 2, 8, D), BF), vm((16, 8, D), BF), vm((16, 8, D), BF), vm((16, 8, D), BF),
+            vm((8, D), F32), vm((8, D), F32), vm((8, D), F32), vm((16, 8, D), F32),
+            vm((4, 8, 3 * GW), F32), vm((8, D), F32), vm((8, D), F32),
+            DMA((12,)), DMA((9,)), DMA((3,)), DMA((2,)),
         ],
         compiler_params=pltpu.CompilerParams(
-            collective_id=3, has_side_effects=True, vmem_limit_bytes=44 * 2**20
+            collective_id=3, has_side_effects=True, vmem_limit_bytes=52 * 2**20
         ),
         name="attn_backward",
-    )(p, q, kv, d_attn, branch)
+    )(p, *rest)
 
 
 def per_device(
@@ -893,20 +899,26 @@
     grad_bf = cotangent.reshape(TOK, D)
     grad_out = grad_bf.astype(F32)
 
-    route = expert_ids.reshape(TOK * 2)
-    marks = (route[:, None] == jnp.arange(experts, dtype=jnp.int32)[None, :]).astype(jnp.int32)
-    earlier = jnp.cumsum(marks, axis=0) - marks
-    block = (route % 2) * 32 + (route // 4) * 2 + (route % 4) // 2
-    slot = block * 16 + c * capacity + jnp.sum(earlier * marks, axis=1)
-    slot_pair = slot.reshape(TOK, 2)
+    routes = expert_ids.reshape(TOK, 2)
     gates = gate_values.reshape(TOK, 2)
-    slot_ids = jnp.arange(slots, dtype=jnp.int32)
-    pick_0 = slot_pair[:, 0][:, None] == slot_ids[None, :]
-    pick_1 = slot_pair[:, 1][:, None] == slot_ids[None, :]
-    pick = (pick_0 | pick_1).astype(BF)
-    gate_of = jnp.where(pick_0, gates[:, :1], 0.0) + jnp.where(pick_1, gates[:, 1:], 0.0)
-    gate_slot = jnp.sum(gate_of, axis=0)
-    d_eo = (dot(pick, grad_bf, TN) * gate_slot[:, None]).astype(BF)
+    expert_list = jnp.arange(experts, dtype=jnp.int32)[None, :]
+    marks = jnp.concatenate(
+        [(routes[:, :1] == expert_list), (routes[:, 1:] == expert_list)], axis=1
+    ).astype(BF)
+    lower = jnp.tril(jnp.ones((TOK, TOK), BF), -1)
+    earlier = dot(lower, marks, NN)
+    marks = marks.astype(F32)
+    firsts = jnp.sum(marks[:, :experts], axis=0, keepdims=True)
+    rank_0 = jnp.sum(earlier[:, :experts] * marks[:, :experts], axis=1)
+    rank_1 = jnp.sum((earlier[:, experts:] + firsts) * marks[:, experts:], axis=1)
+    blocks = (routes % 2) * 32 + (routes // 4) * 2 + (routes % 4) // 2
+    places = blocks * 16 + c * capacity + jnp.stack([rank_0, rank_1], axis=1).astype(jnp.int32)
+    slot_ids = jnp.arange(slots, dtype=jnp.int32)[None, :]
+    picks = jnp.concatenate(
+        [(places[:, :1] == slot_ids), (places[:, 1:] == slot_ids)], axis=0
+    ).astype(BF)
+    gated = jnp.concatenate([gates[:, :1] * grad_out, gates[:, 1:] * grad_out], axis=0).astype(BF)
+    d_eo = dot(picks, gated, TN).astype(BF)
 
     slab = w_qkv.reshape(6, 3, GROUPS, GW).transpose(2, 0, 1, 3).reshape(GROUPS, 6, 3 * GW)
     notes = jnp.concatenate(
@@ -943,8 +955,8 @@
     qkv = dot(normed, weight, NN).astype(BF)
     queries = qkv[:, :GW]
     table = lax.dynamic_slice(rel_table, (0, z * GH), (BUCKETS, GH)).astype(F32)
-    attn, attn_part, probs, kv_all, d_eo_all, out_weights = attn_forward(
-        table, queries, qkv[:, GW:].reshape(4, TOK, 2 * GW), query_docs, key_docs, d_eo, out_slab
+    attn, attn_part, probs, kv_all, out_weights, d_eo_all = attn_forward(
+        table, queries, qkv[:, GW:].reshape(4, TOK, 2 * GW), query_docs, key_docs, out_slab, d_eo
     )
     attn = attn.transpose(1, 0, 2).reshape(TOK, D)
     attention_weight = out_weights[:, :, :12, :].reshape(D, D)
@@ -953,58 +965,38 @@
     middle = inputs + dot(attn, attention_weight, NN)
     moe_float, norm_two_back = jax.vjp(scale_rows, middle, gain_two)
     moe_in = moe_float.astype(BF)
-    send_rows = dot(pick, moe_in, TN).astype(BF)
+    send_rows = dot(picks, jnp.concatenate([moe_in, moe_in], axis=0), TN).astype(BF)
     home, expert_out, expert_in_grad, expert_out_grad = run_experts(
         send_rows, d_eo_all, w_in[0], w_out[0]
     )
-    moe_in_grad = dot(pick, home, NN)
+    home_picked = dot(picks, home, NN)
+    moe_in_grad = home_picked[:TOK] + home_picked[TOK:]
     middle_part, gain_two_grad = norm_two_back(moe_in_grad)
     middle_grad = grad_out + middle_part
     branch = middle_grad.astype(BF)
     d_attn = dot(branch, attention_weight, NT).astype(BF)
     d_attn = d_attn.reshape(TOK, GROUPS, GW).transpose(1, 0, 2)
 
-    d_q, table_part, kv_parts, branch_all = attn_backward(probs, queries, kv_all, d_attn, branch)
-    d_kv = jnp.sum(kv_parts.astype(F32), axis=0).astype(BF)
-    d_kv = d_kv.reshape(2, 2, TOK, 2, GW).transpose(0, 1, 3, 2, 4).reshape(2, 512, GW)
-    d_kv = jnp.concatenate([d_kv[1], d_kv[0]], axis=1)
-    d_qkv = jnp.concatenate([d_q, d_kv], axis=1)
-    normed_part = dot(d_qkv, weight, NT).astype(BF).reshape(4, TOK, D)
-    normed_part = z_exchange(normed_part, 8, "normed_grads")
-    normed_grad = jnp.sum(normed_part.astype(F32), axis=0)
-    _, norm_one_back = jax.vjp(scale_rows, inputs, gain_one)
-    input_part, gain_one_grad = norm_one_back(normed_grad)
-    input_grad = middle_grad + input_part
-
-    both = jnp.concatenate([pick_0, pick_1], axis=0).astype(BF)
-    picked = dot(both, expert_out, NN).reshape(2, TOK, D)
+    small = jnp.concatenate(
+        [jnp.zeros((1, D), F32), gain_two_grad.reshape(1, D), jnp.zeros((6, D), F32)]
+    )
+    input_grad, qkv_sum, att_sum, small_sum = attn_backward(
+        probs, queries, kv_all, d_attn, branch, weight, normed, attn_part, small, own_tokens,
+        gain_one.reshape(1, D), middle_grad,
+    )
+
+    picked = dot(picks, expert_out, NN).reshape(2, TOK, D)
     block_out = middle + gates[:, :1] * picked[0] + gates[:, 1:] * picked[1]
     gate_grad = jnp.sum(picked * grad_out[None], axis=2).T
 
-    qkv_part = dot(normed, d_qkv, TN).astype(BF).reshape(32, 24, 3 * GW)
-    att_part = dot(attn_part, branch_all.reshape(512, D), TN).astype(BF).reshape(32, 6, D)
-    att_part = jnp.pad(att_part, ((0, 0), (0, 2), (0, 0)))
-    table_sum = jnp.sum(table_part, axis=2).reshape(1, GH * BUCKETS)
-    small = jnp.stack(
-        [
-            jnp.pad(gain_one_grad.reshape(32, 24), ((0, 0), (0, 104))),
-            jnp.pad(gain_two_grad.reshape(32, 24), ((0, 0), (0, 104))),
-            jnp.broadcast_to(jnp.pad(table_sum, ((0, 0), (0, 128 - GH * BUCKETS))), (32, 128)),
-        ],
-        axis=1,
-    )
-    small = jnp.pad(small, ((0, 0), (0, 5), (0, 0)))
-    qkv_sum, att_sum, small_sum = weight_sums(qkv_part, att_part, small)
     qkv_grad = qkv_sum[:, :6, :].reshape(GROUPS, 6, 3, GW).transpose(1, 2, 0, 3).reshape(6, 3 * D)
     attn_out_grad = att_sum[:6]
-    place_in = (y * 2 + c) % 4
+    place_in = chip_of(z, x, y) * 2 + c
     gains = lax.dynamic_slice(jnp.sum(small_sum[:, :2, :], axis=0), (0, place_in * 6), (2, 6))
-    table_grad = (
-        small_sum[:, 2, : GH * BUCKETS].reshape(GROUPS * GH, BUCKETS).T
-    )
+    table_grad = small_sum[:, 2, : GH * BUCKETS].reshape(GROUPS * GH, BUCKETS).T
     return (
         block_out.reshape(1, TOK, D).astype(BF),
-        input_grad.reshape(1, TOK, D).astype(BF),
+        input_grad.reshape(1, TOK, D),
         gate_grad.reshape(1, TOK, 2),
         gains[0],
         qkv_grad,

time: 268 us -> 247 us (0.922)
  Pallas kernels: 208 us -> 196 us
  local copies, waits for them, and re-layouts: 36.7 us -> 31.2 us
    pallas_call x3 -> x1, Pallas kernels: 76.3 us -> 31.3 us  [run_comm(): pl.pallas_call(kernel, out_shape=outs, in_specs=[ANY] * len(args), out_sp...]
    pallas_call x1, Pallas kernels: 26.2 us -> 57.1 us  [attn_backward(): pl.pallas_call(attn_backward_kernel, out_shape=(jax.ShapeDtypeStruct((TOK...]
    unnamed x95 -> x69, local copies, waits for them, and re-layouts: 23.1 us -> 16.3 us
    dot_general x10 -> x8, matrix products: 9.96 us -> 8.42 us  [dot(): return lax.dot_general(a, b, dims, preferred_element_type=F32)]
where the time goes in v5:
time: 247 us; the launch traced here: 246 us
  Pallas kernels  196 us (79%)
  local copies, waits for them, and re-layouts  31.2 us (13%)
  other arithmetic  9.08 us (4%)
  matrix products  8.42 us (3%)
    pallas_call x1, Pallas kernels, attn_backward(): pl.pallas_call(attn_backward_kernel, out_shape=(jax.ShapeDtypeStruct((TOK...  57.1 us
    pallas_call x1, Pallas kernels, run_experts(): pl.pallas_call(experts_kernel, out_shape=(jax.ShapeDtypeStruct((1024, D),...  57 us
    pallas_call x1, Pallas kernels, attn_forward(): pl.pallas_call(attn_forward_kernel, out_shape=(jax.ShapeDtypeStruct((4, T...  50.5 us
    pallas_call x1, Pallas kernels, run_comm(): pl.pallas_call(kernel, out_shape=outs, in_specs=[ANY] * len(args), out_sp...  31.3 us
    unnamed x69, local copies, waits for them, and re-layouts  16.3 us
    dot_general x8, matrix products, dot(): return lax.dot_general(a, b, dims, preferred_element_type=F32)  8.42 us

profile of v5, /device:TPU:1, one launch (start us, length us, event | category | flops | bytes accessed | tf_op | source)
XLA Modules:
  0.0 246.0 jit_solution(5036477833507249538)
XLA Ops:
  0.7 0.8 slice_bitcast_fusion.7
  1.6 0.2 fusion.15
  1.9 0.7 fusion.22
  2.9 0.8 slice_bitcast_fusion.3
  3.7 1.1 multiply_convert_fusion.3
  4.9 0.8 convolution_convert_fusion.1.d_eo
  6.1 0.3 concatenate.33
  6.6 31.3 %start_exchange.1 = (bf16[4,128,768]{2,1,0:T(8,128)(2,1)S(1)}, bf16[32,2,16,576]{3,2,1,0:T(8,128)(2,1)S(1)}) custom-call(bf16[128,768]{1,0:T(8,128)(2,1)S(1)} %bitcast.89, bf16[4,16,576]{2,1,0:T(8,128)(2,1)S(1)} %maximum_select_fusion.wmsg), custom_call_target="tpu_custom_call" | custom-call | tf_op jit(solution)/shard_map/start_exchange/pallas_call | solution.py:94
  38.0 1.0 copy-done.5
  39.0 0.7 slice_convert_fusion
  39.9 0.2 multiply_reduce_fusion
  40.1 0.6 fusion.29
  40.7 1.1 multiply_convert_fusion
  41.8 3.0 %reshape.182.weight = bf16[768,576]{1,0:T(8,128)(2,1)} reshape(bf16[32,2,12,576]{3,2,1,0:T(8,128)(2,1)} %bitcast.93) | data formatting | bytes 1769472 | tf_op jit(solution)/shard_map/reshape | solution.py:945
  44.8 2.2 convolution_convert_fusion.2
  47.0 0.2 slice.126
  47.3 0.9 slice.102
  48.3 0.6 dynamic-slice_bitcast_fusion
  48.8 0.8 copy.45.qd
  49.7 0.6 constant_dynamic-slice_fusion.2
  50.3 1.4 copy.52
  51.6 0.7 convert_element_type.120.tab
  52.4 0.9 maximum_select_fusion.1.wa
  53.3 50.5 %attn_forward.1 = (bf16[4,128,192]{2,1,0:T(8,128)(2,1)S(1)}, bf16[512,192]{1,0:T(8,128)(2,1)S(1)}, bf16[3,512,2048]{2,1,0:T(8,128)(2,1)}, bf16[2048,384]{1,0:T(8...) custom-call(f32[32,3]{1,0:T(8,128)S(1)} %convert_element_type.120.tab, ...), custom_call_target="tpu_custom_call" | custom-call | tf_op jit(solution)/shard_map/attn_forward/pallas_call | solution.py:555
  103.8 1.1 copy-done.2
  104.9 1.1 copy-done.3
  106.1 1.1 copy-done.4
  107.2 0.7 copy-done.6
  107.9 0.7 copy-done.8
  108.6 2.3 reshape.189
  111.1 0.5 multiply_reduce_fusion.3
  111.6 0.5 copy-done.25
  112.4 1.7 convolution_convert_fusion.x16
  114.1 57.0 %experts.1 = (bf16[1024,768]{1,0:T(8,128)(2,1)S(1)}, bf16[1024,768]{1,0:T(8,128)(2,1)S(1)}, f32[768,1536]{1,0:T(8,128)}, f32[1536,768]{1,0:T(8,128)}) custom-call(bf16[1024,768]{1,0:T(8,128)(2,1)S(1)} %convolution_convert_fusion.x16, bf16[1024,768]{1,0:T(8,128)(2,1)} %copy-done.4, bf16[768,1536]{1,0:T(8,128)(2,1)} %bitcast.105, bf16[1536,768]{1,0:T(8,128)(2,1)} %bitcast.106), custom_call_target="tpu_custom_call" | custom-call | tf_op jit(solution)/shard_map/experts/pallas_call | solution.py:359
  171.2 1.2 fusion.2
  172.5 0.6 fusion.30
  173.3 0.9 fusion.32
  174.2 1.2 convolution_convert_fusion.3
  175.5 1.1 copy.47
  176.9 1.1 fusion.1.normed
  178.2 57.1 %attn_backward.1 = (bf16[128,768]{1,0:T(8,128)(2,1)S(1)}, f32[4,8,576]{2,1,0:T(8,128)S(1)}, f32[8,768]{1,0:T(8,128)S(1)}, f32[4,8,768]{2,1,0:T(8,128)S(1)}) custom-call(bf16[3,512,2048]{2,1,0:T(8,128)(2,1)} %get-tuple-element.32.p, bf16[512,192]{1,0:T(8,128)(2,1)S(1)} %slice.125.q, bf16[2048,384]{1,0:T(8,128)(2,1)} %copy-done.3, ...), custom_call_target="tpu_custom_call" | custom-call | tf_op jit(solution)/shard_map/attn_backward/pallas_call | solution.py:850
  235.5 0.7 reshape.195
  236.4 0.5 slice_bitcast_fusion
  236.9 0.7 reshape_squeeze.3
  237.6 0.7 copy.77
  238.3 0.6 copy.78
  238.9 4.9 %copy.79 = f32[1,768,1536]{2,1,0:T(8,128)} copy(f32[1,768,1536]{2,1,0:T(8,128)} %bitcast.104) | data formatting | bytes 9437184
  243.8 2.2 copy.80
  (108 shorter events, 2.9 us)
Async XLA Ops:
  0.6 49.0 %copy-start = (bf16[32,12]{0,1:T(8,128)(2,1)S(1)}, bf16[32,12]{0,1:T(8,128)(2,1)}, u32[]{:S(2)}) copy-start(bf16[32,12]{0,1:T(8,128)(2,1)} %param.16) | copy-start | bytes 2308
  2.8 2.1 copy-start.11
  2.8 2.9 %copy-start.17 = (bf16[6,2304]{1,0:T(8,128)(2,1)S(1)}, bf16[6,2304]{1,0:T(8,128)(2,1)}, u32[]{:S(2)}) copy-start(bf16[6,2304]{1,0:T(8,128)(2,1)} %param.14) | copy-start | bytes 82948
  2.9 1.9 copy-start.14
  3.7 1.1 copy-start.19
  3.7 1.1 copy-start.21
  3.7 2.2 copy-start.29
  3.7 2.3 copy-start.27
  3.7 2.3 copy-start.28
  4.9 1.7 copy-start.1
  37.9 1.1 copy-start.5
  103.8 1.1 copy-start.2
  104.9 1.1 copy-start.3
  106.1 1.1 copy-start.4
  107.2 0.7 copy-start.6
  107.9 0.7 copy-start.8
  108.6 2.3 copy-start.9
  110.9 1.2 copy-start.16
  111.0 1.4 copy-start.12
  111.6 0.5 copy-start.25
  111.6 59.5 %copy-start.23 = (f32[128]{0:T(128)}, f32[128]{0:T(128)S(1)}, u32[]{:S(2)}) copy-start(f32[128]{0:T(128)S(1)} %fusion.23) | copy-start | bytes 1540
  114.1 57.1 %copy-start.10 = (bf16[1,128,768]{2,1,0:T(8,128)(2,1)S(1)}, bf16[1,128,768]{2,1,0:T(8,128)(2,1)}, u32[]{:S(2)}) copy-start(bf16[1,128,768]{2,1,0:T(8,128)(2,1)} %param.23) | copy-start | bytes 589828
  114.1 57.1 %copy-start.13 = (pred[128,1024]{1,0:T(32,128)(4,1)S(1)}, pred[128,1024]{1,0:T(32,128)(4,1)}, u32[]{:S(2)}) copy-start(pred[128,1024]{1,0:T(32,128)(4,1)} %copy-done.11) | copy-start | bytes 393220
  114.1 57.1 %copy-start.15 = (pred[128,1024]{1,0:T(32,128)(4,1)S(1)}, pred[128,1024]{1,0:T(32,128)(4,1)}, u32[]{:S(2)}) copy-start(pred[128,1024]{1,0:T(32,128)(4,1)} %copy-done.14) | copy-start | bytes 393220
  172.5 0.7 copy-start.24
  172.5 0.8 copy-start.26
  172.5 0.8 copy-start.20
  172.5 0.8 copy-start.22
  174.2 2.7 %copy-start.18 = (f32[512]{0:T(512)S(1)}, f32[512]{0:T(512)}, u32[]{:S(2)}) copy-start(f32[512]{0:T(512)} %get-tuple-element.53) | copy-start | bytes 6148
  175.5 2.8 %copy-start.7 = (bf16[512,192]{1,0:T(8,128)(2,1)S(1)}, bf16[512,192]{1,0:T(8,128)(2,1)}, u32[]{:S(2)}) copy-start(bf16[512,192]{1,0:T(8,128)(2,1)} %copy-done.6) | copy-start | bytes 589828
  237.6 6.2 %slice-start = ((s8[4718592]{0:T(1024)(128)(4,1)}), s8[4194304]{0:T(1024)(128)(4,1)S(1)}, s32[]{:S(2)}) async-start(s8[4718592]{0:T(1024)(128)(4,1)} %bitcast.101), calls=%async_computation | async-start | bytes 8388608
  238.9 4.9 %slice-start.1 = ((s8[4718592]{0:T(1024)(128)(4,1)}), s8[524288]{0:T(1024)(128)(4,1)S(1)}, s32[]{:S(2)}) async-start(s8[4718592]{0:T(1024)(128)(4,1)} %bitcast.101), calls=%async_computation.1 | async-start | bytes 1048576

commit v6 on v5

--- a/solution.py
+++ b/solution.py
@@ -149,61 +149,6 @@
     @pl.when(y % 2 != c)
     def _():
         wait_bytes(rows.at[pl.ds(0, 16)], send)
-
-
-def start_kernel(tok, wmsg, tok_all, w_all, wm, wo, send, recv, core_recv, own):
-    z, x, y, c = place()
-    sib = (z, x, y, 1 - c)
-    keep(wmsg, wm, own)
-    expected = greet_chips(z, x, y, c)
-    for k in range(1, 4):
-        signal(((z + k) % 4, x, y, c))
-    arrive(expected + 3)
-    push(wmsg, wo, send.at[0], core_recv.at[0], sib)
-    for k in range(1, 4):
-        push(tok, tok_all.at[z], send.at[1], recv.at[0], ((z + k) % 4, x, y, c))
-    keep(tok, tok_all.at[z], recv.at[0])
-    wait_bytes(wm, own)
-    wait_bytes(wo, core_recv.at[0])
-    wm[...] = wm[...] + wo[...]
-    half = z * 8 + x * 2 + y // 2
-    to_chips(
-        z, x, y, c, lambda there: wm.at[there[0]], w_all.at[half, y % 2], send.at[2], recv.at[1]
-    )
-    wait_bytes(w_all.at[:, c], recv.at[1])
-    push(w_all.at[:, c], w_all.at[:, c], send.at[3], core_recv.at[1], sib)
-    wait_bytes(tok_all, recv.at[0])
-    wait_bytes(w_all.at[:, 1 - c], core_recv.at[1])
-    wait_bytes(wo, send.at[0])
-    wait_bytes(tok_all.at[pl.ds(0, 3)], send.at[1])
-    wait_bytes(w_all.at[pl.ds(0, 31), c], send.at[2])
-
-    @pl.when(y % 2 != c)
-    def _():
-        wait_bytes(w_all.at[0, c], send.at[2])
-
-    wait_bytes(w_all.at[:, c], send.at[3])
-
-
-def start_exchange(tok, wmsg):
-    return run_comm(
-        start_kernel,
-        (tok, wmsg),
-        (
-            jax.ShapeDtypeStruct((4, TOK, D), BF),
-            jax.ShapeDtypeStruct((32, 2, 16, 3 * GW), BF),
-        ),
-        [
-            pltpu.VMEM((4, 16, 3 * GW), BF),
-            pltpu.VMEM((4, 16, 3 * GW), BF),
-            DMA((4,)),
-            DMA((2,)),
-            DMA((2,)),
-            DMA,
-        ],
-        0,
-        "start_exchange",
-    )
 
 
 FH = 1536
@@ -412,37 +357,51 @@
 
 
 def attn_forward_kernel(
-    tab, q, kv, qd, kd, wa, d_eo,
-    attn_all, part, p_out, kv_out, wa_all, d_rows,
-    kv_s, v_s, qm, bias, s_s, p_s, wm, wo, xo,
+    tab, tok, wmsg, wa, d_eo,
+    attn_all, part, p_out, kv_out, wa_all, d_rows, normed, weight, q, gains,
+    wm, wo, w_s, tok_s, select, picker, qd, kd,
+    kv, kv_s, v_s, qm, bias, s_s, p_s, xo,
     send, recv, kv_recv, core_recv, own,
 ):
     z, x, y, c = place()
     sib = (z, x, y, 1 - c)
     mine = pl.ds(pl.multiple_of(c * 512, 512), 512)
     theirs = pl.ds(pl.multiple_of((1 - c) * 512, 512), 512)
+    me = block_of(z, x, y)
+    keep(wa, wa_all.at[z, x, y, c], own.at[0])
     expected = greet_chips(z, x, y, c)
     for k in range(1, 4):
         signal(((z + k) % 4, x, y, c))
         signal((z, (x + k) % 4, y, c))
-    arrive(expected + 6)
-    for k in range(1, 4):
-        for b in range(4):
-            push(
-                kv.at[b], kv_s.at[block_cols(b, x)], send.at[0], kv_recv.at[4 - k],
-                (z, (x + k) % 4, y, c),
-            )
-    for b in range(4):
-        keep(kv.at[b], kv_s.at[block_cols(b, x)], kv_recv.at[0])
-    push(wa, wo, send.at[1], core_recv.at[0], sib)
+        signal((z, x, (y + k) % 4, c))
+    arrive(expected + 9)
+    push(wmsg, wo, send.at[0], core_recv.at[0], sib)
+    for k in range(1, 4):
+        push(tok, tok_s.at[z], send.at[1], recv.at[0], ((z + k) % 4, x, y, c))
+    keep(tok, tok_s.at[z], recv.at[0])
     push(d_eo.at[theirs], xo, send.at[2], core_recv.at[1], sib)
-    for h in range(GH):
-        head_cols = lax.broadcasted_iota(jnp.int32, (1, GW), 1) // HD == h
-        qm[h] = jnp.where(head_cols, q[...] * 0.125, 0.0).astype(BF)
     wait_bytes(wo, core_recv.at[0])
-    wm[...] = wa[...] + wo[...]
-    wait_bytes(xo, core_recv.at[1])
-    xo[...] = xo[...] + d_eo[mine, :]
+    wm[...] = wmsg[...] + wo[...]
+    to_chips(
+        z, x, y, c, lambda there: wm.at[there[0]], w_s.at[pl.ds(me, 16)], send.at[3], recv.at[1]
+    )
+    for k in range(1, 4):
+        push(wa, wa_all.at[z, x, y, c], send.at[4], recv.at[2], ((z + k) % 4, x, y, c))
+
+    row = lax.broadcasted_iota(jnp.int32, (1, 1024), 1)
+    r, half, at = row & 15, row >> 9, (row >> 4) & 31
+    row_z, row_x, row_y = at >> 3, (at >> 1) & 3, (at & 1) * 2 + half
+    feature = jnp.where(r < 12, (row_z * 16 + row_x * 4 + row_y) * 12 + r, -1)
+    select[...] = jnp.where(
+        lax.broadcasted_iota(jnp.int32, (D, 1024), 0) == feature, 1.0, 0.0
+    ).astype(BF)
+    j = lax.broadcasted_iota(jnp.int32, (32, 1024), 0)
+    gain_rows = (j < 4) & (r >> 1 == 6 + (j >> 1)) & (row_z >> 1 == j & 1)
+    notes = (r == 12 + c) & (row_y == y)
+    key_rows = (j >= 8) & (row_z * 4 + row_x == j - 8)
+    query_rows = (j >= 24) & (row_z == j - 24) & (row_x == x)
+    picker[...] = jnp.where(gain_rows | (notes & (key_rows | query_rows)), 1.0, 0.0).astype(BF)
+    xo_ready = core_recv.at[1]
 
     def tables(h):
         for dist in range(2):
@@ -455,6 +414,51 @@
         bias[h, 3] = jnp.full((TOK, TOK), tab[BUCKETS - 1, h], F32)
 
     loop(0, GH, tables)
+    wait_bytes(xo, xo_ready)
+    xo[...] = xo[...] + d_eo[mine, :]
+    wait_bytes(w_s.at[mine], recv.at[1])
+    push(w_s.at[mine], w_s.at[mine], send.at[5], core_recv.at[2], sib)
+    wait_bytes(wa_all.at[z, x, y, c], own.at[0])
+    wait_bytes(wa_all.at[pl.ds(0, 3), x, y, c], recv.at[2])
+    for k in range(1, 4):
+        push(
+            wa_all.at[:, x, y, c], wa_all.at[:, x, y, c], send.at[6], recv.at[3],
+            (z, (x + k) % 4, y, c),
+        )
+    wait_bytes(w_s.at[theirs], core_recv.at[2])
+    picked = dot(picker[...], w_s[...], NN)
+    gain = jnp.concatenate([picked[0:1, :384], picked[1:2, :384]], axis=1)
+    gains[0:1, :] = gain
+    gains[1:2, :] = jnp.concatenate([picked[2:3, :384], picked[3:4, :384]], axis=1)
+    gains[2:8, :] = jnp.zeros((6, D), F32)
+    kd[...] = picked[8:24, 384:512]
+    qd[...] = picked[24:32, 384:512].T
+    weight[...] = dot(select[...], w_s[...], NN).astype(BF)
+    wait_bytes(tok_s, recv.at[0])
+    for b in range(4):
+        v = tok_s[b].astype(F32)
+        normed[b * TOK : (b + 1) * TOK, :] = scale_rows(v, gain).astype(BF)
+    qkv = dot(normed[...], weight[...], NN).astype(BF)
+    q[...] = qkv[:, :GW]
+    for b in range(4):
+        kv[b] = qkv[b * TOK : (b + 1) * TOK, GW:]
+    for k in range(1, 4):
+        for b in range(4):
+            push(
+                kv.at[b], kv_s.at[block_cols(b, x)], send.at[7], kv_recv.at[4 - k],
+                (z, (x + k) % 4, y, c),
+            )
+    for b in range(4):
+        keep(kv.at[b], kv_s.at[block_cols(b, x)], kv_recv.at[0])
+    wait_bytes(wa_all.at[:, pl.ds(0, 3), y, c], recv.at[3])
+    for k in range(1, 4):
+        push(
+            wa_all.at[:, :, y, c], wa_all.at[:, :, y, c], send.at[8], recv.at[4],
+            (z, x, (y + k) % 4, c),
+        )
+    for h in range(GH):
+        head_cols = lax.broadcasted_iota(jnp.int32, (1, GW), 1) // HD == h
+        qm[h] = jnp.where(head_cols, q[...] * 0.125, 0.0).astype(BF)
     for k in range(4):
         kx = (x + k) % 4
         if k == 0:
@@ -468,21 +472,20 @@
             for h in range(GH):
                 s_s[h, b * TOK :, cols] = dot(qm[h, b * TOK :, :], kv_s[cols, :GW], NT)
     keep(kv_s, kv_out, own.at[1])
-    half = z * 8 + x * 2 + y // 2
-    to_chips(z, x, y, c, lambda there: wm, wa_all.at[half, y % 2], send.at[3], recv.at[0])
-    me = block_of(z, x, y)
     to_chips(
         z, x, y, c,
         lambda there: xo.at[pl.ds(pl.multiple_of(block_of(*there[:3]) - c * 512, 16), 16)],
-        d_rows.at[pl.ds(me, 16)], send.at[4], recv.at[1],
-    )
+        d_rows.at[pl.ds(me, 16)], send.at[9], recv.at[5],
+    )
+    wait_bytes(wa_all.at[:, :, pl.ds(0, 3), c], recv.at[4])
+    push(wa_all.at[:, :, :, c], wa_all.at[:, :, :, c], send.at[10], core_recv.at[3], sib)
 
     def head(h):
         head_cols = lax.broadcasted_iota(jnp.int32, (1, GW), 1) // HD == h
         far = tab[BUCKETS - 1, h]
         for zq in range(4):
             rows = pl.ds(zq * TOK, TOK)
-            docs = qd[rows, :]
+            docs = qd[:, zq : zq + 1]
             top = None
             for zk in range(zq + 1):
                 for kx in range(4):
@@ -492,7 +495,8 @@
                         s = s + far
                     else:
                         s = s + bias[h, table_kind(zq, zk, x, kx)]
-                    s = jnp.where(docs == kd[:, cols], s, masked)
+                    kb = zk * 4 + kx
+                    s = jnp.where(docs == kd[kb : kb + 1, :], s, masked)
                     s_s[h, rows, cols] = s
                     top = s if top is None else jnp.maximum(top, s)
             top = jnp.max(top, axis=1, keepdims=True)
@@ -522,36 +526,35 @@
         there = (z + k) % 4
         push(
             part.at[pl.ds(pl.multiple_of(there * TOK, TOK), TOK)], attn_all.at[z],
-            send.at[6], recv.at[2], (there, x, y, c),
+            send.at[11], recv.at[6], (there, x, y, c),
         )
-    keep(part.at[pl.ds(pl.multiple_of(z * TOK, TOK), TOK)], attn_all.at[z], recv.at[2])
+    keep(part.at[pl.ds(pl.multiple_of(z * TOK, TOK), TOK)], attn_all.at[z], recv.at[6])
     keep(p_s, p_out, own.at[2])
-    wait_bytes(wa_all.at[:, c], recv.at[0])
-    push(wa_all.at[:, c], wa_all.at[:, c], send.at[5], core_recv.at[2], sib)
-    wait_bytes(d_rows.at[mine], recv.at[1])
-    push(d_rows.at[mine], d_rows.at[mine], send.at[7], core_recv.at[3], sib)
-    wait_bytes(attn_all, recv.at[2])
-    wait_bytes(wa_all.at[:, 1 - c], core_recv.at[2])
-    wait_bytes(d_rows.at[theirs], core_recv.at[3])
+    wait_bytes(d_rows.at[mine], recv.at[5])
+    push(d_rows.at[mine], d_rows.at[mine], send.at[12], core_recv.at[4], sib)
+    wait_bytes(attn_all, recv.at[6])
+    wait_bytes(wa_all.at[:, :, :, 1 - c], core_recv.at[3])
+    wait_bytes(d_rows.at[theirs], core_recv.at[4])
     wait_bytes(kv_s, own.at[1])
     wait_bytes(p_s, own.at[2])
-    wait_bytes(kv_s.at[pl.ds(0, 1536)], send.at[0])
-    wait_bytes(wo, send.at[1])
-    wait_bytes(wa_all.at[pl.ds(0, 31), c], send.at[3])
-
-    @pl.when(y % 2 != c)
-    def _():
-        wait_bytes(wa_all.at[0, c], send.at[3])
-
-    wait_bytes(wa_all.at[:, c], send.at[5])
-    wait_bytes(attn_all.at[pl.ds(0, 3)], send.at[6])
+    wait_bytes(wo, send.at[0])
+    wait_bytes(tok_s.at[pl.ds(0, 3)], send.at[1])
     wait_bytes(xo, send.at[2])
-    sent_to_chips(d_rows, y, c, send.at[4])
-    wait_bytes(d_rows.at[mine], send.at[7])
-
-
-def attn_forward(tab, q, kv, qd, kd, wa, d_eo):
+    sent_to_chips(w_s, y, c, send.at[3])
+    wait_bytes(wa_all.at[pl.ds(0, 3), x, y, c], send.at[4])
+    wait_bytes(w_s.at[mine], send.at[5])
+    wait_bytes(wa_all.at[:, pl.ds(0, 3), y, c], send.at[6])
+    wait_bytes(kv_s.at[pl.ds(0, 1536)], send.at[7])
+    wait_bytes(wa_all.at[:, :, pl.ds(0, 3), c], send.at[8])
+    sent_to_chips(d_rows, y, c, send.at[9])
+    wait_bytes(wa_all.at[:, :, :, c], send.at[10])
+    wait_bytes(attn_all.at[pl.ds(0, 3)], send.at[11])
+    wait_bytes(d_rows.at[mine], send.at[12])
+
+
+def attn_forward(tab, tok, wmsg, wa, d_eo):
     probs = (GH, 512, 2048)
+    vm = pltpu.VMEM
     return pl.pallas_call(
         attn_forward_kernel,
         out_shape=(
@@ -559,32 +562,29 @@
             jax.ShapeDtypeStruct((512, GW), BF),
             jax.ShapeDtypeStruct(probs, BF),
             jax.ShapeDtypeStruct((2048, 2 * GW), BF),
-            jax.ShapeDtypeStruct((32, 2, 16, D), BF),
+            jax.ShapeDtypeStruct((4, 4, 4, 2, 8, D), BF),
             jax.ShapeDtypeStruct((1024, D), BF),
+            jax.ShapeDtypeStruct((512, D), BF),
+            jax.ShapeDtypeStruct((D, 3 * GW), BF),
+            jax.ShapeDtypeStruct((512, GW), BF),
+            jax.ShapeDtypeStruct((8, D), F32),
         ),
-        in_specs=[SMEM] + [VMEM] * 6,
-        out_specs=(ANY, VMEM, ANY, ANY, ANY, ANY),
+        in_specs=[SMEM, VMEM, VMEM, VMEM, VMEM],
+        out_specs=(ANY, VMEM, ANY, ANY, ANY, ANY, VMEM, VMEM, VMEM, VMEM),
         scratch_shapes=[
-            pltpu.VMEM((2048, 2 * GW), BF),
-            pltpu.VMEM((2048, GW), BF),
-            pltpu.VMEM((GH, 512, GW), BF),
-            pltpu.VMEM((GH, 4, TOK, TOK), F32),
-            pltpu.VMEM(probs, F32),
-            pltpu.VMEM(probs, BF),
-            pltpu.VMEM((16, D), BF),
-            pltpu.VMEM((16, D), BF),
-            pltpu.VMEM((512, D), BF),
-            DMA((8,)),
-            DMA((3,)),
-            DMA((4,)),
-            DMA((4,)),
-            DMA((3,)),
+            vm((4, 16, 3 * GW), BF), vm((4, 16, 3 * GW), BF), vm((1024, 3 * GW), BF),
+            vm((4, TOK, D), BF), vm((D, 1024), BF), vm((32, 1024), BF),
+            vm((TOK, 8), F32), vm((16, TOK), F32),
+            vm((4, TOK, 2 * GW), BF), vm((2048, 2 * GW), BF), vm((2048, GW), BF),
+            vm((GH, 512, GW), BF), vm((GH, 4, TOK, TOK), F32), vm(probs, F32), vm(probs, BF),
+            vm((512, D), BF),
+            DMA((13,)), DMA((7,)), DMA((4,)), DMA((5,)), DMA((3,)),
         ],
         compiler_params=pltpu.CompilerParams(
-            collective_id=2, has_side_effects=True, vmem_limit_bytes=44 * 2**20
+            collective_id=2, has_side_effects=True, vmem_limit_bytes=48 * 2**20
         ),
         name="attn_forward",
-    )(tab, q, kv, qd, kd, wa, d_eo)
+    )(tab, tok, wmsg, wa, d_eo)
 
 
 def attn_backward_kernel(
@@ -616,6 +616,10 @@
             signal((k, source // 8, (source // 2) % 4, source % 2))
 
     loop(0, 4, greet)
+    v_s[...] = kv[:, GW:]
+    for h in range(GH):
+        head_cols = lax.broadcasted_iota(jnp.int32, (1, GW), 1) // HD == h
+        qm[h] = jnp.where(head_cols, q[...] * 0.125, 0.0).astype(BF)
     arrive(15 + 3 + 1 + 4 - jnp.where(source == p32, 1, 0))
     for k in range(1, 4):
         there = (z + k) % 4
@@ -625,10 +629,6 @@
     for k in range(1, 4):
         push(branch, branch_all.at[z_rows], send.at[1], recv.at[1], ((z + k) % 4, x, y, c))
     keep(branch, branch_all.at[z_rows], recv.at[1])
-    v_s[...] = kv[:, GW:]
-    for h in range(GH):
-        head_cols = lax.broadcasted_iota(jnp.int32, (1, GW), 1) // HD == h
-        qm[h] = jnp.where(head_cols, q[...] * 0.125, 0.0).astype(BF)
     wait_bytes(do_s, recv.at[0])
     for h in range(GH):
         head_cols = lax.broadcasted_iota(jnp.int32, (1, GW), 1) // HD == h
@@ -921,45 +921,28 @@
     d_eo = dot(picks, gated, TN).astype(BF)
 
     slab = w_qkv.reshape(6, 3, GROUPS, GW).transpose(2, 0, 1, 3).reshape(GROUPS, 6, 3 * GW)
-    notes = jnp.concatenate(
-        [
-            gain_attn, gain_moe, jnp.zeros((116,), BF),
-            doc_ids.reshape(TOK).astype(BF), jnp.zeros((3 * GW - 256,), BF),
-        ]
-    )
-    notes = jnp.broadcast_to(notes, (GROUPS, 1, 3 * GW))
+    place_in = chip_of(z, x, y) * 2 + c
+    among = (place_in % 64) * 6
+    row_one = lax.dynamic_update_slice(jnp.zeros((3 * GW,), BF), gain_attn, (among,))
+    row_one = lax.dynamic_update_slice(row_one, doc_ids.reshape(TOK).astype(BF), (384,))
+    row_two = lax.dynamic_update_slice(jnp.zeros((3 * GW,), BF), gain_moe, (among,))
+    note_one = jnp.broadcast_to(row_one, (GROUPS, 1, 3 * GW))
+    note_two = jnp.broadcast_to(row_two, (GROUPS, 1, 3 * GW))
     nothing = jnp.zeros((GROUPS, 6, 3 * GW), BF)
+    none = nothing[:, :1]
     message = jnp.where(
         c == 0,
-        jnp.concatenate([slab, nothing, notes, nothing[:, :3]], axis=1),
-        jnp.concatenate([nothing, slab, nothing[:, :1], notes, nothing[:, :2]], axis=1),
-    )
-    zero_rows = jnp.zeros((6, D), BF)
-    out_slab = jnp.where(
-        c == 0,
-        jnp.concatenate([w_attn_out, zero_rows, zero_rows[:4]], axis=0),
-        jnp.concatenate([zero_rows, w_attn_out, zero_rows[:4]], axis=0),
-    )
-    tok_all, w_all = start_exchange(own_tokens, message)
-
-    weight = w_all[:, :, :12, :].reshape(D, 3 * GW)
-    gain_one = w_all[:, :, 12:14, 0:6].reshape(D).astype(F32)
-    gain_two = w_all[:, :, 12:14, 6:12].reshape(D).astype(F32)
-    doc_rows = w_all[:, :, 12:14, 128:256].reshape(16, 4, 2, TOK)
-    doc_rows = lax.dynamic_slice(doc_rows, (0, y, c, 0), (16, 1, 1, TOK)).reshape(16, TOK).astype(F32)
-    key_docs = doc_rows.reshape(1, 2048)
-    query_docs = lax.dynamic_slice(doc_rows.reshape(4, 4, TOK), (0, x, 0), (4, 1, TOK)).reshape(512, 1)
-
-    inputs_all = tok_all.reshape(512, D).astype(F32)
-    normed = scale_rows(inputs_all, gain_one).astype(BF)
-    qkv = dot(normed, weight, NN).astype(BF)
-    queries = qkv[:, :GW]
+        jnp.concatenate([slab, nothing, note_one, none, note_two, none], axis=1),
+        jnp.concatenate([nothing, slab, none, note_one, none, note_two], axis=1),
+    )
+    out_slab = jnp.concatenate([w_attn_out, jnp.zeros((2, D), BF)], axis=0)
     table = lax.dynamic_slice(rel_table, (0, z * GH), (BUCKETS, GH)).astype(F32)
-    attn, attn_part, probs, kv_all, out_weights, d_eo_all = attn_forward(
-        table, queries, qkv[:, GW:].reshape(4, TOK, 2 * GW), query_docs, key_docs, out_slab, d_eo
-    )
+    (
+        attn, attn_part, probs, kv_all, out_weights, d_eo_all, normed, weight, queries, gain_rows,
+    ) = attn_forward(table, own_tokens, message, out_slab, d_eo)
+    gain_one, gain_two = gain_rows[0], gain_rows[1]
     attn = attn.transpose(1, 0, 2).reshape(TOK, D)
-    attention_weight = out_weights[:, :, :12, :].reshape(D, D)
+    attention_weight = out_weights[:, :, :, :, :6, :].reshape(D, D)
 
     inputs = own_tokens.astype(F32)
     middle = inputs + dot(attn, attention_weight, NN)
@@ -991,7 +974,6 @@
 
     qkv_grad = qkv_sum[:, :6, :].reshape(GROUPS, 6, 3, GW).transpose(1, 2, 0, 3).reshape(6, 3 * D)
     attn_out_grad = att_sum[:6]
-    place_in = chip_of(z, x, y) * 2 + c
     gains = lax.dynamic_slice(jnp.sum(small_sum[:, :2, :], axis=0), (0, place_in * 6), (2, 6))
     table_grad = small_sum[:, 2, : GH * BUCKETS].reshape(GROUPS * GH, BUCKETS).T
     return (

time: 247 us -> 221 us (0.89)
  local copies, waits for them, and re-layouts: 31.2 us -> 21.7 us
  Pallas kernels: 196 us -> 187 us
  other arithmetic: 9.08 us -> 3.59 us
    pallas_call x1 -> x0, Pallas kernels: 31.3 us -> none  [run_comm(): pl.pallas_call(kernel, out_shape=outs, in_specs=[ANY] * len(args), out_sp...]
    pallas_call x1, Pallas kernels: 50.5 us -> 71.2 us  [attn_forward(): pl.pallas_call(attn_forward_kernel, out_shape=(jax.ShapeDtypeStruct((4, T...]
    reshape x4 -> x1, local copies, waits for them, and re-layouts: 6.67 us -> 1.24 us  [per_device(): attention_weight = out_weights[:, :, :, :, :6, :].reshape(D, D)]
    unnamed x69 -> x25, local copies, waits for them, and re-layouts: 16.3 us -> 12.7 us
    convert_element_type x4 -> x0, other arithmetic: 3 us -> none  [the longest x2 2.25 us: per_device(): normed = scale_rows(inputs_all, gain_one).astype(BF)]
    dot_general x8 -> x7, matrix products: 8.42 us -> 7.05 us  [dot(): return lax.dot_general(a, b, dims, preferred_element_type=F32)]
where the time goes in v6:
time: 221 us
  Pallas kernels  187 us (85%)
  local copies, waits for them, and re-layouts  21.7 us (10%)
  matrix products  7.05 us (3%)
  other arithmetic  3.59 us (2%)
    pallas_call x1, Pallas kernels, attn_forward(): pl.pallas_call(attn_forward_kernel, out_shape=(jax.ShapeDtypeStruct((4, T...  71.2 us
    pallas_call x1, Pallas kernels, attn_backward(): pl.pallas_call(attn_backward_kernel, out_shape=(jax.ShapeDtypeStruct((TOK...  58.7 us
    pallas_call x1, Pallas kernels, run_experts(): pl.pallas_call(experts_kernel, out_shape=(jax.ShapeDtypeStruct((1024, D),...  57.4 us
    unnamed x25, local copies, waits for them, and re-layouts  12.7 us
    dot_general x7, matrix products, dot(): return lax.dot_general(a, b, dims, preferred_element_type=F32)  7.05 us

profile of v6, /device:TPU:1, one launch (start us, length us, event | category | flops | bytes accessed | tf_op | source)
XLA Modules:
  0.0 220.6 jit_solution(5011834043898543624)
XLA Ops:
  0.7 0.7 copy-done
  1.3 0.1 copy.42
  1.5 0.9 reshape.94
  2.4 0.1 reshape.95
  2.5 0.8 dynamic_update_slice.9
  3.4 0.7 convert_bitcast_fusion
  4.0 0.2 dynamic_update_slice.10
  4.2 0.8 dynamic_update_slice.11
  5.1 0.3 concatenate.25
  5.4 0.3 concatenate.26
  5.7 0.7 concatenate.27.wa
  6.4 0.8 slice_bitcast_fusion.3
  7.2 1.1 multiply_convert_fusion.2
  8.3 0.2 fusion.13
  8.5 0.1 slice_reduce_fusion
  8.6 0.1 fusion.16
  8.8 0.1 iota_compare_fusion
  8.9 0.1 iota_compare_fusion.1
  9.1 2.0 convolution_convert_fusion.1.d_eo
  11.0 71.2 %attn_forward.1 = (bf16[4,128,192]{2,1,0:T(8,128)(2,1)S(1)}, bf16[512,192]{1,0:T(8,128)(2,1)S(1)}, bf16[3,512,2048]{2,1,0:T(8,128)(2,1)}, bf16[2048,384]{1,0:T(8...) custom-call(f32[32,3]{1,0:T(8,128)S(1)} %convert_element_type.52.tab, ...), custom_call_target="tpu_custom_call" | custom-call | tf_op jit(solution)/shard_map/attn_forward/pallas_call | solution.py:558
  82.2 1.1 copy-done.2
  83.4 1.0 copy-done.3
  84.3 0.9 copy-done.4
  85.2 0.2 copy.37
  85.4 1.2 reshape.99
  86.6 1.7 multiply_reduce_fusion.2
  88.4 0.1 multiply_convert_fusion
  88.5 0.8 convolution_convert_fusion.x16
  89.3 57.4 %experts.1 = (bf16[1024,768]{1,0:T(8,128)(2,1)S(1)}, bf16[1024,768]{1,0:T(8,128)(2,1)S(1)}, f32[768,1536]{1,0:T(8,128)}, f32[1536,768]{1,0:T(8,128)}) custom-call(bf16[1024,768]{1,0:T(8,128)(2,1)S(1)} %convolution_convert_fusion.x16, bf16[1024,768]{1,0:T(8,128)(2,1)} %get-tuple-element.31.d_rows, bf16[768,1536]{1,0:T(8,128)(2,1)} %bitcast.83, ...), custom_call_target="tpu_custom_call" | custom-call | tf_op jit(solution)/shard_map/experts/pallas_call | solution.py:304
  146.8 0.6 fusion.27
  147.4 0.2 multiply_reduce_fusion
  147.5 0.1 copy-done.6
  147.7 1.2 fusion
  149.0 0.9 fusion.29
  149.9 0.4 copy-done.5
  150.3 0.5 convolution_convert_fusion.2
  150.8 0.2 copy.38
  151.0 0.2 copy.39
  151.3 58.7 %attn_backward.1 = (bf16[128,768]{1,0:T(8,128)(2,1)S(1)}, f32[4,8,576]{2,1,0:T(8,128)S(1)}, f32[8,768]{1,0:T(8,128)S(1)}, f32[4,8,768]{2,1,0:T(8,128)S(1)}) custom-call(bf16[3,512,2048]{2,1,0:T(8,128)(2,1)} %get-tuple-element.33.p, bf16[512,192]{1,0:T(8,128)(2,1)S(1)} %get-tuple-element.34.q, bf16[2048,384]{1,0:T(8,128)(2,1)} %copy-done.2, ...), custom_call_target="tpu_custom_call" | custom-call | tf_op jit(solution)/shard_map/attn_backward/pallas_call | solution.py:850
  210.0 0.1 constant_dynamic-slice_fusion
  210.1 0.5 slice_bitcast_fusion
  210.7 0.1 reshape.104
  210.8 0.7 reshape.105
  211.6 0.7 reshape_squeeze.3
  212.2 0.7 copy.69
  212.9 0.6 copy.70
  213.5 4.9 %copy.71 = f32[1,768,1536]{2,1,0:T(8,128)} copy(f32[1,768,1536]{2,1,0:T(8,128)} %bitcast.82) | data formatting | bytes 9437184
  218.4 2.2 copy.72
  (45 shorter events, 0.5 us)
Async XLA Ops:
  0.6 0.7 copy-start
  0.7 7.6 %copy-start.7 = (s32[1,128,2]{1,2,0:T(2,128)S(1)}, s32[1,128,2]{1,2,0:T(2,128)}, u32[]{:S(2)}) copy-start(s32[1,128,2]{1,2,0:T(2,128)} %param.20) | copy-start | bytes 3076
  8.2 2.8 %copy-start.1 = (bf16[1,128,768]{2,1,0:T(8,128)(2,1)S(1)}, bf16[1,128,768]{2,1,0:T(8,128)(2,1)}, u32[]{:S(2)}) copy-start(bf16[1,128,768]{2,1,0:T(8,128)(2,1)} %param.12) | copy-start | bytes 589828
  82.2 1.1 copy-start.2
  83.4 1.0 copy-start.3
  84.3 0.9 copy-start.4
  146.7 0.9 copy-start.6
  149.0 1.3 copy-start.5
  212.2 6.2 %slice-start = ((s8[4718592]{0:T(1024)(128)(4,1)}), s8[4194304]{0:T(1024)(128)(4,1)S(1)}, s32[]{:S(2)}) async-start(s8[4718592]{0:T(1024)(128)(4,1)} %bitcast.79), calls=%async_computation | async-start | bytes 8388608
  213.5 4.9 %slice-start.1 = ((s8[4718592]{0:T(1024)(128)(4,1)}), s8[524288]{0:T(1024)(128)(4,1)S(1)}, s32[]{:S(2)}) async-start(s8[4718592]{0:T(1024)(128)(4,1)} %bitcast.79), calls=%async_computation.1 | async-start | bytes 1048576

commit v7 on v6

--- a/solution.py
+++ b/solution.py
@@ -387,6 +387,13 @@
     )
     for k in range(1, 4):
         push(wa, wa_all.at[z, x, y, c], send.at[4], recv.at[2], ((z + k) % 4, x, y, c))
+    wait_bytes(xo, core_recv.at[1])
+    xo[...] = xo[...] + d_eo[mine, :]
+    to_chips(
+        z, x, y, c,
+        lambda there: xo.at[pl.ds(pl.multiple_of(block_of(*there[:3]) - c * 512, 16), 16)],
+        d_rows.at[pl.ds(me, 16)], send.at[9], recv.at[5],
+    )
 
     row = lax.broadcasted_iota(jnp.int32, (1, 1024), 1)
     r, half, at = row & 15, row >> 9, (row >> 4) & 31
@@ -401,7 +408,6 @@
     key_rows = (j >= 8) & (row_z * 4 + row_x == j - 8)
     query_rows = (j >= 24) & (row_z == j - 24) & (row_x == x)
     picker[...] = jnp.where(gain_rows | (notes & (key_rows | query_rows)), 1.0, 0.0).astype(BF)
-    xo_ready = core_recv.at[1]
 
     def tables(h):
         for dist in range(2):
@@ -414,8 +420,6 @@
         bias[h, 3] = jnp.full((TOK, TOK), tab[BUCKETS - 1, h], F32)
 
     loop(0, GH, tables)
-    wait_bytes(xo, xo_ready)
-    xo[...] = xo[...] + d_eo[mine, :]
     wait_bytes(w_s.at[mine], recv.at[1])
     push(w_s.at[mine], w_s.at[mine], send.at[5], core_recv.at[2], sib)
     wait_bytes(wa_all.at[z, x, y, c], own.at[0])
@@ -472,11 +476,8 @@
             for h in range(GH):
                 s_s[h, b * TOK :, cols] = dot(qm[h, b * TOK :, :], kv_s[cols, :GW], NT)
     keep(kv_s, kv_out, own.at[1])
-    to_chips(
-        z, x, y, c,
-        lambda there: xo.at[pl.ds(pl.multiple_of(block_of(*there[:3]) - c * 512, 16), 16)],
-        d_rows.at[pl.ds(me, 16)], send.at[9], recv.at[5],
-    )
+    wait_bytes(d_rows.at[mine], recv.at[5])
+    push(d_rows.at[mine], d_rows.at[mine], send.at[12], core_recv.at[4], sib)
     wait_bytes(wa_all.at[:, :, pl.ds(0, 3), c], recv.at[4])
     push(wa_all.at[:, :, :, c], wa_all.at[:, :, :, c], send.at[10], core_recv.at[3], sib)
 
@@ -530,8 +531,6 @@
         )
     keep(part.at[pl.ds(pl.multiple_of(z * TOK, TOK), TOK)], attn_all.at[z], recv.at[6])
     keep(p_s, p_out, own.at[2])
-    wait_bytes(d_rows.at[mine], recv.at[5])
-    push(d_rows.at[mine], d_rows.at[mine], send.at[12], core_recv.at[4], sib)
     wait_bytes(attn_all, recv.at[6])
     wait_bytes(wa_all.at[:, :, :, 1 - c], core_recv.at[3])
     wait_bytes(d_rows.at[theirs], core_recv.at[4])
@@ -636,53 +635,50 @@
             dm[h, b * TOK : (b + 1) * TOK, :] = jnp.where(head_cols, do_s[b], 0.0).astype(BF)
     wait_bytes(p_s, own.at[0])
 
-    def key_sums(left, right, first):
+    def key_sums(left, right, m, pair):
         for k in (1, 2, 3, 0):
             kx = (x + k) % 4
-            for b in range(4):
+            for b in (2 * pair, 2 * pair + 1):
                 cols = block_cols(b, kx)
                 total = None
                 for h in range(GH):
                     one = dot(left[h, b * TOK :, cols], right[h, b * TOK :, :], TN)
                     total = one if total is None else total + one
                 side = GW * (b % 2)
-                messages[k, first + b // 2, :, side : side + GW] = total.astype(BF)
-            for m in range(first, first + 2):
-                if k:
-                    push(
-                        messages.at[k, m], parts.at[x, m], send.at[2], recv.at[2],
-                        (z, kx, y, c),
-                    )
-                else:
-                    keep(messages.at[k, m], parts.at[x, m], recv.at[2])
-
-    key_sums(p_s, dm, 0)
-
-    def head(h):
-        head_cols = lax.broadcasted_iota(jnp.int32, (1, GW), 1) // HD == h
-        for zk in range(4):
-            cols = pl.ds(zk * 512, 512)
-            dp_s[zk * TOK :, cols] = dot(dm[h, zk * TOK :, :], v_s[cols, :], NT)
-        near[...] = jnp.zeros_like(near)
-        for zq in range(4):
-            rows = pl.ds(zq * TOK, TOK)
+                messages[k, m, :, side : side + GW] = total.astype(BF)
+            if k:
+                push(messages.at[k, m], parts.at[x, m], send.at[2], recv.at[2], (z, kx, y, c))
+            else:
+                keep(messages.at[k, m], parts.at[x, m], recv.at[2])
+
+    key_sums(p_s, dm, 0, 0)
+    key_sums(p_s, dm, 1, 1)
+    near[...] = jnp.zeros_like(near)
+
+    def score_grads(zq):
+        rows = pl.ds(zq * TOK, TOK)
+        width = (zq + 1) * 512
+
+        def head(h):
+            head_cols = lax.broadcasted_iota(jnp.int32, (1, GW), 1) // HD == h
+            dp_s[:, :width] = dot(dm[h, rows, :], v_s[:width, :], NT)
             acc = jnp.zeros((TOK, TOK), F32)
             for kb in range(4 * (zq + 1)):
                 cols = pl.ds(kb * TOK, TOK)
-                acc = acc + p_s[h, rows, cols].astype(F32) * dp_s[rows, cols]
+                acc = acc + p_s[h, rows, cols].astype(F32) * dp_s[:, cols]
             delta = jnp.sum(acc, axis=1, keepdims=True)
             far = jnp.zeros((TOK, TOK), F32)
             for zk in range(zq + 1):
                 for kx in range(4):
                     cols = pl.ds((zk * 4 + kx) * TOK, TOK)
-                    ds = (p_s[h, rows, cols].astype(F32) * (dp_s[rows, cols] - delta)).astype(BF)
+                    ds = (p_s[h, rows, cols].astype(F32) * (dp_s[:, cols] - delta)).astype(BF)
                     ds_s[h, rows, cols] = ds
                     if zk < zq - 1:
                         far = far + ds.astype(F32)
                     else:
-                        near[table_kind(zq, zk, x, kx)] += ds.astype(F32)
-            near[3] += far
-            width = (zq + 1) * 512
+                        near[h, table_kind(zq, zk, x, kx)] += ds.astype(F32)
+            if zq > 1:
+                near[h, 3] += far
             o = (dot(ds_s[h, rows, :width], kv[:width, :GW], NN) * 0.125).astype(BF)
 
             @pl.when(h == 0)
@@ -693,9 +689,19 @@
             def _():
                 dq[rows, :] = jnp.where(head_cols, o, dq[rows, :])
 
+        loop(0, GH, head)
+
+    score_grads(3)
+    score_grads(2)
+    key_sums(ds_s, qm, 3, 1)
+    score_grads(1)
+    score_grads(0)
+    key_sums(ds_s, qm, 2, 0)
+
+    def bucket_sums(h):
         for dist in range(2):
             n = near_distance(dist)
-            held = near[1 + dist]
+            held = near[h, 1 + dist]
             bounds = [-(10**6)] + bucket_edges + [10**6]
             for b in range(BUCKETS):
                 low, high = bounds[b], bounds[b + 1]
@@ -710,10 +716,9 @@
                     tab[h, b : b + 1, :] = inside
                 else:
                     tab[h, b : b + 1, :] += inside
-        tab[h, BUCKETS - 1 :, :] += jnp.sum(near[3], axis=0, keepdims=True)
-
-    loop(0, GH, head)
-    key_sums(ds_s, qm, 2)
+        tab[h, BUCKETS - 1 :, :] += jnp.sum(near[h, 3], axis=0, keepdims=True)
+
+    loop(0, GH, bucket_sums)
 
     wait_bytes(branch_all, recv.at[1])
     att_f[0:GW, :] = dot(attn_part[...], branch_all[...], TN)
@@ -724,6 +729,18 @@
     s_own[...] = small[...]
     for h in range(GH):
         s_own[2:3, BUCKETS * h : BUCKETS * (h + 1)] = jnp.sum(tab[h].T, axis=0, keepdims=True)
+
+    wait_bytes(a_sib, core_recv.at[1])
+
+    def att_blocks(i):
+        there = peer(i)
+        j = there[1] * 4 + there[2]
+        a_tot[j] = (a_blk[j, c].astype(F32) + a_sib[j].astype(F32)).astype(BF)
+        push(a_tot.at[j], a_in.at[p16], send.at[6], recv.at[4], there)
+
+    loop(1, 16, att_blocks)
+    a_tot[p16] = (a_blk[p16, c].astype(F32) + a_sib[p16].astype(F32)).astype(BF)
+    keep(a_tot.at[p16], a_in.at[p16], recv.at[4])
 
     wait_bytes(parts, recv.at[2])
     d_qkv[:, :GW] = dq[...]
@@ -735,7 +752,8 @@
             for k in range(1, 4):
                 total = total + parts[k, m, :, side : side + GW].astype(F32)
             d_qkv[rows, at : at + GW] = total.astype(BF)
-    n_part[...] = dot(d_qkv[...], weight[...], NT).astype(BF)
+    d_normed = dot(d_qkv[...], weight[...], NT)
+    n_part[...] = d_normed.astype(BF)
     for k in range(1, 4):
         there = (z + k) % 4
         push(
@@ -743,21 +761,17 @@
             send.at[3], recv.at[3], (there, x, y, c),
         )
     keep(n_part.at[z_rows], normed_in.at[z], recv.at[3])
+    along = jnp.sum(d_normed * normed[...].astype(F32), axis=0, keepdims=True)
+    s_own[0:1, :] = along / gain[...]
+    push(s_own, s_sib, send.at[8], core_recv.at[2], sib)
     total = dot(normed[...], d_qkv[...], TN)
     for j in range(32):
         q_blk[j // 2, j % 2] = total[24 * j : 24 * j + 24].astype(BF)
     push(q_blk.at[:, 1 - c], q_sib, send.at[5], core_recv.at[0], sib)
-    wait_bytes(a_sib, core_recv.at[1])
-
-    def att_blocks(i):
-        there = peer(i)
-        j = there[1] * 4 + there[2]
-        a_tot[j] = (a_blk[j, c].astype(F32) + a_sib[j].astype(F32)).astype(BF)
-        push(a_tot.at[j], a_in.at[p16], send.at[6], recv.at[4], there)
-
-    loop(1, 16, att_blocks)
-    a_tot[p16] = (a_blk[p16, c].astype(F32) + a_sib[p16].astype(F32)).astype(BF)
-    keep(a_tot.at[p16], a_in.at[p16], recv.at[4])
+    wait_bytes(s_sib, core_recv.at[2])
+    s_tot[...] = s_own[...] + s_sib[...]
+    loop(1, 16, lambda i: push(s_tot, s_in.at[p16], send.at[9], recv.at[6], peer(i)))
+    keep(s_tot, s_in.at[p16], recv.at[6])
     wait_bytes(q_sib, core_recv.at[0])
 
     def qkv_blocks(i):
@@ -770,23 +784,14 @@
     q_tot[p16] = (q_blk[p16, c].astype(F32) + q_sib[p16].astype(F32)).astype(BF)
     keep(q_tot.at[p16], q_in.at[p16], recv.at[5])
 
-    wait_bytes(normed_in, recv.at[3])
-    d_normed = normed_in[0].astype(F32)
-    for k in range(1, 4):
-        d_normed = d_normed + normed_in[k].astype(F32)
-    v = tok[...].astype(F32)
-    r = lax.rsqrt(jnp.mean(v * v, axis=1, keepdims=True) + norm_eps)
-    unit = v * r
-    s_own[0:1, :] = jnp.sum(d_normed * unit, axis=0, keepdims=True)
-    push(s_own, s_sib, send.at[8], core_recv.at[2], sib)
-    d_unit = d_normed * gain[...]
-    d_in = r * (d_unit - unit * jnp.mean(d_unit * unit, axis=1, keepdims=True))
-    input_grad[...] = (d_middle[...] + d_in).astype(BF)
-    wait_bytes(s_sib, core_recv.at[2])
-    s_tot[...] = s_own[...] + s_sib[...]
-    loop(1, 16, lambda i: push(s_tot, s_in.at[p16], send.at[9], recv.at[6], peer(i)))
-    keep(s_tot, s_in.at[p16], recv.at[6])
-
+    wait_bytes(s_in, recv.at[6])
+    s_total = s_in[0]
+    for k in range(1, 16):
+        s_total = s_total + s_in[k]
+    s_sum[...] = s_total
+    for k in range(1, 4):
+        push(s_sum, small_out.at[z], send.at[11], recv.at[8], ((z + k) % 4, x, y, c))
+    keep(s_sum, small_out.at[z], recv.at[8])
     wait_bytes(q_in, recv.at[5])
     q_total = q_in[0].astype(F32)
     for k in range(1, 16):
@@ -813,14 +818,17 @@
         a_total = a_total + a_in[k].astype(F32)
     att_sum[...] = a_total
     keep(att_sum, att_out, own.at[1])
-    wait_bytes(s_in, recv.at[6])
-    s_total = s_in[0]
-    for k in range(1, 16):
-        s_total = s_total + s_in[k]
-    s_sum[...] = s_total
-    for k in range(1, 4):
-        push(s_sum, small_out.at[z], send.at[11], recv.at[8], ((z + k) % 4, x, y, c))
-    keep(s_sum, small_out.at[z], recv.at[8])
+    wait_bytes(normed_in, recv.at[3])
+    d_normed = normed_in[0].astype(F32)
+    for k in range(1, 4):
+        d_normed = d_normed + normed_in[k].astype(F32)
+    v = tok[...].astype(F32)
+    r = lax.rsqrt(jnp.mean(v * v, axis=1, keepdims=True) + norm_eps)
+    unit = v * r
+    d_unit = d_normed * gain[...]
+    d_in = r * (d_unit - unit * jnp.mean(d_unit * unit, axis=1, keepdims=True))
+    input_grad[...] = (d_middle[...] + d_in).astype(BF)
+
     wait_bytes(att_sum, own.at[1])
     wait_bytes(qkv_out, recv.at[7])
     wait_bytes(small_out, recv.at[8])
@@ -859,7 +867,7 @@
         out_specs=(VMEM, ANY, ANY, ANY),
         scratch_shapes=[
             vm(probs, BF), vm((2048, GW), BF), vm((4, TOK, GW), BF), vm((GH, 512, GW), BF),
-            vm((GH, 512, GW), BF), vm((512, 2048), F32), vm(probs, BF), vm((4, TOK, TOK), F32),
+            vm((GH, 512, GW), BF), vm((TOK, 2048), F32), vm(probs, BF), vm((GH, 4, TOK, TOK), F32),
             vm((4, 4, TOK, 2 * GW), BF), vm((4, 4, TOK, 2 * GW), BF), vm((512, D), BF),
             vm((512, GW), BF), vm((GH, BUCKETS, TOK), F32),
             vm((512, 3 * GW), BF), vm((512, D), BF), vm((4, TOK, D), BF), vm((GW + 8, D), F32),

time: 221 us -> 223 us (level)
    pallas_call x1, Pallas kernels: 71.2 us -> 75.6 us  [attn_forward(): pl.pallas_call(attn_forward_kernel, out_shape=(jax.ShapeDtypeStruct((4, T...]
    pallas_call x1, Pallas kernels: 58.7 us -> 55.8 us  [attn_backward(): pl.pallas_call(attn_backward_kernel, out_shape=(jax.ShapeDtypeStruct((TOK...]
where the time goes in v7:
time: 223 us; the launch traced here: 222 us
  Pallas kernels  188 us (84%)
  local copies, waits for them, and re-layouts  21.7 us (10%)
  matrix products  7.05 us (3%)
  other arithmetic  3.59 us (2%)
    pallas_call x1, Pallas kernels, attn_forward(): pl.pallas_call(attn_forward_kernel, out_shape=(jax.ShapeDtypeStruct((4, T...  75.6 us
    pallas_call x1, Pallas kernels, run_experts(): pl.pallas_call(experts_kernel, out_shape=(jax.ShapeDtypeStruct((1024, D),...  57 us
    pallas_call x1, Pallas kernels, attn_backward(): pl.pallas_call(attn_backward_kernel, out_shape=(jax.ShapeDtypeStruct((TOK...  55.8 us
    unnamed x25, local copies, waits for them, and re-layouts  12.7 us
    dot_general x7, matrix products, dot(): return lax.dot_general(a, b, dims, preferred_element_type=F32)  7.05 us

profile of v7, /device:TPU:1, one launch (start us, length us, event | category | flops | bytes accessed | tf_op | source)
XLA Modules:
  0.0 221.7 jit_solution(11804174400512824054)
XLA Ops:
  0.7 0.7 copy-done
  1.3 0.1 copy.42
  1.5 0.9 reshape.94
  2.4 0.1 reshape.95
  2.5 0.8 dynamic_update_slice.9
  3.4 0.7 convert_bitcast_fusion
  4.0 0.2 dynamic_update_slice.10
  4.2 0.8 dynamic_update_slice.11
  5.1 0.3 concatenate.25
  5.4 0.3 concatenate.26
  5.7 0.7 concatenate.27.wa
  6.4 0.8 slice_bitcast_fusion.3
  7.2 1.1 multiply_convert_fusion.2
  8.3 0.2 fusion.13
  8.5 0.1 slice_reduce_fusion
  8.6 0.1 fusion.16
  8.8 0.1 iota_compare_fusion
  8.9 0.1 iota_compare_fusion.1
  9.1 2.0 convolution_convert_fusion.1.d_eo
  11.0 75.6 %attn_forward.1 = (bf16[4,128,192]{2,1,0:T(8,128)(2,1)S(1)}, bf16[512,192]{1,0:T(8,128)(2,1)S(1)}, bf16[3,512,2048]{2,1,0:T(8,128)(2,1)}, bf16[2048,384]{1,0:T(8...) custom-call(f32[32,3]{1,0:T(8,128)S(1)} %convert_element_type.52.tab, ...), custom_call_target="tpu_custom_call" | custom-call | tf_op jit(solution)/shard_map/attn_forward/pallas_call | solution.py:557
  86.6 1.1 copy-done.2
  87.8 1.0 copy-done.3
  88.8 0.9 copy-done.4
  89.6 0.2 copy.37
  89.8 1.2 reshape.99
  91.0 1.7 multiply_reduce_fusion.2
  92.8 0.1 multiply_convert_fusion
  92.9 0.8 convolution_convert_fusion.x16
  93.7 57.0 %experts.1 = (bf16[1024,768]{1,0:T(8,128)(2,1)S(1)}, bf16[1024,768]{1,0:T(8,128)(2,1)S(1)}, f32[768,1536]{1,0:T(8,128)}, f32[1536,768]{1,0:T(8,128)}) custom-call(bf16[1024,768]{1,0:T(8,128)(2,1)S(1)} %convolution_convert_fusion.x16, bf16[1024,768]{1,0:T(8,128)(2,1)} %get-tuple-element.31.d_rows, bf16[768,1536]{1,0:T(8,128)(2,1)} %bitcast.83, ...), custom_call_target="tpu_custom_call" | custom-call | tf_op jit(solution)/shard_map/experts/pallas_call | solution.py:304
  150.8 0.6 fusion.27
  151.4 0.2 multiply_reduce_fusion
  151.5 0.1 copy-done.6
  151.7 1.2 fusion
  153.0 0.9 fusion.29
  153.9 0.4 copy-done.5
  154.3 0.5 convolution_convert_fusion.2
  154.8 0.2 copy.38
  155.0 0.2 copy.39
  155.3 55.8 %attn_backward.1 = (bf16[128,768]{1,0:T(8,128)(2,1)S(1)}, f32[4,8,576]{2,1,0:T(8,128)S(1)}, f32[8,768]{1,0:T(8,128)S(1)}, f32[4,8,768]{2,1,0:T(8,128)S(1)}) custom-call(bf16[3,512,2048]{2,1,0:T(8,128)(2,1)} %get-tuple-element.33.p, bf16[512,192]{1,0:T(8,128)(2,1)S(1)} %get-tuple-element.34.q, bf16[2048,384]{1,0:T(8,128)(2,1)} %copy-done.2, ...), custom_call_target="tpu_custom_call" | custom-call | tf_op jit(solution)/shard_map/attn_backward/pallas_call | solution.py:858
  211.1 0.1 constant_dynamic-slice_fusion
  211.2 0.5 slice_bitcast_fusion
  211.8 0.1 reshape.104
  211.9 0.7 reshape.105
  212.7 0.7 reshape_squeeze.3
  213.3 0.7 copy.69
  214.0 0.6 copy.70
  214.6 4.9 %copy.71 = f32[1,768,1536]{2,1,0:T(8,128)} copy(f32[1,768,1536]{2,1,0:T(8,128)} %bitcast.82) | data formatting | bytes 9437184
  219.6 2.2 copy.72
  (45 shorter events, 0.5 us)
Async XLA Ops:
  0.6 0.7 copy-start
  0.7 7.6 %copy-start.7 = (s32[1,128,2]{1,2,0:T(2,128)S(1)}, s32[1,128,2]{1,2,0:T(2,128)}, u32[]{:S(2)}) copy-start(s32[1,128,2]{1,2,0:T(2,128)} %param.20) | copy-start | bytes 3076
  8.2 2.8 %copy-start.1 = (bf16[1,128,768]{2,1,0:T(8,128)(2,1)S(1)}, bf16[1,128,768]{2,1,0:T(8,128)(2,1)}, u32[]{:S(2)}) copy-start(bf16[1,128,768]{2,1,0:T(8,128)(2,1)} %param.12) | copy-start | bytes 589828
  86.6 1.1 copy-start.2
  87.8 1.0 copy-start.3
  88.8 0.9 copy-start.4
  150.8 0.9 copy-start.6
  153.0 1.3 copy-start.5
  213.3 6.2 %slice-start = ((s8[4718592]{0:T(1024)(128)(4,1)}), s8[4194304]{0:T(1024)(128)(4,1)S(1)}, s32[]{:S(2)}) async-start(s8[4718592]{0:T(1024)(128)(4,1)} %bitcast.79), calls=%async_computation | async-start | bytes 8388608
  214.6 4.9 %slice-start.1 = ((s8[4718592]{0:T(1024)(128)(4,1)}), s8[524288]{0:T(1024)(128)(4,1)S(1)}, s32[]{:S(2)}) async-start(s8[4718592]{0:T(1024)(128)(4,1)} %bitcast.79), calls=%async_computation.1 | async-start | bytes 1048576

commit v8 on v7

--- a/solution.py
+++ b/solution.py
@@ -156,8 +156,9 @@
 
 
 def experts_kernel(
-    x16, d_rows, w_in, w_out, home_in, home_out, g_in, g_out,
-    xs, xo, rows, dv, w1, w2, dh, hidden, dact, in_h, out_h, in_o, out_o, stage_out, stage_in,
+    attn, w_proj, tok, gains, picks, d_rows, w_in, w_out,
+    home_in, home_out, g_in, g_out, middle,
+    x16, xo, rows, dv, w1, w2, dh, hidden, dact, in_h, out_h, in_o, out_o, stage_out, stage_in,
     send, recv, core_recv, own, staged,
 ):
     z, x, y, c = place()
@@ -166,19 +167,26 @@
     at_theirs = pl.multiple_of((1 - c) * 512, 512)
     mine, theirs = pl.ds(at_mine, 512), pl.ds(at_theirs, 512)
     me = block_of(z, x, y)
-    keep(x16.at[mine], xs, own.at[0])
     keep(d_rows, dv, own.at[1])
     keep(w_out, w2, own.at[2])
     keep(w_in, w1, own.at[3])
     expected = greet_chips(z, x, y, c)
+    total = tok[...].astype(F32)
+    for k in range(GROUPS):
+        total = total + dot(attn[k], w_proj[GW * k : GW * (k + 1), :], NN)
+    middle[...] = total
+    moe_in = scale_rows(total, gains[1:2, :]).astype(BF)
+    for n in range(0, 1024, WIDE):
+        x16[n : n + WIDE, :] = (
+            dot(picks[:TOK, n : n + WIDE], moe_in, TN) + dot(picks[TOK:, n : n + WIDE], moe_in, TN)
+        ).astype(BF)
     arrive(expected)
     push(x16.at[theirs], xo, send.at[0], core_recv.at[0], sib)
-    wait_bytes(xs, own.at[0])
     wait_bytes(xo, core_recv.at[0])
-    xs[...] = xs[...] + xo[...]
+    xo[...] = xo[...] + x16[mine, :]
     to_chips(
         z, x, y, c,
-        lambda there: xs.at[pl.ds(pl.multiple_of(block_of(*there[:3]) - c * 512, 16), 16)],
+        lambda there: xo.at[pl.ds(pl.multiple_of(block_of(*there[:3]) - c * 512, 16), 16)],
         rows.at[pl.ds(me, 16)], send.at[1], recv.at[0],
     )
     wait_bytes(dv, own.at[1])
@@ -297,7 +305,7 @@
     wait_bytes(home_out.at[mine], send.at[8])
 
 
-def run_experts(x16, d_rows, w_in, w_out):
+def run_experts(*args):
     whole_rows = pltpu.VMEM((1024, D), BF)
     half_rows = pltpu.VMEM((512, D), BF)
     hid = pltpu.VMEM((1024, FH), BF)
@@ -308,11 +316,12 @@
             jax.ShapeDtypeStruct((1024, D), BF),
             jax.ShapeDtypeStruct((D, FH), F32),
             jax.ShapeDtypeStruct((FH, D), F32),
+            jax.ShapeDtypeStruct((TOK, D), F32),
         ),
-        in_specs=[ANY] * 4,
-        out_specs=(ANY,) * 4,
+        in_specs=[pl.BlockSpec(memory_space=pltpu.VMEM)] * 5 + [ANY] * 3,
+        out_specs=(ANY,) * 4 + (pl.BlockSpec(memory_space=pltpu.VMEM),),
         scratch_shapes=[
-            half_rows, half_rows, whole_rows, whole_rows,
+            whole_rows, half_rows, whole_rows, whole_rows,
             pltpu.VMEM((D, FH), BF), pltpu.VMEM((FH, D), BF), pltpu.VMEM((1024, FH), F32),
             hid, hid, whole_rows, whole_rows, half_rows, half_rows,
             pltpu.VMEM((2, WIDE, D), F32), pltpu.VMEM((2, WIDE, FH), F32),
@@ -322,7 +331,7 @@
             collective_id=1, has_side_effects=True, vmem_limit_bytes=48 * 2**20
         ),
         name="experts",
-    )(x16, d_rows, w_in, w_out)
+    )(*args)
 
 
 def device_of(d):
@@ -387,13 +396,6 @@
     )
     for k in range(1, 4):
         push(wa, wa_all.at[z, x, y, c], send.at[4], recv.at[2], ((z + k) % 4, x, y, c))
-    wait_bytes(xo, core_recv.at[1])
-    xo[...] = xo[...] + d_eo[mine, :]
-    to_chips(
-        z, x, y, c,
-        lambda there: xo.at[pl.ds(pl.multiple_of(block_of(*there[:3]) - c * 512, 16), 16)],
-        d_rows.at[pl.ds(me, 16)], send.at[9], recv.at[5],
-    )
 
     row = lax.broadcasted_iota(jnp.int32, (1, 1024), 1)
     r, half, at = row & 15, row >> 9, (row >> 4) & 31
@@ -420,6 +422,8 @@
         bias[h, 3] = jnp.full((TOK, TOK), tab[BUCKETS - 1, h], F32)
 
     loop(0, GH, tables)
+    wait_bytes(xo, core_recv.at[1])
+    xo[...] = xo[...] + d_eo[mine, :]
     wait_bytes(w_s.at[mine], recv.at[1])
     push(w_s.at[mine], w_s.at[mine], send.at[5], core_recv.at[2], sib)
     wait_bytes(wa_all.at[z, x, y, c], own.at[0])
@@ -476,8 +480,11 @@
             for h in range(GH):
                 s_s[h, b * TOK :, cols] = dot(qm[h, b * TOK :, :], kv_s[cols, :GW], NT)
     keep(kv_s, kv_out, own.at[1])
-    wait_bytes(d_rows.at[mine], recv.at[5])
-    push(d_rows.at[mine], d_rows.at[mine], send.at[12], core_recv.at[4], sib)
+    to_chips(
+        z, x, y, c,
+        lambda there: xo.at[pl.ds(pl.multiple_of(block_of(*there[:3]) - c * 512, 16), 16)],
+        d_rows.at[pl.ds(me, 16)], send.at[9], recv.at[5],
+    )
     wait_bytes(wa_all.at[:, :, pl.ds(0, 3), c], recv.at[4])
     push(wa_all.at[:, :, :, c], wa_all.at[:, :, :, c], send.at[10], core_recv.at[3], sib)
 
@@ -531,6 +538,8 @@
         )
     keep(part.at[pl.ds(pl.multiple_of(z * TOK, TOK), TOK)], attn_all.at[z], recv.at[6])
     keep(p_s, p_out, own.at[2])
+    wait_bytes(d_rows.at[mine], recv.at[5])
+    push(d_rows.at[mine], d_rows.at[mine], send.at[12], core_recv.at[4], sib)
     wait_bytes(attn_all, recv.at[6])
     wait_bytes(wa_all.at[:, :, :, 1 - c], core_recv.at[3])
     wait_bytes(d_rows.at[theirs], core_recv.at[4])
@@ -587,11 +596,11 @@
 
 
 def attn_backward_kernel(
-    p, q, kv, d_attn, branch, weight, normed, attn_part, small, tok, gain, d_middle,
+    p, q, kv, home, picks, middle, gains, cotangent, w_proj, weight, normed, attn_part, tok,
     input_grad, qkv_out, att_out, small_out,
     p_s, v_s, do_s, dm, qm, dp_s, ds_s, near, messages, parts, branch_all, dq, tab,
     d_qkv, n_part, normed_in, att_f, q_blk, q_sib, q_tot, q_in, a_blk, a_sib, a_tot, a_in,
-    s_own, s_sib, s_tot, s_in, qkv_sum, att_sum, s_sum, send, recv, core_recv, own,
+    s_own, s_sib, s_tot, s_in, qkv_sum, att_sum, s_sum, d_attn, branch, d_middle, send, recv, core_recv, own,
 ):
     z, x, y, c = place()
     sib = (z, x, y, 1 - c)
@@ -619,6 +628,19 @@
     for h in range(GH):
         head_cols = lax.broadcasted_iota(jnp.int32, (1, GW), 1) // HD == h
         qm[h] = jnp.where(head_cols, q[...] * 0.125, 0.0).astype(BF)
+    d_moe = dot(picks[:TOK, :], home[...], NN) + dot(picks[TOK:, :], home[...], NN)
+    mid = middle[...]
+    mid_r = lax.rsqrt(jnp.mean(mid * mid, axis=1, keepdims=True) + norm_eps)
+    mid_unit = mid * mid_r
+    s_own[...] = jnp.zeros_like(s_own)
+    s_own[1:2, :] = jnp.sum(d_moe * mid_unit, axis=0, keepdims=True)
+    d_mid_unit = d_moe * gains[1:2, :]
+    d_mid = mid_r * (d_mid_unit - mid_unit * jnp.mean(d_mid_unit * mid_unit, axis=1, keepdims=True))
+    d_mid = cotangent[...].astype(F32) + d_mid
+    d_middle[...] = d_mid
+    branch[...] = d_mid.astype(BF)
+    for k in range(GROUPS):
+        d_attn[k] = dot(branch[...], w_proj[GW * k : GW * (k + 1), :], NT).astype(BF)
     arrive(15 + 3 + 1 + 4 - jnp.where(source == p32, 1, 0))
     for k in range(1, 4):
         there = (z + k) % 4
@@ -726,7 +748,6 @@
     for j in range(32):
         a_blk[j // 2, j % 2] = att_f[6 * j : 6 * j + 8, :].astype(BF)
     push(a_blk.at[:, 1 - c], a_sib, send.at[4], core_recv.at[1], sib)
-    s_own[...] = small[...]
     for h in range(GH):
         s_own[2:3, BUCKETS * h : BUCKETS * (h + 1)] = jnp.sum(tab[h].T, axis=0, keepdims=True)
 
@@ -762,7 +783,7 @@
         )
     keep(n_part.at[z_rows], normed_in.at[z], recv.at[3])
     along = jnp.sum(d_normed * normed[...].astype(F32), axis=0, keepdims=True)
-    s_own[0:1, :] = along / gain[...]
+    s_own[0:1, :] = along / gains[0:1, :]
     push(s_own, s_sib, send.at[8], core_recv.at[2], sib)
     total = dot(normed[...], d_qkv[...], TN)
     for j in range(32):
@@ -825,7 +846,7 @@
     v = tok[...].astype(F32)
     r = lax.rsqrt(jnp.mean(v * v, axis=1, keepdims=True) + norm_eps)
     unit = v * r
-    d_unit = d_normed * gain[...]
+    d_unit = d_normed * gains[0:1, :]
     d_in = r * (d_unit - unit * jnp.mean(d_unit * unit, axis=1, keepdims=True))
     input_grad[...] = (d_middle[...] + d_in).astype(BF)
 
@@ -876,10 +897,11 @@
             vm((16, 2, 8, D), BF), vm((16, 8, D), BF), vm((16, 8, D), BF), vm((16, 8, D), BF),
             vm((8, D), F32), vm((8, D), F32), vm((8, D), F32), vm((16, 8, D), F32),
             vm((4, 8, 3 * GW), F32), vm((8, D), F32), vm((8, D), F32),
+            vm((4, TOK, GW), BF), vm((TOK, D), BF), vm((TOK, D), F32),
             DMA((12,)), DMA((9,)), DMA((3,)), DMA((2,)),
         ],
         compiler_params=pltpu.CompilerParams(
-            collective_id=3, has_side_effects=True, vmem_limit_bytes=52 * 2**20
+            collective_id=3, has_side_effects=True, vmem_limit_bytes=54 * 2**20
         ),
         name="attn_backward",
     )(p, *rest)
@@ -948,32 +970,13 @@
     (
         attn, attn_part, probs, kv_all, out_weights, d_eo_all, normed, weight, queries, gain_rows,
     ) = attn_forward(table, own_tokens, message, out_slab, d_eo)
-    gain_one, gain_two = gain_rows[0], gain_rows[1]
-    attn = attn.transpose(1, 0, 2).reshape(TOK, D)
     attention_weight = out_weights[:, :, :, :, :6, :].reshape(D, D)
-
-    inputs = own_tokens.astype(F32)
-    middle = inputs + dot(attn, attention_weight, NN)
-    moe_float, norm_two_back = jax.vjp(scale_rows, middle, gain_two)
-    moe_in = moe_float.astype(BF)
-    send_rows = dot(picks, jnp.concatenate([moe_in, moe_in], axis=0), TN).astype(BF)
-    home, expert_out, expert_in_grad, expert_out_grad = run_experts(
-        send_rows, d_eo_all, w_in[0], w_out[0]
-    )
-    home_picked = dot(picks, home, NN)
-    moe_in_grad = home_picked[:TOK] + home_picked[TOK:]
-    middle_part, gain_two_grad = norm_two_back(moe_in_grad)
-    middle_grad = grad_out + middle_part
-    branch = middle_grad.astype(BF)
-    d_attn = dot(branch, attention_weight, NT).astype(BF)
-    d_attn = d_attn.reshape(TOK, GROUPS, GW).transpose(1, 0, 2)
-
-    small = jnp.concatenate(
-        [jnp.zeros((1, D), F32), gain_two_grad.reshape(1, D), jnp.zeros((6, D), F32)]
+    home, expert_out, expert_in_grad, expert_out_grad, middle = run_experts(
+        attn, attention_weight, own_tokens, gain_rows, picks, d_eo_all, w_in[0], w_out[0]
     )
     input_grad, qkv_sum, att_sum, small_sum = attn_backward(
-        probs, queries, kv_all, d_attn, branch, weight, normed, attn_part, small, own_tokens,
-        gain_one.reshape(1, D), middle_grad,
+        probs, queries, kv_all, home, picks, middle, gain_rows, grad_bf, attention_weight, weight,
+        normed, attn_part, own_tokens,
     )
 
     picked = dot(picks, expert_out, NN).reshape(2, TOK, D)

time: 223 us -> 224 us (level)
  local copies, waits for them, and re-layouts: 21.7 us -> 26.1 us
  matrix products: 7.05 us -> 3.39 us
    pallas_call x1, Pallas kernels: 75.6 us -> 71.2 us  [attn_forward(): pl.pallas_call(attn_forward_kernel, out_shape=(jax.ShapeDtypeStruct((4, T...]
    unnamed x25 -> x57, local copies, waits for them, and re-layouts: 12.7 us -> 17.1 us
    dot_general x7 -> x3, matrix products: 7.05 us -> 3.39 us  [dot(): return lax.dot_general(a, b, dims, preferred_element_type=F32)]
    pallas_call x1, Pallas kernels: 55.8 us -> 58.2 us  [attn_backward(): pl.pallas_call(attn_backward_kernel, out_shape=(jax.ShapeDtypeStruct((TOK...]
where the time goes in v8:
time: 224 us; the launch traced here: 222 us
  Pallas kernels  186 us (83%)
  local copies, waits for them, and re-layouts  26.1 us (12%)
  other arithmetic  4.64 us (2%)
  matrix products  3.39 us (2%)
    pallas_call x1, Pallas kernels, attn_forward(): pl.pallas_call(attn_forward_kernel, out_shape=(jax.ShapeDtypeStruct((4, T...  71.2 us
    pallas_call x1, Pallas kernels, attn_backward(): pl.pallas_call(attn_backward_kernel, out_shape=(jax.ShapeDtypeStruct((TOK...  58.2 us
    pallas_call x1, Pallas kernels, run_experts(): pl.pallas_call(experts_kernel, out_shape=(jax.ShapeDtypeStruct((1024, D),...  57.1 us
    unnamed x57, local copies, waits for them, and re-layouts  17.1 us

profile of v8, /device:TPU:1, one launch (start us, length us, event | category | flops | bytes accessed | tf_op | source)
XLA Modules:
  0.0 221.7 jit_solution(4143776129919866215)
XLA Ops:
  0.7 0.6 copy-done
  1.3 0.7 convert_bitcast_fusion
  2.0 0.8 slice_bitcast_fusion.3
  2.8 0.8 slice_bitcast_fusion.7
  3.5 0.8 dynamic_update_slice.9
  4.4 0.2 dynamic_update_slice.10
  4.5 0.8 dynamic_update_slice.11
  5.4 0.1 copy.36
  5.5 0.7 concatenate.21.wa
  6.2 0.9 reshape.66
  7.2 0.1 reshape.67
  7.3 0.2 fusion.9
  7.5 0.1 slice_reduce_fusion
  7.6 0.1 fusion.12
  7.7 0.7 fusion.16
  8.5 0.3 concatenate.20
  8.7 0.3 concatenate.19
  9.0 0.1 iota_compare_fusion.1
  9.2 0.1 iota_compare_fusion
  9.4 0.8 bitcast_convert_fusion
  10.2 0.1 multiply_convert_fusion.1
  10.3 0.1 fusion.22.picks
  10.4 1.9 convolution_convert_fusion.d_eo
  12.4 71.2 %attn_forward.1 = (bf16[4,128,192]{2,1,0:T(8,128)(2,1)S(1)}, bf16[512,192]{1,0:T(8,128)(2,1)S(1)}, bf16[3,512,2048]{2,1,0:T(8,128)(2,1)}, bf16[2048,384]{1,0:T(8...) custom-call(f32[32,3]{1,0:T(8,128)S(1)} %convert_element_type.35.tab, ...), custom_call_target="tpu_custom_call" | custom-call | tf_op jit(solution)/shard_map/attn_forward/pallas_call | solution.py:566
  83.6 1.1 copy-done.4
  84.7 1.0 copy-done.8
  85.7 0.9 copy-done.9
  86.6 0.7 copy-done.10
  87.3 0.7 copy-done.12
  88.0 0.7 copy-done.13
  88.7 0.4 reshape.71.w_proj
  89.1 0.9 copy-done.11
  90.1 57.1 %experts.1 = (bf16[1024,768]{1,0:T(8,128)(2,1)S(1)}, bf16[1024,768]{1,0:T(8,128)(2,1)S(1)}, f32[768,1536]{1,0:T(8,128)}, f32[1536,768]{1,0:T(8,128)}, f32[128,768]{1,0:T(8,128)S(1)}) custom-call(bf16[4,128,192]{2,1,0:T(8,128)(2,1)S(1)} %copy-done.11, bf16[768,768]{1,0:T(8,128)(2,1)S(1)} %reshape.71.w_proj, bf16[128,768]{1,0:T(8,128)(2,1)S(1)} %bitcast.59, ...), custom_call_target="tpu_custom_call" | custom-call | tf_op jit(solution)/shard_map/experts/pallas_call | solution.py:312
  147.2 1.1 copy-done.5
  148.3 0.8 copy-done.6
  149.1 58.2 %attn_backward.1 = (bf16[128,768]{1,0:T(8,128)(2,1)}, f32[4,8,576]{2,1,0:T(8,128)}, f32[8,768]{1,0:T(8,128)}, f32[4,8,768]{2,1,0:T(8,128)}) custom-call(bf16[3,512,2048]{2,1,0:T(8,128)(2,1)} %get-tuple-element.35.p, bf16[512,192]{1,0:T(8,128)(2,1)} %copy-done.13, bf16[2048,384]{1,0:T(8,128)(2,1)} %copy-done.4, bf16[1024,768]{1,0:T(8,128)(2,1)} %copy-done.5, ...), custom_call_target="tpu_custom_call" | custom-call | tf_op jit(solution)/shard_map/attn_backward/pallas_call | solution.py:879
  207.4 1.2 fusion
  208.6 0.8 fusion.7
  209.5 0.7 slice_reduce_fusion.2
  210.2 0.9 slice_reduce_fusion.1
  211.2 0.5 slice_bitcast_fusion
  211.7 0.7 reshape_squeeze.3
  212.4 0.1 reshape.74
  212.5 0.7 reshape.75
  213.3 0.7 copy.61
  213.9 0.6 copy.62
  214.6 4.9 %copy.63 = f32[1,768,1536]{2,1,0:T(8,128)} copy(f32[1,768,1536]{2,1,0:T(8,128)} %bitcast.64) | data formatting | bytes 9437184
  219.5 2.2 copy.64
  (61 shorter events, 0.4 us)
Async XLA Ops:
  0.6 0.7 copy-start
  0.7 8.7 %copy-start.15 = (bf16[1,128,768]{2,1,0:T(8,128)(2,1)S(1)}, bf16[1,128,768]{2,1,0:T(8,128)(2,1)}, u32[]{:S(2)}) copy-start(bf16[1,128,768]{2,1,0:T(8,128)(2,1)} %param.23) | copy-start | bytes 589828
  9.2 1.2 copy-start.17
  9.4 1.1 copy-start.19
  10.3 2.1 copy-start.3
  10.4 78.7 %copy-start.2 = (bf16[256,1024]{1,0:T(8,128)(2,1)}, bf16[256,1024]{1,0:T(8,128)(2,1)S(1)}, u32[]{:S(2)}) copy-start(bf16[256,1024]{1,0:T(8,128)(2,1)S(1)} %fusion.22.picks) | copy-start | bytes 1572868
  83.6 1.1 copy-start.4
  84.7 1.0 copy-start.8
  85.7 0.9 copy-start.9
  86.6 0.7 copy-start.10
  87.3 0.7 copy-start.12
  88.0 0.7 copy-start.13
  88.7 58.5 %copy-start.14 = (f32[8,768]{1,0:T(8,128)}, f32[8,768]{1,0:T(8,128)S(1)}, u32[]{:S(2)}) copy-start(f32[8,768]{1,0:T(8,128)S(1)} %get-tuple-element.31.gains) | copy-start | bytes 73732
  89.1 1.0 copy-start.11
  90.1 57.1 %copy-start.1 = (bf16[768,768]{1,0:T(8,128)(2,1)}, bf16[768,768]{1,0:T(8,128)(2,1)S(1)}, u32[]{:S(2)}) copy-start(bf16[768,768]{1,0:T(8,128)(2,1)S(1)} %reshape.71.w_proj) | copy-start | bytes 3538948
  147.2 1.1 copy-start.5
  148.3 0.8 copy-start.6
  149.1 58.2 %copy-start.16 = (f32[128,768]{1,0:T(8,128)S(1)}, f32[128,768]{1,0:T(8,128)}, u32[]{:S(2)}) copy-start(f32[128,768]{1,0:T(8,128)} %bitcast_convert_fusion) | copy-start | bytes 1179652
  149.1 58.2 %copy-start.18 = (pred[128,1024]{1,0:T(32,128)(4,1)S(1)}, pred[128,1024]{1,0:T(32,128)(4,1)}, u32[]{:S(2)}) copy-start(pred[128,1024]{1,0:T(32,128)(4,1)} %copy-done.17) | copy-start | bytes 393220
  149.1 58.2 %copy-start.20 = (pred[128,1024]{1,0:T(32,128)(4,1)S(1)}, pred[128,1024]{1,0:T(32,128)(4,1)}, u32[]{:S(2)}) copy-start(pred[128,1024]{1,0:T(32,128)(4,1)} %copy-done.19) | copy-start | bytes 393220
  207.3 1.3 copy-start.7
  207.3 2.1 copy-start.22
  208.6 4.7 %copy-start.21 = (bf16[128,768]{1,0:T(8,128)(2,1)S(1)}, bf16[128,768]{1,0:T(8,128)(2,1)}, u32[]{:S(2)}) copy-start(bf16[128,768]{1,0:T(8,128)(2,1)} %get-tuple-element.42) | copy-start | bytes 589828
  208.6 5.3 %copy-start.23 = (f32[8,768]{1,0:T(8,128)S(1)}, f32[8,768]{1,0:T(8,128)}, u32[]{:S(2)}) copy-start(f32[8,768]{1,0:T(8,128)} %get-tuple-element.45) | copy-start | bytes 73732
  213.3 6.2 %slice-start = ((s8[4718592]{0:T(1024)(128)(4,1)}), s8[4194304]{0:T(1024)(128)(4,1)S(1)}, s32[]{:S(2)}) async-start(s8[4718592]{0:T(1024)(128)(4,1)} %bitcast.61), calls=%async_computation | async-start | bytes 8388608
  214.6 4.9 %slice-start.1 = ((s8[4718592]{0:T(1024)(128)(4,1)}), s8[524288]{0:T(1024)(128)(4,1)S(1)}, s32[]{:S(2)}) async-start(s8[4718592]{0:T(1024)(128)(4,1)} %bitcast.61), calls=%async_computation.1 | async-start | bytes 1048576

commit v9 on v8

--- a/solution.py
+++ b/solution.py
@@ -156,10 +156,10 @@
 
 
 def experts_kernel(
-    attn, w_proj, tok, gains, picks, d_rows, w_in, w_out,
+    attn_at, w_proj_at, tok_at, gains_at, picks_at, d_rows, w_in, w_out,
     home_in, home_out, g_in, g_out, middle,
-    x16, xo, rows, dv, w1, w2, dh, hidden, dact, in_h, out_h, in_o, out_o, stage_out, stage_in,
-    send, recv, core_recv, own, staged,
+    attn, w_proj, tok, gains, picks, x16, xo, rows, dv, w1, w2, dh, hidden, dact, in_h, out_h, in_o, out_o, stage_out, stage_in,
+    send, recv, core_recv, own, staged, fetched,
 ):
     z, x, y, c = place()
     sib = (z, x, y, 1 - c)
@@ -167,10 +167,17 @@
     at_theirs = pl.multiple_of((1 - c) * 512, 512)
     mine, theirs = pl.ds(at_mine, 512), pl.ds(at_theirs, 512)
     me = block_of(z, x, y)
+    fetches = (
+        (attn_at, attn), (w_proj_at, w_proj), (tok_at, tok), (gains_at, gains), (picks_at, picks)
+    )
+    for k, (source, target) in enumerate(fetches):
+        keep(source, target, fetched.at[k])
     keep(d_rows, dv, own.at[1])
     keep(w_out, w2, own.at[2])
     keep(w_in, w1, own.at[3])
     expected = greet_chips(z, x, y, c)
+    for k, (_, target) in enumerate(fetches):
+        wait_bytes(target, fetched.at[k])
     total = tok[...].astype(F32)
     for k in range(GROUPS):
         total = total + dot(attn[k], w_proj[GW * k : GW * (k + 1), :], NN)
@@ -318,14 +325,16 @@
             jax.ShapeDtypeStruct((FH, D), F32),
             jax.ShapeDtypeStruct((TOK, D), F32),
         ),
-        in_specs=[pl.BlockSpec(memory_space=pltpu.VMEM)] * 5 + [ANY] * 3,
+        in_specs=[ANY] * 8,
         out_specs=(ANY,) * 4 + (pl.BlockSpec(memory_space=pltpu.VMEM),),
         scratch_shapes=[
+            pltpu.VMEM((4, TOK, GW), BF), pltpu.VMEM((D, D), BF), pltpu.VMEM((TOK, D), BF),
+            pltpu.VMEM((8, D), F32), pltpu.VMEM((2 * TOK, 1024), BF),
             whole_rows, half_rows, whole_rows, whole_rows,
             pltpu.VMEM((D, FH), BF), pltpu.VMEM((FH, D), BF), pltpu.VMEM((1024, FH), F32),
             hid, hid, whole_rows, whole_rows, half_rows, half_rows,
             pltpu.VMEM((2, WIDE, D), F32), pltpu.VMEM((2, WIDE, FH), F32),
-            DMA((9,)), DMA((3,)), DMA((6,)), DMA((4,)), DMA((4,)),
+            DMA((9,)), DMA((3,)), DMA((6,)), DMA((4,)), DMA((4,)), DMA((5,)),
         ],
         compiler_params=pltpu.CompilerParams(
             collective_id=1, has_side_effects=True, vmem_limit_bytes=48 * 2**20
@@ -366,9 +375,9 @@
 
 
 def attn_forward_kernel(
-    tab, tok, wmsg, wa, d_eo,
-    attn_all, part, p_out, kv_out, wa_all, d_rows, normed, weight, q, gains,
-    wm, wo, w_s, tok_s, select, picker, qd, kd,
+    tab, tok, w_qkv, notes, wa, routes, gates, cotangent,
+    attn_all, part, p_out, kv_out, wa_all, d_rows, normed, weight, q, gains, picks,
+    d_eo, wmsg, wm, wo, w_s, tok_s, select, picker, qd, kd,
     kv, kv_s, v_s, qm, bias, s_s, p_s, xo,
     send, recv, kv_recv, core_recv, own,
 ):
@@ -383,12 +392,25 @@
         signal(((z + k) % 4, x, y, c))
         signal((z, (x + k) % 4, y, c))
         signal((z, x, (y + k) % 4, c))
+    lift = lax.broadcasted_iota(jnp.int32, (16, 8), 0)
+    below = lax.broadcasted_iota(jnp.int32, (16, 8), 1)
+    lift = jnp.where((lift == 6 * c + below) & (below < 6), 1.0, 0.0)
+    lift = jnp.where(
+        (below >= 6) & (lax.broadcasted_iota(jnp.int32, (16, 8), 0) == 12 + c + 2 * (below - 6)),
+        1.0, lift,
+    ).astype(BF)
+    for g in range(GROUPS):
+        for t in range(3):
+            at = t * D + g * GW
+            both = jnp.concatenate(
+                [w_qkv[:, at : at + GW].astype(F32), notes[:, t * GW : (t + 1) * GW]], axis=0
+            ).astype(BF)
+            wmsg[g, :, t * GW : (t + 1) * GW] = dot(lift, both, NN).astype(BF)
     arrive(expected + 9)
     push(wmsg, wo, send.at[0], core_recv.at[0], sib)
     for k in range(1, 4):
         push(tok, tok_s.at[z], send.at[1], recv.at[0], ((z + k) % 4, x, y, c))
     keep(tok, tok_s.at[z], recv.at[0])
-    push(d_eo.at[theirs], xo, send.at[2], core_recv.at[1], sib)
     wait_bytes(wo, core_recv.at[0])
     wm[...] = wmsg[...] + wo[...]
     to_chips(
@@ -396,6 +418,34 @@
     )
     for k in range(1, 4):
         push(wa, wa_all.at[z, x, y, c], send.at[4], recv.at[2], ((z + k) % 4, x, y, c))
+
+    expert = lax.broadcasted_iota(jnp.int32, (1, 64), 1)
+    first = jnp.where(routes[:, 0:1] == expert, 1.0, 0.0)
+    second = jnp.where(routes[:, 1:2] == expert, 1.0, 0.0)
+    lower = jnp.where(
+        lax.broadcasted_iota(jnp.int32, (TOK, TOK), 0)
+        > lax.broadcasted_iota(jnp.int32, (TOK, TOK), 1), 1.0, 0.0,
+    ).astype(BF)
+    before = jnp.sum(first, axis=0, keepdims=True)
+    rank_1 = jnp.sum(dot(lower, first.astype(BF), NN) * first, axis=1, keepdims=True)
+    rank_2 = jnp.sum(
+        (dot(lower, second.astype(BF), NN) + before) * second, axis=1, keepdims=True
+    )
+    slot = lax.broadcasted_iota(jnp.int32, (TOK, 1024), 1)
+    g_rows = cotangent[...].astype(F32)
+    gated = []
+    for side, rank in enumerate((rank_1, rank_2)):
+        e = routes[:, side : side + 1]
+        block = ((e & 1) * 32 + (e >> 2) * 2 + ((e >> 1) & 1)) * 16 + 8 * c
+        here = slot - block == rank.astype(jnp.int32)
+        picks[side * TOK : (side + 1) * TOK, :] = jnp.where(here, 1.0, 0.0).astype(BF)
+        gated.append((gates[:, side : side + 1] * g_rows).astype(BF))
+    for n in range(0, 1024, WIDE):
+        d_eo[n : n + WIDE, :] = (
+            dot(picks[:TOK, n : n + WIDE], gated[0], TN)
+            + dot(picks[TOK:, n : n + WIDE], gated[1], TN)
+        ).astype(BF)
+    push(d_eo.at[theirs], xo, send.at[2], core_recv.at[1], sib)
 
     row = lax.broadcasted_iota(jnp.int32, (1, 1024), 1)
     r, half, at = row & 15, row >> 9, (row >> 4) & 31
@@ -560,7 +610,7 @@
     wait_bytes(d_rows.at[mine], send.at[12])
 
 
-def attn_forward(tab, tok, wmsg, wa, d_eo):
+def attn_forward(*args):
     probs = (GH, 512, 2048)
     vm = pltpu.VMEM
     return pl.pallas_call(
@@ -576,10 +626,12 @@
             jax.ShapeDtypeStruct((D, 3 * GW), BF),
             jax.ShapeDtypeStruct((512, GW), BF),
             jax.ShapeDtypeStruct((8, D), F32),
+            jax.ShapeDtypeStruct((2 * TOK, 1024), BF),
         ),
-        in_specs=[SMEM, VMEM, VMEM, VMEM, VMEM],
-        out_specs=(ANY, VMEM, ANY, ANY, ANY, ANY, VMEM, VMEM, VMEM, VMEM),
+        in_specs=[SMEM] + [VMEM] * 7,
+        out_specs=(ANY, VMEM, ANY, ANY, ANY, ANY, VMEM, VMEM, VMEM, VMEM, VMEM),
         scratch_shapes=[
+            vm((1024, D), BF), vm((4, 16, 3 * GW), BF),
             vm((4, 16, 3 * GW), BF), vm((4, 16, 3 * GW), BF), vm((1024, 3 * GW), BF),
             vm((4, TOK, D), BF), vm((D, 1024), BF), vm((32, 1024), BF),
             vm((TOK, 8), F32), vm((16, TOK), F32),
@@ -592,15 +644,18 @@
             collective_id=2, has_side_effects=True, vmem_limit_bytes=48 * 2**20
         ),
         name="attn_forward",
-    )(tab, tok, wmsg, wa, d_eo)
+    )(*args)
 
 
 def attn_backward_kernel(
-    p, q, kv, home, picks, middle, gains, cotangent, w_proj, weight, normed, attn_part, tok,
+    p, q_at, kv_at, home_at, picks_at, middle_at, gains_at, cotangent_at, w_proj_at, weight_at,
+    normed_at, attn_part_at, tok_at,
     input_grad, qkv_out, att_out, small_out,
     p_s, v_s, do_s, dm, qm, dp_s, ds_s, near, messages, parts, branch_all, dq, tab,
     d_qkv, n_part, normed_in, att_f, q_blk, q_sib, q_tot, q_in, a_blk, a_sib, a_tot, a_in,
-    s_own, s_sib, s_tot, s_in, qkv_sum, att_sum, s_sum, d_attn, branch, d_middle, send, recv, core_recv, own,
+    s_own, s_sib, s_tot, s_in, qkv_sum, att_sum, s_sum, d_attn, branch, d_middle,
+    q, kv, home, picks, middle, gains, cotangent, w_proj, weight, normed, attn_part, tok,
+    send, recv, core_recv, own, fetched,
 ):
     z, x, y, c = place()
     sib = (z, x, y, 1 - c)
@@ -612,6 +667,13 @@
     def peer(i):
         return z, (x + i // 4) % 4, (y + i % 4) % 4, c
 
+    fetches = (
+        (home_at, home), (picks_at, picks), (middle_at, middle), (gains_at, gains),
+        (cotangent_at, cotangent), (w_proj_at, w_proj), (kv_at, kv), (q_at, q),
+        (weight_at, weight), (normed_at, normed), (attn_part_at, attn_part), (tok_at, tok),
+    )
+    for k, (source_ref, target) in enumerate(fetches):
+        keep(source_ref, target, fetched.at[k])
     keep(p, p_s, own.at[0])
     loop(1, 16, lambda i: signal(peer(i)))
     for k in range(1, 4):
@@ -624,10 +686,8 @@
             signal((k, source // 8, (source // 2) % 4, source % 2))
 
     loop(0, 4, greet)
-    v_s[...] = kv[:, GW:]
-    for h in range(GH):
-        head_cols = lax.broadcasted_iota(jnp.int32, (1, GW), 1) // HD == h
-        qm[h] = jnp.where(head_cols, q[...] * 0.125, 0.0).astype(BF)
+    for k in range(6):
+        wait_bytes(fetches[k][1], fetched.at[k])
     d_moe = dot(picks[:TOK, :], home[...], NN) + dot(picks[TOK:, :], home[...], NN)
     mid = middle[...]
     mid_r = lax.rsqrt(jnp.mean(mid * mid, axis=1, keepdims=True) + norm_eps)
@@ -641,6 +701,12 @@
     branch[...] = d_mid.astype(BF)
     for k in range(GROUPS):
         d_attn[k] = dot(branch[...], w_proj[GW * k : GW * (k + 1), :], NT).astype(BF)
+    for k in range(6, 12):
+        wait_bytes(fetches[k][1], fetched.at[k])
+    v_s[...] = kv[:, GW:]
+    for h in range(GH):
+        head_cols = lax.broadcasted_iota(jnp.int32, (1, GW), 1) // HD == h
+        qm[h] = jnp.where(head_cols, q[...] * 0.125, 0.0).astype(BF)
     arrive(15 + 3 + 1 + 4 - jnp.where(source == p32, 1, 0))
     for k in range(1, 4):
         there = (z + k) % 4
@@ -884,7 +950,7 @@
             jax.ShapeDtypeStruct((8, D), F32),
             jax.ShapeDtypeStruct((4, 8, D), F32),
         ),
-        in_specs=[ANY] + [VMEM] * len(rest),
+        in_specs=[ANY] * (1 + len(rest)),
         out_specs=(VMEM, ANY, ANY, ANY),
         scratch_shapes=[
             vm(probs, BF), vm((2048, GW), BF), vm((4, TOK, GW), BF), vm((GH, 512, GW), BF),
@@ -898,7 +964,10 @@
             vm((8, D), F32), vm((8, D), F32), vm((8, D), F32), vm((16, 8, D), F32),
             vm((4, 8, 3 * GW), F32), vm((8, D), F32), vm((8, D), F32),
             vm((4, TOK, GW), BF), vm((TOK, D), BF), vm((TOK, D), F32),
-            DMA((12,)), DMA((9,)), DMA((3,)), DMA((2,)),
+            vm((512, GW), BF), vm((2048, 2 * GW), BF), vm((1024, D), BF), vm((2 * TOK, 1024), BF),
+            vm((TOK, D), F32), vm((8, D), F32), vm((TOK, D), BF), vm((D, D), BF),
+            vm((D, 3 * GW), BF), vm((512, D), BF), vm((512, GW), BF), vm((TOK, D), BF),
+            DMA((12,)), DMA((9,)), DMA((3,)), DMA((2,)), DMA((12,)),
         ],
         compiler_params=pltpu.CompilerParams(
             collective_id=3, has_side_effects=True, vmem_limit_bytes=54 * 2**20
@@ -922,54 +991,33 @@
     cotangent,
 ):
     z, x, y, c = place()
-    experts = 64
-    capacity = 8
-    slots = 2 * experts * capacity
     own_tokens = tokens.reshape(TOK, D)
     grad_bf = cotangent.reshape(TOK, D)
     grad_out = grad_bf.astype(F32)
 
-    routes = expert_ids.reshape(TOK, 2)
     gates = gate_values.reshape(TOK, 2)
-    expert_list = jnp.arange(experts, dtype=jnp.int32)[None, :]
-    marks = jnp.concatenate(
-        [(routes[:, :1] == expert_list), (routes[:, 1:] == expert_list)], axis=1
-    ).astype(BF)
-    lower = jnp.tril(jnp.ones((TOK, TOK), BF), -1)
-    earlier = dot(lower, marks, NN)
-    marks = marks.astype(F32)
-    firsts = jnp.sum(marks[:, :experts], axis=0, keepdims=True)
-    rank_0 = jnp.sum(earlier[:, :experts] * marks[:, :experts], axis=1)
-    rank_1 = jnp.sum((earlier[:, experts:] + firsts) * marks[:, experts:], axis=1)
-    blocks = (routes % 2) * 32 + (routes // 4) * 2 + (routes % 4) // 2
-    places = blocks * 16 + c * capacity + jnp.stack([rank_0, rank_1], axis=1).astype(jnp.int32)
-    slot_ids = jnp.arange(slots, dtype=jnp.int32)[None, :]
-    picks = jnp.concatenate(
-        [(places[:, :1] == slot_ids), (places[:, 1:] == slot_ids)], axis=0
-    ).astype(BF)
-    gated = jnp.concatenate([gates[:, :1] * grad_out, gates[:, 1:] * grad_out], axis=0).astype(BF)
-    d_eo = dot(picks, gated, TN).astype(BF)
-
-    slab = w_qkv.reshape(6, 3, GROUPS, GW).transpose(2, 0, 1, 3).reshape(GROUPS, 6, 3 * GW)
+
     place_in = chip_of(z, x, y) * 2 + c
-    among = (place_in % 64) * 6
-    row_one = lax.dynamic_update_slice(jnp.zeros((3 * GW,), BF), gain_attn, (among,))
-    row_one = lax.dynamic_update_slice(row_one, doc_ids.reshape(TOK).astype(BF), (384,))
-    row_two = lax.dynamic_update_slice(jnp.zeros((3 * GW,), BF), gain_moe, (among,))
-    note_one = jnp.broadcast_to(row_one, (GROUPS, 1, 3 * GW))
-    note_two = jnp.broadcast_to(row_two, (GROUPS, 1, 3 * GW))
-    nothing = jnp.zeros((GROUPS, 6, 3 * GW), BF)
-    none = nothing[:, :1]
-    message = jnp.where(
-        c == 0,
-        jnp.concatenate([slab, nothing, note_one, none, note_two, none], axis=1),
-        jnp.concatenate([nothing, slab, none, note_one, none, note_two], axis=1),
-    )
+    lane = jnp.arange(3 * GW, dtype=jnp.int32)[None, :]
+    both_gains = jnp.stack([gain_attn, gain_moe]).astype(F32)
+    notes = jnp.concatenate(
+        [
+            jnp.zeros((2, 384), F32),
+            jnp.pad(doc_ids.reshape(1, TOK).astype(F32), ((0, 1), (0, 0))),
+            jnp.zeros((2, 64), F32),
+        ],
+        axis=1,
+    )
+    for k in range(6):
+        notes = jnp.where(lane == (place_in % 64) * 6 + k, both_gains[:, k : k + 1], notes)
     out_slab = jnp.concatenate([w_attn_out, jnp.zeros((2, D), BF)], axis=0)
     table = lax.dynamic_slice(rel_table, (0, z * GH), (BUCKETS, GH)).astype(F32)
     (
         attn, attn_part, probs, kv_all, out_weights, d_eo_all, normed, weight, queries, gain_rows,
-    ) = attn_forward(table, own_tokens, message, out_slab, d_eo)
+        picks,
+    ) = attn_forward(
+        table, own_tokens, w_qkv, notes, out_slab, expert_ids.reshape(TOK, 2), gates, grad_bf
+    )
     attention_weight = out_weights[:, :, :, :, :6, :].reshape(D, D)
     home, expert_out, expert_in_grad, expert_out_grad, middle = run_experts(
         attn, attention_weight, own_tokens, gain_rows, picks, d_eo_all, w_in[0], w_out[0]

time: 224 us -> 219 us (0.978)
    pallas_call x1, Pallas kernels: 58.2 us -> 55.7 us  [attn_backward(): pl.pallas_call(attn_backward_kernel, out_shape=(jax.ShapeDtypeStruct((TOK...]
    unnamed x57 -> x51, local copies, waits for them, and re-layouts: 17.1 us -> 19.6 us
where the time goes in v9:
time: 219 us; the launch traced here: 217 us
  Pallas kernels  184 us (84%)
  local copies, waits for them, and re-layouts  26.2 us (12%)
  other arithmetic  4.14 us (2%)
    pallas_call x1, Pallas kernels, attn_forward(): pl.pallas_call(attn_forward_kernel, out_shape=(jax.ShapeDtypeStruct((4, T...  70.8 us
    pallas_call x1, Pallas kernels, run_experts(): pl.pallas_call(experts_kernel, out_shape=(jax.ShapeDtypeStruct((1024, D),...  57.9 us
    pallas_call x1, Pallas kernels, attn_backward(): pl.pallas_call(attn_backward_kernel, out_shape=(jax.ShapeDtypeStruct((TOK...  55.7 us
    unnamed x51, local copies, waits for them, and re-layouts  19.6 us

profile of v9, /device:TPU:1, one launch (start us, length us, event | category | flops | bytes accessed | tf_op | source)
XLA Modules:
  0.0 216.8 jit_solution(1814218630071090742)
XLA Ops:
  0.6 0.0 copy-start
  0.7 0.7 copy-done
  1.3 0.7 convert_element_type.21
  2.0 0.7 maximum_convert_fusion
  2.7 0.3 slice_reduce_fusion.9
  3.0 0.1 fusion.12.notes
  3.1 0.1 copy.35
  3.2 0.7 concatenate.7.wa
  3.9 0.8 copy.31
  4.7 0.8 copy.32
  5.5 0.2 slice_reduce_fusion.1
  5.7 1.0 bitcast_convert_fusion
  6.6 0.0 copy-start.4
  6.6 0.9 copy-done.4
  7.6 0.9 copy-done.5
  8.5 0.8 copy-done.16
  9.3 70.8 %attn_forward.1 = (bf16[4,128,192]{2,1,0:T(8,128)(2,1)S(1)}, bf16[512,192]{1,0:T(8,128)(2,1)S(1)}, bf16[3,512,2048]{2,1,0:T(8,128)(2,1)}, bf16[2048,384]{1,0:T(8...) custom-call(f32[32,3]{1,0:T(8,128)S(1)} %convert_element_type.19.tab, ...), custom_call_target="tpu_custom_call" | custom-call | tf_op jit(solution)/shard_map/attn_forward/pallas_call | solution.py:616
  80.0 0.0 copy-start.7
  80.1 1.1 copy-done.7
  81.2 0.9 copy-done.11
  82.1 0.9 copy-done.12
  83.0 0.7 copy-done.13
  83.7 0.7 copy-done.14
  84.4 2.5 %reshape.90.w_proj_at = bf16[768,768]{1,0:T(8,128)(2,1)S(1)} reshape(bf16[4,4,4,2,6,768]{5,4,3,2,1,0:T(8,128)(2,1)} %bitcast.50) | data formatting | bytes 2359296 | tf_op jit(solution)/shard_map/reshape | solution.py:1021
  86.9 0.0 copy-done.6
  87.0 0.0 copy-start.1
  87.0 57.9 %experts.1 = (bf16[1024,768]{1,0:T(8,128)(2,1)S(1)}, bf16[1024,768]{1,0:T(8,128)(2,1)S(1)}, f32[768,1536]{1,0:T(8,128)}, f32[1536,768]{1,0:T(8,128)}, f32[128,768]{1,0:T(8,128)S(1)}) custom-call(bf16[4,128,192]{2,1,0:T(8,128)(2,1)S(1)} %get-tuple-element.30.attn_at, bf16[768,768]{1,0:T(8,128)(2,1)S(1)} %reshape.90.w_proj_at, bf16[128,768]{1,0:T(8,128)(2,1)S(1)} %bitcast.40, ...), custom_call_target="tpu_custom_call" | custom-call | tf_op jit(solution)/shard_map/experts/pallas_call | solution.py:319
  144.9 0.0 copy-done.2
  144.9 0.0 copy-start.8
  144.9 1.1 copy-done.8
  146.0 0.8 copy-done.9
  146.8 55.7 %attn_backward.1 = (bf16[128,768]{1,0:T(8,128)(2,1)}, f32[4,8,576]{2,1,0:T(8,128)}, f32[8,768]{1,0:T(8,128)}, f32[4,8,768]{2,1,0:T(8,128)}) custom-call(bf16[3,512,2048]{2,1,0:T(8,128)(2,1)} %get-tuple-element.37.p, bf16[512,192]{1,0:T(8,128)(2,1)} %copy-done.14, bf16[2048,384]{1,0:T(8,128)(2,1)} %copy-done.7, bf16[1024,768]{1,0:T(8,128)(2,1)} %copy-done.8, ...), custom_call_target="tpu_custom_call" | custom-call | tf_op jit(solution)/shard_map/attn_backward/pallas_call | solution.py:945
  202.5 1.2 fusion
  203.7 0.0 copy-done.10
  203.7 0.8 fusion.4
  204.6 0.0 copy-done.18
  204.6 0.7 slice_reduce_fusion.3
  205.3 0.9 slice_reduce_fusion.2
  206.2 0.1 constant_dynamic-slice_fusion
  206.3 0.5 slice_bitcast_fusion
  206.8 0.7 reshape_squeeze.3
  207.5 0.1 reshape.93
  207.7 0.7 reshape.94
  208.4 0.7 copy.40
  209.1 0.6 copy.41
  209.7 4.9 %copy.42 = f32[1,768,1536]{2,1,0:T(8,128)} copy(f32[1,768,1536]{2,1,0:T(8,128)} %bitcast.47) | data formatting | bytes 9437184
  214.6 0.0 slice-done.1
  214.6 2.2 %copy.43 = f32[1,1536,768]{2,1,0:T(8,128)} copy(f32[1,1536,768]{2,1,0:T(8,128)S(1)} %bitcast.46) | data formatting | bytes 9437184
  (35 shorter events, 0.1 us)
Async XLA Ops:
  0.6 0.7 copy-start
  6.6 0.9 copy-start.4
  7.6 0.9 copy-start.5
  8.5 0.8 copy-start.16
  9.3 77.7 %copy-start.6 = (bf16[1,128,768]{2,1,0:T(8,128)(2,1)S(1)}, bf16[1,128,768]{2,1,0:T(8,128)(2,1)}, u32[]{:S(2)}) copy-start(bf16[1,128,768]{2,1,0:T(8,128)(2,1)} %param.12) | copy-start | bytes 589828
  80.0 1.1 copy-start.7
  81.2 0.9 copy-start.11
  82.1 0.9 copy-start.12
  83.0 0.7 copy-start.13
  83.7 0.7 copy-start.14
  84.4 60.5 %copy-start.2 = (bf16[256,1024]{1,0:T(8,128)(2,1)}, bf16[256,1024]{1,0:T(8,128)(2,1)S(1)}, u32[]{:S(2)}) copy-start(bf16[256,1024]{1,0:T(8,128)(2,1)S(1)} %get-tuple-element.33.picks_at) | copy-start | bytes 1572868
  84.4 60.5 %copy-start.15 = (f32[8,768]{1,0:T(8,128)}, f32[8,768]{1,0:T(8,128)S(1)}, u32[]{:S(2)}) copy-start(f32[8,768]{1,0:T(8,128)S(1)} %get-tuple-element.32.gains_at) | copy-start | bytes 73732
  87.0 57.9 %copy-start.1 = (bf16[768,768]{1,0:T(8,128)(2,1)}, bf16[768,768]{1,0:T(8,128)(2,1)S(1)}, u32[]{:S(2)}) copy-start(bf16[768,768]{1,0:T(8,128)(2,1)S(1)} %reshape.90.w_proj_at) | copy-start | bytes 3538948
  144.9 1.1 copy-start.8
  146.0 0.8 copy-start.9
  146.8 55.7 %copy-start.3 = (bf16[256,1024]{1,0:T(8,128)(2,1)S(1)}, bf16[256,1024]{1,0:T(8,128)(2,1)}, u32[]{:S(2)}) copy-start(bf16[256,1024]{1,0:T(8,128)(2,1)} %copy-done.2) | copy-start | bytes 1572868
  202.5 1.3 copy-start.10
  202.5 2.1 copy-start.18
  203.7 4.7 %copy-start.17 = (bf16[128,768]{1,0:T(8,128)(2,1)S(1)}, bf16[128,768]{1,0:T(8,128)(2,1)}, u32[]{:S(2)}) copy-start(bf16[128,768]{1,0:T(8,128)(2,1)} %get-tuple-element.44) | copy-start | bytes 589828
  203.7 5.3 %copy-start.19 = (f32[8,768]{1,0:T(8,128)S(1)}, f32[8,768]{1,0:T(8,128)}, u32[]{:S(2)}) copy-start(f32[8,768]{1,0:T(8,128)} %get-tuple-element.47) | copy-start | bytes 73732
  208.4 6.2 %slice-start = ((s8[4718592]{0:T(1024)(128)(4,1)}), s8[4194304]{0:T(1024)(128)(4,1)S(1)}, s32[]{:S(2)}) async-start(s8[4718592]{0:T(1024)(128)(4,1)} %bitcast.44), calls=%async_computation | async-start | bytes 8388608
  209.7 4.9 %slice-start.1 = ((s8[4718592]{0:T(1024)(128)(4,1)}), s8[524288]{0:T(1024)(128)(4,1)S(1)}, s32[]{:S(2)}) async-start(s8[4718592]{0:T(1024)(128)(4,1)} %bitcast.44), calls=%async_computation.1 | async-start | bytes 1048576

commit v10 on v9

--- a/solution.py
+++ b/solution.py
@@ -22,6 +22,7 @@
 AXES = ("ctx_0", "ctx_1", "exp_0", "exp_1")
 MESH = pl.DeviceIdType.MESH
 ANY = pl.BlockSpec(memory_space=pl.ANY)
+HBM = pl.BlockSpec(memory_space=pltpu.HBM)
 BF = jnp.bfloat16
 F32 = jnp.float32
 
@@ -157,8 +158,8 @@
 
 def experts_kernel(
     attn_at, w_proj_at, tok_at, gains_at, picks_at, d_rows, w_in, w_out,
-    home_in, home_out, g_in, g_out, middle,
-    attn, w_proj, tok, gains, picks, x16, xo, rows, dv, w1, w2, dh, hidden, dact, in_h, out_h, in_o, out_o, stage_out, stage_in,
+    home_in, home_out, g_in, g_out, middle_out,
+    middle, attn, w_proj, tok, gains, picks, x16, xo, rows, dv, w1, w2, dh, hidden, dact, in_h, out_h, in_o, out_o, stage_out, stage_in,
     send, recv, core_recv, own, staged, fetched,
 ):
     z, x, y, c = place()
@@ -182,6 +183,7 @@
     for k in range(GROUPS):
         total = total + dot(attn[k], w_proj[GW * k : GW * (k + 1), :], NN)
     middle[...] = total
+    keep(middle, middle_out, own.at[0])
     moe_in = scale_rows(total, gains[1:2, :]).astype(BF)
     for n in range(0, 1024, WIDE):
         x16[n : n + WIDE, :] = (
@@ -310,6 +312,7 @@
     wait_bytes(home_out.at[theirs], core_recv.at[5])
     wait_bytes(home_in.at[mine], send.at[7])
     wait_bytes(home_out.at[mine], send.at[8])
+    wait_bytes(middle, own.at[0])
 
 
 def run_experts(*args):
@@ -325,9 +328,10 @@
             jax.ShapeDtypeStruct((FH, D), F32),
             jax.ShapeDtypeStruct((TOK, D), F32),
         ),
-        in_specs=[ANY] * 8,
-        out_specs=(ANY,) * 4 + (pl.BlockSpec(memory_space=pltpu.VMEM),),
+        in_specs=[HBM, ANY] + [HBM] * 6,
+        out_specs=(HBM,) * 5,
         scratch_shapes=[
+            pltpu.VMEM((TOK, D), F32),
             pltpu.VMEM((4, TOK, GW), BF), pltpu.VMEM((D, D), BF), pltpu.VMEM((TOK, D), BF),
             pltpu.VMEM((8, D), F32), pltpu.VMEM((2 * TOK, 1024), BF),
             whole_rows, half_rows, whole_rows, whole_rows,
@@ -337,7 +341,7 @@
             DMA((9,)), DMA((3,)), DMA((6,)), DMA((4,)), DMA((4,)), DMA((5,)),
         ],
         compiler_params=pltpu.CompilerParams(
-            collective_id=1, has_side_effects=True, vmem_limit_bytes=48 * 2**20
+            collective_id=1, has_side_effects=True, vmem_limit_bytes=63 * 2**20
         ),
         name="experts",
     )(*args)
@@ -375,9 +379,9 @@
 
 
 def attn_forward_kernel(
-    tab, tok, w_qkv, notes, wa, routes, gates, cotangent,
-    attn_all, part, p_out, kv_out, wa_all, d_rows, normed, weight, q, gains, picks,
-    d_eo, wmsg, wm, wo, w_s, tok_s, select, picker, qd, kd,
+    tab, tok, w_qkv, notes, wa, routes, gates, cotangent_at,
+    attn_all, part_out, p_out, kv_out, wa_all, d_rows, normed_out, weight_out, q_out, gains_out,
+    picks_out, part, normed, weight, q, gains, picks, cotangent, d_eo, wmsg, wm, wo, w_s, tok_s, select, picker, qd, kd,
     kv, kv_s, v_s, qm, bias, s_s, p_s, xo,
     send, recv, kv_recv, core_recv, own,
 ):
@@ -387,6 +391,7 @@
     theirs = pl.ds(pl.multiple_of((1 - c) * 512, 512), 512)
     me = block_of(z, x, y)
     keep(wa, wa_all.at[z, x, y, c], own.at[0])
+    keep(cotangent_at, cotangent, own.at[3])
     expected = greet_chips(z, x, y, c)
     for k in range(1, 4):
         signal(((z + k) % 4, x, y, c))
@@ -432,6 +437,7 @@
         (dot(lower, second.astype(BF), NN) + before) * second, axis=1, keepdims=True
     )
     slot = lax.broadcasted_iota(jnp.int32, (TOK, 1024), 1)
+    wait_bytes(cotangent, own.at[3])
     g_rows = cotangent[...].astype(F32)
     gated = []
     for side, rank in enumerate((rank_1, rank_2)):
@@ -446,6 +452,7 @@
             + dot(picks[TOK:, n : n + WIDE], gated[1], TN)
         ).astype(BF)
     push(d_eo.at[theirs], xo, send.at[2], core_recv.at[1], sib)
+    keep(picks, picks_out, own.at[4])
 
     row = lax.broadcasted_iota(jnp.int32, (1, 1024), 1)
     r, half, at = row & 15, row >> 9, (row >> 4) & 31
@@ -500,6 +507,7 @@
     q[...] = qkv[:, :GW]
     for b in range(4):
         kv[b] = qkv[b * TOK : (b + 1) * TOK, GW:]
+    results = ((normed, normed_out), (weight, weight_out), (q, q_out), (gains, gains_out))
     for k in range(1, 4):
         for b in range(4):
             push(
@@ -508,6 +516,8 @@
             )
     for b in range(4):
         keep(kv.at[b], kv_s.at[block_cols(b, x)], kv_recv.at[0])
+    for k, (source, target) in enumerate(results):
+        keep(source, target, own.at[5 + k])
     wait_bytes(wa_all.at[:, pl.ds(0, 3), y, c], recv.at[3])
     for k in range(1, 4):
         push(
@@ -588,6 +598,7 @@
         )
     keep(part.at[pl.ds(pl.multiple_of(z * TOK, TOK), TOK)], attn_all.at[z], recv.at[6])
     keep(p_s, p_out, own.at[2])
+    keep(part, part_out, own.at[9])
     wait_bytes(d_rows.at[mine], recv.at[5])
     push(d_rows.at[mine], d_rows.at[mine], send.at[12], core_recv.at[4], sib)
     wait_bytes(attn_all, recv.at[6])
@@ -595,6 +606,10 @@
     wait_bytes(d_rows.at[theirs], core_recv.at[4])
     wait_bytes(kv_s, own.at[1])
     wait_bytes(p_s, own.at[2])
+    wait_bytes(picks, own.at[4])
+    for k, (source, _) in enumerate(results):
+        wait_bytes(source, own.at[5 + k])
+    wait_bytes(part, own.at[9])
     wait_bytes(wo, send.at[0])
     wait_bytes(tok_s.at[pl.ds(0, 3)], send.at[1])
     wait_bytes(xo, send.at[2])
@@ -628,20 +643,22 @@
             jax.ShapeDtypeStruct((8, D), F32),
             jax.ShapeDtypeStruct((2 * TOK, 1024), BF),
         ),
-        in_specs=[SMEM] + [VMEM] * 7,
-        out_specs=(ANY, VMEM, ANY, ANY, ANY, ANY, VMEM, VMEM, VMEM, VMEM, VMEM),
+        in_specs=[SMEM, HBM, VMEM, VMEM, HBM, VMEM, VMEM, HBM],
+        out_specs=(HBM,) * 11,
         scratch_shapes=[
-            vm((1024, D), BF), vm((4, 16, 3 * GW), BF),
+            vm((512, GW), BF), vm((512, D), BF), vm((D, 3 * GW), BF), vm((512, GW), BF),
+            vm((8, D), F32), vm((2 * TOK, 1024), BF),
+            vm((TOK, D), BF), vm((1024, D), BF), vm((4, 16, 3 * GW), BF),
             vm((4, 16, 3 * GW), BF), vm((4, 16, 3 * GW), BF), vm((1024, 3 * GW), BF),
             vm((4, TOK, D), BF), vm((D, 1024), BF), vm((32, 1024), BF),
             vm((TOK, 8), F32), vm((16, TOK), F32),
             vm((4, TOK, 2 * GW), BF), vm((2048, 2 * GW), BF), vm((2048, GW), BF),
             vm((GH, 512, GW), BF), vm((GH, 4, TOK, TOK), F32), vm(probs, F32), vm(probs, BF),
             vm((512, D), BF),
-            DMA((13,)), DMA((7,)), DMA((4,)), DMA((5,)), DMA((3,)),
+            DMA((13,)), DMA((7,)), DMA((4,)), DMA((5,)), DMA((10,)),
         ],
         compiler_params=pltpu.CompilerParams(
-            collective_id=2, has_side_effects=True, vmem_limit_bytes=48 * 2**20
+            collective_id=2, has_side_effects=True, vmem_limit_bytes=63 * 2**20
         ),
         name="attn_forward",
     )(*args)
@@ -950,7 +967,7 @@
             jax.ShapeDtypeStruct((8, D), F32),
             jax.ShapeDtypeStruct((4, 8, D), F32),
         ),
-        in_specs=[ANY] * (1 + len(rest)),
+        in_specs=[HBM] * (1 + len(rest)),
         out_specs=(VMEM, ANY, ANY, ANY),
         scratch_shapes=[
             vm(probs, BF), vm((2048, GW), BF), vm((4, TOK, GW), BF), vm((GH, 512, GW), BF),
@@ -970,7 +987,7 @@
             DMA((12,)), DMA((9,)), DMA((3,)), DMA((2,)), DMA((12,)),
         ],
         compiler_params=pltpu.CompilerParams(
-            collective_id=3, has_side_effects=True, vmem_limit_bytes=54 * 2**20
+            collective_id=3, has_side_effects=True, vmem_limit_bytes=63 * 2**20
         ),
         name="attn_backward",
     )(p, *rest)

time: 219 us -> 215 us (0.982)
  local copies, waits for them, and re-layouts: 26.2 us -> 19.2 us
    unnamed x51 -> x25, local copies, waits for them, and re-layouts: 19.6 us -> 11.4 us
where the time goes in v10:
time: 215 us; the launch traced here: 213 us
  Pallas kernels  185 us (86%)
  local copies, waits for them, and re-layouts  19.2 us (9%)
  other arithmetic  5.34 us (2%)
  matrix products  2.69 us (1%)
    pallas_call x1, Pallas kernels, attn_forward(): pl.pallas_call(attn_forward_kernel, out_shape=(jax.ShapeDtypeStruct((4, T...  71.3 us
    pallas_call x1, Pallas kernels, run_experts(): pl.pallas_call(experts_kernel, out_shape=(jax.ShapeDtypeStruct((1024, D),...  58 us
    pallas_call x1, Pallas kernels, attn_backward(): pl.pallas_call(attn_backward_kernel, out_shape=(jax.ShapeDtypeStruct((TOK...  55.7 us
    unnamed x25, local copies, waits for them, and re-layouts  11.4 us

profile of v10, /device:TPU:1, one launch (start us, length us, event | category | flops | bytes accessed | tf_op | source)
XLA Modules:
  0.0 213.1 jit_solution(791497256713098540)
XLA Ops:
  0.6 0.0 copy-start
  0.7 0.7 copy-done
  1.3 0.7 convert_element_type.21
  2.0 0.7 maximum_convert_fusion
  2.7 0.3 slice_reduce_fusion.9
  3.0 0.7 fusion.12.notes
  3.7 0.1 copy.35
  3.8 0.6 convert_element_type.19.tab
  4.4 1.3 concatenate.7.wa
  5.7 1.4 copy.31
  7.1 0.8 copy.32
  7.9 0.0 copy-start.3
  7.9 0.2 slice_reduce_fusion.1
  8.1 1.0 bitcast_convert_fusion
  9.1 0.0 copy-done.3
  9.1 71.3 %attn_forward.1 = (bf16[4,128,192]{2,1,0:T(8,128)(2,1)}, bf16[512,192]{1,0:T(8,128)(2,1)}, bf16[3,512,2048]{2,1,0:T(8,128)(2,1)}, bf16[2048,384]{1,0:T(8,128)(2,...) custom-call(f32[32,3]{1,0:T(8,128)} %convert_element_type.19.tab, ...), custom_call_target="tpu_custom_call" | custom-call | tf_op jit(solution)/shard_map/attn_forward/pallas_call | solution.py:631
  80.4 3.2 %reshape.90.w_proj_at = bf16[768,768]{1,0:T(8,128)(2,1)} reshape(bf16[4,4,4,2,6,768]{5,4,3,2,1,0:T(8,128)(2,1)} %bitcast.47) | data formatting | bytes 2359296 | tf_op jit(solution)/shard_map/reshape | solution.py:1038
  83.6 58.0 %experts.1 = (bf16[1024,768]{1,0:T(8,128)(2,1)}, bf16[1024,768]{1,0:T(8,128)(2,1)}, f32[768,1536]{1,0:T(8,128)}, f32[1536,768]{1,0:T(8,128)}, f32[128,768]{1,0:T(8,128)}) custom-call(bf16[4,128,192]{2,1,0:T(8,128)(2,1)} %get-tuple-element.30.attn_at, bf16[768,768]{1,0:T(8,128)(2,1)} %reshape.90.w_proj_at, bf16[128,768]{1,0:T(8,128)(2,1)} %bitcast.45, ...), custom_call_target="tpu_custom_call" | custom-call | tf_op jit(solution)/shard_map/experts/pallas_call | solution.py:322
  141.6 0.0 copy-start.1
  141.6 55.7 %attn_backward.1 = (bf16[128,768]{1,0:T(8,128)(2,1)}, f32[4,8,576]{2,1,0:T(8,128)}, f32[8,768]{1,0:T(8,128)}, f32[4,8,768]{2,1,0:T(8,128)}) custom-call(bf16[3,512,2048]{2,1,0:T(8,128)(2,1)} %get-tuple-element.37.p, bf16[512,192]{1,0:T(8,128)(2,1)} %get-tuple-element.38.q_at, bf16[2048,384]{1,0:T(8,128)(2,1)} %get-tuple-element.39.kv_at, ...), custom_call_target="tpu_custom_call" | custom-call | tf_op jit(solution)/shard_map/attn_backward/pallas_call | solution.py:962
  197.3 0.0 copy-done.1
  197.3 0.0 copy-start.2
  197.4 0.0 copy-start.5
  197.4 2.7 %fusion = (f32[256]{0:T(256)}, f32[256,768]{1,0:T(8,128)S(1)}) fusion(f32[128,768]{1,0:T(8,128)S(1)} %bitcast_convert_fusion, bf16[256,1024]{1,0:T(8,128)(2,1)S(1)} %copy-done.1, bf16[1024,768]{1,0:T(8,128)(2,1)} %get-tuple-element.36), kind=kOutput, calls=%fused_computation.1 | convolution fusion | flops 403046144 | bytes 3277824 | tf_op jit(solution)/shard_map/dot_general | solution.py:360
  200.0 0.0 copy-start.4
  200.1 0.0 copy-start.6
  200.1 0.0 copy-done.2
  200.1 0.8 fusion.4
  200.9 0.0 copy-done.5
  200.9 0.7 slice_reduce_fusion.3
  201.6 0.9 slice_reduce_fusion.2
  202.6 0.1 constant_dynamic-slice_fusion
  202.6 0.5 slice_bitcast_fusion
  203.2 0.7 reshape_squeeze.3
  203.8 0.1 reshape.93
  204.0 0.7 reshape.94
  204.7 0.0 copy-done.4
  204.7 0.0 slice-start
  204.7 0.7 copy.40
  205.4 0.0 copy-done.6
  205.4 0.6 copy.41
  206.0 0.0 slice-start.1
  206.0 4.9 %copy.42 = f32[1,768,1536]{2,1,0:T(8,128)} copy(f32[1,768,1536]{2,1,0:T(8,128)} %bitcast.39) | data formatting | bytes 9437184
  210.9 0.0 slice-done
  210.9 0.0 slice-done.1
  210.9 2.2 %copy.43 = f32[1,1536,768]{2,1,0:T(8,128)} copy(f32[1,1536,768]{2,1,0:T(8,128)S(1)} %bitcast.38) | data formatting | bytes 9437184
  (11 shorter events, 0.1 us)
Async XLA Ops:
  0.6 0.7 copy-start
  7.9 1.2 copy-start.3
  141.6 55.7 %copy-start.1 = (bf16[256,1024]{1,0:T(8,128)(2,1)S(1)}, bf16[256,1024]{1,0:T(8,128)(2,1)}, u32[]{:S(2)}) copy-start(bf16[256,1024]{1,0:T(8,128)(2,1)} %get-tuple-element.33.picks_at) | copy-start | bytes 1572868
  197.3 2.7 %copy-start.2 = (f32[128,768]{1,0:T(8,128)S(1)}, f32[128,768]{1,0:T(8,128)}, u32[]{:S(2)}) copy-start(f32[128,768]{1,0:T(8,128)} %get-tuple-element.35.middle_at) | copy-start | bytes 1179652
  197.4 3.5 %copy-start.5 = (f32[4,8,576]{2,1,0:T(8,128)S(1)}, f32[4,8,576]{2,1,0:T(8,128)}, u32[]{:S(2)}) copy-start(f32[4,8,576]{2,1,0:T(8,128)} %get-tuple-element.46) | copy-start | bytes 221188
  200.0 4.7 %copy-start.4 = (bf16[128,768]{1,0:T(8,128)(2,1)S(1)}, bf16[128,768]{1,0:T(8,128)(2,1)}, u32[]{:S(2)}) copy-start(bf16[128,768]{1,0:T(8,128)(2,1)} %get-tuple-element.44) | copy-start | bytes 589828
  200.1 5.3 %copy-start.6 = (f32[8,768]{1,0:T(8,128)S(1)}, f32[8,768]{1,0:T(8,128)}, u32[]{:S(2)}) copy-start(f32[8,768]{1,0:T(8,128)} %get-tuple-element.47) | copy-start | bytes 73732
  204.7 6.2 %slice-start = ((s8[4718592]{0:T(1024)(128)(4,1)}), s8[4194304]{0:T(1024)(128)(4,1)S(1)}, s32[]{:S(2)}) async-start(s8[4718592]{0:T(1024)(128)(4,1)} %bitcast.36), calls=%async_computation | async-start | bytes 8388608
  206.0 4.9 %slice-start.1 = ((s8[4718592]{0:T(1024)(128)(4,1)}), s8[524288]{0:T(1024)(128)(4,1)S(1)}, s32[]{:S(2)}) async-start(s8[4718592]{0:T(1024)(128)(4,1)} %bitcast.36), calls=%async_computation.1 | async-start | bytes 1048576

commit v11 on v10

--- a/solution.py
+++ b/solution.py
@@ -413,14 +413,14 @@
             wmsg[g, :, t * GW : (t + 1) * GW] = dot(lift, both, NN).astype(BF)
     arrive(expected + 9)
     push(wmsg, wo, send.at[0], core_recv.at[0], sib)
-    for k in range(1, 4):
-        push(tok, tok_s.at[z], send.at[1], recv.at[0], ((z + k) % 4, x, y, c))
-    keep(tok, tok_s.at[z], recv.at[0])
     wait_bytes(wo, core_recv.at[0])
     wm[...] = wmsg[...] + wo[...]
     to_chips(
         z, x, y, c, lambda there: wm.at[there[0]], w_s.at[pl.ds(me, 16)], send.at[3], recv.at[1]
     )
+    for k in range(1, 4):
+        push(tok, tok_s.at[z], send.at[1], recv.at[0], ((z + k) % 4, x, y, c))
+    keep(tok, tok_s.at[z], recv.at[0])
     for k in range(1, 4):
         push(wa, wa_all.at[z, x, y, c], send.at[4], recv.at[2], ((z + k) % 4, x, y, c))
 

time: 215 us -> 215 us (level)
  no operation moved by 1% of the time
where the time goes in v11:
time: 215 us; the launch traced here: 213 us
  Pallas kernels  185 us (86%)
  local copies, waits for them, and re-layouts  19.2 us (9%)
  other arithmetic  5.34 us (2%)
  matrix products  2.69 us (1%)
    pallas_call x1, Pallas kernels, attn_forward(): pl.pallas_call(attn_forward_kernel, out_shape=(jax.ShapeDtypeStruct((4, T...  72.7 us
    pallas_call x1, Pallas kernels, run_experts(): pl.pallas_call(experts_kernel, out_shape=(jax.ShapeDtypeStruct((1024, D),...  56.7 us
    pallas_call x1, Pallas kernels, attn_backward(): pl.pallas_call(attn_backward_kernel, out_shape=(jax.ShapeDtypeStruct((TOK...  55.3 us
    unnamed x25, local copies, waits for them, and re-layouts  11.4 us

profile of v11, /device:TPU:1, one launch (start us, length us, event | category | flops | bytes accessed | tf_op | source)
XLA Modules:
  0.0 212.8 jit_solution(15035951727889605445)
XLA Ops:
  0.6 0.0 copy-start
  0.7 0.7 copy-done
  1.3 0.7 convert_element_type.21
  2.0 0.7 maximum_convert_fusion
  2.7 0.3 slice_reduce_fusion.9
  3.0 0.7 fusion.12.notes
  3.7 0.1 copy.35
  3.8 0.6 convert_element_type.19.tab
  4.4 1.3 concatenate.7.wa
  5.7 1.4 copy.31
  7.1 0.8 copy.32
  7.9 0.0 copy-start.3
  7.9 0.2 slice_reduce_fusion.1
  8.1 1.0 bitcast_convert_fusion
  9.1 0.0 copy-done.3
  9.1 72.7 %attn_forward.1 = (bf16[4,128,192]{2,1,0:T(8,128)(2,1)}, bf16[512,192]{1,0:T(8,128)(2,1)}, bf16[3,512,2048]{2,1,0:T(8,128)(2,1)}, bf16[2048,384]{1,0:T(8,128)(2,...) custom-call(f32[32,3]{1,0:T(8,128)} %convert_element_type.19.tab, ...), custom_call_target="tpu_custom_call" | custom-call | tf_op jit(solution)/shard_map/attn_forward/pallas_call | solution.py:631
  81.8 3.2 %reshape.90.w_proj_at = bf16[768,768]{1,0:T(8,128)(2,1)} reshape(bf16[4,4,4,2,6,768]{5,4,3,2,1,0:T(8,128)(2,1)} %bitcast.47) | data formatting | bytes 2359296 | tf_op jit(solution)/shard_map/reshape | solution.py:1038
  85.0 56.7 %experts.1 = (bf16[1024,768]{1,0:T(8,128)(2,1)}, bf16[1024,768]{1,0:T(8,128)(2,1)}, f32[768,1536]{1,0:T(8,128)}, f32[1536,768]{1,0:T(8,128)}, f32[128,768]{1,0:T(8,128)}) custom-call(bf16[4,128,192]{2,1,0:T(8,128)(2,1)} %get-tuple-element.30.attn_at, bf16[768,768]{1,0:T(8,128)(2,1)} %reshape.90.w_proj_at, bf16[128,768]{1,0:T(8,128)(2,1)} %bitcast.45, ...), custom_call_target="tpu_custom_call" | custom-call | tf_op jit(solution)/shard_map/experts/pallas_call | solution.py:322
  141.8 0.0 copy-start.1
  141.8 55.3 %attn_backward.1 = (bf16[128,768]{1,0:T(8,128)(2,1)}, f32[4,8,576]{2,1,0:T(8,128)}, f32[8,768]{1,0:T(8,128)}, f32[4,8,768]{2,1,0:T(8,128)}) custom-call(bf16[3,512,2048]{2,1,0:T(8,128)(2,1)} %get-tuple-element.37.p, bf16[512,192]{1,0:T(8,128)(2,1)} %get-tuple-element.38.q_at, bf16[2048,384]{1,0:T(8,128)(2,1)} %get-tuple-element.39.kv_at, ...), custom_call_target="tpu_custom_call" | custom-call | tf_op jit(solution)/shard_map/attn_backward/pallas_call | solution.py:962
  197.1 0.0 copy-done.1
  197.1 0.0 copy-start.2
  197.1 0.0 copy-start.5
  197.1 2.7 %fusion = (f32[256]{0:T(256)}, f32[256,768]{1,0:T(8,128)S(1)}) fusion(f32[128,768]{1,0:T(8,128)S(1)} %bitcast_convert_fusion, bf16[256,1024]{1,0:T(8,128)(2,1)S(1)} %copy-done.1, bf16[1024,768]{1,0:T(8,128)(2,1)} %get-tuple-element.36), kind=kOutput, calls=%fused_computation.1 | convolution fusion | flops 403046144 | bytes 3277824 | tf_op jit(solution)/shard_map/dot_general | solution.py:360
  199.8 0.0 copy-start.4
  199.8 0.0 copy-start.6
  199.8 0.0 copy-done.2
  199.8 0.8 fusion.4
  200.6 0.0 copy-done.5
  200.6 0.7 slice_reduce_fusion.3
  201.4 0.9 slice_reduce_fusion.2
  202.3 0.1 constant_dynamic-slice_fusion
  202.4 0.5 slice_bitcast_fusion
  202.9 0.7 reshape_squeeze.3
  203.6 0.1 reshape.93
  203.7 0.7 reshape.94
  204.4 0.0 copy-done.4
  204.4 0.0 slice-start
  204.5 0.7 copy.40
  205.1 0.0 copy-done.6
  205.1 0.6 copy.41
  205.7 0.0 slice-start.1
  205.7 4.9 %copy.42 = f32[1,768,1536]{2,1,0:T(8,128)} copy(f32[1,768,1536]{2,1,0:T(8,128)} %bitcast.39) | data formatting | bytes 9437184
  210.7 0.0 slice-done
  210.7 0.0 slice-done.1
  210.7 2.2 %copy.43 = f32[1,1536,768]{2,1,0:T(8,128)} copy(f32[1,1536,768]{2,1,0:T(8,128)S(1)} %bitcast.38) | data formatting | bytes 9437184
  (11 shorter events, 0.1 us)
Async XLA Ops:
  0.6 0.7 copy-start
  7.9 1.2 copy-start.3
  141.8 55.3 %copy-start.1 = (bf16[256,1024]{1,0:T(8,128)(2,1)S(1)}, bf16[256,1024]{1,0:T(8,128)(2,1)}, u32[]{:S(2)}) copy-start(bf16[256,1024]{1,0:T(8,128)(2,1)} %get-tuple-element.33.picks_at) | copy-start | bytes 1572868
  197.1 2.7 %copy-start.2 = (f32[128,768]{1,0:T(8,128)S(1)}, f32[128,768]{1,0:T(8,128)}, u32[]{:S(2)}) copy-start(f32[128,768]{1,0:T(8,128)} %get-tuple-element.35.middle_at) | copy-start | bytes 1179652
  197.1 3.5 %copy-start.5 = (f32[4,8,576]{2,1,0:T(8,128)S(1)}, f32[4,8,576]{2,1,0:T(8,128)}, u32[]{:S(2)}) copy-start(f32[4,8,576]{2,1,0:T(8,128)} %get-tuple-element.46) | copy-start | bytes 221188
  199.8 4.7 %copy-start.4 = (bf16[128,768]{1,0:T(8,128)(2,1)S(1)}, bf16[128,768]{1,0:T(8,128)(2,1)}, u32[]{:S(2)}) copy-start(bf16[128,768]{1,0:T(8,128)(2,1)} %get-tuple-element.44) | copy-start | bytes 589828
  199.8 5.3 %copy-start.6 = (f32[8,768]{1,0:T(8,128)S(1)}, f32[8,768]{1,0:T(8,128)}, u32[]{:S(2)}) copy-start(f32[8,768]{1,0:T(8,128)} %get-tuple-element.47) | copy-start | bytes 73732
  204.4 6.2 %slice-start = ((s8[4718592]{0:T(1024)(128)(4,1)}), s8[4194304]{0:T(1024)(128)(4,1)S(1)}, s32[]{:S(2)}) async-start(s8[4718592]{0:T(1024)(128)(4,1)} %bitcast.36), calls=%async_computation | async-start | bytes 8388608
  205.7 4.9 %slice-start.1 = ((s8[4718592]{0:T(1024)(128)(4,1)}), s8[524288]{0:T(1024)(128)(4,1)S(1)}, s32[]{:S(2)}) async-start(s8[4718592]{0:T(1024)(128)(4,1)} %bitcast.36), calls=%async_computation.1 | async-start | bytes 1048576
